TPU v7x, 32 devices: a whole 2x2x4 slice. The times are simulated.
32 devices in a mesh: geom: 2 (over x), op: 8 (over z, y), col: 2 (over core).
Axes of the slice: x: 2, y: 2, z: 4, core: 2. Of those that a mesh axis runs over, the one named last changes fastest.
Arguments:
- wave_coef: float32 [2048, 1024], P('geom', 'col'), parts along dimension 0, may hold values from -6 to 6
- diag_energy: float32 [2048, 1024], P('geom', 'col'), parts along dimension 0, may hold values from -4 to 4
- left_block: bfloat16 [32, 1024, 1024], P(('geom', 'op')), parts along dimension 0, may hold values from -0.1875 to 0.1875
- right_block: bfloat16 [32, 1024, 1024], P(('geom', 'op'), None, 'col'), parts along dimension 0, may hold values from -0.1875 to 0.1875
- block_mask: int32 [32, 8, 8], P(('geom', 'op')), parts along dimension 0, may hold values 0 or 1
Outputs:
- new_wave: float32 [2048, 1024], P('geom', 'col'), parts along dimension 0
There are 2 independent parts, one for each index of `geom`. A program takes and returns all parts, laid end to end along the dimension named above; each array names one. Nothing has to cross between parts.
All inputs are finite; a program needn't handle non-finite values. No bound on the sum of `block_mask` on one device may be relied on, other than what follows from the above.
Results may differ from a plain program's by a relative error of at most 0.0042.
The roundings to bfloat16 on the way count: a program that leaves them out, or rounds other values in their place, can miss the bound.
Values may be sent and summed in bfloat16 or wider, within the bound.
No kernel may reach another device: no remote copies, remote signals or barrier semaphores. Data moves between devices by JAX's collectives and lax.ppermute only.
A program may use at most 64 MiB of HBM per device.

v0:
```python
import jax
import jax.numpy as jnp
from jax import lax
from jax.sharding import PartitionSpec as P

M = 1024
STEPS = 2


def apply_mask(left_block, block_mask):
    total, width, _ = left_block.shape
    blocks = block_mask.shape[1]
    inside = width // blocks
    grid = left_block.reshape(total, blocks, inside, blocks, inside)
    keep = block_mask.astype(jnp.bfloat16)[:, :, None, :, None]
    return (grid * keep).reshape(total, width, width)


def correct(coef, sigma, diag_energy, correlation, weight, cells):
    theta = correlation / cells / (weight / cells + 1e-06)
    spacing = diag_energy - theta
    correction = (sigma - theta * coef) * spacing / jnp.maximum(spacing * spacing, 1.0)
    return coef - correction


def update_cols(coef, sigma, diag_energy, cells):
    correlation, weight = lax.psum((jnp.sum(coef * sigma), jnp.sum(coef * coef)), "col")
    moved = correct(coef, sigma, diag_energy, correlation, weight, cells)
    norm_sum = lax.psum(jnp.sum(moved * moved), "col")
    return moved * lax.rsqrt(norm_sum / cells + 1e-06)


def local(wave_coef, diag_energy, left_block, right_block, block_mask):
    masked = apply_mask(left_block, block_mask)
    cells = float(M * M)
    coef = wave_coef
    wave = wave_coef.astype(jnp.bfloat16)
    for step in range(STEPS):
        wave = coef.astype(jnp.bfloat16)
        inner = jnp.einsum(
            "mj,kjc->kmc",
            lax.all_gather(wave, "col", axis=1, tiled=True),
            right_block,
            preferred_element_type=jnp.float32,
        ).astype(jnp.bfloat16)
        partial_sum = jnp.einsum("kab,kbc->ac", masked, inner, preferred_element_type=jnp.float32)
        sigma = lax.psum(partial_sum, "op")
        coef = update_cols(coef, sigma, diag_energy, cells)
    return coef


def solution(mesh):
    in_specs = (
        P("geom", "col"),
        P("geom", "col"),
        P(("geom", "op"), None, None),
        P(("geom", "op"), None, "col"),
        P(("geom", "op"), None, None),
    )
    out_specs = P("geom", "col")
    return jax.shard_map(local, mesh=mesh, in_specs=in_specs, out_specs=out_specs, check_vma=False)
```

profile of v0, /device:TPU:0, one launch (start us, length us, event | category | flops | bytes accessed | tf_op | source)
XLA Modules:
  0.0 309.6 jit_solution(6017176165767036142)
XLA Ops:
  6.5 0.0 copy-start
  6.5 0.0 copy-start.1
  6.5 0.0 all-gather.3.cloned.1.call-start
  6.5 2.9 convert_element_type.22
  9.4 0.0 all-gather.3.cloned.1.call-update
  9.4 0.0 all-reduce.5.cloned.1.call-start
  9.5 0.0 copy-done.1
  9.5 2.5 mul.65
  12.0 7.4 %mul.66 = bf16[2,1024,1024]{2,1,0:T(8,128)(2,1)} reshape(bf16[2,8,128,8,128]{4,3,2,1,0:T(8,128)(2,1)} %mul.65) | data formatting | bytes 8388608 | tf_op jit(solution)/shard_map/mul | solution.py:16
  19.4 8.0 %mul.67 = bf16[2,1024,1024]{2,1,0:T(8,128)(2,1)} multiply(bf16[2,1024,1024]{2,1,0:T(8,128)(2,1)} %param.7, bf16[2,1024,1024]{2,1,0:T(8,128)(2,1)} %mul.66) | non-fusion elementwise | flops 2097152 | bytes 12582912 | tf_op jit(solution)/shard_map/mul | solution.py:16
  27.5 0.0 all-gather.3.cloned.1.call-done
  27.5 0.0 copy-done
  27.5 8.7 %fusion.10 = f32[1024,512]{1,0:T(8,128)} fusion(bf16[2,1024,1024]{2,1,0:T(8,128)(2,1)} %mul.67, bf16[2,1024,512]{2,1,0:T(8,128)(2,1)S(1)} %copy-done, bf16[1024,1024]{1,0:T(8,128)(2,1)} %all-gather.3.cloned.1.call-done), kind=kOutput, calls=%fused_computation.19 | convolution fusion | flops 4296015872 | bytes 10485760 | tf_op jit(solution)/shard_map/kab,kbc->ac/dot_general | solution.py:46
  36.1 0.0 all-reduce.5.cloned.1.call-update
  36.2 0.0 all-gather.5.cloned.1.call-start
  36.2 104.2 %all-reduce.5.cloned.1.call-done = f32[1024,512]{1,0:T(8,128)} async-done(((f32[1024,512]{1,0:T(8,128)}), f32[1024,512]{1,0:T(8,128)}) %all-reduce.5.cloned.1.call-update) | async-done | bytes 2097168 | tf_op jit(solution)/shard_map/psum | solution.py:47
  140.4 3.4 %multiply_reduce_fusion.4 = (f32[]{:T(128)}, f32[]{:T(128)}) fusion(f32[1024,512]{1,0:T(8,128)} %param.5, f32[1024,512]{1,0:T(8,128)} %all-reduce.5.cloned.1.call-done), kind=kLoop, calls=%fused_computation.15 | loop fusion | flops 2097150 | bytes 4194312 | tf_op jit(solution)/shard_map/reduce_sum | solution.py:27
  143.8 3.1 %all-reduce.1 = (f32[]{:T(128)}, f32[]{:T(128)}) all-reduce(f32[]{:T(128)} %get-tuple-element.8, f32[]{:T(128)} %get-tuple-element.7), channel_id=1, replica_groups=mesh['geom'=2,'op'=8,'col'=2] {'col'}, use_global_device_ids=true, to_apply=%region_2.0 | all-reduce | flops 2 | bytes 16 | tf_op jit(solution)/shard_map/psum | solution.py:27
  148.2 5.6 %multiply_reduce_fusion.3 = (f32[]{:T(128)}, f32[1024,512]{1,0:T(8,128)}) fusion(f32[1024,512]{1,0:T(8,128)} %param.5, f32[1024,512]{1,0:T(8,128)} %param.6, f32[1024,512]{1,0:T(8,128)} %all-reduce.5.cloned.1.call-done, f32[]{:T(128)S(6)} %div.32), kind=kLoop, calls=%fused_computation.13 | loop fusion | flops 5242879 | bytes 8388616 | tf_op jit(solution)/shard_map/reduce_sum | solution.py:29
  153.8 3.1 %psum.59 = f32[]{:T(128)} all-reduce(f32[]{:T(128)} %get-tuple-element.15), channel_id=1, replica_groups=mesh['geom'=2,'op'=8,'col'=2] {'col'}, use_global_device_ids=true, to_apply=%region_6.0 | all-reduce | flops 1 | bytes 8 | tf_op jit(solution)/shard_map/psum | solution.py:29
  157.6 2.8 multiply_convert_fusion
  160.4 0.0 all-gather.5.cloned.1.call-update
  160.4 0.0 all-reduce.7.cloned.1.call-start
  160.5 10.4 %all-gather.5.cloned.1.call-done = bf16[1024,1024]{1,0:T(8,128)(2,1)} async-done(((bf16[1024,512]{1,0:T(8,128)(2,1)}), bf16[1024,1024]{1,0:T(8,128)(2,1)}) %all-gather.5.cloned.1.call-update) | async-done | bytes 2097168 | tf_op jit(solution)/shard_map/all_gather | solution.py:42
  170.9 8.6 %fusion.13 = f32[1024,512]{1,0:T(8,128)} fusion(bf16[2,1024,1024]{2,1,0:T(8,128)(2,1)} %mul.67, bf16[2,1024,512]{2,1,0:T(8,128)(2,1)S(1)} %copy-done, bf16[1024,1024]{1,0:T(8,128)(2,1)} %all-gather.5.cloned.1.call-done), kind=kOutput, calls=%fused_computation.20 | convolution fusion | flops 4296015872 | bytes 10485760 | tf_op jit(solution)/shard_map/kab,kbc->ac/dot_general | solution.py:46
  179.6 0.0 all-reduce.7.cloned.1.call-update
  179.6 103.2 %all-reduce.7.cloned.1.call-done = f32[1024,512]{1,0:T(8,128)} async-done(((f32[1024,512]{1,0:T(8,128)}), f32[1024,512]{1,0:T(8,128)}) %all-reduce.7.cloned.1.call-update) | async-done | bytes 2097168 | tf_op jit(solution)/shard_map/psum | solution.py:47
  282.8 3.4 %multiply_reduce_fusion.1 = (f32[]{:T(128)}, f32[]{:T(128)}) fusion(f32[1024,512]{1,0:T(8,128)} %get-tuple-element.16, f32[]{:T(128)S(6)} %rsqrt.6, f32[1024,512]{1,0:T(8,128)} %all-reduce.7.cloned.1.call-done), kind=kLoop, calls=%fused_computation.10 | loop fusion | flops 2621438 | bytes 4194316 | tf_op jit(solution)/shard_map/reduce_sum | solution.py:27
  286.2 3.1 all-reduce
  290.4 5.6 %multiply_reduce_fusion = (f32[]{:T(128)}, f32[1024,512]{1,0:T(8,128)}) fusion(f32[1024,512]{1,0:T(8,128)} %param.6, f32[1024,512]{1,0:T(8,128)} %all-reduce.7.cloned.1.call-done, f32[]{:T(128)S(6)} %div.37, f32[1024,512]{1,0:T(8,128)} %get-tuple-element.16, f32[]{:T(128)S(6)} %rsqrt.6), kind=kLoop, calls=%fused_computation.8 | loop fusion | flops 5767167 | bytes 8388620 | tf_op jit(solution)/shard_map/reduce_sum | solution.py:29
  296.1 3.2 %psum.63 = f32[]{:T(128)} all-reduce(f32[]{:T(128)} %get-tuple-element.13), channel_id=1, replica_groups=mesh['geom'=2,'op'=8,'col'=2] {'col'}, use_global_device_ids=true, to_apply=%region_13.0 | all-reduce | flops 1 | bytes 8 | tf_op jit(solution)/shard_map/psum | solution.py:29
  300.0 3.1 %broadcast_multiply_fusion = f32[1024,512]{1,0:T(8,128)} fusion(f32[1024,512]{1,0:T(8,128)} %get-tuple-element.14, f32[]{:T(128)S(6)} %rsqrt.7), kind=kLoop, calls=%fused_computation.21 | loop fusion | flops 524288 | bytes 4194308 | tf_op jit(solution)/shard_map/mul | solution.py:30
  (1 shorter events, 0.0 us)
Async XLA Ops:
  6.5 20.9 %copy-start = (bf16[2,1024,512]{2,1,0:T(8,128)(2,1)S(1)}, bf16[2,1024,512]{2,1,0:T(8,128)(2,1)}, u32[]{:S(2)}) copy-start(bf16[2,1024,512]{2,1,0:T(8,128)(2,1)} %param.8) | copy-start | bytes 6291460
  6.5 2.9 copy-start.1
  6.5 20.9 %all-gather.3.cloned.1.call-start = ((), (), s32[]{:S(2)}) async-start(), calls=%async_computation | async-start | bytes 3145728 | tf_op jit(solution)/shard_map/all_gather | solution.py:42
  9.4 131.0 %all-reduce.5.cloned.1.call-start = ((), (), s32[]{:S(2)}) async-start(), calls=%async_computation.1 | async-start | bytes 4194304 | tf_op jit(solution)/shard_map/psum | solution.py:47
  36.2 134.7 %all-gather.5.cloned.1.call-start = ((), (), s32[]{:S(2)}) async-start(), calls=%async_computation.2 | async-start | bytes 3145728 | tf_op jit(solution)/shard_map/all_gather | solution.py:42
  160.4 122.3 %all-reduce.7.cloned.1.call-start = ((), (), s32[]{:S(2)}) async-start(), calls=%async_computation.3 | async-start | bytes 4194304 | tf_op jit(solution)/shard_map/psum | solution.py:47
Sparse Core Ops, SparseCore 0:
  9.5 13.2 all-gather.2
  36.3 104.1 all-reduce.4
  160.6 10.2 all-gather.4
  179.7 103.0 all-reduce.6
where the time goes:
time: 310 us
  waiting for transfers between devices  218 us (70%)
  other arithmetic  34.9 us (11%)
  matrix products  17.3 us (6%)
  between operations  17 us (5%)
  blocking collectives  12.5 us (4%)
  local copies, waits for them, and re-layouts  9.93 us (3%)
    psum x2, waiting for transfers between devices, local(): sigma = lax.psum(partial_sum, 'op')  207 us
    dot_general x2, matrix products, local(): jnp.einsum('kab,kbc->ac', masked, inner, preferred_element_type=jnp.float32)  17.3 us
    reduce_sum x2, other arithmetic, update_cols(): norm_sum = lax.psum(jnp.sum(moved * moved), 'col')  11.2 us
    all_gather x2, waiting for transfers between devices, local(): lax.all_gather(wave, 'col', axis=1, tiled=True)  10.4 us
    mul x2, local copies, waits for them, and re-layouts, apply_mask(): return (grid * keep).reshape(total, width, width)  9.92 us
    mul x1, other arithmetic, apply_mask(): return (grid * keep).reshape(total, width, width)  8.04 us
    reduce_sum x2, other arithmetic, update_cols(): jnp.sum(coef * coef)  6.78 us
    psum x2, blocking collectives, update_cols(): norm_sum = lax.psum(jnp.sum(moved * moved), 'col')  6.27 us
  transfers between devices with their start and end apart: 4, of which 3 were waited for; matrix products, arithmetic and copies ran while one was open for 6% of the time, Pallas kernels for 0%

commit v1 on v0

v1 whole, which is shorter than its diff:
```python
import functools

import jax
import jax.numpy as jnp
from jax import lax
from jax.experimental import pallas as pl
from jax.experimental.pallas import tpu as pltpu
from jax.sharding import PartitionSpec as P

STEPS = 2
EPS = 1e-06
TOP = 0.1875
BOTH = ("op", "col")


def any_spec():
    return pl.BlockSpec(memory_space=pl.ANY)


def smem_spec():
    return pl.BlockSpec(memory_space=pltpu.SMEM)


def load(src, dst, sem):
    copy = pltpu.make_async_copy(src, dst, sem)
    copy.start()
    return copy


def mask_rows(mask_ref, left_ref, masked_ref, blocks, first):
    pairs, rows, width = left_ref.shape
    inside = width // blocks
    for k in range(pairs):
        for i in range(rows // inside):
            for j in range(blocks):
                keep = mask_ref[k * blocks * blocks + (first + i) * blocks + j]
                block = left_ref[k, i * inside:(i + 1) * inside, j * inside:(j + 1) * inside]
                masked_ref[i * inside:(i + 1) * inside, k * width + j * inside:k * width + (j + 1) * inside] = (
                    jnp.where(keep != 0, block, jnp.zeros_like(block)))


def first_kernel(count, blocks, place_ref, mask_ref, *refs):
    pieces, (right_ref, left_ref, inner_out, send_out, wave, right, left, inner, masked, sems, out_sem) = (
        refs[:count], refs[count:])
    pairs, width, cols = right.shape
    rows = left.shape[1]
    first = pl.multiple_of(place_ref[0], rows)
    got = []
    for p, piece in enumerate(pieces):
        at = (pl.ds(pl.multiple_of(place_ref[1 + 2 * p], piece.shape[0]), piece.shape[0]),
              pl.ds(pl.multiple_of(place_ref[2 + 2 * p], cols), cols))
        got.append(load(piece, wave.at[at], sems.at[p]))
    rights = [load(right_ref.at[k], right.at[k], sems.at[count + k]) for k in range(pairs)]
    lefts = [load(left_ref.at[k, pl.ds(first, rows)], left.at[k], sems.at[count + pairs + k]) for k in range(pairs)]
    for copy in got:
        copy.wait()
    for k in range(pairs):
        rights[k].wait()
        for r in range(width // rows):
            inner[k * width + r * rows:k * width + (r + 1) * rows, :] = jnp.dot(
                wave[r * rows:(r + 1) * rows, :], right[k], preferred_element_type=jnp.float32).astype(jnp.bfloat16)
    out = load(inner, inner_out, out_sem)
    for copy in lefts:
        copy.wait()
    mask_rows(mask_ref, left, masked, blocks, place_ref[0] // (width // blocks))
    send_out[...] = jnp.dot(masked[...], inner[...], preferred_element_type=jnp.float32)
    out.wait()


def second_kernel(count, blocks, place_ref, mask_ref, *refs):
    pieces, (send_ref, inner_ref, left_ref, keep_out, corr_out, own, send, left, inner, masked, sems) = (
        refs[:count], refs[count:])
    pairs, rows, width = left.shape
    kept = pl.multiple_of(rows - place_ref[0], rows)
    got = [load(inner_ref, inner, sems.at[0])]
    lefts = [load(left_ref.at[k, pl.ds(kept, rows)], left.at[k], sems.at[1 + k]) for k in range(pairs)]
    got.append(load(send_ref, send, sems.at[1 + pairs]))
    for p, piece in enumerate(pieces):
        at = pl.ds(pl.multiple_of(place_ref[1 + 2 * p], piece.shape[0]), piece.shape[0])
        got.append(load(piece, own.at[at], sems.at[2 + pairs + p]))
    for copy in lefts:
        copy.wait()
    mask_rows(mask_ref, left, masked, blocks, (rows - place_ref[0]) // (width // blocks))
    for copy in got:
        copy.wait()
    keep_out[...] = jnp.dot(masked[...], inner[...], preferred_element_type=jnp.float32)
    first = pl.multiple_of(place_ref[0], rows)
    product = (own[pl.ds(first, rows), :].astype(jnp.float32) * send[...]
               + own[pl.ds(kept, rows), :].astype(jnp.float32) * keep_out[...])
    corr_out[...] = jnp.full(corr_out.shape, jnp.sum(product), jnp.float32)


def sigma_halves(place, mask, own, other, right, left, blocks):
    pairs, width, cols = right.shape
    half = width // 2
    sds = jax.ShapeDtypeStruct
    bf16, f32 = jnp.bfloat16, jnp.float32
    pieces = [p.astype(bf16) for p in own] + other
    flops = 2 * pairs * width * cols
    vmem = pltpu.CompilerParams(vmem_limit_bytes=32 * 2 ** 20)
    inner, send = pl.pallas_call(
        functools.partial(first_kernel, len(pieces), blocks),
        out_shape=(sds((pairs * width, cols), bf16), sds((half, cols), f32)),
        in_specs=[smem_spec(), smem_spec()] + [any_spec()] * (len(pieces) + 2),
        out_specs=(any_spec(), pl.BlockSpec(memory_space=pltpu.VMEM)),
        scratch_shapes=[
            pltpu.VMEM((width, width), bf16),
            pltpu.VMEM((pairs, width, cols), bf16),
            pltpu.VMEM((pairs, half, width), bf16),
            pltpu.VMEM((pairs * width, cols), bf16),
            pltpu.VMEM((half, pairs * width), bf16),
            pltpu.SemaphoreType.DMA((len(pieces) + 2 * pairs,)),
            pltpu.SemaphoreType.DMA(()),
        ],
        compiler_params=vmem,
        cost_estimate=pl.CostEstimate(flops=flops * (width + half), bytes_accessed=8 * 2 ** 20, transcendentals=0),
        name="inner_and_sent_half",
    )(place, mask, *pieces, right, left)
    return inner, send


def sigma_kept(place, mask, own, send, inner, left, blocks):
    pairs, width, _ = left.shape
    half, cols = send.shape
    sds = jax.ShapeDtypeStruct
    bf16, f32 = jnp.bfloat16, jnp.float32
    return pl.pallas_call(
        functools.partial(second_kernel, len(own), blocks),
        out_shape=(sds((half, cols), f32), sds((8, 128), f32)),
        in_specs=[smem_spec(), smem_spec()] + [any_spec()] * (len(own) + 3),
        out_specs=(pl.BlockSpec(memory_space=pltpu.VMEM), pl.BlockSpec(memory_space=pltpu.VMEM)),
        scratch_shapes=[
            pltpu.VMEM((width, cols), own[0].dtype),
            pltpu.VMEM((half, cols), f32),
            pltpu.VMEM((pairs, half, width), bf16),
            pltpu.VMEM((pairs * width, cols), bf16),
            pltpu.VMEM((half, pairs * width), bf16),
            pltpu.SemaphoreType.DMA((len(own) + 2 + pairs,)),
        ],
        compiler_params=pltpu.CompilerParams(vmem_limit_bytes=32 * 2 ** 20),
        cost_estimate=pl.CostEstimate(
            flops=2 * pairs * width * cols * half, bytes_accessed=8 * 2 ** 20, transcendentals=0),
        name="kept_half",
    )(place, mask, *own, send, inner, left)


def local(ops, cols, wave_coef, diag_energy, left, right, block_mask):
    f32, f16, bf16 = jnp.float32, jnp.float16, jnp.bfloat16
    pairs, width, _ = left.shape
    own_cols = right.shape[2]
    blocks = block_mask.shape[1]
    cells = float(width * width)
    half, quarter = width // 2, width // 4
    me, core = lax.axis_index("op"), lax.axis_index("col")
    order = ((1, 2), (2, 1))

    def swap(x, stage):
        pairing = []
        for o in range(ops):
            for c in range(cols):
                bit = order[c % 2][stage] if stage < 2 else 1 << stage
                pairing.append((o * cols + c, (o ^ bit) * cols + c))
        return lax.ppermute(x, BOTH, pairing)

    def across(x):
        return lax.ppermute(x, "col", [(c, c ^ 1) for c in range(cols)])

    stages = ops.bit_length() - 1
    low, high = me % 2, (me // 2) % 2

    def bits(c):
        return jnp.where(c == 0, low, high), jnp.where(c == 0, high, low)

    bit0, bit1 = bits(core)
    there0, there1 = bits(1 - core)
    row = bit0 * half + bit1 * quarter
    zero = jnp.zeros((), jnp.int32)

    def quarters(b0, b1):
        return [b0 * half + b1 * quarter, b0 * half + (1 - b1) * quarter,
                (1 - b0) * half + b1 * quarter, (1 - b0) * half + (1 - b1) * quarter]

    sent = (1 - bit0) * half
    mask = block_mask.reshape(-1)
    diag = lax.dynamic_slice(diag_energy, (row, zero), (quarter, own_cols))
    coef = lax.dynamic_slice(wave_coef, (row, zero), (quarter, own_cols))

    reach = float(pairs * ops * width) * TOP * TOP

    own = [wave_coef]
    wave = wave_coef.astype(bf16)
    other = [across(wave)]
    weight = jnp.sum(wave_coef * wave_coef)
    weight = weight + across(weight)
    norm = jnp.ones((), f32)
    for step in range(STEPS):
        if step == 0:
            place = [sent, zero, core * own_cols, zero, (1 - core) * own_cols]
        else:
            place = [sent]
            for c, (b0, b1) in ((core, (bit0, bit1)), (1 - core, (there0, there1))):
                for first in quarters(b0, b1):
                    place += [first, c * own_cols]
        place = jnp.stack(place).astype(jnp.int32)
        inner, send = sigma_halves(place, mask, own, other, right, left, blocks)
        length = jnp.sqrt(weight) + 1e-30
        scale = 32768.0 / (reach * length)
        got = swap((send * scale).astype(f16), 0)
        keep, corr = sigma_kept(place, mask, own, send, inner, left, blocks)
        corr = corr + across(corr)
        corr = corr + swap(corr, 0)
        keep = keep * scale + got.astype(f32)
        send = lax.dynamic_slice(keep, ((1 - bit1) * quarter, zero), (quarter, own_cols)).astype(f16)
        keep = lax.dynamic_slice(keep, (bit1 * quarter, zero), (quarter, own_cols))
        got = swap(send, 1)
        corr = corr + swap(corr, 1)
        keep = keep + got.astype(f32)
        for stage in range(2, stages):
            send = keep.astype(f16)
            got = swap(send, stage)
            corr = corr + swap(corr, stage)
            keep = send.astype(f32) + got.astype(f32)
        sigma = keep * (norm / scale)
        square = norm * norm
        theta = (corr[0, 0] * square / cells) / (weight * square / cells + EPS)
        spacing = diag - theta
        correction = (sigma - theta * coef) * spacing / jnp.maximum(spacing * spacing, 1.0)
        moved = coef - correction
        last = step == STEPS - 1
        if last:
            shrink = 32768.0 / ((1.0 + jnp.abs(theta) + reach) * (length * norm))
            moved = moved * shrink
            piece = moved.astype(f16)
        else:
            piece = moved.astype(bf16)
        weight = jnp.full((8, 128), jnp.sum(moved * moved), f32)
        p1 = swap(piece, 1)
        p2 = swap(piece, 0)
        p3 = swap(p1, 0)
        weight = weight + across(weight)
        weight = weight + swap(weight, 1)
        weight = (weight + swap(weight, 0))[0, 0]
        if not last:
            norm = lax.rsqrt(weight / cells + EPS)
            coef = moved * norm
            own = [piece, p1, p2, p3]
            other = [across(p) for p in own]
        else:
            norm = lax.rsqrt(weight / cells + EPS * shrink * shrink)
            near0, near1 = jnp.where(bit1 == 0, piece, p1), jnp.where(bit1 == 0, p1, piece)
            far0, far1 = jnp.where(bit1 == 0, p2, p3), jnp.where(bit1 == 0, p3, p2)
            full = jnp.concatenate([
                jnp.where(bit0 == 0, near0, far0), jnp.where(bit0 == 0, near1, far1),
                jnp.where(bit0 == 0, far0, near0), jnp.where(bit0 == 0, far1, near1)], axis=0)
            return full.astype(f32) * norm


def solution(mesh):
    in_specs = (
        P("geom", "col"),
        P("geom", "col"),
        P(("geom", "op"), None, None),
        P(("geom", "op"), None, "col"),
        P(("geom", "op"), None, None),
    )
    body = functools.partial(local, mesh.shape["op"], mesh.shape["col"])
    return jax.shard_map(body, mesh=mesh, in_specs=in_specs, out_specs=P("geom", "col"), check_vma=False)
```

time: 310 us -> 151 us (0.49)
  waiting for transfers between devices: 218 us -> 55.4 us
  starting transfers between devices: 0.13 us -> 35.4 us
  other arithmetic: 34.9 us -> 15.8 us
  matrix products: 17.3 us -> 0 us
  Pallas kernels: 0 us -> 16.8 us
  blocking collectives: 12.5 us -> 0 us
  between operations: 17 us -> 5.86 us
  local copies, waits for them, and re-layouts: 9.93 us -> 20.8 us
    psum x2 -> x0, waiting for transfers between devices: 207 us -> none  [local(): sigma = lax.psum(partial_sum, 'op')]
    ppermute x0 -> x32, waiting for transfers between devices: none -> 55.4 us  [the longest x22 51.8 us: swap(): return lax.ppermute(x, BOTH, pairing)]
    ppermute x0 -> x32, starting transfers between devices: none -> 35.4 us  [the longest x22 33.7 us: swap(): return lax.ppermute(x, BOTH, pairing)]
    dot_general x2 -> x0, matrix products: 17.3 us -> none  [local(): jnp.einsum('kab,kbc->ac', masked, inner, preferred_element_type=jnp.float32)]
    unnamed x4 -> x28, local copies, waits for them, and re-layouts: 0.01 us -> 17.1 us
    pallas_call x0 -> x4, Pallas kernels: none -> 16.8 us  [the longest x2 10.2 us: sigma_halves(): pl.pallas_call(functools.partial(first_kernel, len(pieces), blocks), out_...]
    psum x4 -> x0, blocking collectives: 12.5 us -> none  [the longest x2 6.27 us: update_cols(): norm_sum = lax.psum(jnp.sum(moved * moved), 'col')]
    reduce_sum x4 -> x3, other arithmetic: 18 us -> 7.41 us  [the longest x2 3.97 us: local(): weight = jnp.full((8, 128), jnp.sum(moved * moved), f32)]
  transfers between devices with their start and end apart: 4 -> 32, of which waited for: 3 -> 20; matrix products, arithmetic and copies ran while one was open for 6% -> 4% of each run, Pallas kernels for 0% -> 4%
where the time goes in v1:
time: 151 us; the launch traced here: 150 us
  waiting for transfers between devices  55.4 us (37%)
  starting transfers between devices  35.4 us (23%)
  local copies, waits for them, and re-layouts  20.8 us (14%)
  Pallas kernels  16.8 us (11%)
  other arithmetic  15.8 us (10%)
  between operations  5.86 us (4%)
    ppermute x22, waiting for transfers between devices, swap(): return lax.ppermute(x, BOTH, pairing)  51.8 us
    ppermute x22, starting transfers between devices, swap(): return lax.ppermute(x, BOTH, pairing)  33.7 us
    unnamed x28, local copies, waits for them, and re-layouts  17.1 us
    pallas_call x2, Pallas kernels, sigma_halves(): pl.pallas_call(functools.partial(first_kernel, len(pieces), blocks), out_...  10.2 us
    pallas_call x2, Pallas kernels, sigma_kept(): pl.pallas_call(functools.partial(second_kernel, len(own), blocks), out_sh...  6.57 us
    reduce_sum x2, other arithmetic, local(): weight = jnp.full((8, 128), jnp.sum(moved * moved), f32)  3.97 us
    ppermute x10, waiting for transfers between devices, across(): return lax.ppermute(x, 'col', [(c, c ^ 1) for c in range(cols)])  3.62 us
    reduce_sum x1, other arithmetic, local(): weight = jnp.sum(wave_coef * wave_coef)  3.44 us
  transfers between devices with their start and end apart: 32, of which 20 were waited for; matrix products, arithmetic and copies ran while one was open for 4% of the time, Pallas kernels for 4%

profile of v1, /device:TPU:0, one launch (start us, length us, event | category | flops | bytes accessed | tf_op | source)
XLA Modules:
  0.0 150.0 jit_solution(7697802504957574592)
XLA Ops:
  0.0 3.4 %multiply_reduce_fusion = (f32[]{:T(128)}, bf16[1024,512]{1,0:T(8,128)(2,1)S(1)}) fusion(f32[1024,512]{1,0:T(8,128)} %refs_0_.1), kind=kLoop, calls=%fused_computation.1 | loop fusion | flops 1572863 | bytes 3145732 | tf_op jit(solution)/shard_map/reduce_sum | solution.py:193
  3.9 1.0 copy-done.7
  5.1 1.3 collective-permute-done.1
  7.7 1.0 copy-done.11
  8.7 2.2 %copy-done = bf16[2,1024,1024]{2,1,0:T(8,128)(2,1)S(1)} copy-done((bf16[2,1024,1024]{2,1,0:T(8,128)(2,1)S(1)}, bf16[2,1024,1024]{2,1,0:T(8,128)(2,1)}, u32[]{:S(2)}) %copy-start) | copy-done | bytes 4194328
  10.9 1.2 copy-done.8
  12.1 1.6 %copy-done.9 = bf16[2,1024,512]{2,1,0:T(8,128)(2,1)S(1)} copy-done((bf16[2,1024,512]{2,1,0:T(8,128)(2,1)S(1)}, bf16[2,1024,512]{2,1,0:T(8,128)(2,1)}, u32[]{:S(2)}) %copy-start.9) | copy-done | bytes 2097176
  13.7 1.2 copy-done.12
  14.9 5.2 %inner_and_sent_half.2 = (bf16[2048,512]{1,0:T(8,128)(2,1)S(1)}, f32[512,512]{1,0:T(8,128)S(1)}) custom-call(s32[5]{0:T(128)S(1)} %stack.51.place_ref, s32[128]{0:T(128)S(1)} %reshape.7.mask_ref, bf16[1024,512]{1,0:T(8,128)(2,1)S(1)} %copy-done.8, bf16[1024,512]{1,0:T(8,128)(2,1)S(1)} %copy-done.12, bf16[2,1024,512]{2,1,0:T(8,128)(2,1)S(1)} %copy-done.9, ...), custom_call_target="tpu_custom_call" | custom-call | flops 3221225472 | bytes 8388608 | tf_op jit(solution)/shard_map/inner_and_sent_half/pallas_call | solution.py:101
  20.1 1.3 copy-done.5
  21.4 0.9 multiply_convert_fusion.1
  22.3 2.8 %collective-permute-start.2 = (f16[512,512]{1,0:T(8,128)(2,1)}, f16[512,512]{1,0:T(8,128)(2,1)}, u32[]{:S(2)}, u32[]{:S(2)}) collective-permute-start(f16[512,512]{1,0:T(8,128)(2,1)} %multiply_convert_fusion.1), channel_id=1, source_target_pairs={{0,2},{1,5},{2,0},{3,7},{4,6},{5,1},{6,4},{7,3},{8,10},{9,13},{10,... | collective-permute-start | bytes 1572872 | tf_op jit(solution)/shard_map/ppermute | solution.py:163
  25.2 2.2 %copy-done.1 = bf16[2,1024,1024]{2,1,0:T(8,128)(2,1)S(1)} copy-done((bf16[2,1024,1024]{2,1,0:T(8,128)(2,1)S(1)}, bf16[2,1024,1024]{2,1,0:T(8,128)(2,1)}, u32[]{:S(2)}) %copy-start.1) | copy-done | bytes 4194328
  27.4 1.6 %copy-done.6 = bf16[2048,512]{1,0:T(8,128)(2,1)S(1)} copy-done((bf16[2048,512]{1,0:T(8,128)(2,1)S(1)}, bf16[2048,512]{1,0:T(8,128)(2,1)}, u32[]{:S(2)}) %copy-start.6) | copy-done | bytes 2097176
  29.0 3.2 %kept_half.2 = (f32[512,512]{1,0:T(8,128)S(1)}, f32[8,128]{1,0:T(8,128)S(1)}) custom-call(s32[5]{0:T(128)S(1)} %stack.51.place_ref, s32[128]{0:T(128)S(1)} %reshape.7.mask_ref, f32[1024,512]{1,0:T(8,128)S(1)} %copy-done.4, f32[512,512]{1,0:T(8,128)S(1)} %get-tuple-element.13.refs_1_, bf16[2048,512]{1,0:T(8,128)(2,1)S(1)} %copy-done.6, ...), custom_call_target="tpu_custom_call" | custom-call | flops 1073741824 | bytes 8388608 | tf_op jit(solution)/shard_map/kept_half/pallas_call | solution.py:127
  32.7 1.2 convert_add_fusion.1
  33.9 2.1 %collective-permute-start.3 = (f16[256,512]{1,0:T(8,128)(2,1)S(1)}, f16[256,512]{1,0:T(8,128)(2,1)}, u32[]{:S(2)}, u32[]{:S(2)}) collective-permute-start(f16[256,512]{1,0:T(8,128)(2,1)S(1)} %dynamic-slice_convert_fusion.1), channel_id=1, source_target_pairs={{0,4},{1,3},{2,6},{3,1},{4,0},{5,7},{6,2},{7,5},{8,12},{9,11},{10,... | collective-permute-start | bytes 786440 | tf_op jit(solution)/shard_map/ppermute | solution.py:163
  36.1 4.5 %collective-permute-done.3 = f16[256,512]{1,0:T(8,128)(2,1)} collective-permute-done((f16[256,512]{1,0:T(8,128)(2,1)S(1)}, f16[256,512]{1,0:T(8,128)(2,1)}, u32[]{:S(2)}, u32[]{:S(2)}) %collective-permute-start.3) | collective-permute-done | bytes 262176 | tf_op jit(solution)/shard_map/ppermute | solution.py:163
  40.6 1.0 add_convert_fusion.1
  41.6 3.1 %collective-permute-start.4 = (f16[256,512]{1,0:T(8,128)(2,1)S(1)}, f16[256,512]{1,0:T(8,128)(2,1)S(1)}, u32[]{:S(2)}, u32[]{:S(2)}) collective-permute-start(f16[256,512]{1,0:T(8,128)(2,1)S(1)} %add_convert_fusion.1), channel_id=1, source_target_pairs={{0,8},{1,9},{2,10},{3,11},{4,12},{5,13},{6,14},{7,15},{8,0},{9,1},... | collective-permute-start | bytes 786440 | tf_op jit(solution)/shard_map/ppermute | solution.py:163
  44.7 1.2 collective-permute-done.5
  45.9 1.5 %collective-permute-start.6 = (f32[8,128]{1,0:T(8,128)S(1)}, f32[8,128]{1,0:T(8,128)S(1)}, u32[]{:S(2)}, u32[]{:S(2)}) collective-permute-start(f32[8,128]{1,0:T(8,128)S(1)} %add.143), channel_id=1, source_target_pairs={{0,2},{1,5},{2,0},{3,7},{4,6},{5,1},{6,4},{7,3},{8,10},{9,13},{10,... | collective-permute-start | bytes 12296 | tf_op jit(solution)/shard_map/ppermute | solution.py:163
  47.4 2.1 %collective-permute-done.6 = f32[8,128]{1,0:T(8,128)S(1)} collective-permute-done((f32[8,128]{1,0:T(8,128)S(1)}, f32[8,128]{1,0:T(8,128)S(1)}, u32[]{:S(2)}, u32[]{:S(2)}) %collective-permute-start.6) | collective-permute-done | bytes 4128 | tf_op jit(solution)/shard_map/ppermute | solution.py:163
  49.5 1.6 %collective-permute-start.7 = (f32[8,128]{1,0:T(8,128)S(1)}, f32[8,128]{1,0:T(8,128)S(1)}, u32[]{:S(2)}, u32[]{:S(2)}) collective-permute-start(f32[8,128]{1,0:T(8,128)S(1)} %add.144), channel_id=1, source_target_pairs={{0,4},{1,3},{2,6},{3,1},{4,0},{5,7},{6,2},{7,5},{8,12},{9,11},{10,... | collective-permute-start | bytes 12296 | tf_op jit(solution)/shard_map/ppermute | solution.py:163
  51.0 2.4 %collective-permute-done.7 = f32[8,128]{1,0:T(8,128)S(1)} collective-permute-done((f32[8,128]{1,0:T(8,128)S(1)}, f32[8,128]{1,0:T(8,128)S(1)}, u32[]{:S(2)}, u32[]{:S(2)}) %collective-permute-start.7) | collective-permute-done | bytes 4128 | tf_op jit(solution)/shard_map/ppermute | solution.py:163
  53.5 4.5 %collective-permute-done.8 = f32[8,128]{1,0:T(8,128)S(1)} collective-permute-done((f32[8,128]{1,0:T(8,128)S(1)}, f32[8,128]{1,0:T(8,128)S(1)}, u32[]{:S(2)}, u32[]{:S(2)}) %collective-permute-start.8) | collective-permute-done | bytes 4128 | tf_op jit(solution)/shard_map/ppermute | solution.py:163
  59.3 2.0 %multiply_reduce_fusion.2 = (f32[]{:T(128)}, f32[256,512]{1,0:T(8,128)S(1)}) fusion(f32[1024,512]{1,0:T(8,128)} %param.6, s32[]{:T(128)S(6)} %select_n.84, f32[]{:T(128)S(6)} %div.65, f32[]{:T(128)S(6)} %div.61, f16[256,512]{1,0:T(8,128)(2,1)S(1)} %collective-permute-done.4, f16[256,512]{1,0:T(8,128)(2,1)S(1)} %add_convert_fusion.1, f32[1024,512]{1,0:T(8,128)S(1)} %copy-done.4), kind=kLoop, calls=%fused_computation.10 | loop fusion | flops 1835007 | bytes 2097168 | tf_op jit(solution)/shard_map/reduce_sum | solution.py:236
  61.3 1.2 collective-permute-start.12
  62.6 1.5 %collective-permute-start.13 = (bf16[256,512]{1,0:T(8,128)(2,1)S(1)}, bf16[256,512]{1,0:T(8,128)(2,1)S(1)}, u32[]{:S(2)}, u32[]{:S(2)}) collective-permute-start(bf16[256,512]{1,0:T(8,128)(2,1)S(1)} %convert_element_type.63.refs_0_), channel_id=1, source_target_pairs={{0,2},{1,5},{2,0},{3,7},{4,6},{5,1},{6,4},{7,3},{8,10},{9,13},{10,... | collective-permute-start | bytes 786440 | tf_op jit(solution)/shard_map/ppermute | solution.py:163
  64.1 5.4 %collective-permute-done.12.refs_1_ = bf16[256,512]{1,0:T(8,128)(2,1)S(1)} collective-permute-done((bf16[256,512]{1,0:T(8,128)(2,1)S(1)}, bf16[256,512]{1,0:T(8,128)(2,1)S(1)}, u32[]{:S(2)}, u32[]{:S(2)}) %collective-permute-start.12) | collective-permute-done | bytes 262176 | tf_op jit(solution)/shard_map/ppermute | solution.py:163
  69.5 1.3 collective-permute-start.14
  70.8 0.7 broadcast_in_dim.6
  72.6 3.3 %collective-permute-done.14.refs_3_ = bf16[256,512]{1,0:T(8,128)(2,1)S(1)} collective-permute-done((bf16[256,512]{1,0:T(8,128)(2,1)S(1)}, bf16[256,512]{1,0:T(8,128)(2,1)S(1)}, u32[]{:S(2)}, u32[]{:S(2)}) %collective-permute-start.14) | collective-permute-done | bytes 262176 | tf_op jit(solution)/shard_map/ppermute | solution.py:163
  75.8 0.7 broadcast_add_fusion.1
  76.5 1.3 collective-permute-start.10
  77.9 2.3 %collective-permute-done.10 = f32[8,128]{1,0:T(8,128)S(1)} collective-permute-done((f32[8,128]{1,0:T(8,128)S(1)}, f32[8,128]{1,0:T(8,128)S(1)}, u32[]{:S(2)}, u32[]{:S(2)}) %collective-permute-start.10) | collective-permute-done | bytes 4128 | tf_op jit(solution)/shard_map/ppermute | solution.py:163
  80.2 0.7 fusion.1
  80.9 1.4 collective-permute-start.11
  82.4 2.2 %collective-permute-done.11 = f32[8,128]{1,0:T(8,128)S(1)} collective-permute-done((f32[8,128]{1,0:T(8,128)S(1)}, f32[8,128]{1,0:T(8,128)S(1)}, u32[]{:S(2)}, u32[]{:S(2)}) %collective-permute-start.11) | collective-permute-done | bytes 4128 | tf_op jit(solution)/shard_map/ppermute | solution.py:163
  85.9 2.2 %copy-done.2 = bf16[2,1024,1024]{2,1,0:T(8,128)(2,1)S(1)} copy-done((bf16[2,1024,1024]{2,1,0:T(8,128)(2,1)S(1)}, bf16[2,1024,1024]{2,1,0:T(8,128)(2,1)}, u32[]{:S(2)}) %copy-start.2) | copy-done | bytes 4194328
  88.0 1.6 %copy-done.10 = bf16[2,1024,512]{2,1,0:T(8,128)(2,1)S(1)} copy-done((bf16[2,1024,512]{2,1,0:T(8,128)(2,1)S(1)}, bf16[2,1024,512]{2,1,0:T(8,128)(2,1)}, u32[]{:S(2)}) %copy-start.10) | copy-done | bytes 2097176
  89.6 5.1 %inner_and_sent_half.3 = (bf16[2048,512]{1,0:T(8,128)(2,1)S(1)}, f32[512,512]{1,0:T(8,128)S(1)}) custom-call(s32[17]{0:T(128)S(1)} %stack.60.place_ref, s32[128]{0:T(128)S(1)} %reshape.7.mask_ref, bf16[256,512]{1,0:T(8,128)(2,1)S(1)} %convert_element_type.63.refs_0_, bf16[256,512]{1,0:T(8,128)(2,1)S(1)} %collective-permute-done.12.refs_1_, ...), custom_call_target="tpu_custom_call" | custom-call | flops 3221225472 | bytes 8388608 | tf_op jit(solution)/shard_map/inner_and_sent_half/pallas_call | solution.py:101
  94.9 1.4 collective-permute-start.19
  96.3 3.4 %kept_half.3 = (f32[512,512]{1,0:T(8,128)S(1)}, f32[8,128]{1,0:T(8,128)S(1)}) custom-call(s32[17]{0:T(128)S(1)} %stack.60.place_ref, s32[128]{0:T(128)S(1)} %reshape.7.mask_ref, bf16[256,512]{1,0:T(8,128)(2,1)S(1)} %convert_element_type.63.refs_0_, bf16[256,512]{1,0:T(8,128)(2,1)S(1)} %collective-permute-done.12.refs_1_, ...), custom_call_target="tpu_custom_call" | custom-call | flops 1073741824 | bytes 8388608 | tf_op jit(solution)/shard_map/kept_half/pallas_call | solution.py:127
  99.6 4.5 %collective-permute-done.19 = f16[512,512]{1,0:T(8,128)(2,1)S(1)} collective-permute-done((f16[512,512]{1,0:T(8,128)(2,1)S(1)}, f16[512,512]{1,0:T(8,128)(2,1)S(1)}, u32[]{:S(2)}, u32[]{:S(2)}) %collective-permute-start.19) | collective-permute-done | bytes 524320 | tf_op jit(solution)/shard_map/ppermute | solution.py:163
  104.3 1.3 collective-permute-start.20
  105.7 5.9 %collective-permute-done.20 = f16[256,512]{1,0:T(8,128)(2,1)S(1)} collective-permute-done((f16[256,512]{1,0:T(8,128)(2,1)S(1)}, f16[256,512]{1,0:T(8,128)(2,1)S(1)}, u32[]{:S(2)}, u32[]{:S(2)}) %collective-permute-start.20) | collective-permute-done | bytes 262176 | tf_op jit(solution)/shard_map/ppermute | solution.py:163
  112.0 1.2 collective-permute-done.22
  113.2 0.9 collective-permute-start.23
  114.1 2.7 %collective-permute-done.23 = f32[8,128]{1,0:T(8,128)S(1)} collective-permute-done((f32[8,128]{1,0:T(8,128)S(1)}, f32[8,128]{1,0:T(8,128)S(1)}, u32[]{:S(2)}, u32[]{:S(2)}) %collective-permute-start.23) | collective-permute-done | bytes 4128 | tf_op jit(solution)/shard_map/ppermute | solution.py:163
  116.8 2.0 %collective-permute-start.24 = (f32[8,128]{1,0:T(8,128)S(1)}, f32[8,128]{1,0:T(8,128)S(1)}, u32[]{:S(2)}, u32[]{:S(2)}) collective-permute-start(f32[8,128]{1,0:T(8,128)S(1)} %add.164), channel_id=1, source_target_pairs={{0,4},{1,3},{2,6},{3,1},{4,0},{5,7},{6,2},{7,5},{8,12},{9,11},{10,... | collective-permute-start | bytes 12296 | tf_op jit(solution)/shard_map/ppermute | solution.py:163
  118.8 2.0 %collective-permute-done.24 = f32[8,128]{1,0:T(8,128)S(1)} collective-permute-done((f32[8,128]{1,0:T(8,128)S(1)}, f32[8,128]{1,0:T(8,128)S(1)}, u32[]{:S(2)}, u32[]{:S(2)}) %collective-permute-start.24) | collective-permute-done | bytes 4128 | tf_op jit(solution)/shard_map/ppermute | solution.py:163
  120.8 2.2 %collective-permute-start.25 = (f32[8,128]{1,0:T(8,128)S(1)}, f32[8,128]{1,0:T(8,128)S(1)}, u32[]{:S(2)}, u32[]{:S(2)}) collective-permute-start(f32[8,128]{1,0:T(8,128)S(1)} %add.165), channel_id=1, source_target_pairs={{0,8},{1,9},{2,10},{3,11},{4,12},{5,13},{6,14},{7,15},{8,0},{9,1},... | collective-permute-start | bytes 12296 | tf_op jit(solution)/shard_map/ppermute | solution.py:163
  124.4 0.9 collective-permute-done.25
  126.6 2.0 %multiply_reduce_fusion.1 = (f32[]{:T(128)}, f32[256,512]{1,0:T(8,128)S(1)}) fusion(f32[]{:T(128)S(6)} %div.74, f32[1024,512]{1,0:T(8,128)} %param.6, s32[]{:T(128)S(6)} %select_n.84, f32[]{:T(128)S(6)} %div.72, f32[]{:T(128)S(6)} %div.69, f16[256,512]{1,0:T(8,128)(2,1)S(1)} %collective-permute-done.21, f16[256,512]{1,0:T(8,128)(2,1)S(1)} %add_convert_fusion, ...), kind=kLoop, calls=%fused_computation.6 | loop fusion | flops 2097151 | bytes 2097176 | tf_op jit(solution)/shard_map/reduce_sum | solution.py:236
  128.6 1.6 %collective-permute-start.26 = (f16[256,512]{1,0:T(8,128)(2,1)S(1)}, f16[256,512]{1,0:T(8,128)(2,1)S(1)}, u32[]{:S(2)}, u32[]{:S(2)}) collective-permute-start(f16[256,512]{1,0:T(8,128)(2,1)S(1)} %convert_element_type.71), channel_id=1, source_target_pairs={{0,4},{1,3},{2,6},{3,1},{4,0},{5,7},{6,2},{7,5},{8,12},{9,11},{10,... | collective-permute-start | bytes 786440 | tf_op jit(solution)/shard_map/ppermute | solution.py:163
  131.0 1.2 collective-permute-start.27
  132.2 4.0 %collective-permute-done.26 = f16[256,512]{1,0:T(8,128)(2,1)S(1)} collective-permute-done((f16[256,512]{1,0:T(8,128)(2,1)S(1)}, f16[256,512]{1,0:T(8,128)(2,1)S(1)}, u32[]{:S(2)}, u32[]{:S(2)}) %collective-permute-start.26) | collective-permute-done | bytes 262176 | tf_op jit(solution)/shard_map/ppermute | solution.py:163
  136.3 1.4 collective-permute-start.28
  138.3 2.5 %collective-permute-start.30 = (f32[8,128]{1,0:T(8,128)S(1)}, f32[8,128]{1,0:T(8,128)S(1)}, u32[]{:S(2)}, u32[]{:S(2)}) collective-permute-start(f32[8,128]{1,0:T(8,128)S(1)} %broadcast_add_fusion), channel_id=1, source_target_pairs={{0,4},{1,3},{2,6},{3,1},{4,0},{5,7},{6,2},{7,5},{8,12},{9,11},{10,... | collective-permute-start | bytes 12296 | tf_op jit(solution)/shard_map/ppermute | solution.py:163
  140.9 1.6 %collective-permute-done.30 = f32[8,128]{1,0:T(8,128)S(1)} collective-permute-done((f32[8,128]{1,0:T(8,128)S(1)}, f32[8,128]{1,0:T(8,128)S(1)}, u32[]{:S(2)}, u32[]{:S(2)}) %collective-permute-start.30) | collective-permute-done | bytes 4128 | tf_op jit(solution)/shard_map/ppermute | solution.py:163
  143.1 0.7 collective-permute-start.31
  143.8 3.0 %collective-permute-done.31 = f32[8,128]{1,0:T(8,128)S(1)} collective-permute-done((f32[8,128]{1,0:T(8,128)S(1)}, f32[8,128]{1,0:T(8,128)S(1)}, u32[]{:S(2)}, u32[]{:S(2)}) %collective-permute-start.31) | collective-permute-done | bytes 4128 | tf_op jit(solution)/shard_map/ppermute | solution.py:163
  148.3 1.7 %convert_multiply_fusion = f32[1024,512]{1,0:T(8,128)} fusion(f16[256,512]{1,0:T(8,128)(2,1)S(1)} %get-tuple-element.30, f16[256,512]{1,0:T(8,128)(2,1)S(1)} %get-tuple-element.29, f16[256,512]{1,0:T(8,128)(2,1)S(1)} %get-tuple-element.28, f16[256,512]{1,0:T(8,128)(2,1)S(1)} %get-tuple-element.27, f32[]{:T(128)S(6)} %rsqrt.7), kind=kLoop, calls=%fused_computation | loop fusion | flops 2621440 | bytes 3145732 | tf_op jit(solution)/shard_map/mul | solution.py:255
  (70 shorter events, 7.8 us)
Async XLA Ops:
  0.0 4.9 %copy-start.13 = (s32[2,8,8]{2,1,0:T(8,128)S(1)}, s32[2,8,8]{2,1,0:T(8,128)}, u32[]{:S(2)}) copy-start(s32[2,8,8]{2,1,0:T(8,128)} %param.9) | copy-start | bytes 1540
  3.4 4.2 %collective-permute-start = (bf16[1024,512]{1,0:T(8,128)(2,1)S(1)}, bf16[1024,512]{1,0:T(8,128)(2,1)S(1)}, u32[]{:S(2)}, u32[]{:S(2)}) collective-permute-start(bf16[1024,512]{1,0:T(8,128)(2,1)S(1)} %get-tuple-element.26.refs_0_), channel_id=1, source_target_pairs={{0,1},{1,0},{2,3},{3,2},{4,5},{5,4},{6,7},{7,6},{8,9},{9,8},{10,11... | collective-permute-start | bytes 3145736 | tf_op jit(solution)/shard_map/ppermute | solution.py:166
  3.9 1.0 copy-start.7
  4.9 1.5 %collective-permute-start.1 = (f32[]{:T(128)}, f32[]{:T(128)}, u32[]{:S(2)}, u32[]{:S(2)}) collective-permute-start(f32[]{:T(128)} %get-tuple-element.25), channel_id=1, source_target_pairs={{0,1},{1,0},{2,3},{3,2},{4,5},{5,4},{6,7},{7,6},{8,9},{9,8},{10,11... | collective-permute-start | bytes 20 | tf_op jit(solution)/shard_map/ppermute | solution.py:166
  7.7 1.0 copy-start.11
  8.7 2.2 %copy-start = (bf16[2,1024,1024]{2,1,0:T(8,128)(2,1)S(1)}, bf16[2,1024,1024]{2,1,0:T(8,128)(2,1)}, u32[]{:S(2)}) copy-start(bf16[2,1024,1024]{2,1,0:T(8,128)(2,1)} %refs_6_.1) | copy-start | bytes 12582916
  10.9 1.2 copy-start.8
  12.1 1.6 %copy-start.9 = (bf16[2,1024,512]{2,1,0:T(8,128)(2,1)S(1)}, bf16[2,1024,512]{2,1,0:T(8,128)(2,1)}, u32[]{:S(2)}) copy-start(bf16[2,1024,512]{2,1,0:T(8,128)(2,1)} %refs_8_.1) | copy-start | bytes 6291460
  13.7 1.2 copy-start.12
  14.9 10.3 %copy-start.4 = (f32[1024,512]{1,0:T(8,128)S(1)}, f32[1024,512]{1,0:T(8,128)}, u32[]{:S(2)}) copy-start(f32[1024,512]{1,0:T(8,128)} %refs_0_.1) | copy-start | bytes 6291460
  20.1 1.3 copy-start.5
  22.3 10.3 %collective-permute-start.2 = (f16[512,512]{1,0:T(8,128)(2,1)}, f16[512,512]{1,0:T(8,128)(2,1)}, u32[]{:S(2)}, u32[]{:S(2)}) collective-permute-start(f16[512,512]{1,0:T(8,128)(2,1)} %multiply_convert_fusion.1), channel_id=1, source_target_pairs={{0,2},{1,5},{2,0},{3,7},{4,6},{5,1},{6,4},{7,3},{8,10},{9,13},{10,... | collective-permute-start | bytes 1572872 | tf_op jit(solution)/shard_map/ppermute | solution.py:163
  25.2 2.2 %copy-start.1 = (bf16[2,1024,1024]{2,1,0:T(8,128)(2,1)S(1)}, bf16[2,1024,1024]{2,1,0:T(8,128)(2,1)}, u32[]{:S(2)}) copy-start(bf16[2,1024,1024]{2,1,0:T(8,128)(2,1)} %refs_6_.1) | copy-start | bytes 12582916
  27.4 1.6 %copy-start.6 = (bf16[2048,512]{1,0:T(8,128)(2,1)S(1)}, bf16[2048,512]{1,0:T(8,128)(2,1)}, u32[]{:S(2)}) copy-start(bf16[2048,512]{1,0:T(8,128)(2,1)} %copy-done.5) | copy-start | bytes 6291460
  33.9 6.6 %collective-permute-start.3 = (f16[256,512]{1,0:T(8,128)(2,1)S(1)}, f16[256,512]{1,0:T(8,128)(2,1)}, u32[]{:S(2)}, u32[]{:S(2)}) collective-permute-start(f16[256,512]{1,0:T(8,128)(2,1)S(1)} %dynamic-slice_convert_fusion.1), channel_id=1, source_target_pairs={{0,4},{1,3},{2,6},{3,1},{4,0},{5,7},{6,2},{7,5},{8,12},{9,11},{10,... | collective-permute-start | bytes 786440 | tf_op jit(solution)/shard_map/ppermute | solution.py:163
  41.6 17.7 %collective-permute-start.4 = (f16[256,512]{1,0:T(8,128)(2,1)S(1)}, f16[256,512]{1,0:T(8,128)(2,1)S(1)}, u32[]{:S(2)}, u32[]{:S(2)}) collective-permute-start(f16[256,512]{1,0:T(8,128)(2,1)S(1)} %add_convert_fusion.1), channel_id=1, source_target_pairs={{0,8},{1,9},{2,10},{3,11},{4,12},{5,13},{6,14},{7,15},{8,0},{9,1},... | collective-permute-start | bytes 786440 | tf_op jit(solution)/shard_map/ppermute | solution.py:163
  44.7 1.2 collective-permute-start.5
  45.9 3.6 %collective-permute-start.6 = (f32[8,128]{1,0:T(8,128)S(1)}, f32[8,128]{1,0:T(8,128)S(1)}, u32[]{:S(2)}, u32[]{:S(2)}) collective-permute-start(f32[8,128]{1,0:T(8,128)S(1)} %add.143), channel_id=1, source_target_pairs={{0,2},{1,5},{2,0},{3,7},{4,6},{5,1},{6,4},{7,3},{8,10},{9,13},{10,... | collective-permute-start | bytes 12296 | tf_op jit(solution)/shard_map/ppermute | solution.py:163
  49.5 4.0 %collective-permute-start.7 = (f32[8,128]{1,0:T(8,128)S(1)}, f32[8,128]{1,0:T(8,128)S(1)}, u32[]{:S(2)}, u32[]{:S(2)}) collective-permute-start(f32[8,128]{1,0:T(8,128)S(1)} %add.144), channel_id=1, source_target_pairs={{0,4},{1,3},{2,6},{3,1},{4,0},{5,7},{6,2},{7,5},{8,12},{9,11},{10,... | collective-permute-start | bytes 12296 | tf_op jit(solution)/shard_map/ppermute | solution.py:163
  53.5 4.5 %collective-permute-start.8 = (f32[8,128]{1,0:T(8,128)S(1)}, f32[8,128]{1,0:T(8,128)S(1)}, u32[]{:S(2)}, u32[]{:S(2)}) collective-permute-start(f32[8,128]{1,0:T(8,128)S(1)} %add.145), channel_id=1, source_target_pairs={{0,8},{1,9},{2,10},{3,11},{4,12},{5,13},{6,14},{7,15},{8,0},{9,1},... | collective-permute-start | bytes 12296 | tf_op jit(solution)/shard_map/ppermute | solution.py:163
  61.3 8.1 %collective-permute-start.12 = (bf16[256,512]{1,0:T(8,128)(2,1)S(1)}, bf16[256,512]{1,0:T(8,128)(2,1)S(1)}, u32[]{:S(2)}, u32[]{:S(2)}) collective-permute-start(bf16[256,512]{1,0:T(8,128)(2,1)S(1)} %convert_element_type.63.refs_0_), channel_id=1, source_target_pairs={{0,4},{1,3},{2,6},{3,1},{4,0},{5,7},{6,2},{7,5},{8,12},{9,11},{10,... | collective-permute-start | bytes 786440 | tf_op jit(solution)/shard_map/ppermute | solution.py:163
  62.6 9.6 %collective-permute-start.13 = (bf16[256,512]{1,0:T(8,128)(2,1)S(1)}, bf16[256,512]{1,0:T(8,128)(2,1)S(1)}, u32[]{:S(2)}, u32[]{:S(2)}) collective-permute-start(bf16[256,512]{1,0:T(8,128)(2,1)S(1)} %convert_element_type.63.refs_0_), channel_id=1, source_target_pairs={{0,2},{1,5},{2,0},{3,7},{4,6},{5,1},{6,4},{7,3},{8,10},{9,13},{10,... | collective-permute-start | bytes 786440 | tf_op jit(solution)/shard_map/ppermute | solution.py:163
  69.5 6.4 %collective-permute-start.14 = (bf16[256,512]{1,0:T(8,128)(2,1)S(1)}, bf16[256,512]{1,0:T(8,128)(2,1)S(1)}, u32[]{:S(2)}, u32[]{:S(2)}) collective-permute-start(bf16[256,512]{1,0:T(8,128)(2,1)S(1)} %collective-permute-done.12.refs_1_), channel_id=1, source_target_pairs={{0,2},{1,5},{2,0},{3,7},{4,6},{5,1},{6,4},{7,3},{8,10},{9,13},{10,... | collective-permute-start | bytes 786440 | tf_op jit(solution)/shard_map/ppermute | solution.py:163
  71.5 4.4 %collective-permute-start.9 = (f32[8,128]{1,0:T(8,128)S(1)}, f32[8,128]{1,0:T(8,128)S(1)}, u32[]{:S(2)}, u32[]{:S(2)}) collective-permute-start(f32[8,128]{1,0:T(8,128)S(1)} %broadcast_in_dim.6), channel_id=1, source_target_pairs={{0,1},{1,0},{2,3},{3,2},{4,5},{5,4},{6,7},{7,6},{8,9},{9,8},{10,11... | collective-permute-start | bytes 12296 | tf_op jit(solution)/shard_map/ppermute | solution.py:166
  71.6 14.2 %collective-permute-start.15 = (bf16[256,512]{1,0:T(8,128)(2,1)S(1)}, bf16[256,512]{1,0:T(8,128)(2,1)S(1)}, u32[]{:S(2)}, u32[]{:S(2)}) collective-permute-start(bf16[256,512]{1,0:T(8,128)(2,1)S(1)} %convert_element_type.63.refs_0_), channel_id=1, source_target_pairs={{0,1},{1,0},{2,3},{3,2},{4,5},{5,4},{6,7},{7,6},{8,9},{9,8},{10,11... | collective-permute-start | bytes 786440 | tf_op jit(solution)/shard_map/ppermute | solution.py:166
  72.1 13.8 %collective-permute-start.16 = (bf16[256,512]{1,0:T(8,128)(2,1)S(1)}, bf16[256,512]{1,0:T(8,128)(2,1)S(1)}, u32[]{:S(2)}, u32[]{:S(2)}) collective-permute-start(bf16[256,512]{1,0:T(8,128)(2,1)S(1)} %collective-permute-done.12.refs_1_), channel_id=1, source_target_pairs={{0,1},{1,0},{2,3},{3,2},{4,5},{5,4},{6,7},{7,6},{8,9},{9,8},{10,11... | collective-permute-start | bytes 786440 | tf_op jit(solution)/shard_map/ppermute | solution.py:166
  72.1 13.7 %collective-permute-start.17 = (bf16[256,512]{1,0:T(8,128)(2,1)S(1)}, bf16[256,512]{1,0:T(8,128)(2,1)S(1)}, u32[]{:S(2)}, u32[]{:S(2)}) collective-permute-start(bf16[256,512]{1,0:T(8,128)(2,1)S(1)} %collective-permute-done.13.refs_2_), channel_id=1, source_target_pairs={{0,1},{1,0},{2,3},{3,2},{4,5},{5,4},{6,7},{7,6},{8,9},{9,8},{10,11... | collective-permute-start | bytes 786440 | tf_op jit(solution)/shard_map/ppermute | solution.py:166
  75.8 10.0 %collective-permute-start.18 = (bf16[256,512]{1,0:T(8,128)(2,1)S(1)}, bf16[256,512]{1,0:T(8,128)(2,1)S(1)}, u32[]{:S(2)}, u32[]{:S(2)}) collective-permute-start(bf16[256,512]{1,0:T(8,128)(2,1)S(1)} %collective-permute-done.14.refs_3_), channel_id=1, source_target_pairs={{0,1},{1,0},{2,3},{3,2},{4,5},{5,4},{6,7},{7,6},{8,9},{9,8},{10,11... | collective-permute-start | bytes 786440 | tf_op jit(solution)/shard_map/ppermute | solution.py:166
  76.5 3.7 %collective-permute-start.10 = (f32[8,128]{1,0:T(8,128)S(1)}, f32[8,128]{1,0:T(8,128)S(1)}, u32[]{:S(2)}, u32[]{:S(2)}) collective-permute-start(f32[8,128]{1,0:T(8,128)S(1)} %broadcast_add_fusion.1), channel_id=1, source_target_pairs={{0,4},{1,3},{2,6},{3,1},{4,0},{5,7},{6,2},{7,5},{8,12},{9,11},{10,... | collective-permute-start | bytes 12296 | tf_op jit(solution)/shard_map/ppermute | solution.py:163
  80.9 3.7 %collective-permute-start.11 = (f32[8,128]{1,0:T(8,128)S(1)}, f32[8,128]{1,0:T(8,128)S(1)}, u32[]{:S(2)}, u32[]{:S(2)}) collective-permute-start(f32[8,128]{1,0:T(8,128)S(1)} %fusion.1), channel_id=1, source_target_pairs={{0,2},{1,5},{2,0},{3,7},{4,6},{5,1},{6,4},{7,3},{8,10},{9,13},{10,... | collective-permute-start | bytes 12296 | tf_op jit(solution)/shard_map/ppermute | solution.py:163
  85.8 2.2 %copy-start.2 = (bf16[2,1024,1024]{2,1,0:T(8,128)(2,1)S(1)}, bf16[2,1024,1024]{2,1,0:T(8,128)(2,1)}, u32[]{:S(2)}) copy-start(bf16[2,1024,1024]{2,1,0:T(8,128)(2,1)} %refs_6_.1) | copy-start | bytes 12582916
  88.0 1.6 %copy-start.10 = (bf16[2,1024,512]{2,1,0:T(8,128)(2,1)S(1)}, bf16[2,1024,512]{2,1,0:T(8,128)(2,1)}, u32[]{:S(2)}) copy-start(bf16[2,1024,512]{2,1,0:T(8,128)(2,1)} %refs_8_.1) | copy-start | bytes 6291460
  89.6 6.7 %copy-start.3 = (bf16[2,1024,1024]{2,1,0:T(8,128)(2,1)S(1)}, bf16[2,1024,1024]{2,1,0:T(8,128)(2,1)}, u32[]{:S(2)}) copy-start(bf16[2,1024,1024]{2,1,0:T(8,128)(2,1)} %refs_6_.1) | copy-start | bytes 12582916
  94.9 9.2 %collective-permute-start.19 = (f16[512,512]{1,0:T(8,128)(2,1)S(1)}, f16[512,512]{1,0:T(8,128)(2,1)S(1)}, u32[]{:S(2)}, u32[]{:S(2)}) collective-permute-start(f16[512,512]{1,0:T(8,128)(2,1)S(1)} %multiply_convert_fusion), channel_id=1, source_target_pairs={{0,2},{1,5},{2,0},{3,7},{4,6},{5,1},{6,4},{7,3},{8,10},{9,13},{10,... | collective-permute-start | bytes 1572872 | tf_op jit(solution)/shard_map/ppermute | solution.py:163
  104.3 7.3 %collective-permute-start.20 = (f16[256,512]{1,0:T(8,128)(2,1)S(1)}, f16[256,512]{1,0:T(8,128)(2,1)S(1)}, u32[]{:S(2)}, u32[]{:S(2)}) collective-permute-start(f16[256,512]{1,0:T(8,128)(2,1)S(1)} %dynamic-slice_convert_fusion), channel_id=1, source_target_pairs={{0,4},{1,3},{2,6},{3,1},{4,0},{5,7},{6,2},{7,5},{8,12},{9,11},{10,... | collective-permute-start | bytes 786440 | tf_op jit(solution)/shard_map/ppermute | solution.py:163
  111.7 14.9 %collective-permute-start.21 = (f16[256,512]{1,0:T(8,128)(2,1)S(1)}, f16[256,512]{1,0:T(8,128)(2,1)S(1)}, u32[]{:S(2)}, u32[]{:S(2)}) collective-permute-start(f16[256,512]{1,0:T(8,128)(2,1)S(1)} %add_convert_fusion), channel_id=1, source_target_pairs={{0,8},{1,9},{2,10},{3,11},{4,12},{5,13},{6,14},{7,15},{8,0},{9,1},... | collective-permute-start | bytes 786440 | tf_op jit(solution)/shard_map/ppermute | solution.py:163
  112.0 1.2 collective-permute-start.22
  113.2 3.6 %collective-permute-start.23 = (f32[8,128]{1,0:T(8,128)S(1)}, f32[8,128]{1,0:T(8,128)S(1)}, u32[]{:S(2)}, u32[]{:S(2)}) collective-permute-start(f32[8,128]{1,0:T(8,128)S(1)} %add.163), channel_id=1, source_target_pairs={{0,2},{1,5},{2,0},{3,7},{4,6},{5,1},{6,4},{7,3},{8,10},{9,13},{10,... | collective-permute-start | bytes 12296 | tf_op jit(solution)/shard_map/ppermute | solution.py:163
  116.8 4.0 %collective-permute-start.24 = (f32[8,128]{1,0:T(8,128)S(1)}, f32[8,128]{1,0:T(8,128)S(1)}, u32[]{:S(2)}, u32[]{:S(2)}) collective-permute-start(f32[8,128]{1,0:T(8,128)S(1)} %add.164), channel_id=1, source_target_pairs={{0,4},{1,3},{2,6},{3,1},{4,0},{5,7},{6,2},{7,5},{8,12},{9,11},{10,... | collective-permute-start | bytes 12296 | tf_op jit(solution)/shard_map/ppermute | solution.py:163
  120.8 4.5 %collective-permute-start.25 = (f32[8,128]{1,0:T(8,128)S(1)}, f32[8,128]{1,0:T(8,128)S(1)}, u32[]{:S(2)}, u32[]{:S(2)}) collective-permute-start(f32[8,128]{1,0:T(8,128)S(1)} %add.165), channel_id=1, source_target_pairs={{0,8},{1,9},{2,10},{3,11},{4,12},{5,13},{6,14},{7,15},{8,0},{9,1},... | collective-permute-start | bytes 12296 | tf_op jit(solution)/shard_map/ppermute | solution.py:163
  128.6 7.6 %collective-permute-start.26 = (f16[256,512]{1,0:T(8,128)(2,1)S(1)}, f16[256,512]{1,0:T(8,128)(2,1)S(1)}, u32[]{:S(2)}, u32[]{:S(2)}) collective-permute-start(f16[256,512]{1,0:T(8,128)(2,1)S(1)} %convert_element_type.71), channel_id=1, source_target_pairs={{0,4},{1,3},{2,6},{3,1},{4,0},{5,7},{6,2},{7,5},{8,12},{9,11},{10,... | collective-permute-start | bytes 786440 | tf_op jit(solution)/shard_map/ppermute | solution.py:163
  130.9 6.7 %collective-permute-start.29 = (f32[8,128]{1,0:T(8,128)S(1)}, f32[8,128]{1,0:T(8,128)S(1)}, u32[]{:S(2)}, u32[]{:S(2)}) collective-permute-start(f32[8,128]{1,0:T(8,128)S(1)} %broadcast_in_dim.7), channel_id=1, source_target_pairs={{0,1},{1,0},{2,3},{3,2},{4,5},{5,4},{6,7},{7,6},{8,9},{9,8},{10,11... | collective-permute-start | bytes 12296 | tf_op jit(solution)/shard_map/ppermute | solution.py:166
  131.0 17.0 %collective-permute-start.27 = (f16[256,512]{1,0:T(8,128)(2,1)S(1)}, f16[256,512]{1,0:T(8,128)(2,1)S(1)}, u32[]{:S(2)}, u32[]{:S(2)}) collective-permute-start(f16[256,512]{1,0:T(8,128)(2,1)S(1)} %convert_element_type.71), channel_id=1, source_target_pairs={{0,2},{1,5},{2,0},{3,7},{4,6},{5,1},{6,4},{7,3},{8,10},{9,13},{10,... | collective-permute-start | bytes 786440 | tf_op jit(solution)/shard_map/ppermute | solution.py:163
  136.3 11.7 %collective-permute-start.28 = (f16[256,512]{1,0:T(8,128)(2,1)S(1)}, f16[256,512]{1,0:T(8,128)(2,1)S(1)}, u32[]{:S(2)}, u32[]{:S(2)}) collective-permute-start(f16[256,512]{1,0:T(8,128)(2,1)S(1)} %collective-permute-done.26), channel_id=1, source_target_pairs={{0,2},{1,5},{2,0},{3,7},{4,6},{5,1},{6,4},{7,3},{8,10},{9,13},{10,... | collective-permute-start | bytes 786440 | tf_op jit(solution)/shard_map/ppermute | solution.py:163
  138.3 4.1 %collective-permute-start.30 = (f32[8,128]{1,0:T(8,128)S(1)}, f32[8,128]{1,0:T(8,128)S(1)}, u32[]{:S(2)}, u32[]{:S(2)}) collective-permute-start(f32[8,128]{1,0:T(8,128)S(1)} %broadcast_add_fusion), channel_id=1, source_target_pairs={{0,4},{1,3},{2,6},{3,1},{4,0},{5,7},{6,2},{7,5},{8,12},{9,11},{10,... | collective-permute-start | bytes 12296 | tf_op jit(solution)/shard_map/ppermute | solution.py:163
  143.1 3.7 %collective-permute-start.31 = (f32[8,128]{1,0:T(8,128)S(1)}, f32[8,128]{1,0:T(8,128)S(1)}, u32[]{:S(2)}, u32[]{:S(2)}) collective-permute-start(f32[8,128]{1,0:T(8,128)S(1)} %fusion), channel_id=1, source_target_pairs={{0,2},{1,5},{2,0},{3,7},{4,6},{5,1},{6,4},{7,3},{8,10},{9,13},{10,... | collective-permute-start | bytes 12296 | tf_op jit(solution)/shard_map/ppermute | solution.py:163

commit v2 on v1

--- a/solution.py
+++ b/solution.py
@@ -15,6 +15,10 @@
 
 def any_spec():
     return pl.BlockSpec(memory_space=pl.ANY)
+
+
+def hbm_spec():
+    return pl.BlockSpec(memory_space=pltpu.HBM)
 
 
 def smem_spec():
@@ -87,7 +91,7 @@
     first = pl.multiple_of(place_ref[0], rows)
     product = (own[pl.ds(first, rows), :].astype(jnp.float32) * send[...]
                + own[pl.ds(kept, rows), :].astype(jnp.float32) * keep_out[...])
-    corr_out[...] = jnp.full(corr_out.shape, jnp.sum(product), jnp.float32)
+    corr_out[0, 0] = jnp.sum(product)
 
 
 def sigma_halves(place, mask, own, other, right, left, blocks):
@@ -97,11 +101,11 @@
     bf16, f32 = jnp.bfloat16, jnp.float32
     pieces = [p.astype(bf16) for p in own] + other
     flops = 2 * pairs * width * cols
-    vmem = pltpu.CompilerParams(vmem_limit_bytes=32 * 2 ** 20)
+    vmem = pltpu.CompilerParams(vmem_limit_bytes=20 * 2 ** 20)
     inner, send = pl.pallas_call(
         functools.partial(first_kernel, len(pieces), blocks),
         out_shape=(sds((pairs * width, cols), bf16), sds((half, cols), f32)),
-        in_specs=[smem_spec(), smem_spec()] + [any_spec()] * (len(pieces) + 2),
+        in_specs=[smem_spec(), smem_spec()] + [any_spec()] * len(pieces) + [hbm_spec()] * 2,
         out_specs=(any_spec(), pl.BlockSpec(memory_space=pltpu.VMEM)),
         scratch_shapes=[
             pltpu.VMEM((width, width), bf16),
@@ -126,9 +130,9 @@
     bf16, f32 = jnp.bfloat16, jnp.float32
     return pl.pallas_call(
         functools.partial(second_kernel, len(own), blocks),
-        out_shape=(sds((half, cols), f32), sds((8, 128), f32)),
-        in_specs=[smem_spec(), smem_spec()] + [any_spec()] * (len(own) + 3),
-        out_specs=(pl.BlockSpec(memory_space=pltpu.VMEM), pl.BlockSpec(memory_space=pltpu.VMEM)),
+        out_shape=(sds((half, cols), f32), sds((1, 1), f32)),
+        in_specs=[smem_spec(), smem_spec()] + [any_spec()] * (len(own) + 2) + [hbm_spec()],
+        out_specs=(pl.BlockSpec(memory_space=pltpu.VMEM), smem_spec()),
         scratch_shapes=[
             pltpu.VMEM((width, cols), own[0].dtype),
             pltpu.VMEM((half, cols), f32),
@@ -137,7 +141,7 @@
             pltpu.VMEM((half, pairs * width), bf16),
             pltpu.SemaphoreType.DMA((len(own) + 2 + pairs,)),
         ],
-        compiler_params=pltpu.CompilerParams(vmem_limit_bytes=32 * 2 ** 20),
+        compiler_params=pltpu.CompilerParams(vmem_limit_bytes=20 * 2 ** 20),
         cost_estimate=pl.CostEstimate(
             flops=2 * pairs * width * cols * half, bytes_accessed=8 * 2 ** 20, transcendentals=0),
         name="kept_half",
@@ -207,6 +211,7 @@
         scale = 32768.0 / (reach * length)
         got = swap((send * scale).astype(f16), 0)
         keep, corr = sigma_kept(place, mask, own, send, inner, left, blocks)
+        corr = corr.reshape(())
         corr = corr + across(corr)
         corr = corr + swap(corr, 0)
         keep = keep * scale + got.astype(f32)
@@ -222,7 +227,7 @@
             keep = send.astype(f32) + got.astype(f32)
         sigma = keep * (norm / scale)
         square = norm * norm
-        theta = (corr[0, 0] * square / cells) / (weight * square / cells + EPS)
+        theta = (corr * square / cells) / (weight * square / cells + EPS)
         spacing = diag - theta
         correction = (sigma - theta * coef) * spacing / jnp.maximum(spacing * spacing, 1.0)
         moved = coef - correction
@@ -233,13 +238,15 @@
             piece = moved.astype(f16)
         else:
             piece = moved.astype(bf16)
-        weight = jnp.full((8, 128), jnp.sum(moved * moved), f32)
+        weight = jnp.sum(moved * moved)
         p1 = swap(piece, 1)
         p2 = swap(piece, 0)
+        weight = weight + across(weight)
+        p1, weight = lax.optimization_barrier((p1, weight))
         p3 = swap(p1, 0)
-        weight = weight + across(weight)
         weight = weight + swap(weight, 1)
-        weight = (weight + swap(weight, 0))[0, 0]
+        p3, weight = lax.optimization_barrier((p3, weight))
+        weight = weight + swap(weight, 0)
         if not last:
             norm = lax.rsqrt(weight / cells + EPS)
             coef = moved * norm

time: 151 us -> 144 us (0.954)
  waiting for transfers between devices: 55.4 us -> 30.9 us
  starting transfers between devices: 35.4 us -> 50.6 us
  between operations: 5.86 us -> 13.4 us
  local copies, waits for them, and re-layouts: 20.8 us -> 17.3 us
  other arithmetic: 15.8 us -> 13.1 us
    ppermute x22, waiting for transfers between devices: 51.8 us -> 24.5 us  [swap(): return lax.ppermute(x, BOTH, pairing)]
    ppermute x22, starting transfers between devices: 33.7 us -> 49.5 us  [swap(): return lax.ppermute(x, BOTH, pairing)]
    ppermute x10, waiting for transfers between devices: 3.62 us -> 6.35 us  [across(): return lax.ppermute(x, 'col', [(c, c ^ 1) for c in range(cols)])]
    add x14 -> x0, other arithmetic: 2.68 us -> none  [the longest x2 1.32 us: local(): weight = weight + across(weight)]
    slice x4 -> x0, local copies, waits for them, and re-layouts: 2.12 us -> none  [the longest x2 1.09 us: local(): theta = corr[0, 0] * square / cells / (weight * square / cells + EPS)]
  transfers between devices with their start and end apart: 32 -> 32, of which waited for: 20 -> 21; matrix products, arithmetic and copies ran while one was open for 4% -> 0% of each run, Pallas kernels for 4% -> 5%
where the time goes in v2:
time: 144 us; the launch traced here: 143 us
  starting transfers between devices  50.6 us (35%)
  waiting for transfers between devices  30.9 us (21%)
  Pallas kernels  17.8 us (12%)
  local copies, waits for them, and re-layouts  17.3 us (12%)
  between operations  13.4 us (9%)
  other arithmetic  13.1 us (9%)
    ppermute x22, starting transfers between devices, swap(): return lax.ppermute(x, BOTH, pairing)  49.5 us
    ppermute x22, waiting for transfers between devices, swap(): return lax.ppermute(x, BOTH, pairing)  24.5 us
    unnamed x28, local copies, waits for them, and re-layouts  17.1 us
    pallas_call x2, Pallas kernels, sigma_halves(): pl.pallas_call(functools.partial(first_kernel, len(pieces), blocks), out_...  10.2 us
    pallas_call x2, Pallas kernels, sigma_kept(): pl.pallas_call(functools.partial(second_kernel, len(own), blocks), out_sh...  7.6 us
    ppermute x10, waiting for transfers between devices, across(): return lax.ppermute(x, 'col', [(c, c ^ 1) for c in range(cols)])  6.35 us
    reduce_sum x2, other arithmetic, local(): weight = jnp.sum(moved * moved)  3.98 us
    reduce_sum x1, other arithmetic, local(): weight = jnp.sum(wave_coef * wave_coef)  3.44 us
  transfers between devices with their start and end apart: 32, of which 21 were waited for; matrix products, arithmetic and copies ran while one was open for 0% of the time, Pallas kernels for 5%

profile of v2, /device:TPU:0, one launch (start us, length us, event | category | flops | bytes accessed | tf_op | source)
XLA Modules:
  0.0 143.1 jit_solution(18124471486991484852)
XLA Ops:
  0.0 3.4 %multiply_reduce_fusion = (f32[]{:T(128)}, bf16[1024,512]{1,0:T(8,128)(2,1)S(1)}) fusion(f32[1024,512]{1,0:T(8,128)} %refs_0_.1), kind=kLoop, calls=%fused_computation.1 | loop fusion | flops 1572863 | bytes 3145732 | tf_op jit(solution)/shard_map/reduce_sum | solution.py:197
  3.4 0.5 collective-permute-start
  3.9 1.0 copy-done.7
  5.1 1.3 collective-permute-done.1
  7.7 1.0 copy-done.11
  8.7 2.2 %copy-done = bf16[2,1024,1024]{2,1,0:T(8,128)(2,1)S(1)} copy-done((bf16[2,1024,1024]{2,1,0:T(8,128)(2,1)S(1)}, bf16[2,1024,1024]{2,1,0:T(8,128)(2,1)}, u32[]{:S(2)}) %copy-start) | copy-done | bytes 4194328
  10.9 1.2 copy-done.8
  12.1 1.6 %copy-done.9 = bf16[2,1024,512]{2,1,0:T(8,128)(2,1)S(1)} copy-done((bf16[2,1024,512]{2,1,0:T(8,128)(2,1)S(1)}, bf16[2,1024,512]{2,1,0:T(8,128)(2,1)}, u32[]{:S(2)}) %copy-start.9) | copy-done | bytes 2097176
  13.7 1.2 copy-done.12
  14.9 5.2 %inner_and_sent_half.2 = (bf16[2048,512]{1,0:T(8,128)(2,1)S(1)}, f32[512,512]{1,0:T(8,128)S(1)}) custom-call(s32[5]{0:T(128)S(1)} %stack.51.place_ref, s32[128]{0:T(128)S(1)} %reshape.9.mask_ref, bf16[1024,512]{1,0:T(8,128)(2,1)S(1)} %copy-done.8, bf16[1024,512]{1,0:T(8,128)(2,1)S(1)} %copy-done.12, bf16[2,1024,512]{2,1,0:T(8,128)(2,1)S(1)} %copy-done.9, ...), custom_call_target="tpu_custom_call" | custom-call | flops 3221225472 | bytes 8388608 | tf_op jit(solution)/shard_map/inner_and_sent_half/pallas_call | solution.py:105
  20.1 1.3 copy-done.5
  21.4 0.9 multiply_convert_fusion.1
  22.3 2.8 %collective-permute-start.2 = (f16[512,512]{1,0:T(8,128)(2,1)}, f16[512,512]{1,0:T(8,128)(2,1)}, u32[]{:S(2)}, u32[]{:S(2)}) collective-permute-start(f16[512,512]{1,0:T(8,128)(2,1)} %multiply_convert_fusion.1), channel_id=1, source_target_pairs={{0,2},{1,5},{2,0},{3,7},{4,6},{5,1},{6,4},{7,3},{8,10},{9,13},{10,... | collective-permute-start | bytes 1572872 | tf_op jit(solution)/shard_map/ppermute | solution.py:167
  25.2 2.2 %copy-done.1 = bf16[2,1024,1024]{2,1,0:T(8,128)(2,1)S(1)} copy-done((bf16[2,1024,1024]{2,1,0:T(8,128)(2,1)S(1)}, bf16[2,1024,1024]{2,1,0:T(8,128)(2,1)}, u32[]{:S(2)}) %copy-start.1) | copy-done | bytes 4194328
  27.4 1.6 %copy-done.6 = bf16[2048,512]{1,0:T(8,128)(2,1)S(1)} copy-done((bf16[2048,512]{1,0:T(8,128)(2,1)S(1)}, bf16[2048,512]{1,0:T(8,128)(2,1)}, u32[]{:S(2)}) %copy-start.6) | copy-done | bytes 2097176
  29.0 3.7 %kept_half.2 = (f32[512,512]{1,0:T(8,128)S(1)}, f32[1,1]{1,0:T(1,128)}) custom-call(s32[5]{0:T(128)S(1)} %stack.51.place_ref, s32[128]{0:T(128)S(1)} %reshape.9.mask_ref, f32[1024,512]{1,0:T(8,128)S(1)} %copy-done.4, f32[512,512]{1,0:T(8,128)S(1)} %get-tuple-element.21.refs_1_, bf16[2048,512]{1,0:T(8,128)(2,1)S(1)} %copy-done.6, ...), custom_call_target="tpu_custom_call" | custom-call | flops 1073741824 | bytes 8388608 | tf_op jit(solution)/shard_map/kept_half/pallas_call | solution.py:131
  32.7 1.2 convert_add_fusion.1
  34.0 2.1 %collective-permute-start.3 = (f16[256,512]{1,0:T(8,128)(2,1)S(1)}, f16[256,512]{1,0:T(8,128)(2,1)}, u32[]{:S(2)}, u32[]{:S(2)}) collective-permute-start(f16[256,512]{1,0:T(8,128)(2,1)S(1)} %dynamic-slice_convert_fusion.1), channel_id=1, source_target_pairs={{0,4},{1,3},{2,6},{3,1},{4,0},{5,7},{6,2},{7,5},{8,12},{9,11},{10,... | collective-permute-start | bytes 786440 | tf_op jit(solution)/shard_map/ppermute | solution.py:167
  36.1 4.5 %collective-permute-done.3 = f16[256,512]{1,0:T(8,128)(2,1)} collective-permute-done((f16[256,512]{1,0:T(8,128)(2,1)S(1)}, f16[256,512]{1,0:T(8,128)(2,1)}, u32[]{:S(2)}, u32[]{:S(2)}) %collective-permute-start.3) | collective-permute-done | bytes 262176 | tf_op jit(solution)/shard_map/ppermute | solution.py:167
  40.6 1.0 add_convert_fusion.1
  41.6 3.1 %collective-permute-start.4 = (f16[256,512]{1,0:T(8,128)(2,1)S(1)}, f16[256,512]{1,0:T(8,128)(2,1)S(1)}, u32[]{:S(2)}, u32[]{:S(2)}) collective-permute-start(f16[256,512]{1,0:T(8,128)(2,1)S(1)} %add_convert_fusion.1), channel_id=1, source_target_pairs={{0,8},{1,9},{2,10},{3,11},{4,12},{5,13},{6,14},{7,15},{8,0},{9,1},... | collective-permute-start | bytes 786440 | tf_op jit(solution)/shard_map/ppermute | solution.py:167
  44.7 1.3 collective-permute-done.5
  47.2 2.9 %collective-permute-start.6 = (f32[]{:T(128)}, f32[]{:T(128)}, u32[]{:S(2)}, u32[]{:S(2)}) collective-permute-start(f32[]{:T(128)} %add.143), channel_id=1, source_target_pairs={{0,2},{1,5},{2,0},{3,7},{4,6},{5,1},{6,4},{7,3},{8,10},{9,13},{10,... | collective-permute-start | bytes 20 | tf_op jit(solution)/shard_map/ppermute | solution.py:167
  50.1 0.8 collective-permute-done.6
  51.5 2.9 %collective-permute-start.7 = (f32[]{:T(128)}, f32[]{:T(128)}, u32[]{:S(2)}, u32[]{:S(2)}) collective-permute-start(f32[]{:T(128)} %add.144), channel_id=1, source_target_pairs={{0,4},{1,3},{2,6},{3,1},{4,0},{5,7},{6,2},{7,5},{8,12},{9,11},{10,... | collective-permute-start | bytes 20 | tf_op jit(solution)/shard_map/ppermute | solution.py:167
  54.4 0.8 collective-permute-done.7
  55.8 1.4 collective-permute-start.8
  57.2 3.2 %collective-permute-done.8 = f32[]{:T(128)} collective-permute-done((f32[]{:T(128)}, f32[]{:T(128)}, u32[]{:S(2)}, u32[]{:S(2)}) %collective-permute-start.8) | collective-permute-done | bytes 36 | tf_op jit(solution)/shard_map/ppermute | solution.py:167
  61.0 2.0 %multiply_reduce_fusion.2 = (f32[]{:T(128)}, f32[256,512]{1,0:T(8,128)S(1)}) fusion(f32[1024,512]{1,0:T(8,128)} %param.6, s32[]{:T(128)S(6)} %select_n.84, f32[]{:T(128)S(6)} %div.60, f32[]{:T(128)S(6)} %div.57, f16[256,512]{1,0:T(8,128)(2,1)S(1)} %collective-permute-done.4, f16[256,512]{1,0:T(8,128)(2,1)S(1)} %add_convert_fusion.1, f32[1024,512]{1,0:T(8,128)S(1)} %copy-done.4), kind=kLoop, calls=%fused_computation.10 | loop fusion | flops 1835007 | bytes 2097168 | tf_op jit(solution)/shard_map/reduce_sum | solution.py:241
  63.1 1.6 %collective-permute-start.9 = (bf16[256,512]{1,0:T(8,128)(2,1)S(1)}, bf16[256,512]{1,0:T(8,128)(2,1)S(1)}, u32[]{:S(2)}, u32[]{:S(2)}) collective-permute-start(bf16[256,512]{1,0:T(8,128)(2,1)S(1)} %convert_element_type.63.refs_0_), channel_id=1, source_target_pairs={{0,4},{1,3},{2,6},{3,1},{4,0},{5,7},{6,2},{7,5},{8,12},{9,11},{10,... | collective-permute-start | bytes 786440 | tf_op jit(solution)/shard_map/ppermute | solution.py:167
  64.7 1.5 %collective-permute-start.14 = (bf16[256,512]{1,0:T(8,128)(2,1)S(1)}, bf16[256,512]{1,0:T(8,128)(2,1)S(1)}, u32[]{:S(2)}, u32[]{:S(2)}) collective-permute-start(bf16[256,512]{1,0:T(8,128)(2,1)S(1)} %convert_element_type.63.refs_0_), channel_id=1, source_target_pairs={{0,2},{1,5},{2,0},{3,7},{4,6},{5,1},{6,4},{7,3},{8,10},{9,13},{10,... | collective-permute-start | bytes 786440 | tf_op jit(solution)/shard_map/ppermute | solution.py:167
  66.2 1.3 collective-permute-done.10
  68.7 0.8 collective-permute-done.9.refs_1_
  69.5 1.5 %collective-permute-start.11 = (bf16[256,512]{1,0:T(8,128)(2,1)S(1)}, bf16[256,512]{1,0:T(8,128)(2,1)S(1)}, u32[]{:S(2)}, u32[]{:S(2)}) collective-permute-start(bf16[256,512]{1,0:T(8,128)(2,1)S(1)} %collective-permute-done.9.refs_1_), channel_id=1, source_target_pairs={{0,2},{1,5},{2,0},{3,7},{4,6},{5,1},{6,4},{7,3},{8,10},{9,13},{10,... | collective-permute-start | bytes 786440 | tf_op jit(solution)/shard_map/ppermute | solution.py:167
  71.0 0.5 collective-permute-start.16
  71.5 2.8 %collective-permute-start.12 = (f32[]{:T(128)}, f32[]{:T(128)}, u32[]{:S(2)}, u32[]{:S(2)}) collective-permute-start(f32[]{:T(128)} %add.148), channel_id=1, source_target_pairs={{0,4},{1,3},{2,6},{3,1},{4,0},{5,7},{6,2},{7,5},{8,12},{9,11},{10,... | collective-permute-start | bytes 20 | tf_op jit(solution)/shard_map/ppermute | solution.py:167
  74.4 0.7 collective-permute-done.12
  76.0 2.9 %collective-permute-start.13 = (f32[]{:T(128)}, f32[]{:T(128)}, u32[]{:S(2)}, u32[]{:S(2)}) collective-permute-start(f32[]{:T(128)} %add.149), channel_id=1, source_target_pairs={{0,2},{1,5},{2,0},{3,7},{4,6},{5,1},{6,4},{7,3},{8,10},{9,13},{10,... | collective-permute-start | bytes 20 | tf_op jit(solution)/shard_map/ppermute | solution.py:167
  78.9 0.7 collective-permute-done.13
  80.4 2.2 %copy-done.2 = bf16[2,1024,1024]{2,1,0:T(8,128)(2,1)S(1)} copy-done((bf16[2,1024,1024]{2,1,0:T(8,128)(2,1)S(1)}, bf16[2,1024,1024]{2,1,0:T(8,128)(2,1)}, u32[]{:S(2)}) %copy-start.2) | copy-done | bytes 4194328
  82.5 1.6 %copy-done.10 = bf16[2,1024,512]{2,1,0:T(8,128)(2,1)S(1)} copy-done((bf16[2,1024,512]{2,1,0:T(8,128)(2,1)S(1)}, bf16[2,1024,512]{2,1,0:T(8,128)(2,1)}, u32[]{:S(2)}) %copy-start.10) | copy-done | bytes 2097176
  84.1 5.1 %inner_and_sent_half.3 = (bf16[2048,512]{1,0:T(8,128)(2,1)S(1)}, f32[512,512]{1,0:T(8,128)S(1)}) custom-call(s32[17]{0:T(128)S(1)} %stack.60.place_ref, s32[128]{0:T(128)S(1)} %reshape.9.mask_ref, bf16[256,512]{1,0:T(8,128)(2,1)S(1)} %convert_element_type.63.refs_0_, bf16[256,512]{1,0:T(8,128)(2,1)S(1)} %collective-permute-done.9.refs_1_, ...), custom_call_target="tpu_custom_call" | custom-call | flops 3221225472 | bytes 8388608 | tf_op jit(solution)/shard_map/inner_and_sent_half/pallas_call | solution.py:105
  89.4 1.6 %collective-permute-start.19 = (f16[512,512]{1,0:T(8,128)(2,1)S(1)}, f16[512,512]{1,0:T(8,128)(2,1)S(1)}, u32[]{:S(2)}, u32[]{:S(2)}) collective-permute-start(f16[512,512]{1,0:T(8,128)(2,1)S(1)} %multiply_convert_fusion), channel_id=1, source_target_pairs={{0,2},{1,5},{2,0},{3,7},{4,6},{5,1},{6,4},{7,3},{8,10},{9,13},{10,... | collective-permute-start | bytes 1572872 | tf_op jit(solution)/shard_map/ppermute | solution.py:167
  91.0 3.9 %kept_half.3 = (f32[512,512]{1,0:T(8,128)S(1)}, f32[1,1]{1,0:T(1,128)}) custom-call(s32[17]{0:T(128)S(1)} %stack.60.place_ref, s32[128]{0:T(128)S(1)} %reshape.9.mask_ref, bf16[256,512]{1,0:T(8,128)(2,1)S(1)} %convert_element_type.63.refs_0_, bf16[256,512]{1,0:T(8,128)(2,1)S(1)} %collective-permute-done.9.refs_1_, ...), custom_call_target="tpu_custom_call" | custom-call | flops 1073741824 | bytes 8388608 | tf_op jit(solution)/shard_map/kept_half/pallas_call | solution.py:131
  94.8 3.8 %collective-permute-done.19 = f16[512,512]{1,0:T(8,128)(2,1)S(1)} collective-permute-done((f16[512,512]{1,0:T(8,128)(2,1)S(1)}, f16[512,512]{1,0:T(8,128)(2,1)S(1)}, u32[]{:S(2)}, u32[]{:S(2)}) %collective-permute-start.19) | collective-permute-done | bytes 524320 | tf_op jit(solution)/shard_map/ppermute | solution.py:167
  98.8 1.6 %collective-permute-start.20 = (f16[256,512]{1,0:T(8,128)(2,1)S(1)}, f16[256,512]{1,0:T(8,128)(2,1)S(1)}, u32[]{:S(2)}, u32[]{:S(2)}) collective-permute-start(f16[256,512]{1,0:T(8,128)(2,1)S(1)} %dynamic-slice_convert_fusion), channel_id=1, source_target_pairs={{0,4},{1,3},{2,6},{3,1},{4,0},{5,7},{6,2},{7,5},{8,12},{9,11},{10,... | collective-permute-start | bytes 786440 | tf_op jit(solution)/shard_map/ppermute | solution.py:167
  100.4 4.9 %collective-permute-done.20 = f16[256,512]{1,0:T(8,128)(2,1)S(1)} collective-permute-done((f16[256,512]{1,0:T(8,128)(2,1)S(1)}, f16[256,512]{1,0:T(8,128)(2,1)S(1)}, u32[]{:S(2)}, u32[]{:S(2)}) %collective-permute-start.20) | collective-permute-done | bytes 262176 | tf_op jit(solution)/shard_map/ppermute | solution.py:167
  105.4 0.4 collective-permute-start.21
  105.9 1.2 collective-permute-done.22
  108.4 2.8 %collective-permute-start.23 = (f32[]{:T(128)}, f32[]{:T(128)}, u32[]{:S(2)}, u32[]{:S(2)}) collective-permute-start(f32[]{:T(128)} %add.163), channel_id=1, source_target_pairs={{0,2},{1,5},{2,0},{3,7},{4,6},{5,1},{6,4},{7,3},{8,10},{9,13},{10,... | collective-permute-start | bytes 20 | tf_op jit(solution)/shard_map/ppermute | solution.py:167
  111.3 0.7 collective-permute-done.23
  112.7 3.2 %collective-permute-start.24 = (f32[]{:T(128)}, f32[]{:T(128)}, u32[]{:S(2)}, u32[]{:S(2)}) collective-permute-start(f32[]{:T(128)} %add.164), channel_id=1, source_target_pairs={{0,4},{1,3},{2,6},{3,1},{4,0},{5,7},{6,2},{7,5},{8,12},{9,11},{10,... | collective-permute-start | bytes 20 | tf_op jit(solution)/shard_map/ppermute | solution.py:167
  115.8 0.4 collective-permute-done.24
  116.9 4.0 %collective-permute-start.25 = (f32[]{:T(128)}, f32[]{:T(128)}, u32[]{:S(2)}, u32[]{:S(2)}) collective-permute-start(f32[]{:T(128)} %add.165), channel_id=1, source_target_pairs={{0,8},{1,9},{2,10},{3,11},{4,12},{5,13},{6,14},{7,15},{8,0},{9,1},... | collective-permute-start | bytes 20 | tf_op jit(solution)/shard_map/ppermute | solution.py:167
  121.0 0.4 collective-permute-done.25
  122.2 2.0 %multiply_reduce_fusion.1 = (f32[]{:T(128)}, f32[256,512]{1,0:T(8,128)S(1)}) fusion(f32[]{:T(128)S(6)} %div.69, f32[1024,512]{1,0:T(8,128)} %param.6, s32[]{:T(128)S(6)} %select_n.84, f32[]{:T(128)S(6)} %div.67, f32[]{:T(128)S(6)} %div.64, f16[256,512]{1,0:T(8,128)(2,1)S(1)} %collective-permute-done.21, f16[256,512]{1,0:T(8,128)(2,1)S(1)} %add_convert_fusion, ...), kind=kLoop, calls=%fused_computation.6 | loop fusion | flops 2097151 | bytes 2097176 | tf_op jit(solution)/shard_map/reduce_sum | solution.py:241
  124.2 1.8 %collective-permute-start.26 = (f16[256,512]{1,0:T(8,128)(2,1)S(1)}, f16[256,512]{1,0:T(8,128)(2,1)S(1)}, u32[]{:S(2)}, u32[]{:S(2)}) collective-permute-start(f16[256,512]{1,0:T(8,128)(2,1)S(1)} %convert_element_type.71), channel_id=1, source_target_pairs={{0,4},{1,3},{2,6},{3,1},{4,0},{5,7},{6,2},{7,5},{8,12},{9,11},{10,... | collective-permute-start | bytes 786440 | tf_op jit(solution)/shard_map/ppermute | solution.py:167
  126.0 1.2 collective-permute-done.27
  128.6 2.0 %collective-permute-done.26 = f16[256,512]{1,0:T(8,128)(2,1)S(1)} collective-permute-done((f16[256,512]{1,0:T(8,128)(2,1)S(1)}, f16[256,512]{1,0:T(8,128)(2,1)S(1)}, u32[]{:S(2)}, u32[]{:S(2)}) %collective-permute-start.26) | collective-permute-done | bytes 262176 | tf_op jit(solution)/shard_map/ppermute | solution.py:167
  130.6 1.5 %collective-permute-start.29 = (f16[256,512]{1,0:T(8,128)(2,1)S(1)}, f16[256,512]{1,0:T(8,128)(2,1)S(1)}, u32[]{:S(2)}, u32[]{:S(2)}) collective-permute-start(f16[256,512]{1,0:T(8,128)(2,1)S(1)} %collective-permute-done.26), channel_id=1, source_target_pairs={{0,2},{1,5},{2,0},{3,7},{4,6},{5,1},{6,4},{7,3},{8,10},{9,13},{10,... | collective-permute-start | bytes 786440 | tf_op jit(solution)/shard_map/ppermute | solution.py:167
  132.1 0.5 collective-permute-start.28
  132.7 3.6 %collective-permute-start.30 = (f32[]{:T(128)}, f32[]{:T(128)}, u32[]{:S(2)}, u32[]{:S(2)}) collective-permute-start(f32[]{:T(128)} %add.169), channel_id=1, source_target_pairs={{0,4},{1,3},{2,6},{3,1},{4,0},{5,7},{6,2},{7,5},{8,12},{9,11},{10,... | collective-permute-start | bytes 20 | tf_op jit(solution)/shard_map/ppermute | solution.py:167
  137.2 2.9 %collective-permute-start.31 = (f32[]{:T(128)}, f32[]{:T(128)}, u32[]{:S(2)}, u32[]{:S(2)}) collective-permute-start(f32[]{:T(128)} %add.170), channel_id=1, source_target_pairs={{0,2},{1,5},{2,0},{3,7},{4,6},{5,1},{6,4},{7,3},{8,10},{9,13},{10,... | collective-permute-start | bytes 20 | tf_op jit(solution)/shard_map/ppermute | solution.py:167
  141.5 1.7 %convert_multiply_fusion = f32[1024,512]{1,0:T(8,128)} fusion(f16[256,512]{1,0:T(8,128)(2,1)S(1)} %get-tuple-element.46, f16[256,512]{1,0:T(8,128)(2,1)S(1)} %get-tuple-element.45, f16[256,512]{1,0:T(8,128)(2,1)S(1)} %get-tuple-element.44, f16[256,512]{1,0:T(8,128)(2,1)S(1)} %get-tuple-element.43, f32[]{:T(128)S(6)} %rsqrt.7), kind=kLoop, calls=%fused_computation | loop fusion | flops 2621440 | bytes 3145732 | tf_op jit(solution)/shard_map/mul | solution.py:262
  (50 shorter events, 2.1 us)
Async XLA Ops:
  0.0 4.9 %copy-start.13 = (s32[2,8,8]{2,1,0:T(8,128)S(1)}, s32[2,8,8]{2,1,0:T(8,128)}, u32[]{:S(2)}) copy-start(s32[2,8,8]{2,1,0:T(8,128)} %param.9) | copy-start | bytes 1540
  3.4 4.2 %collective-permute-start = (bf16[1024,512]{1,0:T(8,128)(2,1)S(1)}, bf16[1024,512]{1,0:T(8,128)(2,1)S(1)}, u32[]{:S(2)}, u32[]{:S(2)}) collective-permute-start(bf16[1024,512]{1,0:T(8,128)(2,1)S(1)} %get-tuple-element.42.refs_0_), channel_id=1, source_target_pairs={{0,1},{1,0},{2,3},{3,2},{4,5},{5,4},{6,7},{7,6},{8,9},{9,8},{10,11... | collective-permute-start | bytes 3145736 | tf_op jit(solution)/shard_map/ppermute | solution.py:170
  3.9 1.0 copy-start.7
  4.9 1.5 %collective-permute-start.1 = (f32[]{:T(128)}, f32[]{:T(128)}, u32[]{:S(2)}, u32[]{:S(2)}) collective-permute-start(f32[]{:T(128)} %get-tuple-element.41), channel_id=1, source_target_pairs={{0,1},{1,0},{2,3},{3,2},{4,5},{5,4},{6,7},{7,6},{8,9},{9,8},{10,11... | collective-permute-start | bytes 20 | tf_op jit(solution)/shard_map/ppermute | solution.py:170
  7.7 1.0 copy-start.11
  8.7 2.2 %copy-start = (bf16[2,1024,1024]{2,1,0:T(8,128)(2,1)S(1)}, bf16[2,1024,1024]{2,1,0:T(8,128)(2,1)}, u32[]{:S(2)}) copy-start(bf16[2,1024,1024]{2,1,0:T(8,128)(2,1)} %refs_6_.1) | copy-start | bytes 12582916
  10.9 1.2 copy-start.8
  12.1 1.6 %copy-start.9 = (bf16[2,1024,512]{2,1,0:T(8,128)(2,1)S(1)}, bf16[2,1024,512]{2,1,0:T(8,128)(2,1)}, u32[]{:S(2)}) copy-start(bf16[2,1024,512]{2,1,0:T(8,128)(2,1)} %refs_8_.1) | copy-start | bytes 6291460
  13.7 1.2 copy-start.12
  14.9 10.3 %copy-start.4 = (f32[1024,512]{1,0:T(8,128)S(1)}, f32[1024,512]{1,0:T(8,128)}, u32[]{:S(2)}) copy-start(f32[1024,512]{1,0:T(8,128)} %refs_0_.1) | copy-start | bytes 6291460
  20.1 1.3 copy-start.5
  22.3 10.4 %collective-permute-start.2 = (f16[512,512]{1,0:T(8,128)(2,1)}, f16[512,512]{1,0:T(8,128)(2,1)}, u32[]{:S(2)}, u32[]{:S(2)}) collective-permute-start(f16[512,512]{1,0:T(8,128)(2,1)} %multiply_convert_fusion.1), channel_id=1, source_target_pairs={{0,2},{1,5},{2,0},{3,7},{4,6},{5,1},{6,4},{7,3},{8,10},{9,13},{10,... | collective-permute-start | bytes 1572872 | tf_op jit(solution)/shard_map/ppermute | solution.py:167
  25.2 2.2 %copy-start.1 = (bf16[2,1024,1024]{2,1,0:T(8,128)(2,1)S(1)}, bf16[2,1024,1024]{2,1,0:T(8,128)(2,1)}, u32[]{:S(2)}) copy-start(bf16[2,1024,1024]{2,1,0:T(8,128)(2,1)} %refs_6_.1) | copy-start | bytes 12582916
  27.4 1.6 %copy-start.6 = (bf16[2048,512]{1,0:T(8,128)(2,1)S(1)}, bf16[2048,512]{1,0:T(8,128)(2,1)}, u32[]{:S(2)}) copy-start(bf16[2048,512]{1,0:T(8,128)(2,1)} %copy-done.5) | copy-start | bytes 6291460
  34.0 6.5 %collective-permute-start.3 = (f16[256,512]{1,0:T(8,128)(2,1)S(1)}, f16[256,512]{1,0:T(8,128)(2,1)}, u32[]{:S(2)}, u32[]{:S(2)}) collective-permute-start(f16[256,512]{1,0:T(8,128)(2,1)S(1)} %dynamic-slice_convert_fusion.1), channel_id=1, source_target_pairs={{0,4},{1,3},{2,6},{3,1},{4,0},{5,7},{6,2},{7,5},{8,12},{9,11},{10,... | collective-permute-start | bytes 786440 | tf_op jit(solution)/shard_map/ppermute | solution.py:167
  41.6 19.4 %collective-permute-start.4 = (f16[256,512]{1,0:T(8,128)(2,1)S(1)}, f16[256,512]{1,0:T(8,128)(2,1)S(1)}, u32[]{:S(2)}, u32[]{:S(2)}) collective-permute-start(f16[256,512]{1,0:T(8,128)(2,1)S(1)} %add_convert_fusion.1), channel_id=1, source_target_pairs={{0,8},{1,9},{2,10},{3,11},{4,12},{5,13},{6,14},{7,15},{8,0},{9,1},... | collective-permute-start | bytes 786440 | tf_op jit(solution)/shard_map/ppermute | solution.py:167
  44.7 1.3 collective-permute-start.5
  47.2 3.7 %collective-permute-start.6 = (f32[]{:T(128)}, f32[]{:T(128)}, u32[]{:S(2)}, u32[]{:S(2)}) collective-permute-start(f32[]{:T(128)} %add.143), channel_id=1, source_target_pairs={{0,2},{1,5},{2,0},{3,7},{4,6},{5,1},{6,4},{7,3},{8,10},{9,13},{10,... | collective-permute-start | bytes 20 | tf_op jit(solution)/shard_map/ppermute | solution.py:167
  51.5 3.8 %collective-permute-start.7 = (f32[]{:T(128)}, f32[]{:T(128)}, u32[]{:S(2)}, u32[]{:S(2)}) collective-permute-start(f32[]{:T(128)} %add.144), channel_id=1, source_target_pairs={{0,4},{1,3},{2,6},{3,1},{4,0},{5,7},{6,2},{7,5},{8,12},{9,11},{10,... | collective-permute-start | bytes 20 | tf_op jit(solution)/shard_map/ppermute | solution.py:167
  55.8 4.6 %collective-permute-start.8 = (f32[]{:T(128)}, f32[]{:T(128)}, u32[]{:S(2)}, u32[]{:S(2)}) collective-permute-start(f32[]{:T(128)} %add.145), channel_id=1, source_target_pairs={{0,8},{1,9},{2,10},{3,11},{4,12},{5,13},{6,14},{7,15},{8,0},{9,1},... | collective-permute-start | bytes 20 | tf_op jit(solution)/shard_map/ppermute | solution.py:167
  63.1 6.4 %collective-permute-start.9 = (bf16[256,512]{1,0:T(8,128)(2,1)S(1)}, bf16[256,512]{1,0:T(8,128)(2,1)S(1)}, u32[]{:S(2)}, u32[]{:S(2)}) collective-permute-start(bf16[256,512]{1,0:T(8,128)(2,1)S(1)} %convert_element_type.63.refs_0_), channel_id=1, source_target_pairs={{0,4},{1,3},{2,6},{3,1},{4,0},{5,7},{6,2},{7,5},{8,12},{9,11},{10,... | collective-permute-start | bytes 786440 | tf_op jit(solution)/shard_map/ppermute | solution.py:167
  64.7 9.7 %collective-permute-start.14 = (bf16[256,512]{1,0:T(8,128)(2,1)S(1)}, bf16[256,512]{1,0:T(8,128)(2,1)S(1)}, u32[]{:S(2)}, u32[]{:S(2)}) collective-permute-start(bf16[256,512]{1,0:T(8,128)(2,1)S(1)} %convert_element_type.63.refs_0_), channel_id=1, source_target_pairs={{0,2},{1,5},{2,0},{3,7},{4,6},{5,1},{6,4},{7,3},{8,10},{9,13},{10,... | collective-permute-start | bytes 786440 | tf_op jit(solution)/shard_map/ppermute | solution.py:167
  66.2 1.3 collective-permute-start.10
  69.5 6.4 %collective-permute-start.11 = (bf16[256,512]{1,0:T(8,128)(2,1)S(1)}, bf16[256,512]{1,0:T(8,128)(2,1)S(1)}, u32[]{:S(2)}, u32[]{:S(2)}) collective-permute-start(bf16[256,512]{1,0:T(8,128)(2,1)S(1)} %collective-permute-done.9.refs_1_), channel_id=1, source_target_pairs={{0,2},{1,5},{2,0},{3,7},{4,6},{5,1},{6,4},{7,3},{8,10},{9,13},{10,... | collective-permute-start | bytes 786440 | tf_op jit(solution)/shard_map/ppermute | solution.py:167
  71.0 9.3 %collective-permute-start.15 = (bf16[256,512]{1,0:T(8,128)(2,1)S(1)}, bf16[256,512]{1,0:T(8,128)(2,1)S(1)}, u32[]{:S(2)}, u32[]{:S(2)}) collective-permute-start(bf16[256,512]{1,0:T(8,128)(2,1)S(1)} %convert_element_type.63.refs_0_), channel_id=1, source_target_pairs={{0,1},{1,0},{2,3},{3,2},{4,5},{5,4},{6,7},{7,6},{8,9},{9,8},{10,11... | collective-permute-start | bytes 786440 | tf_op jit(solution)/shard_map/ppermute | solution.py:170
  71.0 9.3 %collective-permute-start.16 = (bf16[256,512]{1,0:T(8,128)(2,1)S(1)}, bf16[256,512]{1,0:T(8,128)(2,1)S(1)}, u32[]{:S(2)}, u32[]{:S(2)}) collective-permute-start(bf16[256,512]{1,0:T(8,128)(2,1)S(1)} %collective-permute-done.9.refs_1_), channel_id=1, source_target_pairs={{0,1},{1,0},{2,3},{3,2},{4,5},{5,4},{6,7},{7,6},{8,9},{9,8},{10,11... | collective-permute-start | bytes 786440 | tf_op jit(solution)/shard_map/ppermute | solution.py:170
  71.5 3.5 %collective-permute-start.12 = (f32[]{:T(128)}, f32[]{:T(128)}, u32[]{:S(2)}, u32[]{:S(2)}) collective-permute-start(f32[]{:T(128)} %add.148), channel_id=1, source_target_pairs={{0,4},{1,3},{2,6},{3,1},{4,0},{5,7},{6,2},{7,5},{8,12},{9,11},{10,... | collective-permute-start | bytes 20 | tf_op jit(solution)/shard_map/ppermute | solution.py:167
  74.4 6.0 %collective-permute-start.17 = (bf16[256,512]{1,0:T(8,128)(2,1)S(1)}, bf16[256,512]{1,0:T(8,128)(2,1)S(1)}, u32[]{:S(2)}, u32[]{:S(2)}) collective-permute-start(bf16[256,512]{1,0:T(8,128)(2,1)S(1)} %collective-permute-done.14.refs_2_), channel_id=1, source_target_pairs={{0,1},{1,0},{2,3},{3,2},{4,5},{5,4},{6,7},{7,6},{8,9},{9,8},{10,11... | collective-permute-start | bytes 786440 | tf_op jit(solution)/shard_map/ppermute | solution.py:170
  75.9 4.5 %collective-permute-start.18 = (bf16[256,512]{1,0:T(8,128)(2,1)S(1)}, bf16[256,512]{1,0:T(8,128)(2,1)S(1)}, u32[]{:S(2)}, u32[]{:S(2)}) collective-permute-start(bf16[256,512]{1,0:T(8,128)(2,1)S(1)} %collective-permute-done.11.refs_3_), channel_id=1, source_target_pairs={{0,1},{1,0},{2,3},{3,2},{4,5},{5,4},{6,7},{7,6},{8,9},{9,8},{10,11... | collective-permute-start | bytes 786440 | tf_op jit(solution)/shard_map/ppermute | solution.py:170
  76.0 3.6 %collective-permute-start.13 = (f32[]{:T(128)}, f32[]{:T(128)}, u32[]{:S(2)}, u32[]{:S(2)}) collective-permute-start(f32[]{:T(128)} %add.149), channel_id=1, source_target_pairs={{0,2},{1,5},{2,0},{3,7},{4,6},{5,1},{6,4},{7,3},{8,10},{9,13},{10,... | collective-permute-start | bytes 20 | tf_op jit(solution)/shard_map/ppermute | solution.py:167
  80.3 2.2 %copy-start.2 = (bf16[2,1024,1024]{2,1,0:T(8,128)(2,1)S(1)}, bf16[2,1024,1024]{2,1,0:T(8,128)(2,1)}, u32[]{:S(2)}) copy-start(bf16[2,1024,1024]{2,1,0:T(8,128)(2,1)} %refs_6_.1) | copy-start | bytes 12582916
  82.5 1.6 %copy-start.10 = (bf16[2,1024,512]{2,1,0:T(8,128)(2,1)S(1)}, bf16[2,1024,512]{2,1,0:T(8,128)(2,1)}, u32[]{:S(2)}) copy-start(bf16[2,1024,512]{2,1,0:T(8,128)(2,1)} %refs_8_.1) | copy-start | bytes 6291460
  84.1 6.8 %copy-start.3 = (bf16[2,1024,1024]{2,1,0:T(8,128)(2,1)S(1)}, bf16[2,1024,1024]{2,1,0:T(8,128)(2,1)}, u32[]{:S(2)}) copy-start(bf16[2,1024,1024]{2,1,0:T(8,128)(2,1)} %refs_6_.1) | copy-start | bytes 12582916
  89.4 9.2 %collective-permute-start.19 = (f16[512,512]{1,0:T(8,128)(2,1)S(1)}, f16[512,512]{1,0:T(8,128)(2,1)S(1)}, u32[]{:S(2)}, u32[]{:S(2)}) collective-permute-start(f16[512,512]{1,0:T(8,128)(2,1)S(1)} %multiply_convert_fusion), channel_id=1, source_target_pairs={{0,2},{1,5},{2,0},{3,7},{4,6},{5,1},{6,4},{7,3},{8,10},{9,13},{10,... | collective-permute-start | bytes 1572872 | tf_op jit(solution)/shard_map/ppermute | solution.py:167
  98.8 6.4 %collective-permute-start.20 = (f16[256,512]{1,0:T(8,128)(2,1)S(1)}, f16[256,512]{1,0:T(8,128)(2,1)S(1)}, u32[]{:S(2)}, u32[]{:S(2)}) collective-permute-start(f16[256,512]{1,0:T(8,128)(2,1)S(1)} %dynamic-slice_convert_fusion), channel_id=1, source_target_pairs={{0,4},{1,3},{2,6},{3,1},{4,0},{5,7},{6,2},{7,5},{8,12},{9,11},{10,... | collective-permute-start | bytes 786440 | tf_op jit(solution)/shard_map/ppermute | solution.py:167
  105.4 16.8 %collective-permute-start.21 = (f16[256,512]{1,0:T(8,128)(2,1)S(1)}, f16[256,512]{1,0:T(8,128)(2,1)S(1)}, u32[]{:S(2)}, u32[]{:S(2)}) collective-permute-start(f16[256,512]{1,0:T(8,128)(2,1)S(1)} %add_convert_fusion), channel_id=1, source_target_pairs={{0,8},{1,9},{2,10},{3,11},{4,12},{5,13},{6,14},{7,15},{8,0},{9,1},... | collective-permute-start | bytes 786440 | tf_op jit(solution)/shard_map/ppermute | solution.py:167
  105.8 1.3 collective-permute-start.22
  108.4 3.6 %collective-permute-start.23 = (f32[]{:T(128)}, f32[]{:T(128)}, u32[]{:S(2)}, u32[]{:S(2)}) collective-permute-start(f32[]{:T(128)} %add.163), channel_id=1, source_target_pairs={{0,2},{1,5},{2,0},{3,7},{4,6},{5,1},{6,4},{7,3},{8,10},{9,13},{10,... | collective-permute-start | bytes 20 | tf_op jit(solution)/shard_map/ppermute | solution.py:167
  112.7 3.6 %collective-permute-start.24 = (f32[]{:T(128)}, f32[]{:T(128)}, u32[]{:S(2)}, u32[]{:S(2)}) collective-permute-start(f32[]{:T(128)} %add.164), channel_id=1, source_target_pairs={{0,4},{1,3},{2,6},{3,1},{4,0},{5,7},{6,2},{7,5},{8,12},{9,11},{10,... | collective-permute-start | bytes 20 | tf_op jit(solution)/shard_map/ppermute | solution.py:167
  116.9 4.5 %collective-permute-start.25 = (f32[]{:T(128)}, f32[]{:T(128)}, u32[]{:S(2)}, u32[]{:S(2)}) collective-permute-start(f32[]{:T(128)} %add.165), channel_id=1, source_target_pairs={{0,8},{1,9},{2,10},{3,11},{4,12},{5,13},{6,14},{7,15},{8,0},{9,1},... | collective-permute-start | bytes 20 | tf_op jit(solution)/shard_map/ppermute | solution.py:167
  124.2 6.4 %collective-permute-start.26 = (f16[256,512]{1,0:T(8,128)(2,1)S(1)}, f16[256,512]{1,0:T(8,128)(2,1)S(1)}, u32[]{:S(2)}, u32[]{:S(2)}) collective-permute-start(f16[256,512]{1,0:T(8,128)(2,1)S(1)} %convert_element_type.71), channel_id=1, source_target_pairs={{0,4},{1,3},{2,6},{3,1},{4,0},{5,7},{6,2},{7,5},{8,12},{9,11},{10,... | collective-permute-start | bytes 786440 | tf_op jit(solution)/shard_map/ppermute | solution.py:167
  126.0 1.2 collective-permute-start.27
  130.6 6.5 %collective-permute-start.29 = (f16[256,512]{1,0:T(8,128)(2,1)S(1)}, f16[256,512]{1,0:T(8,128)(2,1)S(1)}, u32[]{:S(2)}, u32[]{:S(2)}) collective-permute-start(f16[256,512]{1,0:T(8,128)(2,1)S(1)} %collective-permute-done.26), channel_id=1, source_target_pairs={{0,2},{1,5},{2,0},{3,7},{4,6},{5,1},{6,4},{7,3},{8,10},{9,13},{10,... | collective-permute-start | bytes 786440 | tf_op jit(solution)/shard_map/ppermute | solution.py:167
  132.1 8.0 %collective-permute-start.28 = (f16[256,512]{1,0:T(8,128)(2,1)S(1)}, f16[256,512]{1,0:T(8,128)(2,1)S(1)}, u32[]{:S(2)}, u32[]{:S(2)}) collective-permute-start(f16[256,512]{1,0:T(8,128)(2,1)S(1)} %convert_element_type.71), channel_id=1, source_target_pairs={{0,2},{1,5},{2,0},{3,7},{4,6},{5,1},{6,4},{7,3},{8,10},{9,13},{10,... | collective-permute-start | bytes 786440 | tf_op jit(solution)/shard_map/ppermute | solution.py:167
  132.7 3.8 %collective-permute-start.30 = (f32[]{:T(128)}, f32[]{:T(128)}, u32[]{:S(2)}, u32[]{:S(2)}) collective-permute-start(f32[]{:T(128)} %add.169), channel_id=1, source_target_pairs={{0,4},{1,3},{2,6},{3,1},{4,0},{5,7},{6,2},{7,5},{8,12},{9,11},{10,... | collective-permute-start | bytes 20 | tf_op jit(solution)/shard_map/ppermute | solution.py:167
  137.2 3.6 %collective-permute-start.31 = (f32[]{:T(128)}, f32[]{:T(128)}, u32[]{:S(2)}, u32[]{:S(2)}) collective-permute-start(f32[]{:T(128)} %add.170), channel_id=1, source_target_pairs={{0,2},{1,5},{2,0},{3,7},{4,6},{5,1},{6,4},{7,3},{8,10},{9,13},{10,... | collective-permute-start | bytes 20 | tf_op jit(solution)/shard_map/ppermute | solution.py:167

commit v3 on v0

v3 whole, which is shorter than its diff:
```python
import functools

import jax
import jax.numpy as jnp
from jax import lax
from jax.experimental import pallas as pl
from jax.experimental.pallas import tpu as pltpu
from jax.sharding import PartitionSpec as P

STEPS = 2
CHUNKS = 2
EPS = 1e-06
TOP = 0.1875
BOTH = ("op", "col")
F32, F16, BF16 = jnp.float32, jnp.float16, jnp.bfloat16
SDS = jax.ShapeDtypeStruct
ANY = pl.BlockSpec(memory_space=pl.ANY)
VMEM = pl.BlockSpec(memory_space=pltpu.VMEM)
SMEM = pl.BlockSpec(memory_space=pltpu.SMEM)
ONE = SDS((1, 1), F32)
ORDER = ((1, 2), (2, 1))


def call(kernel, name, outs, out_specs, in_specs, args, flops, moved, scratch=()):
    return pl.pallas_call(
        kernel, out_shape=outs, in_specs=in_specs, out_specs=out_specs, scratch_shapes=scratch, name=name,
        compiler_params=pltpu.CompilerParams(vmem_limit_bytes=24 * 2 ** 20),
        cost_estimate=pl.CostEstimate(flops=flops, bytes_accessed=moved, transcendentals=0))(*args)


def total(own_ref, other_ref):
    return jnp.full((1, 1), own_ref[0, 0] + other_ref[0, 0], F32)


def scale_of(reach, weight):
    return 32768.0 / (reach * (jnp.sqrt(weight) + 1e-30))


def open_vector(coef):
    rows, cols = coef.shape
    parts = 4
    step = rows // parts

    def kernel(coef_ref, full_ref, wave_ref, weight_ref, sems):
        copies = []
        for p in range(parts):
            at = pl.ds(p * step, step)
            copies.append(pltpu.make_async_copy(coef_ref.at[at], full_ref.at[at], sems.at[p]))
            copies[-1].start()
        weight = jnp.zeros((8, cols), F32)
        for p in range(parts):
            copies[p].wait()
            block = full_ref[p * step:(p + 1) * step, :]
            wave_ref[p * step:(p + 1) * step, :] = block.astype(BF16)
            weight = weight + jnp.sum((block * block).reshape(step // 8, 8, cols), axis=0)
        weight_ref[0, 0] = jnp.sum(weight)

    return call(kernel, "open_vector", (SDS((rows, cols), F32), SDS((rows, cols), BF16), ONE), (VMEM, VMEM, SMEM),
                [ANY], (coef,), 3 * rows * cols, 8 * rows * cols, [pltpu.SemaphoreType.DMA((parts,))])


def masked_halves(left, mask, blocks):
    pairs, width, _ = left.shape
    half, inside = width // 2, width // blocks

    def kernel(mask_ref, left_ref, out_ref, buf, sems):
        copies = {}
        for h in range(2):
            for k in range(pairs):
                at = (k, pl.ds(h * half, half))
                copies[h, k] = pltpu.make_async_copy(left_ref.at[at], buf.at[at], sems.at[h * pairs + k])
                copies[h, k].start()
        for h in range(2):
            for k in range(pairs):
                copies[h, k].wait()
                for i in range(half // inside):
                    for j in range(blocks):
                        keep = mask_ref[(k * blocks + h * half // inside + i) * blocks + j]
                        block = buf[k, h * half + i * inside:h * half + (i + 1) * inside, j * inside:(j + 1) * inside]
                        out_ref[h, i * inside:(i + 1) * inside, k * width + j * inside:k * width + (j + 1) * inside] = (
                            jnp.where(keep != 0, block, jnp.zeros_like(block)))

    return call(kernel, "masked_halves", SDS((2, half, pairs * width), BF16), VMEM, [SMEM, ANY], (mask, left),
                left.size, 4 * left.size,
                [pltpu.VMEM(left.shape, BF16), pltpu.SemaphoreType.DMA((2 * pairs,))])


def sent_half(chunk, reach, place, weights, own, other, right, masked):
    pairs, width, cols = right.shape
    size, half = cols // CHUNKS, width // 2
    at = slice(chunk * size, (chunk + 1) * size)

    def kernel(place_ref, a_ref, b_ref, own_ref, other_ref, right_ref, masked_ref, inner_ref, send_ref):
        scale = scale_of(reach, total(a_ref, b_ref))
        here = pl.ds(pl.multiple_of(place_ref[0], cols), cols)
        there = pl.ds(pl.multiple_of(place_ref[1], cols), cols)
        for k in range(pairs):
            inner_ref[k * width:(k + 1) * width, :] = (
                jnp.dot(own_ref[...], right_ref[k, here, at], preferred_element_type=F32)
                + jnp.dot(other_ref[...], right_ref[k, there, at], preferred_element_type=F32)).astype(BF16)
        send_ref[...] = scale * jnp.dot(masked_ref[place_ref[2]], inner_ref[...], preferred_element_type=F32)

    return call(kernel, "sent_half_%d" % chunk, (SDS((pairs * width, size), BF16), SDS((half, size), F32)),
                (VMEM, VMEM), [SMEM] * 3 + [VMEM] * 4, (place, *weights, own, other, right, masked),
                3 * pairs * width * width * size, 2 ** 20)


def kept_half(reach, place, weights, inner, masked):
    _, half, depth = masked.shape
    size = inner.shape[1]

    def kernel(place_ref, a_ref, b_ref, inner_ref, masked_ref, keep_ref):
        scale = scale_of(reach, total(a_ref, b_ref))
        keep_ref[...] = scale * jnp.dot(masked_ref[1 - place_ref[2]], inner_ref[...], preferred_element_type=F32)

    return call(kernel, "kept_half", SDS((half, size), F32), VMEM, [SMEM] * 3 + [VMEM] * 2,
                (place, *weights, inner, masked), 2 * half * depth * size, 2 ** 20)


def correlate(vector, sigmas):
    rows, cols = vector.shape
    size = cols // len(sigmas)

    def kernel(vector_ref, *refs):
        out = jnp.zeros((8, size), F32)
        for c, sigma_ref in enumerate(refs[:-1]):
            product = vector_ref[:, c * size:(c + 1) * size] * sigma_ref[...]
            out = out + jnp.sum(product.reshape(rows // 8, 8, size), axis=0)
        refs[-1][0, 0] = jnp.sum(out)

    return call(kernel, "correlate", ONE, SMEM, [VMEM] * (1 + len(sigmas)), (vector, *sigmas), 2 * rows * cols, 2 ** 20)


def correct(first, reach, cells, vector, sigmas, diag, corr, weights):
    rows, cols = vector.shape
    size = cols // len(sigmas)

    def kernel(corr_a, corr_b, weight_a, weight_b, vector_ref, diag_ref, *refs):
        sigma_refs, (moved_ref, wave_ref, square_ref) = refs[:-3], refs[-3:]
        weight = total(weight_a, weight_b)
        scale = scale_of(reach, weight)
        norm = jnp.ones((1, 1), F32) if first else lax.rsqrt(weight / cells + EPS)
        square = norm * norm
        theta = (total(corr_a, corr_b) / scale * square / cells) / (weight * square / cells + EPS)
        unit = norm / scale
        out = jnp.zeros((8, size), F32)
        for c, sigma_ref in enumerate(sigma_refs):
            at = slice(c * size, (c + 1) * size)
            coef = vector_ref[:, at] * norm
            spacing = diag_ref[:, at] - theta
            moved = coef - (sigma_ref[...] * unit - theta * coef) * spacing / jnp.maximum(spacing * spacing, 1.0)
            moved_ref[:, at] = moved
            wave_ref[:, at] = moved.astype(BF16)
            out = out + jnp.sum((moved * moved).reshape(rows // 8, 8, size), axis=0)
        square_ref[0, 0] = jnp.sum(out)

    return call(kernel, "correct", (SDS((rows, cols), F32), SDS((rows, cols), BF16), ONE), (VMEM, VMEM, SMEM),
                [SMEM] * 4 + [VMEM] * (2 + len(sigmas)), (*corr, *weights, vector, diag, *sigmas),
                12 * rows * cols, 2 ** 20)


def normalise(cells, vector, weights):
    rows, cols = vector.shape
    parts = 4
    step = rows // parts

    def kernel(weight_a, weight_b, vector_ref, out_ref, buf, sems):
        norm = lax.rsqrt(total(weight_a, weight_b) / cells + EPS)
        copies = []
        for p in range(parts):
            at = pl.ds(p * step, step)
            buf[p * step:(p + 1) * step, :] = vector_ref[p * step:(p + 1) * step, :] * norm
            copies.append(pltpu.make_async_copy(buf.at[at], out_ref.at[at], sems.at[p]))
            copies[-1].start()
        for copy in copies:
            copy.wait()

    return call(kernel, "normalise", SDS((rows, cols), F32), ANY, [SMEM] * 2 + [VMEM], (*weights, vector),
                rows * cols, 8 * rows * cols, [pltpu.VMEM((rows, cols), F32), pltpu.SemaphoreType.DMA((parts,))])


def local(ops, cols, wave_coef, diag_energy, left, right, block_mask):
    pairs, width, _ = left.shape
    own_cols = right.shape[2]
    blocks = block_mask.shape[1]
    cells = float(width * width)
    half, quarter, size = width // 2, width // 4, own_cols // CHUNKS
    stages = ops.bit_length() - 1
    reach = float(pairs * ops * width) * TOP * TOP

    def swap(x, stage):
        pairing = []
        for o in range(ops):
            for c in range(cols):
                bit = ORDER[c % 2][stage] if stage < 2 else 1 << stage
                pairing.append((o * cols + c, (o ^ bit) * cols + c))
        return lax.ppermute(x, BOTH, pairing)

    def across(x):
        return lax.ppermute(x, "col", [(c, c ^ 1) for c in range(cols)])

    me, core = lax.axis_index("op"), lax.axis_index("col")
    low, high = me % 2, (me // 2) % 2
    bit0, bit1 = jnp.where(core == 0, low, high), jnp.where(core == 0, high, low)
    zero = jnp.zeros((), jnp.int32)
    place = jnp.stack([core * own_cols, (1 - core) * own_cols, 1 - bit0]).astype(jnp.int32)

    def reduced(send, keep):
        got = swap(send.astype(F16), 0)
        keep = keep + got.astype(F32)
        send = lax.dynamic_slice(keep, ((1 - bit1) * quarter, zero), (quarter, size)).astype(F16)
        keep = lax.dynamic_slice(keep, (bit1 * quarter, zero), (quarter, size))
        keep = keep + swap(send, 1).astype(F32)
        for stage in range(2, stages):
            send = keep.astype(F16)
            keep = send.astype(F32) + swap(send, stage).astype(F32)
        return keep.astype(F16)

    def gathered(piece):
        p1, p2 = swap(piece, 1), swap(piece, 0)
        p3 = swap(p1, 0)
        near0, near1 = jnp.where(bit1 == 0, piece, p1), jnp.where(bit1 == 0, p1, piece)
        far0, far1 = jnp.where(bit1 == 0, p2, p3), jnp.where(bit1 == 0, p3, p2)
        return jnp.concatenate([
            jnp.where(bit0 == 0, near0, far0), jnp.where(bit0 == 0, near1, far1),
            jnp.where(bit0 == 0, far0, near0), jnp.where(bit0 == 0, far1, near1)], axis=0).astype(F32)

    vector, own, weight = open_vector(wave_coef)
    masked = masked_halves(left, block_mask.reshape(-1), blocks)
    for step in range(STEPS):
        other = across(own)
        weights = (weight, across(weight))
        parts = [sent_half(c, reach, place, weights, own, other, right, masked) for c in range(CHUNKS)]
        sigmas = [gathered(reduced(send, kept_half(reach, place, weights, inner, masked))) for inner, send in parts]
        corr = correlate(vector, sigmas)
        vector, own, weight = correct(
            step == 0, reach, cells, vector, sigmas, diag_energy, (corr, across(corr)), weights)
    return normalise(cells, vector, (weight, across(weight)))


def solution(mesh):
    in_specs = (
        P("geom", "col"),
        P("geom", "col"),
        P(("geom", "op"), None, None),
        P(("geom", "op"), None, "col"),
        P(("geom", "op"), None, None),
    )
    body = functools.partial(local, mesh.shape["op"], mesh.shape["col"])
    return jax.shard_map(body, mesh=mesh, in_specs=in_specs, out_specs=P("geom", "col"), check_vma=False)
```

time: 310 us -> 131 us (0.42)
  waiting for transfers between devices: 218 us -> 43.2 us
  Pallas kernels: 0 us -> 45.9 us
  other arithmetic: 34.9 us -> 3.04 us
  starting transfers between devices: 0.13 us -> 29.8 us
  matrix products: 17.3 us -> 0 us
  between operations: 17 us -> 0.58 us
  blocking collectives: 12.5 us -> 0 us
    psum x2 -> x0, waiting for transfers between devices: 207 us -> none  [local(): sigma = lax.psum(partial_sum, 'op')]
    pallas_call x0 -> x15, Pallas kernels: none -> 45.9 us  [call(): pl.pallas_call(kernel, out_shape=outs, in_specs=in_specs, out_specs=out_s...]
    ppermute x0 -> x31, waiting for transfers between devices: none -> 43.2 us  [the longest x24 37.6 us: swap(): return lax.ppermute(x, BOTH, pairing)]
    ppermute x0 -> x31, starting transfers between devices: none -> 29.8 us  [the longest x24 28.3 us: swap(): return lax.ppermute(x, BOTH, pairing)]
    reduce_sum x4 -> x0, other arithmetic: 18 us -> none  [the longest x2 11.2 us: update_cols(): norm_sum = lax.psum(jnp.sum(moved * moved), 'col')]
    dot_general x2 -> x0, matrix products: 17.3 us -> none  [local(): jnp.einsum('kab,kbc->ac', masked, inner, preferred_element_type=jnp.float32)]
    psum x4 -> x0, blocking collectives: 12.5 us -> none  [the longest x2 6.27 us: update_cols(): norm_sum = lax.psum(jnp.sum(moved * moved), 'col')]
    mul x2 -> x0, other arithmetic: 11.2 us -> none  [the longest x1 8.04 us: apply_mask(): return (grid * keep).reshape(total, width, width)]
  transfers between devices with their start and end apart: 4 -> 31, of which waited for: 3 -> 21; matrix products, arithmetic and copies ran while one was open for 6% -> 2% of each run, Pallas kernels for 0% -> 16%
where the time goes in v3:
time: 131 us
  Pallas kernels  45.9 us (35%)
  waiting for transfers between devices  43.2 us (33%)
  starting transfers between devices  29.8 us (23%)
  local copies, waits for them, and re-layouts  8.37 us (6%)
  other arithmetic  3.04 us (2%)
    pallas_call x15, Pallas kernels, call(): pl.pallas_call(kernel, out_shape=outs, in_specs=in_specs, out_specs=out_s...  45.9 us
    ppermute x24, waiting for transfers between devices, swap(): return lax.ppermute(x, BOTH, pairing)  37.6 us
    ppermute x24, starting transfers between devices, swap(): return lax.ppermute(x, BOTH, pairing)  28.3 us
    unnamed x26, local copies, waits for them, and re-layouts  8.29 us
    ppermute x7, waiting for transfers between devices, across(): return lax.ppermute(x, 'col', [(c, c ^ 1) for c in range(cols)])  5.6 us
  transfers between devices with their start and end apart: 31, of which 21 were waited for; matrix products, arithmetic and copies ran while one was open for 2% of the time, Pallas kernels for 16%

profile of v3, /device:TPU:0, one launch (start us, length us, event | category | flops | bytes accessed | tf_op | source)
XLA Modules:
  0.0 130.9 jit_solution(5463565179976700022)
XLA Ops:
  0.0 1.6 %copy-done.9 = f32[1024,512]{1,0:T(8,128)S(1)} copy-done((f32[1024,512]{1,0:T(8,128)S(1)}, f32[1024,512]{1,0:T(8,128)}, u32[]{:S(2)}) %copy-start.9) | copy-done | bytes 2097176
  1.6 1.0 open_vector.1
  2.6 1.3 %copy-done.6 = f32[1024,512]{1,0:T(8,128)} copy-done((f32[1024,512]{1,0:T(8,128)}, f32[1024,512]{1,0:T(8,128)S(1)}, u32[]{:S(2)}) %copy-start.6) | copy-done | bytes 2097176
  3.9 0.5 collective-permute-start.1
  4.6 2.2 %copy-done.8 = bf16[2,1024,1024]{2,1,0:T(8,128)(2,1)S(1)} copy-done((bf16[2,1024,1024]{2,1,0:T(8,128)(2,1)S(1)}, bf16[2,1024,1024]{2,1,0:T(8,128)(2,1)}, u32[]{:S(2)}) %copy-start.8) | copy-done | bytes 4194328
  6.7 2.0 %masked_halves.1.masked_ref = bf16[2,512,2048]{2,1,0:T(8,128)(2,1)S(1)} custom-call(s32[128]{0:T(128)S(1)} %reshape.3.mask_ref, bf16[2,1024,1024]{2,1,0:T(8,128)(2,1)S(1)} %copy-done.8), custom_call_target="tpu_custom_call" | custom-call | flops 2097152 | bytes 8388608 | tf_op jit(solution)/shard_map/masked_halves/pallas_call | solution.py:25
  8.9 4.8 %sent_half_0.2 = (bf16[2048,256]{1,0:T(8,128)(2,1)S(1)}, f32[512,256]{1,0:T(8,128)S(1)}) custom-call(s32[3]{0:T(128)S(1)} %pad_add_fusion.place_ref, f32[1,1]{1,0:T(1,128)} %get-tuple-element.22.a_ref.weight_a, f32[1,1]{1,0:T(1,128)} %collective-permute-done.b_ref.weight_b, bf16[1024,512]{1,0:T(8,128)(2,1)S(1)} %get-tuple-element.23.own_ref, ...), custom_call_target="tpu_custom_call" | custom-call | flops 1610612736 | bytes 1048576 | tf_op jit(solution)/shard_map/sent_half_0/pallas_call | solution.py:25
  13.7 1.0 copy-done.10
  14.7 3.0 %collective-permute-start.2 = (f16[512,256]{1,0:T(8,128)(2,1)S(1)}, f16[512,256]{1,0:T(8,128)(2,1)}, u32[]{:S(2)}, u32[]{:S(2)}) collective-permute-start(f16[512,256]{1,0:T(8,128)(2,1)S(1)} %convert_element_type.108), channel_id=1, source_target_pairs={{0,2},{1,5},{2,0},{3,7},{4,6},{5,1},{6,4},{7,3},{8,10},{9,13},{10,... | collective-permute-start | bytes 786440 | tf_op jit(solution)/shard_map/ppermute | solution.py:197
  17.8 2.2 %copy-done.1 = bf16[2,512,2048]{2,1,0:T(8,128)(2,1)S(1)} copy-done((bf16[2,512,2048]{2,1,0:T(8,128)(2,1)S(1)}, bf16[2,512,2048]{2,1,0:T(8,128)(2,1)}, u32[]{:S(2)}) %copy-start.1) | copy-done | bytes 4194328
  20.0 5.3 %sent_half_1.2 = (bf16[2048,256]{1,0:T(8,128)(2,1)S(1)}, f32[512,256]{1,0:T(8,128)S(1)}) custom-call(s32[3]{0:T(128)S(1)} %pad_add_fusion.place_ref, f32[1,1]{1,0:T(1,128)} %get-tuple-element.22.a_ref.weight_a, f32[1,1]{1,0:T(1,128)} %collective-permute-done.b_ref.weight_b, bf16[1024,512]{1,0:T(8,128)(2,1)S(1)} %get-tuple-element.23.own_ref, ...), custom_call_target="tpu_custom_call" | custom-call | flops 1610612736 | bytes 1048576 | tf_op jit(solution)/shard_map/sent_half_1/pallas_call | solution.py:25
  25.4 2.5 %kept_half.4 = f32[512,256]{1,0:T(8,128)S(1)} custom-call(s32[3]{0:T(128)S(1)} %pad_add_fusion.place_ref, f32[1,1]{1,0:T(1,128)} %get-tuple-element.22.a_ref.weight_a, f32[1,1]{1,0:T(1,128)} %collective-permute-done.b_ref.weight_b, bf16[2048,256]{1,0:T(8,128)(2,1)S(1)} %copy-done.11, bf16[2,512,2048]{2,1,0:T(8,128)(2,1)S(1)} %copy-done.2), custom_call_target="tpu_custom_call" | custom-call | flops 536870912 | bytes 1048576 | tf_op jit(solution)/shard_map/kept_half/pallas_call | solution.py:25
  27.9 2.5 %kept_half.5 = f32[512,256]{1,0:T(8,128)S(1)} custom-call(s32[3]{0:T(128)S(1)} %pad_add_fusion.place_ref, f32[1,1]{1,0:T(1,128)} %get-tuple-element.22.a_ref.weight_a, f32[1,1]{1,0:T(1,128)} %collective-permute-done.b_ref.weight_b, bf16[2048,256]{1,0:T(8,128)(2,1)S(1)} %get-tuple-element.26.inner_ref, bf16[2,512,2048]{2,1,0:T(8,128)(2,1)S(1)} %copy-done.2), custom_call_target="tpu_custom_call" | custom-call | flops 536870912 | bytes 1048576 | tf_op jit(solution)/shard_map/kept_half/pallas_call | solution.py:25
  30.4 1.0 convert_add_fusion.3
  31.5 2.1 %collective-permute-start.3 = (f16[256,256]{1,0:T(8,128)(2,1)S(1)}, f16[256,256]{1,0:T(8,128)(2,1)S(1)}, u32[]{:S(2)}, u32[]{:S(2)}) collective-permute-start(f16[256,256]{1,0:T(8,128)(2,1)S(1)} %dynamic-slice_convert_fusion.3), channel_id=1, source_target_pairs={{0,4},{1,3},{2,6},{3,1},{4,0},{5,7},{6,2},{7,5},{8,12},{9,11},{10,... | collective-permute-start | bytes 393224 | tf_op jit(solution)/shard_map/ppermute | solution.py:197
  33.8 2.7 %collective-permute-done.3 = f16[256,256]{1,0:T(8,128)(2,1)S(1)} collective-permute-done((f16[256,256]{1,0:T(8,128)(2,1)S(1)}, f16[256,256]{1,0:T(8,128)(2,1)S(1)}, u32[]{:S(2)}, u32[]{:S(2)}) %collective-permute-start.3) | collective-permute-done | bytes 131104 | tf_op jit(solution)/shard_map/ppermute | solution.py:197
  36.6 3.1 %collective-permute-start.4 = (f16[256,256]{1,0:T(8,128)(2,1)S(1)}, f16[256,256]{1,0:T(8,128)(2,1)S(1)}, u32[]{:S(2)}, u32[]{:S(2)}) collective-permute-start(f16[256,256]{1,0:T(8,128)(2,1)S(1)} %add_convert_fusion.7), channel_id=1, source_target_pairs={{0,8},{1,9},{2,10},{3,11},{4,12},{5,13},{6,14},{7,15},{8,0},{9,1},... | collective-permute-start | bytes 393224 | tf_op jit(solution)/shard_map/ppermute | solution.py:197
  39.7 2.7 %collective-permute-start.10 = (f16[256,256]{1,0:T(8,128)(2,1)S(1)}, f16[256,256]{1,0:T(8,128)(2,1)S(1)}, u32[]{:S(2)}, u32[]{:S(2)}) collective-permute-start(f16[256,256]{1,0:T(8,128)(2,1)S(1)} %add_convert_fusion.5), channel_id=1, source_target_pairs={{0,8},{1,9},{2,10},{3,11},{4,12},{5,13},{6,14},{7,15},{8,0},{9,1},... | collective-permute-start | bytes 393224 | tf_op jit(solution)/shard_map/ppermute | solution.py:197
  42.4 6.5 %collective-permute-done.4 = f16[256,256]{1,0:T(8,128)(2,1)S(1)} collective-permute-done((f16[256,256]{1,0:T(8,128)(2,1)S(1)}, f16[256,256]{1,0:T(8,128)(2,1)S(1)}, u32[]{:S(2)}, u32[]{:S(2)}) %collective-permute-start.4) | collective-permute-done | bytes 131104 | tf_op jit(solution)/shard_map/ppermute | solution.py:197
  49.0 1.3 %collective-permute-done.10 = f16[256,256]{1,0:T(8,128)(2,1)S(1)} collective-permute-done((f16[256,256]{1,0:T(8,128)(2,1)S(1)}, f16[256,256]{1,0:T(8,128)(2,1)S(1)}, u32[]{:S(2)}, u32[]{:S(2)}) %collective-permute-start.10) | collective-permute-done | bytes 131104 | tf_op jit(solution)/shard_map/ppermute | solution.py:197
  50.4 0.8 collective-permute-start.11
  51.1 1.6 %collective-permute-start.6 = (f16[256,256]{1,0:T(8,128)(2,1)S(1)}, f16[256,256]{1,0:T(8,128)(2,1)S(1)}, u32[]{:S(2)}, u32[]{:S(2)}) collective-permute-start(f16[256,256]{1,0:T(8,128)(2,1)S(1)} %add_convert_fusion.6), channel_id=1, source_target_pairs={{0,2},{1,5},{2,0},{3,7},{4,6},{5,1},{6,4},{7,3},{8,10},{9,13},{10,... | collective-permute-start | bytes 393224 | tf_op jit(solution)/shard_map/ppermute | solution.py:197
  52.8 2.3 %collective-permute-done.5 = f16[256,256]{1,0:T(8,128)(2,1)S(1)} collective-permute-done((f16[256,256]{1,0:T(8,128)(2,1)S(1)}, f16[256,256]{1,0:T(8,128)(2,1)S(1)}, u32[]{:S(2)}, u32[]{:S(2)}) %collective-permute-start.5) | collective-permute-done | bytes 131104 | tf_op jit(solution)/shard_map/ppermute | solution.py:197
  55.0 1.9 %collective-permute-start.7 = (f16[256,256]{1,0:T(8,128)(2,1)S(1)}, f16[256,256]{1,0:T(8,128)(2,1)S(1)}, u32[]{:S(2)}, u32[]{:S(2)}) collective-permute-start(f16[256,256]{1,0:T(8,128)(2,1)S(1)} %collective-permute-done.5), channel_id=1, source_target_pairs={{0,2},{1,5},{2,0},{3,7},{4,6},{5,1},{6,4},{7,3},{8,10},{9,13},{10,... | collective-permute-start | bytes 393224 | tf_op jit(solution)/shard_map/ppermute | solution.py:197
  57.1 0.8 collective-permute-done.11
  57.8 1.9 %collective-permute-start.13 = (f16[256,256]{1,0:T(8,128)(2,1)S(1)}, f16[256,256]{1,0:T(8,128)(2,1)S(1)}, u32[]{:S(2)}, u32[]{:S(2)}) collective-permute-start(f16[256,256]{1,0:T(8,128)(2,1)S(1)} %collective-permute-done.11), channel_id=1, source_target_pairs={{0,2},{1,5},{2,0},{3,7},{4,6},{5,1},{6,4},{7,3},{8,10},{9,13},{10,... | collective-permute-start | bytes 393224 | tf_op jit(solution)/shard_map/ppermute | solution.py:197
  59.7 0.3 collective-permute-done.7
  60.2 1.7 %collective-permute-done.12 = f16[256,256]{1,0:T(8,128)(2,1)S(1)} collective-permute-done((f16[256,256]{1,0:T(8,128)(2,1)S(1)}, f16[256,256]{1,0:T(8,128)(2,1)S(1)}, u32[]{:S(2)}, u32[]{:S(2)}) %collective-permute-start.12) | collective-permute-done | bytes 131104 | tf_op jit(solution)/shard_map/ppermute | solution.py:197
  61.9 1.4 %collective-permute-done.13 = f16[256,256]{1,0:T(8,128)(2,1)S(1)} collective-permute-done((f16[256,256]{1,0:T(8,128)(2,1)S(1)}, f16[256,256]{1,0:T(8,128)(2,1)S(1)}, u32[]{:S(2)}, u32[]{:S(2)}) %collective-permute-start.13) | collective-permute-done | bytes 131104 | tf_op jit(solution)/shard_map/ppermute | solution.py:197
  63.5 0.2 maximum_convert_fusion
  63.7 0.9 correlate.2.corr_a
  64.8 1.2 collective-permute-done.14.corr_b
  66.0 4.7 %correct.2 = (f32[1024,512]{1,0:T(8,128)S(1)}, bf16[1024,512]{1,0:T(8,128)(2,1)S(1)}, f32[1,1]{1,0:T(1,128)}) custom-call(f32[1,1]{1,0:T(1,128)} %correlate.2.corr_a, f32[1,1]{1,0:T(1,128)} %collective-permute-done.14.corr_b, f32[1,1]{1,0:T(1,128)} %get-tuple-element.22.a_ref.weight_a, f32[1,1]{1,0:T(1,128)} %collective-permute-done.b_ref.weight_b, ...), custom_call_target="tpu_custom_call" | custom-call | flops 6291456 | bytes 1048576 | tf_op jit(solution)/shard_map/correct/pallas_call | solution.py:25
  70.7 0.3 collective-permute-start.16
  71.0 0.3 collective-permute-start.15
  71.3 2.3 %collective-permute-done.15.b_ref.weight_b = f32[1,1]{1,0:T(1,128)} collective-permute-done((f32[1,1]{1,0:T(1,128)}, f32[1,1]{1,0:T(1,128)}, u32[]{:S(2)}, u32[]{:S(2)}) %collective-permute-start.15) | collective-permute-done | bytes 36 | tf_op jit(solution)/shard_map/ppermute | solution.py:200
  73.6 4.1 %sent_half_1.3 = (bf16[2048,256]{1,0:T(8,128)(2,1)S(1)}, f32[512,256]{1,0:T(8,128)S(1)}) custom-call(s32[3]{0:T(128)S(1)} %pad_add_fusion.place_ref, f32[1,1]{1,0:T(1,128)} %get-tuple-element.29.a_ref.weight_a, f32[1,1]{1,0:T(1,128)} %collective-permute-done.15.b_ref.weight_b, bf16[1024,512]{1,0:T(8,128)(2,1)S(1)} %get-tuple-element.30.own_ref, ...), custom_call_target="tpu_custom_call" | custom-call | flops 1610612736 | bytes 1048576 | tf_op jit(solution)/shard_map/sent_half_1/pallas_call | solution.py:25
  77.7 1.5 %collective-permute-start.23 = (f16[512,256]{1,0:T(8,128)(2,1)S(1)}, f16[512,256]{1,0:T(8,128)(2,1)S(1)}, u32[]{:S(2)}, u32[]{:S(2)}) collective-permute-start(f16[512,256]{1,0:T(8,128)(2,1)S(1)} %convert_element_type.135), channel_id=1, source_target_pairs={{0,2},{1,5},{2,0},{3,7},{4,6},{5,1},{6,4},{7,3},{8,10},{9,13},{10,... | collective-permute-start | bytes 786440 | tf_op jit(solution)/shard_map/ppermute | solution.py:197
  79.2 4.2 %sent_half_0.3 = (bf16[2048,256]{1,0:T(8,128)(2,1)S(1)}, f32[512,256]{1,0:T(8,128)S(1)}) custom-call(s32[3]{0:T(128)S(1)} %pad_add_fusion.place_ref, f32[1,1]{1,0:T(1,128)} %get-tuple-element.29.a_ref.weight_a, f32[1,1]{1,0:T(1,128)} %collective-permute-done.15.b_ref.weight_b, bf16[1024,512]{1,0:T(8,128)(2,1)S(1)} %get-tuple-element.30.own_ref, ...), custom_call_target="tpu_custom_call" | custom-call | flops 1610612736 | bytes 1048576 | tf_op jit(solution)/shard_map/sent_half_0/pallas_call | solution.py:25
  83.5 0.7 collective-permute-start.17
  84.1 2.5 %kept_half.6 = f32[512,256]{1,0:T(8,128)S(1)} custom-call(s32[3]{0:T(128)S(1)} %pad_add_fusion.place_ref, f32[1,1]{1,0:T(1,128)} %get-tuple-element.29.a_ref.weight_a, f32[1,1]{1,0:T(1,128)} %collective-permute-done.15.b_ref.weight_b, bf16[2048,256]{1,0:T(8,128)(2,1)S(1)} %get-tuple-element.31.inner_ref, bf16[2,512,2048]{2,1,0:T(8,128)(2,1)S(1)} %copy-done.3), custom_call_target="tpu_custom_call" | custom-call | flops 536870912 | bytes 1048576 | tf_op jit(solution)/shard_map/kept_half/pallas_call | solution.py:25
  86.7 2.5 %kept_half.7 = f32[512,256]{1,0:T(8,128)S(1)} custom-call(s32[3]{0:T(128)S(1)} %pad_add_fusion.place_ref, f32[1,1]{1,0:T(1,128)} %get-tuple-element.29.a_ref.weight_a, f32[1,1]{1,0:T(1,128)} %collective-permute-done.15.b_ref.weight_b, bf16[2048,256]{1,0:T(8,128)(2,1)S(1)} %get-tuple-element.33.inner_ref, bf16[2,512,2048]{2,1,0:T(8,128)(2,1)S(1)} %copy-done.3), custom_call_target="tpu_custom_call" | custom-call | flops 536870912 | bytes 1048576 | tf_op jit(solution)/shard_map/kept_half/pallas_call | solution.py:25
  89.4 0.5 collective-permute-done.17
  90.0 1.6 %collective-permute-start.18 = (f16[256,256]{1,0:T(8,128)(2,1)S(1)}, f16[256,256]{1,0:T(8,128)(2,1)S(1)}, u32[]{:S(2)}, u32[]{:S(2)}) collective-permute-start(f16[256,256]{1,0:T(8,128)(2,1)S(1)} %dynamic-slice_convert_fusion.1), channel_id=1, source_target_pairs={{0,4},{1,3},{2,6},{3,1},{4,0},{5,7},{6,2},{7,5},{8,12},{9,11},{10,... | collective-permute-start | bytes 393224 | tf_op jit(solution)/shard_map/ppermute | solution.py:197
  91.6 2.8 %collective-permute-done.24 = f16[256,256]{1,0:T(8,128)(2,1)S(1)} collective-permute-done((f16[256,256]{1,0:T(8,128)(2,1)S(1)}, f16[256,256]{1,0:T(8,128)(2,1)S(1)}, u32[]{:S(2)}, u32[]{:S(2)}) %collective-permute-start.24) | collective-permute-done | bytes 131104 | tf_op jit(solution)/shard_map/ppermute | solution.py:197
  94.4 0.3 collective-permute-start.25
  94.7 1.0 collective-permute-done.18
  95.8 1.7 %collective-permute-start.19 = (f16[256,256]{1,0:T(8,128)(2,1)S(1)}, f16[256,256]{1,0:T(8,128)(2,1)S(1)}, u32[]{:S(2)}, u32[]{:S(2)}) collective-permute-start(f16[256,256]{1,0:T(8,128)(2,1)S(1)} %add_convert_fusion.3), channel_id=1, source_target_pairs={{0,8},{1,9},{2,10},{3,11},{4,12},{5,13},{6,14},{7,15},{8,0},{9,1},... | collective-permute-start | bytes 393224 | tf_op jit(solution)/shard_map/ppermute | solution.py:197
  97.5 7.8 %collective-permute-done.25 = f16[256,256]{1,0:T(8,128)(2,1)S(1)} collective-permute-done((f16[256,256]{1,0:T(8,128)(2,1)S(1)}, f16[256,256]{1,0:T(8,128)(2,1)S(1)}, u32[]{:S(2)}, u32[]{:S(2)}) %collective-permute-start.25) | collective-permute-done | bytes 131104 | tf_op jit(solution)/shard_map/ppermute | solution.py:197
  105.5 2.3 %collective-permute-done.19 = f16[256,256]{1,0:T(8,128)(2,1)S(1)} collective-permute-done((f16[256,256]{1,0:T(8,128)(2,1)S(1)}, f16[256,256]{1,0:T(8,128)(2,1)S(1)}, u32[]{:S(2)}, u32[]{:S(2)}) %collective-permute-start.19) | collective-permute-done | bytes 131104 | tf_op jit(solution)/shard_map/ppermute | solution.py:197
  107.9 1.5 %collective-permute-start.27 = (f16[256,256]{1,0:T(8,128)(2,1)S(1)}, f16[256,256]{1,0:T(8,128)(2,1)S(1)}, u32[]{:S(2)}, u32[]{:S(2)}) collective-permute-start(f16[256,256]{1,0:T(8,128)(2,1)S(1)} %add_convert_fusion), channel_id=1, source_target_pairs={{0,2},{1,5},{2,0},{3,7},{4,6},{5,1},{6,4},{7,3},{8,10},{9,13},{10,... | collective-permute-start | bytes 393224 | tf_op jit(solution)/shard_map/ppermute | solution.py:197
  109.3 1.1 collective-permute-done.26
  110.4 1.5 %collective-permute-start.28 = (f16[256,256]{1,0:T(8,128)(2,1)S(1)}, f16[256,256]{1,0:T(8,128)(2,1)S(1)}, u32[]{:S(2)}, u32[]{:S(2)}) collective-permute-start(f16[256,256]{1,0:T(8,128)(2,1)S(1)} %collective-permute-done.26), channel_id=1, source_target_pairs={{0,2},{1,5},{2,0},{3,7},{4,6},{5,1},{6,4},{7,3},{8,10},{9,13},{10,... | collective-permute-start | bytes 393224 | tf_op jit(solution)/shard_map/ppermute | solution.py:197
  111.9 0.5 collective-permute-start.21
  112.4 1.8 %collective-permute-done.20 = f16[256,256]{1,0:T(8,128)(2,1)S(1)} collective-permute-done((f16[256,256]{1,0:T(8,128)(2,1)S(1)}, f16[256,256]{1,0:T(8,128)(2,1)S(1)}, u32[]{:S(2)}, u32[]{:S(2)}) %collective-permute-start.20) | collective-permute-done | bytes 131104 | tf_op jit(solution)/shard_map/ppermute | solution.py:197
  114.2 1.4 %collective-permute-start.22 = (f16[256,256]{1,0:T(8,128)(2,1)S(1)}, f16[256,256]{1,0:T(8,128)(2,1)S(1)}, u32[]{:S(2)}, u32[]{:S(2)}) collective-permute-start(f16[256,256]{1,0:T(8,128)(2,1)S(1)} %collective-permute-done.20), channel_id=1, source_target_pairs={{0,2},{1,5},{2,0},{3,7},{4,6},{5,1},{6,4},{7,3},{8,10},{9,13},{10,... | collective-permute-start | bytes 393224 | tf_op jit(solution)/shard_map/ppermute | solution.py:197
  115.9 1.0 collective-permute-done.21
  116.9 2.3 %collective-permute-done.22 = f16[256,256]{1,0:T(8,128)(2,1)S(1)} collective-permute-done((f16[256,256]{1,0:T(8,128)(2,1)S(1)}, f16[256,256]{1,0:T(8,128)(2,1)S(1)}, u32[]{:S(2)}, u32[]{:S(2)}) %collective-permute-start.22) | collective-permute-done | bytes 131104 | tf_op jit(solution)/shard_map/ppermute | solution.py:197
  119.5 0.9 correlate.3.corr_a
  120.5 1.1 collective-permute-done.29.corr_b
  121.6 5.2 %correct.3 = (f32[1024,512]{1,0:T(8,128)S(1)}, bf16[1024,512]{1,0:T(8,128)(2,1)}, f32[1,1]{1,0:T(1,128)}) custom-call(f32[1,1]{1,0:T(1,128)} %correlate.3.corr_a, f32[1,1]{1,0:T(1,128)} %collective-permute-done.29.corr_b, f32[1,1]{1,0:T(1,128)} %get-tuple-element.29.a_ref.weight_a, f32[1,1]{1,0:T(1,128)} %collective-permute-done.15.b_ref.weight_b, ...), custom_call_target="tpu_custom_call" | custom-call | flops 6291456 | bytes 1048576 | tf_op jit(solution)/shard_map/correct/pallas_call | solution.py:25
  126.8 0.3 collective-permute-start.30
  127.1 0.9 collective-permute-done.30.weight_b
  128.1 2.7 %normalise.1 = f32[1024,512]{1,0:T(8,128)} custom-call(f32[1,1]{1,0:T(1,128)} %get-tuple-element.35.weight_a, f32[1,1]{1,0:T(1,128)} %collective-permute-done.30.weight_b, f32[1024,512]{1,0:T(8,128)S(1)} %get-tuple-element.36.vector_ref), custom_call_target="tpu_custom_call" | custom-call | flops 524288 | bytes 4194304 | tf_op jit(solution)/shard_map/normalise/pallas_call | solution.py:25
  (68 shorter events, 2.7 us)
Async XLA Ops:
  0.0 1.6 %copy-start.9 = (f32[1024,512]{1,0:T(8,128)S(1)}, f32[1024,512]{1,0:T(8,128)}, u32[]{:S(2)}) copy-start(f32[1024,512]{1,0:T(8,128)} %coef_ref.1) | copy-start | bytes 6291460
  1.6 2.9 %copy-start.12 = (s32[2,8,8]{2,1,0:T(8,128)S(1)}, s32[2,8,8]{2,1,0:T(8,128)}, u32[]{:S(2)}) copy-start(s32[2,8,8]{2,1,0:T(8,128)} %param.9) | copy-start | bytes 1540
  2.6 1.3 %copy-start.6 = (f32[1024,512]{1,0:T(8,128)}, f32[1024,512]{1,0:T(8,128)S(1)}, u32[]{:S(2)}) copy-start(f32[1024,512]{1,0:T(8,128)S(1)} %get-tuple-element.21.vector_ref) | copy-start | bytes 6291460
  3.9 4.9 %collective-permute-start.1 = (bf16[1024,512]{1,0:T(8,128)(2,1)S(1)}, bf16[1024,512]{1,0:T(8,128)(2,1)}, u32[]{:S(2)}, u32[]{:S(2)}) collective-permute-start(bf16[1024,512]{1,0:T(8,128)(2,1)S(1)} %get-tuple-element.23.own_ref), channel_id=1, source_target_pairs={{0,1},{1,0},{2,3},{3,2},{4,5},{5,4},{6,7},{7,6},{8,9},{9,8},{10,11... | collective-permute-start | bytes 3145736 | tf_op jit(solution)/shard_map/ppermute | solution.py:200
  4.4 4.5 %collective-permute-start = (f32[1,1]{1,0:T(1,128)}, f32[1,1]{1,0:T(1,128)}, u32[]{:S(2)}, u32[]{:S(2)}) collective-permute-start(f32[1,1]{1,0:T(1,128)} %get-tuple-element.22.a_ref.weight_a), channel_id=1, source_target_pairs={{0,1},{1,0},{2,3},{3,2},{4,5},{5,4},{6,7},{7,6},{8,9},{9,8},{10,11... | collective-permute-start | bytes 20 | tf_op jit(solution)/shard_map/ppermute | solution.py:200
  4.5 2.2 %copy-start.8 = (bf16[2,1024,1024]{2,1,0:T(8,128)(2,1)S(1)}, bf16[2,1024,1024]{2,1,0:T(8,128)(2,1)}, u32[]{:S(2)}) copy-start(bf16[2,1024,1024]{2,1,0:T(8,128)(2,1)} %left_ref.1) | copy-start | bytes 12582916
  6.7 2.1 %copy-start.4 = (bf16[2,1024,512]{2,1,0:T(8,128)(2,1)S(1)}, bf16[2,1024,512]{2,1,0:T(8,128)(2,1)}, u32[]{:S(2)}) copy-start(bf16[2,1024,512]{2,1,0:T(8,128)(2,1)} %right_ref.7) | copy-start | bytes 6291460
  8.8 4.9 %copy-start = (bf16[2,512,2048]{2,1,0:T(8,128)(2,1)}, bf16[2,512,2048]{2,1,0:T(8,128)(2,1)S(1)}, u32[]{:S(2)}) copy-start(bf16[2,512,2048]{2,1,0:T(8,128)(2,1)S(1)} %masked_halves.1.masked_ref) | copy-start | bytes 12582916
  13.7 1.0 copy-start.10
  14.7 15.7 %collective-permute-start.2 = (f16[512,256]{1,0:T(8,128)(2,1)S(1)}, f16[512,256]{1,0:T(8,128)(2,1)}, u32[]{:S(2)}, u32[]{:S(2)}) collective-permute-start(f16[512,256]{1,0:T(8,128)(2,1)S(1)} %convert_element_type.108), channel_id=1, source_target_pairs={{0,2},{1,5},{2,0},{3,7},{4,6},{5,1},{6,4},{7,3},{8,10},{9,13},{10,... | collective-permute-start | bytes 786440 | tf_op jit(solution)/shard_map/ppermute | solution.py:197
  17.8 2.2 %copy-start.1 = (bf16[2,512,2048]{2,1,0:T(8,128)(2,1)S(1)}, bf16[2,512,2048]{2,1,0:T(8,128)(2,1)}, u32[]{:S(2)}) copy-start(bf16[2,512,2048]{2,1,0:T(8,128)(2,1)} %copy-done) | copy-start | bytes 12582916
  20.0 5.4 %copy-start.2 = (bf16[2,512,2048]{2,1,0:T(8,128)(2,1)S(1)}, bf16[2,512,2048]{2,1,0:T(8,128)(2,1)}, u32[]{:S(2)}) copy-start(bf16[2,512,2048]{2,1,0:T(8,128)(2,1)} %copy-done) | copy-start | bytes 12582916
  20.0 5.4 %copy-start.11 = (bf16[2048,256]{1,0:T(8,128)(2,1)S(1)}, bf16[2048,256]{1,0:T(8,128)(2,1)}, u32[]{:S(2)}) copy-start(bf16[2048,256]{1,0:T(8,128)(2,1)} %copy-done.10) | copy-start | bytes 3145732
  25.3 8.3 %collective-permute-start.8 = (f16[512,256]{1,0:T(8,128)(2,1)S(1)}, f16[512,256]{1,0:T(8,128)(2,1)S(1)}, u32[]{:S(2)}, u32[]{:S(2)}) collective-permute-start(f16[512,256]{1,0:T(8,128)(2,1)S(1)} %convert_element_type.117), channel_id=1, source_target_pairs={{0,2},{1,5},{2,0},{3,7},{4,6},{5,1},{6,4},{7,3},{8,10},{9,13},{10,... | collective-permute-start | bytes 786440 | tf_op jit(solution)/shard_map/ppermute | solution.py:197
  31.5 5.1 %collective-permute-start.3 = (f16[256,256]{1,0:T(8,128)(2,1)S(1)}, f16[256,256]{1,0:T(8,128)(2,1)S(1)}, u32[]{:S(2)}, u32[]{:S(2)}) collective-permute-start(f16[256,256]{1,0:T(8,128)(2,1)S(1)} %dynamic-slice_convert_fusion.3), channel_id=1, source_target_pairs={{0,4},{1,3},{2,6},{3,1},{4,0},{5,7},{6,2},{7,5},{8,12},{9,11},{10,... | collective-permute-start | bytes 393224 | tf_op jit(solution)/shard_map/ppermute | solution.py:197
  33.7 6.0 %collective-permute-start.9 = (f16[256,256]{1,0:T(8,128)(2,1)S(1)}, f16[256,256]{1,0:T(8,128)(2,1)S(1)}, u32[]{:S(2)}, u32[]{:S(2)}) collective-permute-start(f16[256,256]{1,0:T(8,128)(2,1)S(1)} %dynamic-slice_convert_fusion.2), channel_id=1, source_target_pairs={{0,4},{1,3},{2,6},{3,1},{4,0},{5,7},{6,2},{7,5},{8,12},{9,11},{10,... | collective-permute-start | bytes 393224 | tf_op jit(solution)/shard_map/ppermute | solution.py:197
  36.6 12.3 %collective-permute-start.4 = (f16[256,256]{1,0:T(8,128)(2,1)S(1)}, f16[256,256]{1,0:T(8,128)(2,1)S(1)}, u32[]{:S(2)}, u32[]{:S(2)}) collective-permute-start(f16[256,256]{1,0:T(8,128)(2,1)S(1)} %add_convert_fusion.7), channel_id=1, source_target_pairs={{0,8},{1,9},{2,10},{3,11},{4,12},{5,13},{6,14},{7,15},{8,0},{9,1},... | collective-permute-start | bytes 393224 | tf_op jit(solution)/shard_map/ppermute | solution.py:197
  39.7 10.6 %collective-permute-start.10 = (f16[256,256]{1,0:T(8,128)(2,1)S(1)}, f16[256,256]{1,0:T(8,128)(2,1)S(1)}, u32[]{:S(2)}, u32[]{:S(2)}) collective-permute-start(f16[256,256]{1,0:T(8,128)(2,1)S(1)} %add_convert_fusion.5), channel_id=1, source_target_pairs={{0,8},{1,9},{2,10},{3,11},{4,12},{5,13},{6,14},{7,15},{8,0},{9,1},... | collective-permute-start | bytes 393224 | tf_op jit(solution)/shard_map/ppermute | solution.py:197
  48.9 6.1 %collective-permute-start.5 = (f16[256,256]{1,0:T(8,128)(2,1)S(1)}, f16[256,256]{1,0:T(8,128)(2,1)S(1)}, u32[]{:S(2)}, u32[]{:S(2)}) collective-permute-start(f16[256,256]{1,0:T(8,128)(2,1)S(1)} %add_convert_fusion.6), channel_id=1, source_target_pairs={{0,4},{1,3},{2,6},{3,1},{4,0},{5,7},{6,2},{7,5},{8,12},{9,11},{10,... | collective-permute-start | bytes 393224 | tf_op jit(solution)/shard_map/ppermute | solution.py:197
  50.4 7.5 %collective-permute-start.11 = (f16[256,256]{1,0:T(8,128)(2,1)S(1)}, f16[256,256]{1,0:T(8,128)(2,1)S(1)}, u32[]{:S(2)}, u32[]{:S(2)}) collective-permute-start(f16[256,256]{1,0:T(8,128)(2,1)S(1)} %add_convert_fusion.4), channel_id=1, source_target_pairs={{0,4},{1,3},{2,6},{3,1},{4,0},{5,7},{6,2},{7,5},{8,12},{9,11},{10,... | collective-permute-start | bytes 393224 | tf_op jit(solution)/shard_map/ppermute | solution.py:197
  51.1 8.6 %collective-permute-start.6 = (f16[256,256]{1,0:T(8,128)(2,1)S(1)}, f16[256,256]{1,0:T(8,128)(2,1)S(1)}, u32[]{:S(2)}, u32[]{:S(2)}) collective-permute-start(f16[256,256]{1,0:T(8,128)(2,1)S(1)} %add_convert_fusion.6), channel_id=1, source_target_pairs={{0,2},{1,5},{2,0},{3,7},{4,6},{5,1},{6,4},{7,3},{8,10},{9,13},{10,... | collective-permute-start | bytes 393224 | tf_op jit(solution)/shard_map/ppermute | solution.py:197
  55.0 5.0 %collective-permute-start.7 = (f16[256,256]{1,0:T(8,128)(2,1)S(1)}, f16[256,256]{1,0:T(8,128)(2,1)S(1)}, u32[]{:S(2)}, u32[]{:S(2)}) collective-permute-start(f16[256,256]{1,0:T(8,128)(2,1)S(1)} %collective-permute-done.5), channel_id=1, source_target_pairs={{0,2},{1,5},{2,0},{3,7},{4,6},{5,1},{6,4},{7,3},{8,10},{9,13},{10,... | collective-permute-start | bytes 393224 | tf_op jit(solution)/shard_map/ppermute | solution.py:197
  56.9 5.0 %collective-permute-start.12 = (f16[256,256]{1,0:T(8,128)(2,1)S(1)}, f16[256,256]{1,0:T(8,128)(2,1)S(1)}, u32[]{:S(2)}, u32[]{:S(2)}) collective-permute-start(f16[256,256]{1,0:T(8,128)(2,1)S(1)} %add_convert_fusion.4), channel_id=1, source_target_pairs={{0,2},{1,5},{2,0},{3,7},{4,6},{5,1},{6,4},{7,3},{8,10},{9,13},{10,... | collective-permute-start | bytes 393224 | tf_op jit(solution)/shard_map/ppermute | solution.py:197
  57.8 5.5 %collective-permute-start.13 = (f16[256,256]{1,0:T(8,128)(2,1)S(1)}, f16[256,256]{1,0:T(8,128)(2,1)S(1)}, u32[]{:S(2)}, u32[]{:S(2)}) collective-permute-start(f16[256,256]{1,0:T(8,128)(2,1)S(1)} %collective-permute-done.11), channel_id=1, source_target_pairs={{0,2},{1,5},{2,0},{3,7},{4,6},{5,1},{6,4},{7,3},{8,10},{9,13},{10,... | collective-permute-start | bytes 393224 | tf_op jit(solution)/shard_map/ppermute | solution.py:197
  60.2 3.5 %copy-start.7 = (f32[1024,512]{1,0:T(8,128)S(1)}, f32[1024,512]{1,0:T(8,128)}, u32[]{:S(2)}) copy-start(f32[1024,512]{1,0:T(8,128)} %copy-done.6) | copy-start | bytes 6291460
  63.7 2.3 %copy-start.5 = (f32[1024,512]{1,0:T(8,128)S(1)}, f32[1024,512]{1,0:T(8,128)}, u32[]{:S(2)}) copy-start(f32[1024,512]{1,0:T(8,128)} %diag_ref.3) | copy-start | bytes 6291460
  64.7 8.9 %copy-start.3 = (bf16[2,512,2048]{2,1,0:T(8,128)(2,1)S(1)}, bf16[2,512,2048]{2,1,0:T(8,128)(2,1)}, u32[]{:S(2)}) copy-start(bf16[2,512,2048]{2,1,0:T(8,128)(2,1)} %copy-done) | copy-start | bytes 12582916
  64.7 1.3 collective-permute-start.14
  70.7 2.9 %collective-permute-start.16 = (bf16[1024,512]{1,0:T(8,128)(2,1)S(1)}, bf16[1024,512]{1,0:T(8,128)(2,1)S(1)}, u32[]{:S(2)}, u32[]{:S(2)}) collective-permute-start(bf16[1024,512]{1,0:T(8,128)(2,1)S(1)} %get-tuple-element.30.own_ref), channel_id=1, source_target_pairs={{0,1},{1,0},{2,3},{3,2},{4,5},{5,4},{6,7},{7,6},{8,9},{9,8},{10,11... | collective-permute-start | bytes 3145736 | tf_op jit(solution)/shard_map/ppermute | solution.py:200
  71.0 2.6 %collective-permute-start.15 = (f32[1,1]{1,0:T(1,128)}, f32[1,1]{1,0:T(1,128)}, u32[]{:S(2)}, u32[]{:S(2)}) collective-permute-start(f32[1,1]{1,0:T(1,128)} %get-tuple-element.29.a_ref.weight_a), channel_id=1, source_target_pairs={{0,1},{1,0},{2,3},{3,2},{4,5},{5,4},{6,7},{7,6},{8,9},{9,8},{10,11... | collective-permute-start | bytes 20 | tf_op jit(solution)/shard_map/ppermute | solution.py:200
  77.7 11.5 %collective-permute-start.23 = (f16[512,256]{1,0:T(8,128)(2,1)S(1)}, f16[512,256]{1,0:T(8,128)(2,1)S(1)}, u32[]{:S(2)}, u32[]{:S(2)}) collective-permute-start(f16[512,256]{1,0:T(8,128)(2,1)S(1)} %convert_element_type.135), channel_id=1, source_target_pairs={{0,2},{1,5},{2,0},{3,7},{4,6},{5,1},{6,4},{7,3},{8,10},{9,13},{10,... | collective-permute-start | bytes 786440 | tf_op jit(solution)/shard_map/ppermute | solution.py:197
  83.5 6.4 %collective-permute-start.17 = (f16[512,256]{1,0:T(8,128)(2,1)S(1)}, f16[512,256]{1,0:T(8,128)(2,1)S(1)}, u32[]{:S(2)}, u32[]{:S(2)}) collective-permute-start(f16[512,256]{1,0:T(8,128)(2,1)S(1)} %convert_element_type.126), channel_id=1, source_target_pairs={{0,2},{1,5},{2,0},{3,7},{4,6},{5,1},{6,4},{7,3},{8,10},{9,13},{10,... | collective-permute-start | bytes 786440 | tf_op jit(solution)/shard_map/ppermute | solution.py:197
  89.3 5.0 %collective-permute-start.24 = (f16[256,256]{1,0:T(8,128)(2,1)S(1)}, f16[256,256]{1,0:T(8,128)(2,1)S(1)}, u32[]{:S(2)}, u32[]{:S(2)}) collective-permute-start(f16[256,256]{1,0:T(8,128)(2,1)S(1)} %dynamic-slice_convert_fusion), channel_id=1, source_target_pairs={{0,4},{1,3},{2,6},{3,1},{4,0},{5,7},{6,2},{7,5},{8,12},{9,11},{10,... | collective-permute-start | bytes 393224 | tf_op jit(solution)/shard_map/ppermute | solution.py:197
  90.0 5.8 %collective-permute-start.18 = (f16[256,256]{1,0:T(8,128)(2,1)S(1)}, f16[256,256]{1,0:T(8,128)(2,1)S(1)}, u32[]{:S(2)}, u32[]{:S(2)}) collective-permute-start(f16[256,256]{1,0:T(8,128)(2,1)S(1)} %dynamic-slice_convert_fusion.1), channel_id=1, source_target_pairs={{0,4},{1,3},{2,6},{3,1},{4,0},{5,7},{6,2},{7,5},{8,12},{9,11},{10,... | collective-permute-start | bytes 393224 | tf_op jit(solution)/shard_map/ppermute | solution.py:197
  94.4 10.9 %collective-permute-start.25 = (f16[256,256]{1,0:T(8,128)(2,1)S(1)}, f16[256,256]{1,0:T(8,128)(2,1)S(1)}, u32[]{:S(2)}, u32[]{:S(2)}) collective-permute-start(f16[256,256]{1,0:T(8,128)(2,1)S(1)} %add_convert_fusion.1), channel_id=1, source_target_pairs={{0,8},{1,9},{2,10},{3,11},{4,12},{5,13},{6,14},{7,15},{8,0},{9,1},... | collective-permute-start | bytes 393224 | tf_op jit(solution)/shard_map/ppermute | solution.py:197
  95.8 11.9 %collective-permute-start.19 = (f16[256,256]{1,0:T(8,128)(2,1)S(1)}, f16[256,256]{1,0:T(8,128)(2,1)S(1)}, u32[]{:S(2)}, u32[]{:S(2)}) collective-permute-start(f16[256,256]{1,0:T(8,128)(2,1)S(1)} %add_convert_fusion.3), channel_id=1, source_target_pairs={{0,8},{1,9},{2,10},{3,11},{4,12},{5,13},{6,14},{7,15},{8,0},{9,1},... | collective-permute-start | bytes 393224 | tf_op jit(solution)/shard_map/ppermute | solution.py:197
  105.4 5.0 %collective-permute-start.26 = (f16[256,256]{1,0:T(8,128)(2,1)S(1)}, f16[256,256]{1,0:T(8,128)(2,1)S(1)}, u32[]{:S(2)}, u32[]{:S(2)}) collective-permute-start(f16[256,256]{1,0:T(8,128)(2,1)S(1)} %add_convert_fusion), channel_id=1, source_target_pairs={{0,4},{1,3},{2,6},{3,1},{4,0},{5,7},{6,2},{7,5},{8,12},{9,11},{10,... | collective-permute-start | bytes 393224 | tf_op jit(solution)/shard_map/ppermute | solution.py:197
  107.8 6.4 %collective-permute-start.20 = (f16[256,256]{1,0:T(8,128)(2,1)S(1)}, f16[256,256]{1,0:T(8,128)(2,1)S(1)}, u32[]{:S(2)}, u32[]{:S(2)}) collective-permute-start(f16[256,256]{1,0:T(8,128)(2,1)S(1)} %add_convert_fusion.2), channel_id=1, source_target_pairs={{0,4},{1,3},{2,6},{3,1},{4,0},{5,7},{6,2},{7,5},{8,12},{9,11},{10,... | collective-permute-start | bytes 393224 | tf_op jit(solution)/shard_map/ppermute | solution.py:197
  107.9 7.8 %collective-permute-start.27 = (f16[256,256]{1,0:T(8,128)(2,1)S(1)}, f16[256,256]{1,0:T(8,128)(2,1)S(1)}, u32[]{:S(2)}, u32[]{:S(2)}) collective-permute-start(f16[256,256]{1,0:T(8,128)(2,1)S(1)} %add_convert_fusion), channel_id=1, source_target_pairs={{0,2},{1,5},{2,0},{3,7},{4,6},{5,1},{6,4},{7,3},{8,10},{9,13},{10,... | collective-permute-start | bytes 393224 | tf_op jit(solution)/shard_map/ppermute | solution.py:197
  110.4 5.2 %collective-permute-start.28 = (f16[256,256]{1,0:T(8,128)(2,1)S(1)}, f16[256,256]{1,0:T(8,128)(2,1)S(1)}, u32[]{:S(2)}, u32[]{:S(2)}) collective-permute-start(f16[256,256]{1,0:T(8,128)(2,1)S(1)} %collective-permute-done.26), channel_id=1, source_target_pairs={{0,2},{1,5},{2,0},{3,7},{4,6},{5,1},{6,4},{7,3},{8,10},{9,13},{10,... | collective-permute-start | bytes 393224 | tf_op jit(solution)/shard_map/ppermute | solution.py:197
  111.9 5.0 %collective-permute-start.21 = (f16[256,256]{1,0:T(8,128)(2,1)S(1)}, f16[256,256]{1,0:T(8,128)(2,1)S(1)}, u32[]{:S(2)}, u32[]{:S(2)}) collective-permute-start(f16[256,256]{1,0:T(8,128)(2,1)S(1)} %add_convert_fusion.2), channel_id=1, source_target_pairs={{0,2},{1,5},{2,0},{3,7},{4,6},{5,1},{6,4},{7,3},{8,10},{9,13},{10,... | collective-permute-start | bytes 393224 | tf_op jit(solution)/shard_map/ppermute | solution.py:197
  114.2 5.0 %collective-permute-start.22 = (f16[256,256]{1,0:T(8,128)(2,1)S(1)}, f16[256,256]{1,0:T(8,128)(2,1)S(1)}, u32[]{:S(2)}, u32[]{:S(2)}) collective-permute-start(f16[256,256]{1,0:T(8,128)(2,1)S(1)} %collective-permute-done.20), channel_id=1, source_target_pairs={{0,2},{1,5},{2,0},{3,7},{4,6},{5,1},{6,4},{7,3},{8,10},{9,13},{10,... | collective-permute-start | bytes 393224 | tf_op jit(solution)/shard_map/ppermute | solution.py:197
  120.4 1.2 collective-permute-start.29
  126.8 1.2 collective-permute-start.30

commit v4 on v3

v4 whole, which is shorter than its diff:
```python
import functools

import jax
import jax.numpy as jnp
from jax import lax
from jax.experimental import pallas as pl
from jax.experimental.pallas import tpu as pltpu
from jax.sharding import PartitionSpec as P

STEPS = 2
CHUNKS = 2
EPS = 1e-06
BLOCK = 16
TOP = 0.1875
BOTH = ("op", "col")
F32, F16, BF16 = jnp.float32, jnp.float16, jnp.bfloat16
SDS = jax.ShapeDtypeStruct
ANY = pl.BlockSpec(memory_space=pl.ANY)
VMEM = pl.BlockSpec(memory_space=pltpu.VMEM)
SMEM = pl.BlockSpec(memory_space=pltpu.SMEM)
ONE = SDS((8, 128), F32)
ORDER = ((1, 2), (2, 1))


def call(kernel, name, outs, out_specs, in_specs, args, flops, moved, scratch=(), mib=8):
    return pl.pallas_call(
        kernel, out_shape=outs, in_specs=in_specs, out_specs=out_specs, scratch_shapes=scratch, name=name,
        compiler_params=pltpu.CompilerParams(vmem_limit_bytes=mib * 2 ** 20),
        cost_estimate=pl.CostEstimate(flops=flops, bytes_accessed=moved, transcendentals=0))(*args)


def total(own_ref, other_ref):
    return own_ref[:1, :1] + other_ref[:1, :1]


def put(ref, parts):
    ref[...] = jnp.full(ref.shape, jnp.sum(parts), F32)


def folded(block):
    return jnp.sum(block.reshape(block.shape[0] // 8, 8, block.shape[1]), axis=0)


def scale_of(reach, weight):
    return 32768.0 / (reach * (jnp.sqrt(weight) + 1e-30))


def open_vector(coef):
    rows, cols = coef.shape
    parts = 4
    step = rows // parts

    def kernel(coef_ref, full_ref, wave_ref, weight_ref, sems):
        copies = []
        for p in range(parts):
            at = pl.ds(p * step, step)
            copies.append(pltpu.make_async_copy(coef_ref.at[at], full_ref.at[at], sems.at[p]))
            copies[-1].start()
        weight = jnp.zeros((8, cols), F32)
        for p in range(parts):
            copies[p].wait()
            for r in range(p * step, (p + 1) * step, BLOCK):
                block = full_ref[r:r + BLOCK, :]
                wave_ref[r:r + BLOCK, :] = block.astype(BF16)
                weight = weight + folded(block * block)
        put(weight_ref, weight)

    return call(kernel, "open_vector", (SDS((rows, cols), F32), SDS((rows, cols), BF16), ONE), (VMEM, VMEM, VMEM),
                [ANY], (coef,), 3 * rows * cols, 8 * rows * cols, [pltpu.SemaphoreType.DMA((parts,))])


def first_half():
    me, core = lax.axis_index("op"), lax.axis_index("col")
    bit = 0
    for c, (mask, _) in enumerate(ORDER):
        bit = bit + jnp.where(core == c, (me // mask) % 2, 0)
    return 1 - bit


def masked_half(left, mask, blocks, sent):
    pairs, width, _ = left.shape
    half, inside = width // 2, width // blocks

    def kernel(mask_ref, left_ref, out_ref, buf, sems):
        h = first_half() if sent else 1 - first_half()
        copies = []
        for k in range(pairs):
            copies.append(pltpu.make_async_copy(
                left_ref.at[k, pl.ds(pl.multiple_of(h * half, half), half)], buf.at[k], sems.at[k]))
            copies[-1].start()
        for k in range(pairs):
            copies[k].wait()
            for i in range(half // inside):
                for j in range(blocks):
                    keep = mask_ref[(k * blocks + h * (half // inside) + i) * blocks + j]
                    block = buf[k, i * inside:(i + 1) * inside, j * inside:(j + 1) * inside]
                    out_ref[i * inside:(i + 1) * inside, k * width + j * inside:k * width + (j + 1) * inside] = (
                        jnp.where(keep != 0, block, jnp.zeros_like(block)))

    return call(kernel, "masked_sent" if sent else "masked_kept", SDS((half, pairs * width), BF16), VMEM,
                [SMEM, ANY], (mask, left), left.size, 2 * left.size,
                [pltpu.VMEM((pairs, half, width), BF16), pltpu.SemaphoreType.DMA((pairs,))])


def product(out_ref, at, scale, left_ref, right_ref, parts=4):
    step = left_ref.shape[0] // parts
    for p in range(parts):
        rows = slice(p * step, (p + 1) * step)
        out_ref[rows, at] = scale * jnp.dot(left_ref[rows, :], right_ref[...], preferred_element_type=F32)


def sent_half(chunk, reach, weights, own, other, right, masked):
    pairs, width, cols = right.shape
    size, half = cols // CHUNKS, width // 2
    at = slice(chunk * size, (chunk + 1) * size)
    step = width // 4

    def kernel(a_ref, b_ref, own_ref, other_ref, right_ref, masked_ref, inner_ref, send_ref):
        core = lax.axis_index("col")
        here = pl.ds(pl.multiple_of(core * cols, cols), cols)
        there = pl.ds(pl.multiple_of((1 - core) * cols, cols), cols)
        scale = scale_of(reach, total(a_ref, b_ref))
        for k in range(pairs):
            near, far = right_ref[k, here, at], right_ref[k, there, at]
            for r in range(0, width, step):
                inner_ref[k * width + r:k * width + r + step, :] = (
                    jnp.dot(own_ref[r:r + step, :], near, preferred_element_type=F32)
                    + jnp.dot(other_ref[r:r + step, :], far, preferred_element_type=F32)).astype(BF16)
        product(send_ref, slice(None), scale, masked_ref, inner_ref, 2)

    return call(kernel, "sent_half_%d" % chunk, (SDS((pairs * width, size), BF16), SDS((half, size), F32)),
                (VMEM, VMEM), [VMEM] * 6, (*weights, own, other, right, masked),
                3 * pairs * width * width * size, 2 ** 20)


def kept_half(reach, weights, inner, masked):
    half, depth = masked.shape
    size = inner.shape[1]

    def kernel(a_ref, b_ref, inner_ref, masked_ref, keep_ref):
        product(keep_ref, slice(None), scale_of(reach, total(a_ref, b_ref)), masked_ref, inner_ref, 2)

    return call(kernel, "kept_half", SDS((half, size), F32), VMEM, [VMEM] * 4,
                (*weights, inner, masked), 2 * half * depth * size, 2 ** 20)


def correlate(vector, sigmas):
    rows, cols = vector.shape
    size = cols // len(sigmas)

    def kernel(vector_ref, *refs):
        out = jnp.zeros((8, size), F32)
        for r in range(0, rows, BLOCK):
            for c, sigma_ref in enumerate(refs[:-1]):
                out = out + folded(vector_ref[r:r + BLOCK, c * size:(c + 1) * size] * sigma_ref[r:r + BLOCK, :])
        put(refs[-1], out)

    return call(kernel, "correlate", ONE, VMEM, [VMEM] * (1 + len(sigmas)), (vector, *sigmas), 2 * rows * cols, 2 ** 20)


def correct(first, reach, cells, vector, sigmas, diag, corr, weights):
    rows, cols = vector.shape
    size = cols // len(sigmas)

    def kernel(corr_a, corr_b, weight_a, weight_b, vector_ref, diag_ref, *refs):
        sigma_refs, (moved_ref, wave_ref, square_ref) = refs[:-3], refs[-3:]
        weight = total(weight_a, weight_b)
        scale = scale_of(reach, weight)
        norm = jnp.ones((1, 1), F32) if first else lax.rsqrt(weight / cells + EPS)
        square = norm * norm
        theta = (total(corr_a, corr_b) / scale * square / cells) / (weight * square / cells + EPS)
        unit = norm / scale
        out = jnp.zeros((8, size), F32)
        for r in range(0, rows, BLOCK):
            for c, sigma_ref in enumerate(sigma_refs):
                at = (slice(r, r + BLOCK), slice(c * size, (c + 1) * size))
                coef = vector_ref[at] * norm
                spacing = diag_ref[at] - theta
                slope = spacing / jnp.maximum(spacing * spacing, 1.0)
                moved = coef - (sigma_ref[r:r + BLOCK, :] * unit - theta * coef) * slope
                moved_ref[at] = moved
                wave_ref[at] = moved.astype(BF16)
                out = out + folded(moved * moved)
        put(square_ref, out)

    return call(kernel, "correct", (SDS((rows, cols), F32), SDS((rows, cols), BF16), ONE), (VMEM, VMEM, VMEM),
                [VMEM] * (6 + len(sigmas)), (*corr, *weights, vector, diag, *sigmas), 12 * rows * cols, 2 ** 20)


def normalise(cells, vector, weights):
    rows, cols = vector.shape
    parts = 4
    step = rows // parts

    def kernel(weight_a, weight_b, vector_ref, out_ref, buf, sems):
        norm = lax.rsqrt(total(weight_a, weight_b) / cells + EPS)
        copies = []
        for p in range(parts):
            at = pl.ds(p * step, step)
            for r in range(p * step, (p + 1) * step, BLOCK):
                buf[r:r + BLOCK, :] = vector_ref[r:r + BLOCK, :] * norm
            copies.append(pltpu.make_async_copy(buf.at[at], out_ref.at[at], sems.at[p]))
            copies[-1].start()
        for copy in copies:
            copy.wait()

    return call(kernel, "normalise", SDS((rows, cols), F32), ANY, [VMEM] * 3, (*weights, vector),
                rows * cols, 8 * rows * cols, [pltpu.VMEM((rows, cols), F32), pltpu.SemaphoreType.DMA((parts,))])


def local(ops, cols, wave_coef, diag_energy, left, right, block_mask):
    pairs, width, _ = left.shape
    own_cols = right.shape[2]
    blocks = block_mask.shape[1]
    cells = float(width * width)
    half, quarter, size = width // 2, width // 4, own_cols // CHUNKS
    stages = ops.bit_length() - 1
    reach = float(pairs * ops * width) * TOP * TOP

    def swap(x, stage):
        pairing = []
        for o in range(ops):
            for c in range(cols):
                bit = ORDER[c % 2][stage] if stage < 2 else 1 << stage
                pairing.append((o * cols + c, (o ^ bit) * cols + c))
        return lax.ppermute(x, BOTH, pairing)

    def across(x):
        return lax.ppermute(x, "col", [(c, c ^ 1) for c in range(cols)])

    me, core = lax.axis_index("op"), lax.axis_index("col")
    low, high = me % 2, (me // 2) % 2
    bit0, bit1 = jnp.where(core == 0, low, high), jnp.where(core == 0, high, low)
    zero = jnp.zeros((), jnp.int32)

    def begin(send):
        return swap(send.astype(F16), 0)

    def halve(keep, got):
        keep = keep + got.astype(F32)
        send = lax.dynamic_slice(keep, ((1 - bit1) * quarter, zero), (quarter, size)).astype(F16)
        return send, lax.dynamic_slice(keep, (bit1 * quarter, zero), (quarter, size))

    def finish(keep, got):
        keep = keep + got.astype(F32)
        for stage in range(2, stages):
            send = keep.astype(F16)
            keep = send.astype(F32) + swap(send, stage).astype(F32)
        return keep.astype(F16)

    def gathered(piece):
        p1, p2 = swap(piece, 1), swap(piece, 0)
        p3 = swap(p1, 0)
        near0, near1 = jnp.where(bit1 == 0, piece, p1), jnp.where(bit1 == 0, p1, piece)
        far0, far1 = jnp.where(bit1 == 0, p2, p3), jnp.where(bit1 == 0, p3, p2)
        return jnp.concatenate([
            jnp.where(bit0 == 0, near0, far0), jnp.where(bit0 == 0, near1, far1),
            jnp.where(bit0 == 0, far0, near0), jnp.where(bit0 == 0, far1, near1)], axis=0).astype(F32)

    vector, own, weight = open_vector(wave_coef)
    mask = block_mask.reshape(-1)
    sent, kept = masked_half(left, mask, blocks, True), masked_half(left, mask, blocks, False)
    for step in range(STEPS):
        other = across(own)
        weights = (weight, across(weight))
        inners, keeps, gots = [], [], []
        for c in range(CHUNKS):
            inner, send = sent_half(c, reach, weights, own, other, right, sent)
            gots.append(begin(send))
            inners.append(inner)
            own, other = lax.optimization_barrier((own, other, inner))[:2]
        inners[0] = lax.optimization_barrier((inners[0], inners[-1]))[0]
        sigmas = []
        for c in range(CHUNKS):
            keep = kept_half(reach, weights, inners[c], kept)
            send, keep = halve(keep, gots[c])
            if c + 1 < CHUNKS:
                send, inners[c + 1] = lax.optimization_barrier((send, inners[c + 1]))
            sigmas.append(gathered(finish(keep, swap(send, 1))))
        corr = correlate(vector, sigmas)
        vector, own, weight = correct(
            step == 0, reach, cells, vector, sigmas, diag_energy, (corr, across(corr)), weights)
    return normalise(cells, vector, (weight, across(weight)))


def solution(mesh):
    in_specs = (
        P("geom", "col"),
        P("geom", "col"),
        P(("geom", "op"), None, None),
        P(("geom", "op"), None, "col"),
        P(("geom", "op"), None, None),
    )
    body = functools.partial(local, mesh.shape["op"], mesh.shape["col"])
    return jax.shard_map(body, mesh=mesh, in_specs=in_specs, out_specs=P("geom", "col"), check_vma=False)
```

time: 131 us -> 107 us (0.82)
  Pallas kernels: 45.9 us -> 18.4 us
  starting transfers between devices: 29.8 us -> 31.9 us
    pallas_call x15 -> x16, Pallas kernels: 45.9 us -> 18.4 us  [call(): pl.pallas_call(kernel, out_shape=outs, in_specs=in_specs, out_specs=out_s...]
    ppermute x24, starting transfers between devices: 28.3 us -> 30.5 us  [swap(): return lax.ppermute(x, BOTH, pairing)]
    unnamed x26 -> x34, local copies, waits for them, and re-layouts: 8.29 us -> 9.53 us
  transfers between devices with their start and end apart: 31 -> 31, of which waited for: 21 -> 24; matrix products, arithmetic and copies ran while one was open for 2% -> 2% of each run, Pallas kernels for 16% -> 9%
where the time goes in v4:
time: 107 us; the launch traced here: 106 us
  waiting for transfers between devices  42.9 us (40%)
  starting transfers between devices  31.9 us (30%)
  Pallas kernels  18.4 us (17%)
  local copies, waits for them, and re-layouts  9.61 us (9%)
  other arithmetic  2.95 us (3%)
    ppermute x24, waiting for transfers between devices, swap(): return lax.ppermute(x, BOTH, pairing)  37.4 us
    ppermute x24, starting transfers between devices, swap(): return lax.ppermute(x, BOTH, pairing)  30.5 us
    pallas_call x16, Pallas kernels, call(): pl.pallas_call(kernel, out_shape=outs, in_specs=in_specs, out_specs=out_s...  18.4 us
    unnamed x34, local copies, waits for them, and re-layouts  9.53 us
    ppermute x7, waiting for transfers between devices, across(): return lax.ppermute(x, 'col', [(c, c ^ 1) for c in range(cols)])  5.47 us
  transfers between devices with their start and end apart: 31, of which 24 were waited for; matrix products, arithmetic and copies ran while one was open for 2% of the time, Pallas kernels for 9%

profile of v4, /device:TPU:0, one launch (start us, length us, event | category | flops | bytes accessed | tf_op | source)
XLA Modules:
  0.0 106.4 jit_solution(4535653413045202592)
XLA Ops:
  0.0 1.6 %copy-done.13 = f32[1024,512]{1,0:T(8,128)S(1)} copy-done((f32[1024,512]{1,0:T(8,128)S(1)}, f32[1024,512]{1,0:T(8,128)}, u32[]{:S(2)}) %copy-start.13) | copy-done | bytes 2097176
  1.6 0.5 open_vector.1
  2.1 1.3 %copy-done.9 = f32[1024,512]{1,0:T(8,128)} copy-done((f32[1024,512]{1,0:T(8,128)}, f32[1024,512]{1,0:T(8,128)S(1)}, u32[]{:S(2)}) %copy-start.9) | copy-done | bytes 2097176
  3.4 0.5 collective-permute-start.1
  4.0 2.2 %copy-done.6 = bf16[2,1024,1024]{2,1,0:T(8,128)(2,1)S(1)} copy-done((bf16[2,1024,1024]{2,1,0:T(8,128)(2,1)S(1)}, bf16[2,1024,1024]{2,1,0:T(8,128)(2,1)}, u32[]{:S(2)}) %copy-start.6) | copy-done | bytes 4194328
  6.2 1.3 %masked_sent.1.masked_ref = bf16[512,2048]{1,0:T(8,128)(2,1)S(1)} custom-call(s32[128]{0:T(128)S(1)} %reshape.3.mask_ref, bf16[2,1024,1024]{2,1,0:T(8,128)(2,1)S(1)} %copy-done.6), custom_call_target="tpu_custom_call" | custom-call | flops 2097152 | bytes 4194304 | tf_op jit(solution)/shard_map/masked_sent/pallas_call | solution.py:26
  7.8 1.8 %sent_half_0.2 = (bf16[2048,256]{1,0:T(8,128)(2,1)S(1)}, f32[512,256]{1,0:T(8,128)S(1)}) custom-call(f32[8,128]{1,0:T(8,128)S(1)} %get-tuple-element.32.a_ref.weight_a, f32[8,128]{1,0:T(8,128)S(1)} %collective-permute-done.b_ref.weight_b, bf16[1024,512]{1,0:T(8,128)(2,1)S(1)} %get-tuple-element.35.own_ref, ...), custom_call_target="tpu_custom_call" | custom-call | flops 1610612736 | bytes 1048576 | tf_op jit(solution)/shard_map/sent_half_0/pallas_call | solution.py:26
  9.6 1.0 copy-done.14
  10.6 3.0 %collective-permute-start.2 = (f16[512,256]{1,0:T(8,128)(2,1)S(1)}, f16[512,256]{1,0:T(8,128)(2,1)}, u32[]{:S(2)}, u32[]{:S(2)}) collective-permute-start(f16[512,256]{1,0:T(8,128)(2,1)S(1)} %convert_element_type.108), channel_id=1, source_target_pairs={{0,2},{1,5},{2,0},{3,7},{4,6},{5,1},{6,4},{7,3},{8,10},{9,13},{10,... | collective-permute-start | bytes 786440 | tf_op jit(solution)/shard_map/ppermute | solution.py:226
  13.7 2.2 %copy-done.7 = bf16[2,1024,1024]{2,1,0:T(8,128)(2,1)S(1)} copy-done((bf16[2,1024,1024]{2,1,0:T(8,128)(2,1)S(1)}, bf16[2,1024,1024]{2,1,0:T(8,128)(2,1)}, u32[]{:S(2)}) %copy-start.7) | copy-done | bytes 4194328
  15.9 1.5 %masked_kept.1.masked_ref = bf16[512,2048]{1,0:T(8,128)(2,1)S(1)} custom-call(s32[128]{0:T(128)S(1)} %reshape.3.mask_ref, bf16[2,1024,1024]{2,1,0:T(8,128)(2,1)S(1)} %copy-done.7), custom_call_target="tpu_custom_call" | custom-call | flops 2097152 | bytes 4194304 | tf_op jit(solution)/shard_map/masked_kept/pallas_call | solution.py:26
  17.5 0.6 copy-done.4
  18.4 1.8 %sent_half_1.2 = (bf16[2048,256]{1,0:T(8,128)(2,1)S(1)}, f32[512,256]{1,0:T(8,128)S(1)}) custom-call(f32[8,128]{1,0:T(8,128)S(1)} %get-tuple-element.32.a_ref.weight_a, f32[8,128]{1,0:T(8,128)S(1)} %collective-permute-done.b_ref.weight_b, bf16[1024,512]{1,0:T(8,128)(2,1)S(1)} %get-tuple-element.35.own_ref, bf16[1024,512]{1,0:T(8,128)(2,1)S(1)} %copy-done.12, ...), custom_call_target="tpu_custom_call" | custom-call | flops 1610612736 | bytes 1048576 | tf_op jit(solution)/shard_map/sent_half_1/pallas_call | solution.py:26
  20.3 0.7 kept_half.4
  21.1 1.0 convert_add_fusion.3
  22.2 2.1 %collective-permute-start.3 = (f16[256,256]{1,0:T(8,128)(2,1)S(1)}, f16[256,256]{1,0:T(8,128)(2,1)S(1)}, u32[]{:S(2)}, u32[]{:S(2)}) collective-permute-start(f16[256,256]{1,0:T(8,128)(2,1)S(1)} %dynamic-slice_convert_fusion.3), channel_id=1, source_target_pairs={{0,4},{1,3},{2,6},{3,1},{4,0},{5,7},{6,2},{7,5},{8,12},{9,11},{10,... | collective-permute-start | bytes 393224 | tf_op jit(solution)/shard_map/ppermute | solution.py:226
  24.2 0.7 kept_half.5
  25.0 3.1 %collective-permute-done.8 = f16[512,256]{1,0:T(8,128)(2,1)S(1)} collective-permute-done((f16[512,256]{1,0:T(8,128)(2,1)S(1)}, f16[512,256]{1,0:T(8,128)(2,1)S(1)}, u32[]{:S(2)}, u32[]{:S(2)}) %collective-permute-start.8) | collective-permute-done | bytes 262176 | tf_op jit(solution)/shard_map/ppermute | solution.py:226
  28.1 2.2 %collective-permute-start.9 = (f16[256,256]{1,0:T(8,128)(2,1)S(1)}, f16[256,256]{1,0:T(8,128)(2,1)S(1)}, u32[]{:S(2)}, u32[]{:S(2)}) collective-permute-start(f16[256,256]{1,0:T(8,128)(2,1)S(1)} %dynamic-slice_convert_fusion.2), channel_id=1, source_target_pairs={{0,4},{1,3},{2,6},{3,1},{4,0},{5,7},{6,2},{7,5},{8,12},{9,11},{10,... | collective-permute-start | bytes 393224 | tf_op jit(solution)/shard_map/ppermute | solution.py:226
  30.4 2.6 %collective-permute-start.4 = (f16[256,256]{1,0:T(8,128)(2,1)S(1)}, f16[256,256]{1,0:T(8,128)(2,1)S(1)}, u32[]{:S(2)}, u32[]{:S(2)}) collective-permute-start(f16[256,256]{1,0:T(8,128)(2,1)S(1)} %add_convert_fusion.7), channel_id=1, source_target_pairs={{0,8},{1,9},{2,10},{3,11},{4,12},{5,13},{6,14},{7,15},{8,0},{9,1},... | collective-permute-start | bytes 393224 | tf_op jit(solution)/shard_map/ppermute | solution.py:226
  33.1 1.0 collective-permute-done.9
  34.1 2.7 %collective-permute-start.10 = (f16[256,256]{1,0:T(8,128)(2,1)S(1)}, f16[256,256]{1,0:T(8,128)(2,1)S(1)}, u32[]{:S(2)}, u32[]{:S(2)}) collective-permute-start(f16[256,256]{1,0:T(8,128)(2,1)S(1)} %add_convert_fusion.5), channel_id=1, source_target_pairs={{0,8},{1,9},{2,10},{3,11},{4,12},{5,13},{6,14},{7,15},{8,0},{9,1},... | collective-permute-start | bytes 393224 | tf_op jit(solution)/shard_map/ppermute | solution.py:226
  36.9 2.7 %collective-permute-done.4 = f16[256,256]{1,0:T(8,128)(2,1)S(1)} collective-permute-done((f16[256,256]{1,0:T(8,128)(2,1)S(1)}, f16[256,256]{1,0:T(8,128)(2,1)S(1)}, u32[]{:S(2)}, u32[]{:S(2)}) %collective-permute-start.4) | collective-permute-done | bytes 131104 | tf_op jit(solution)/shard_map/ppermute | solution.py:226
  39.7 2.6 %collective-permute-done.10 = f16[256,256]{1,0:T(8,128)(2,1)S(1)} collective-permute-done((f16[256,256]{1,0:T(8,128)(2,1)S(1)}, f16[256,256]{1,0:T(8,128)(2,1)S(1)}, u32[]{:S(2)}, u32[]{:S(2)}) %collective-permute-start.10) | collective-permute-done | bytes 131104 | tf_op jit(solution)/shard_map/ppermute | solution.py:226
  42.4 0.8 collective-permute-start.11
  43.2 1.1 %collective-permute-start.6 = (f16[256,256]{1,0:T(8,128)(2,1)S(1)}, f16[256,256]{1,0:T(8,128)(2,1)S(1)}, u32[]{:S(2)}, u32[]{:S(2)}) collective-permute-start(f16[256,256]{1,0:T(8,128)(2,1)S(1)} %add_convert_fusion.6), channel_id=1, source_target_pairs={{0,2},{1,5},{2,0},{3,7},{4,6},{5,1},{6,4},{7,3},{8,10},{9,13},{10,... | collective-permute-start | bytes 393224 | tf_op jit(solution)/shard_map/ppermute | solution.py:226
  44.3 0.3 collective-permute-done.5
  44.6 3.8 %collective-permute-start.7 = (f16[256,256]{1,0:T(8,128)(2,1)S(1)}, f16[256,256]{1,0:T(8,128)(2,1)S(1)}, u32[]{:S(2)}, u32[]{:S(2)}) collective-permute-start(f16[256,256]{1,0:T(8,128)(2,1)S(1)} %collective-permute-done.5), channel_id=1, source_target_pairs={{0,2},{1,5},{2,0},{3,7},{4,6},{5,1},{6,4},{7,3},{8,10},{9,13},{10,... | collective-permute-start | bytes 393224 | tf_op jit(solution)/shard_map/ppermute | solution.py:226
  48.4 0.5 collective-permute-done.11
  48.9 2.3 %collective-permute-start.13 = (f16[256,256]{1,0:T(8,128)(2,1)S(1)}, f16[256,256]{1,0:T(8,128)(2,1)S(1)}, u32[]{:S(2)}, u32[]{:S(2)}) collective-permute-start(f16[256,256]{1,0:T(8,128)(2,1)S(1)} %collective-permute-done.11), channel_id=1, source_target_pairs={{0,2},{1,5},{2,0},{3,7},{4,6},{5,1},{6,4},{7,3},{8,10},{9,13},{10,... | collective-permute-start | bytes 393224 | tf_op jit(solution)/shard_map/ppermute | solution.py:226
  51.5 1.9 %collective-permute-done.12 = f16[256,256]{1,0:T(8,128)(2,1)S(1)} collective-permute-done((f16[256,256]{1,0:T(8,128)(2,1)S(1)}, f16[256,256]{1,0:T(8,128)(2,1)S(1)}, u32[]{:S(2)}, u32[]{:S(2)}) %collective-permute-start.12) | collective-permute-done | bytes 131104 | tf_op jit(solution)/shard_map/ppermute | solution.py:226
  53.4 1.4 %collective-permute-done.13 = f16[256,256]{1,0:T(8,128)(2,1)S(1)} collective-permute-done((f16[256,256]{1,0:T(8,128)(2,1)S(1)}, f16[256,256]{1,0:T(8,128)(2,1)S(1)}, u32[]{:S(2)}, u32[]{:S(2)}) %collective-permute-start.13) | collective-permute-done | bytes 131104 | tf_op jit(solution)/shard_map/ppermute | solution.py:226
  55.2 0.3 correlate.2.corr_a
  55.6 1.2 %collective-permute-done.14.corr_b = f32[8,128]{1,0:T(8,128)S(1)} collective-permute-done((f32[8,128]{1,0:T(8,128)S(1)}, f32[8,128]{1,0:T(8,128)S(1)}, u32[]{:S(2)}, u32[]{:S(2)}) %collective-permute-start.14) | collective-permute-done | bytes 4128 | tf_op jit(solution)/shard_map/ppermute | solution.py:229
  56.8 1.0 correct.2
  58.1 0.4 collective-permute-start.15
  58.4 2.2 %collective-permute-done.15.b_ref.weight_b = f32[8,128]{1,0:T(8,128)S(1)} collective-permute-done((f32[8,128]{1,0:T(8,128)S(1)}, f32[8,128]{1,0:T(8,128)S(1)}, u32[]{:S(2)}, u32[]{:S(2)}) %collective-permute-start.15) | collective-permute-done | bytes 4128 | tf_op jit(solution)/shard_map/ppermute | solution.py:229
  60.6 1.8 %sent_half_0.3 = (bf16[2048,256]{1,0:T(8,128)(2,1)S(1)}, f32[512,256]{1,0:T(8,128)S(1)}) custom-call(f32[8,128]{1,0:T(8,128)S(1)} %get-tuple-element.44.a_ref.weight_a, f32[8,128]{1,0:T(8,128)S(1)} %collective-permute-done.15.b_ref.weight_b, bf16[1024,512]{1,0:T(8,128)(2,1)S(1)} %get-tuple-element.47.own_ref, ...), custom_call_target="tpu_custom_call" | custom-call | flops 1610612736 | bytes 1048576 | tf_op jit(solution)/shard_map/sent_half_0/pallas_call | solution.py:26
  62.5 1.5 %collective-permute-start.17 = (f16[512,256]{1,0:T(8,128)(2,1)S(1)}, f16[512,256]{1,0:T(8,128)(2,1)S(1)}, u32[]{:S(2)}, u32[]{:S(2)}) collective-permute-start(f16[512,256]{1,0:T(8,128)(2,1)S(1)} %convert_element_type.126), channel_id=1, source_target_pairs={{0,2},{1,5},{2,0},{3,7},{4,6},{5,1},{6,4},{7,3},{8,10},{9,13},{10,... | collective-permute-start | bytes 786440 | tf_op jit(solution)/shard_map/ppermute | solution.py:226
  63.9 1.8 %sent_half_1.3 = (bf16[2048,256]{1,0:T(8,128)(2,1)S(1)}, f32[512,256]{1,0:T(8,128)S(1)}) custom-call(f32[8,128]{1,0:T(8,128)S(1)} %get-tuple-element.44.a_ref.weight_a, f32[8,128]{1,0:T(8,128)S(1)} %collective-permute-done.15.b_ref.weight_b, bf16[1024,512]{1,0:T(8,128)(2,1)S(1)} %get-tuple-element.47.own_ref, ...), custom_call_target="tpu_custom_call" | custom-call | flops 1610612736 | bytes 1048576 | tf_op jit(solution)/shard_map/sent_half_1/pallas_call | solution.py:26
  65.8 0.7 collective-permute-start.23
  66.5 0.7 kept_half.6
  67.2 1.7 %collective-permute-done.17 = f16[512,256]{1,0:T(8,128)(2,1)S(1)} collective-permute-done((f16[512,256]{1,0:T(8,128)(2,1)S(1)}, f16[512,256]{1,0:T(8,128)(2,1)S(1)}, u32[]{:S(2)}, u32[]{:S(2)}) %collective-permute-start.17) | collective-permute-done | bytes 262176 | tf_op jit(solution)/shard_map/ppermute | solution.py:226
  69.1 0.7 kept_half.7
  69.8 3.6 %collective-permute-done.23 = f16[512,256]{1,0:T(8,128)(2,1)S(1)} collective-permute-done((f16[512,256]{1,0:T(8,128)(2,1)S(1)}, f16[512,256]{1,0:T(8,128)(2,1)S(1)}, u32[]{:S(2)}, u32[]{:S(2)}) %collective-permute-start.23) | collective-permute-done | bytes 262176 | tf_op jit(solution)/shard_map/ppermute | solution.py:226
  73.6 0.5 collective-permute-done.18
  74.1 2.2 %collective-permute-start.19 = (f16[256,256]{1,0:T(8,128)(2,1)S(1)}, f16[256,256]{1,0:T(8,128)(2,1)S(1)}, u32[]{:S(2)}, u32[]{:S(2)}) collective-permute-start(f16[256,256]{1,0:T(8,128)(2,1)S(1)} %add_convert_fusion.3), channel_id=1, source_target_pairs={{0,8},{1,9},{2,10},{3,11},{4,12},{5,13},{6,14},{7,15},{8,0},{9,1},... | collective-permute-start | bytes 393224 | tf_op jit(solution)/shard_map/ppermute | solution.py:226
  76.3 3.5 %collective-permute-done.24 = f16[256,256]{1,0:T(8,128)(2,1)S(1)} collective-permute-done((f16[256,256]{1,0:T(8,128)(2,1)S(1)}, f16[256,256]{1,0:T(8,128)(2,1)S(1)}, u32[]{:S(2)}, u32[]{:S(2)}) %collective-permute-start.24) | collective-permute-done | bytes 131104 | tf_op jit(solution)/shard_map/ppermute | solution.py:226
  79.8 0.8 collective-permute-start.25
  80.6 5.6 %collective-permute-done.19 = f16[256,256]{1,0:T(8,128)(2,1)S(1)} collective-permute-done((f16[256,256]{1,0:T(8,128)(2,1)S(1)}, f16[256,256]{1,0:T(8,128)(2,1)S(1)}, u32[]{:S(2)}, u32[]{:S(2)}) %collective-permute-start.19) | collective-permute-done | bytes 131104 | tf_op jit(solution)/shard_map/ppermute | solution.py:226
  86.3 2.0 %collective-permute-done.25 = f16[256,256]{1,0:T(8,128)(2,1)S(1)} collective-permute-done((f16[256,256]{1,0:T(8,128)(2,1)S(1)}, f16[256,256]{1,0:T(8,128)(2,1)S(1)}, u32[]{:S(2)}, u32[]{:S(2)}) %collective-permute-start.25) | collective-permute-done | bytes 131104 | tf_op jit(solution)/shard_map/ppermute | solution.py:226
  88.5 1.2 %collective-permute-start.21 = (f16[256,256]{1,0:T(8,128)(2,1)S(1)}, f16[256,256]{1,0:T(8,128)(2,1)S(1)}, u32[]{:S(2)}, u32[]{:S(2)}) collective-permute-start(f16[256,256]{1,0:T(8,128)(2,1)S(1)} %add_convert_fusion.2), channel_id=1, source_target_pairs={{0,2},{1,5},{2,0},{3,7},{4,6},{5,1},{6,4},{7,3},{8,10},{9,13},{10,... | collective-permute-start | bytes 393224 | tf_op jit(solution)/shard_map/ppermute | solution.py:226
  89.7 2.0 %collective-permute-done.20 = f16[256,256]{1,0:T(8,128)(2,1)S(1)} collective-permute-done((f16[256,256]{1,0:T(8,128)(2,1)S(1)}, f16[256,256]{1,0:T(8,128)(2,1)S(1)}, u32[]{:S(2)}, u32[]{:S(2)}) %collective-permute-start.20) | collective-permute-done | bytes 131104 | tf_op jit(solution)/shard_map/ppermute | solution.py:226
  91.7 1.1 %collective-permute-start.22 = (f16[256,256]{1,0:T(8,128)(2,1)S(1)}, f16[256,256]{1,0:T(8,128)(2,1)S(1)}, u32[]{:S(2)}, u32[]{:S(2)}) collective-permute-start(f16[256,256]{1,0:T(8,128)(2,1)S(1)} %collective-permute-done.20), channel_id=1, source_target_pairs={{0,2},{1,5},{2,0},{3,7},{4,6},{5,1},{6,4},{7,3},{8,10},{9,13},{10,... | collective-permute-start | bytes 393224 | tf_op jit(solution)/shard_map/ppermute | solution.py:226
  92.8 0.9 collective-permute-start.27
  93.7 1.1 %collective-permute-done.26 = f16[256,256]{1,0:T(8,128)(2,1)S(1)} collective-permute-done((f16[256,256]{1,0:T(8,128)(2,1)S(1)}, f16[256,256]{1,0:T(8,128)(2,1)S(1)}, u32[]{:S(2)}, u32[]{:S(2)}) %collective-permute-start.26) | collective-permute-done | bytes 131104 | tf_op jit(solution)/shard_map/ppermute | solution.py:226
  94.9 0.9 collective-permute-start.28
  95.8 0.9 collective-permute-done.22
  96.9 1.1 %collective-permute-done.27 = f16[256,256]{1,0:T(8,128)(2,1)S(1)} collective-permute-done((f16[256,256]{1,0:T(8,128)(2,1)S(1)}, f16[256,256]{1,0:T(8,128)(2,1)S(1)}, u32[]{:S(2)}, u32[]{:S(2)}) %collective-permute-start.27) | collective-permute-done | bytes 131104 | tf_op jit(solution)/shard_map/ppermute | solution.py:226
  98.1 1.8 %collective-permute-done.28 = f16[256,256]{1,0:T(8,128)(2,1)S(1)} collective-permute-done((f16[256,256]{1,0:T(8,128)(2,1)S(1)}, f16[256,256]{1,0:T(8,128)(2,1)S(1)}, u32[]{:S(2)}, u32[]{:S(2)}) %collective-permute-start.28) | collective-permute-done | bytes 131104 | tf_op jit(solution)/shard_map/ppermute | solution.py:226
  100.5 1.2 %collective-permute-done.29.corr_b = f32[8,128]{1,0:T(8,128)S(1)} collective-permute-done((f32[8,128]{1,0:T(8,128)S(1)}, f32[8,128]{1,0:T(8,128)S(1)}, u32[]{:S(2)}, u32[]{:S(2)}) %collective-permute-start.29) | collective-permute-done | bytes 4128 | tf_op jit(solution)/shard_map/ppermute | solution.py:229
  101.7 2.0 %correct.3 = (f32[1024,512]{1,0:T(8,128)S(1)}, bf16[1024,512]{1,0:T(8,128)(2,1)}, f32[8,128]{1,0:T(8,128)S(1)}) custom-call(f32[8,128]{1,0:T(8,128)S(1)} %correlate.3.corr_a, f32[8,128]{1,0:T(8,128)S(1)} %collective-permute-done.29.corr_b, f32[8,128]{1,0:T(8,128)S(1)} %get-tuple-element.44.a_ref.weight_a, ...), custom_call_target="tpu_custom_call" | custom-call | flops 6291456 | bytes 1048576 | tf_op jit(solution)/shard_map/correct/pallas_call | solution.py:26
  103.8 1.0 collective-permute-done.30.weight_b
  104.8 1.4 %normalise.1 = f32[1024,512]{1,0:T(8,128)} custom-call(f32[8,128]{1,0:T(8,128)S(1)} %get-tuple-element.55.weight_a, f32[8,128]{1,0:T(8,128)S(1)} %collective-permute-done.30.weight_b, f32[1024,512]{1,0:T(8,128)S(1)} %get-tuple-element.56.vector_ref), custom_call_target="tpu_custom_call" | custom-call | flops 524288 | bytes 4194304 | tf_op jit(solution)/shard_map/normalise/pallas_call | solution.py:26
  (76 shorter events, 4.3 us)
Async XLA Ops:
  0.0 1.6 %copy-start.13 = (f32[1024,512]{1,0:T(8,128)S(1)}, f32[1024,512]{1,0:T(8,128)}, u32[]{:S(2)}) copy-start(f32[1024,512]{1,0:T(8,128)} %coef_ref.1) | copy-start | bytes 6291460
  1.6 2.3 %copy-start.16 = (s32[2,8,8]{2,1,0:T(8,128)S(1)}, s32[2,8,8]{2,1,0:T(8,128)}, u32[]{:S(2)}) copy-start(s32[2,8,8]{2,1,0:T(8,128)} %param.9) | copy-start | bytes 1540
  2.1 1.3 %copy-start.9 = (f32[1024,512]{1,0:T(8,128)}, f32[1024,512]{1,0:T(8,128)S(1)}, u32[]{:S(2)}) copy-start(f32[1024,512]{1,0:T(8,128)S(1)} %get-tuple-element.31.vector_ref) | copy-start | bytes 6291460
  3.4 4.1 %collective-permute-start.1 = (bf16[1024,512]{1,0:T(8,128)(2,1)S(1)}, bf16[1024,512]{1,0:T(8,128)(2,1)S(1)}, u32[]{:S(2)}, u32[]{:S(2)}) collective-permute-start(bf16[1024,512]{1,0:T(8,128)(2,1)S(1)} %get-tuple-element.35.own_ref), channel_id=1, source_target_pairs={{0,1},{1,0},{2,3},{3,2},{4,5},{5,4},{6,7},{7,6},{8,9},{9,8},{10,11... | collective-permute-start | bytes 3145736 | tf_op jit(solution)/shard_map/ppermute | solution.py:229
  3.9 3.7 %collective-permute-start = (f32[8,128]{1,0:T(8,128)S(1)}, f32[8,128]{1,0:T(8,128)S(1)}, u32[]{:S(2)}, u32[]{:S(2)}) collective-permute-start(f32[8,128]{1,0:T(8,128)S(1)} %get-tuple-element.32.a_ref.weight_a), channel_id=1, source_target_pairs={{0,1},{1,0},{2,3},{3,2},{4,5},{5,4},{6,7},{7,6},{8,9},{9,8},{10,11... | collective-permute-start | bytes 12296 | tf_op jit(solution)/shard_map/ppermute | solution.py:229
  4.0 2.2 %copy-start.6 = (bf16[2,1024,1024]{2,1,0:T(8,128)(2,1)S(1)}, bf16[2,1024,1024]{2,1,0:T(8,128)(2,1)}, u32[]{:S(2)}) copy-start(bf16[2,1024,1024]{2,1,0:T(8,128)(2,1)} %left_ref.3) | copy-start | bytes 12582916
  6.2 1.6 %copy-start.3 = (bf16[2,1024,512]{2,1,0:T(8,128)(2,1)S(1)}, bf16[2,1024,512]{2,1,0:T(8,128)(2,1)}, u32[]{:S(2)}) copy-start(bf16[2,1024,512]{2,1,0:T(8,128)(2,1)} %right_ref.7) | copy-start | bytes 6291460
  7.5 2.1 %copy-start = (bf16[512,2048]{1,0:T(8,128)(2,1)}, bf16[512,2048]{1,0:T(8,128)(2,1)S(1)}, u32[]{:S(2)}) copy-start(bf16[512,2048]{1,0:T(8,128)(2,1)S(1)} %masked_sent.1.masked_ref) | copy-start | bytes 6291460
  7.8 1.8 %copy-start.11 = (bf16[1024,512]{1,0:T(8,128)(2,1)}, bf16[1024,512]{1,0:T(8,128)(2,1)S(1)}, u32[]{:S(2)}) copy-start(bf16[1024,512]{1,0:T(8,128)(2,1)S(1)} %collective-permute-done.1.other_ref) | copy-start | bytes 3145732
  9.6 1.0 copy-start.14
  10.6 10.4 %collective-permute-start.2 = (f16[512,256]{1,0:T(8,128)(2,1)S(1)}, f16[512,256]{1,0:T(8,128)(2,1)}, u32[]{:S(2)}, u32[]{:S(2)}) collective-permute-start(f16[512,256]{1,0:T(8,128)(2,1)S(1)} %convert_element_type.108), channel_id=1, source_target_pairs={{0,2},{1,5},{2,0},{3,7},{4,6},{5,1},{6,4},{7,3},{8,10},{9,13},{10,... | collective-permute-start | bytes 786440 | tf_op jit(solution)/shard_map/ppermute | solution.py:226
  13.7 2.2 %copy-start.7 = (bf16[2,1024,1024]{2,1,0:T(8,128)(2,1)S(1)}, bf16[2,1024,1024]{2,1,0:T(8,128)(2,1)}, u32[]{:S(2)}) copy-start(bf16[2,1024,1024]{2,1,0:T(8,128)(2,1)} %left_ref.3) | copy-start | bytes 12582916
  15.9 1.6 %copy-start.1 = (bf16[512,2048]{1,0:T(8,128)(2,1)S(1)}, bf16[512,2048]{1,0:T(8,128)(2,1)}, u32[]{:S(2)}) copy-start(bf16[512,2048]{1,0:T(8,128)(2,1)} %copy-done) | copy-start | bytes 6291460
  15.9 2.2 %copy-start.4 = (bf16[2,1024,512]{2,1,0:T(8,128)(2,1)S(1)}, bf16[2,1024,512]{2,1,0:T(8,128)(2,1)}, u32[]{:S(2)}) copy-start(bf16[2,1024,512]{2,1,0:T(8,128)(2,1)} %right_ref.7) | copy-start | bytes 6291460
  15.9 2.5 %copy-start.12 = (bf16[1024,512]{1,0:T(8,128)(2,1)S(1)}, bf16[1024,512]{1,0:T(8,128)(2,1)}, u32[]{:S(2)}) copy-start(bf16[1024,512]{1,0:T(8,128)(2,1)} %copy-done.11) | copy-start | bytes 3145732
  18.4 2.0 %copy-start.15 = (bf16[2048,256]{1,0:T(8,128)(2,1)S(1)}, bf16[2048,256]{1,0:T(8,128)(2,1)}, u32[]{:S(2)}) copy-start(bf16[2048,256]{1,0:T(8,128)(2,1)} %copy-done.14) | copy-start | bytes 3145732
  20.2 7.8 %collective-permute-start.8 = (f16[512,256]{1,0:T(8,128)(2,1)S(1)}, f16[512,256]{1,0:T(8,128)(2,1)S(1)}, u32[]{:S(2)}, u32[]{:S(2)}) collective-permute-start(f16[512,256]{1,0:T(8,128)(2,1)S(1)} %convert_element_type.117), channel_id=1, source_target_pairs={{0,2},{1,5},{2,0},{3,7},{4,6},{5,1},{6,4},{7,3},{8,10},{9,13},{10,... | collective-permute-start | bytes 786440 | tf_op jit(solution)/shard_map/ppermute | solution.py:226
  22.2 8.2 %collective-permute-start.3 = (f16[256,256]{1,0:T(8,128)(2,1)S(1)}, f16[256,256]{1,0:T(8,128)(2,1)S(1)}, u32[]{:S(2)}, u32[]{:S(2)}) collective-permute-start(f16[256,256]{1,0:T(8,128)(2,1)S(1)} %dynamic-slice_convert_fusion.3), channel_id=1, source_target_pairs={{0,4},{1,3},{2,6},{3,1},{4,0},{5,7},{6,2},{7,5},{8,12},{9,11},{10,... | collective-permute-start | bytes 393224 | tf_op jit(solution)/shard_map/ppermute | solution.py:226
  28.1 5.9 %collective-permute-start.9 = (f16[256,256]{1,0:T(8,128)(2,1)S(1)}, f16[256,256]{1,0:T(8,128)(2,1)S(1)}, u32[]{:S(2)}, u32[]{:S(2)}) collective-permute-start(f16[256,256]{1,0:T(8,128)(2,1)S(1)} %dynamic-slice_convert_fusion.2), channel_id=1, source_target_pairs={{0,4},{1,3},{2,6},{3,1},{4,0},{5,7},{6,2},{7,5},{8,12},{9,11},{10,... | collective-permute-start | bytes 393224 | tf_op jit(solution)/shard_map/ppermute | solution.py:226
  30.4 9.2 %collective-permute-start.4 = (f16[256,256]{1,0:T(8,128)(2,1)S(1)}, f16[256,256]{1,0:T(8,128)(2,1)S(1)}, u32[]{:S(2)}, u32[]{:S(2)}) collective-permute-start(f16[256,256]{1,0:T(8,128)(2,1)S(1)} %add_convert_fusion.7), channel_id=1, source_target_pairs={{0,8},{1,9},{2,10},{3,11},{4,12},{5,13},{6,14},{7,15},{8,0},{9,1},... | collective-permute-start | bytes 393224 | tf_op jit(solution)/shard_map/ppermute | solution.py:226
  34.1 8.3 %collective-permute-start.10 = (f16[256,256]{1,0:T(8,128)(2,1)S(1)}, f16[256,256]{1,0:T(8,128)(2,1)S(1)}, u32[]{:S(2)}, u32[]{:S(2)}) collective-permute-start(f16[256,256]{1,0:T(8,128)(2,1)S(1)} %add_convert_fusion.5), channel_id=1, source_target_pairs={{0,8},{1,9},{2,10},{3,11},{4,12},{5,13},{6,14},{7,15},{8,0},{9,1},... | collective-permute-start | bytes 393224 | tf_op jit(solution)/shard_map/ppermute | solution.py:226
  39.6 5.0 %collective-permute-start.5 = (f16[256,256]{1,0:T(8,128)(2,1)S(1)}, f16[256,256]{1,0:T(8,128)(2,1)S(1)}, u32[]{:S(2)}, u32[]{:S(2)}) collective-permute-start(f16[256,256]{1,0:T(8,128)(2,1)S(1)} %add_convert_fusion.6), channel_id=1, source_target_pairs={{0,4},{1,3},{2,6},{3,1},{4,0},{5,7},{6,2},{7,5},{8,12},{9,11},{10,... | collective-permute-start | bytes 393224 | tf_op jit(solution)/shard_map/ppermute | solution.py:226
  42.4 6.5 %collective-permute-start.11 = (f16[256,256]{1,0:T(8,128)(2,1)S(1)}, f16[256,256]{1,0:T(8,128)(2,1)S(1)}, u32[]{:S(2)}, u32[]{:S(2)}) collective-permute-start(f16[256,256]{1,0:T(8,128)(2,1)S(1)} %add_convert_fusion.4), channel_id=1, source_target_pairs={{0,4},{1,3},{2,6},{3,1},{4,0},{5,7},{6,2},{7,5},{8,12},{9,11},{10,... | collective-permute-start | bytes 393224 | tf_op jit(solution)/shard_map/ppermute | solution.py:226
  43.2 8.0 %collective-permute-start.6 = (f16[256,256]{1,0:T(8,128)(2,1)S(1)}, f16[256,256]{1,0:T(8,128)(2,1)S(1)}, u32[]{:S(2)}, u32[]{:S(2)}) collective-permute-start(f16[256,256]{1,0:T(8,128)(2,1)S(1)} %add_convert_fusion.6), channel_id=1, source_target_pairs={{0,2},{1,5},{2,0},{3,7},{4,6},{5,1},{6,4},{7,3},{8,10},{9,13},{10,... | collective-permute-start | bytes 393224 | tf_op jit(solution)/shard_map/ppermute | solution.py:226
  44.6 6.7 %collective-permute-start.7 = (f16[256,256]{1,0:T(8,128)(2,1)S(1)}, f16[256,256]{1,0:T(8,128)(2,1)S(1)}, u32[]{:S(2)}, u32[]{:S(2)}) collective-permute-start(f16[256,256]{1,0:T(8,128)(2,1)S(1)} %collective-permute-done.5), channel_id=1, source_target_pairs={{0,2},{1,5},{2,0},{3,7},{4,6},{5,1},{6,4},{7,3},{8,10},{9,13},{10,... | collective-permute-start | bytes 393224 | tf_op jit(solution)/shard_map/ppermute | solution.py:226
  48.4 5.0 %collective-permute-start.12 = (f16[256,256]{1,0:T(8,128)(2,1)S(1)}, f16[256,256]{1,0:T(8,128)(2,1)S(1)}, u32[]{:S(2)}, u32[]{:S(2)}) collective-permute-start(f16[256,256]{1,0:T(8,128)(2,1)S(1)} %add_convert_fusion.4), channel_id=1, source_target_pairs={{0,2},{1,5},{2,0},{3,7},{4,6},{5,1},{6,4},{7,3},{8,10},{9,13},{10,... | collective-permute-start | bytes 393224 | tf_op jit(solution)/shard_map/ppermute | solution.py:226
  48.9 5.9 %collective-permute-start.13 = (f16[256,256]{1,0:T(8,128)(2,1)S(1)}, f16[256,256]{1,0:T(8,128)(2,1)S(1)}, u32[]{:S(2)}, u32[]{:S(2)}) collective-permute-start(f16[256,256]{1,0:T(8,128)(2,1)S(1)} %collective-permute-done.11), channel_id=1, source_target_pairs={{0,2},{1,5},{2,0},{3,7},{4,6},{5,1},{6,4},{7,3},{8,10},{9,13},{10,... | collective-permute-start | bytes 393224 | tf_op jit(solution)/shard_map/ppermute | solution.py:226
  51.5 3.7 %copy-start.10 = (f32[1024,512]{1,0:T(8,128)S(1)}, f32[1024,512]{1,0:T(8,128)}, u32[]{:S(2)}) copy-start(f32[1024,512]{1,0:T(8,128)} %copy-done.9) | copy-start | bytes 6291460
  55.2 1.6 %copy-start.8 = (f32[1024,512]{1,0:T(8,128)S(1)}, f32[1024,512]{1,0:T(8,128)}, u32[]{:S(2)}) copy-start(f32[1024,512]{1,0:T(8,128)} %diag_ref.3) | copy-start | bytes 6291460
  55.5 5.1 %copy-start.2 = (bf16[512,2048]{1,0:T(8,128)(2,1)S(1)}, bf16[512,2048]{1,0:T(8,128)(2,1)}, u32[]{:S(2)}) copy-start(bf16[512,2048]{1,0:T(8,128)(2,1)} %copy-done) | copy-start | bytes 6291460
  55.6 5.1 %copy-start.5 = (bf16[2,1024,512]{2,1,0:T(8,128)(2,1)S(1)}, bf16[2,1024,512]{2,1,0:T(8,128)(2,1)}, u32[]{:S(2)}) copy-start(bf16[2,1024,512]{2,1,0:T(8,128)(2,1)} %right_ref.7) | copy-start | bytes 6291460
  55.6 1.2 %collective-permute-start.14 = (f32[8,128]{1,0:T(8,128)S(1)}, f32[8,128]{1,0:T(8,128)S(1)}, u32[]{:S(2)}, u32[]{:S(2)}) collective-permute-start(f32[8,128]{1,0:T(8,128)S(1)} %correlate.2.corr_a), channel_id=1, source_target_pairs={{0,1},{1,0},{2,3},{3,2},{4,5},{5,4},{6,7},{7,6},{8,9},{9,8},{10,11... | collective-permute-start | bytes 12296 | tf_op jit(solution)/shard_map/ppermute | solution.py:229
  57.9 2.7 %collective-permute-start.16 = (bf16[1024,512]{1,0:T(8,128)(2,1)S(1)}, bf16[1024,512]{1,0:T(8,128)(2,1)S(1)}, u32[]{:S(2)}, u32[]{:S(2)}) collective-permute-start(bf16[1024,512]{1,0:T(8,128)(2,1)S(1)} %get-tuple-element.47.own_ref), channel_id=1, source_target_pairs={{0,1},{1,0},{2,3},{3,2},{4,5},{5,4},{6,7},{7,6},{8,9},{9,8},{10,11... | collective-permute-start | bytes 3145736 | tf_op jit(solution)/shard_map/ppermute | solution.py:229
  58.1 2.5 %collective-permute-start.15 = (f32[8,128]{1,0:T(8,128)S(1)}, f32[8,128]{1,0:T(8,128)S(1)}, u32[]{:S(2)}, u32[]{:S(2)}) collective-permute-start(f32[8,128]{1,0:T(8,128)S(1)} %get-tuple-element.44.a_ref.weight_a), channel_id=1, source_target_pairs={{0,1},{1,0},{2,3},{3,2},{4,5},{5,4},{6,7},{7,6},{8,9},{9,8},{10,11... | collective-permute-start | bytes 12296 | tf_op jit(solution)/shard_map/ppermute | solution.py:229
  62.5 6.4 %collective-permute-start.17 = (f16[512,256]{1,0:T(8,128)(2,1)S(1)}, f16[512,256]{1,0:T(8,128)(2,1)S(1)}, u32[]{:S(2)}, u32[]{:S(2)}) collective-permute-start(f16[512,256]{1,0:T(8,128)(2,1)S(1)} %convert_element_type.126), channel_id=1, source_target_pairs={{0,2},{1,5},{2,0},{3,7},{4,6},{5,1},{6,4},{7,3},{8,10},{9,13},{10,... | collective-permute-start | bytes 786440 | tf_op jit(solution)/shard_map/ppermute | solution.py:226
  65.8 7.6 %collective-permute-start.23 = (f16[512,256]{1,0:T(8,128)(2,1)S(1)}, f16[512,256]{1,0:T(8,128)(2,1)S(1)}, u32[]{:S(2)}, u32[]{:S(2)}) collective-permute-start(f16[512,256]{1,0:T(8,128)(2,1)S(1)} %convert_element_type.135), channel_id=1, source_target_pairs={{0,2},{1,5},{2,0},{3,7},{4,6},{5,1},{6,4},{7,3},{8,10},{9,13},{10,... | collective-permute-start | bytes 786440 | tf_op jit(solution)/shard_map/ppermute | solution.py:226
  69.0 5.0 %collective-permute-start.18 = (f16[256,256]{1,0:T(8,128)(2,1)S(1)}, f16[256,256]{1,0:T(8,128)(2,1)S(1)}, u32[]{:S(2)}, u32[]{:S(2)}) collective-permute-start(f16[256,256]{1,0:T(8,128)(2,1)S(1)} %dynamic-slice_convert_fusion.1), channel_id=1, source_target_pairs={{0,4},{1,3},{2,6},{3,1},{4,0},{5,7},{6,2},{7,5},{8,12},{9,11},{10,... | collective-permute-start | bytes 393224 | tf_op jit(solution)/shard_map/ppermute | solution.py:226
  73.5 6.2 %collective-permute-start.24 = (f16[256,256]{1,0:T(8,128)(2,1)S(1)}, f16[256,256]{1,0:T(8,128)(2,1)S(1)}, u32[]{:S(2)}, u32[]{:S(2)}) collective-permute-start(f16[256,256]{1,0:T(8,128)(2,1)S(1)} %dynamic-slice_convert_fusion), channel_id=1, source_target_pairs={{0,4},{1,3},{2,6},{3,1},{4,0},{5,7},{6,2},{7,5},{8,12},{9,11},{10,... | collective-permute-start | bytes 393224 | tf_op jit(solution)/shard_map/ppermute | solution.py:226
  74.1 12.1 %collective-permute-start.19 = (f16[256,256]{1,0:T(8,128)(2,1)S(1)}, f16[256,256]{1,0:T(8,128)(2,1)S(1)}, u32[]{:S(2)}, u32[]{:S(2)}) collective-permute-start(f16[256,256]{1,0:T(8,128)(2,1)S(1)} %add_convert_fusion.3), channel_id=1, source_target_pairs={{0,8},{1,9},{2,10},{3,11},{4,12},{5,13},{6,14},{7,15},{8,0},{9,1},... | collective-permute-start | bytes 393224 | tf_op jit(solution)/shard_map/ppermute | solution.py:226
  79.8 8.6 %collective-permute-start.25 = (f16[256,256]{1,0:T(8,128)(2,1)S(1)}, f16[256,256]{1,0:T(8,128)(2,1)S(1)}, u32[]{:S(2)}, u32[]{:S(2)}) collective-permute-start(f16[256,256]{1,0:T(8,128)(2,1)S(1)} %add_convert_fusion.1), channel_id=1, source_target_pairs={{0,8},{1,9},{2,10},{3,11},{4,12},{5,13},{6,14},{7,15},{8,0},{9,1},... | collective-permute-start | bytes 393224 | tf_op jit(solution)/shard_map/ppermute | solution.py:226
  86.3 5.4 %collective-permute-start.20 = (f16[256,256]{1,0:T(8,128)(2,1)S(1)}, f16[256,256]{1,0:T(8,128)(2,1)S(1)}, u32[]{:S(2)}, u32[]{:S(2)}) collective-permute-start(f16[256,256]{1,0:T(8,128)(2,1)S(1)} %add_convert_fusion.2), channel_id=1, source_target_pairs={{0,4},{1,3},{2,6},{3,1},{4,0},{5,7},{6,2},{7,5},{8,12},{9,11},{10,... | collective-permute-start | bytes 393224 | tf_op jit(solution)/shard_map/ppermute | solution.py:226
  88.4 6.5 %collective-permute-start.26 = (f16[256,256]{1,0:T(8,128)(2,1)S(1)}, f16[256,256]{1,0:T(8,128)(2,1)S(1)}, u32[]{:S(2)}, u32[]{:S(2)}) collective-permute-start(f16[256,256]{1,0:T(8,128)(2,1)S(1)} %add_convert_fusion), channel_id=1, source_target_pairs={{0,4},{1,3},{2,6},{3,1},{4,0},{5,7},{6,2},{7,5},{8,12},{9,11},{10,... | collective-permute-start | bytes 393224 | tf_op jit(solution)/shard_map/ppermute | solution.py:226
  88.5 7.3 %collective-permute-start.21 = (f16[256,256]{1,0:T(8,128)(2,1)S(1)}, f16[256,256]{1,0:T(8,128)(2,1)S(1)}, u32[]{:S(2)}, u32[]{:S(2)}) collective-permute-start(f16[256,256]{1,0:T(8,128)(2,1)S(1)} %add_convert_fusion.2), channel_id=1, source_target_pairs={{0,2},{1,5},{2,0},{3,7},{4,6},{5,1},{6,4},{7,3},{8,10},{9,13},{10,... | collective-permute-start | bytes 393224 | tf_op jit(solution)/shard_map/ppermute | solution.py:226
  91.7 5.0 %collective-permute-start.22 = (f16[256,256]{1,0:T(8,128)(2,1)S(1)}, f16[256,256]{1,0:T(8,128)(2,1)S(1)}, u32[]{:S(2)}, u32[]{:S(2)}) collective-permute-start(f16[256,256]{1,0:T(8,128)(2,1)S(1)} %collective-permute-done.20), channel_id=1, source_target_pairs={{0,2},{1,5},{2,0},{3,7},{4,6},{5,1},{6,4},{7,3},{8,10},{9,13},{10,... | collective-permute-start | bytes 393224 | tf_op jit(solution)/shard_map/ppermute | solution.py:226
  92.8 5.3 %collective-permute-start.27 = (f16[256,256]{1,0:T(8,128)(2,1)S(1)}, f16[256,256]{1,0:T(8,128)(2,1)S(1)}, u32[]{:S(2)}, u32[]{:S(2)}) collective-permute-start(f16[256,256]{1,0:T(8,128)(2,1)S(1)} %add_convert_fusion), channel_id=1, source_target_pairs={{0,2},{1,5},{2,0},{3,7},{4,6},{5,1},{6,4},{7,3},{8,10},{9,13},{10,... | collective-permute-start | bytes 393224 | tf_op jit(solution)/shard_map/ppermute | solution.py:226
  94.9 5.0 %collective-permute-start.28 = (f16[256,256]{1,0:T(8,128)(2,1)S(1)}, f16[256,256]{1,0:T(8,128)(2,1)S(1)}, u32[]{:S(2)}, u32[]{:S(2)}) collective-permute-start(f16[256,256]{1,0:T(8,128)(2,1)S(1)} %collective-permute-done.26), channel_id=1, source_target_pairs={{0,2},{1,5},{2,0},{3,7},{4,6},{5,1},{6,4},{7,3},{8,10},{9,13},{10,... | collective-permute-start | bytes 393224 | tf_op jit(solution)/shard_map/ppermute | solution.py:226
  100.4 1.2 %collective-permute-start.29 = (f32[8,128]{1,0:T(8,128)S(1)}, f32[8,128]{1,0:T(8,128)S(1)}, u32[]{:S(2)}, u32[]{:S(2)}) collective-permute-start(f32[8,128]{1,0:T(8,128)S(1)} %correlate.3.corr_a), channel_id=1, source_target_pairs={{0,1},{1,0},{2,3},{3,2},{4,5},{5,4},{6,7},{7,6},{8,9},{9,8},{10,11... | collective-permute-start | bytes 12296 | tf_op jit(solution)/shard_map/ppermute | solution.py:229
  103.6 1.2 %collective-permute-start.30 = (f32[8,128]{1,0:T(8,128)S(1)}, f32[8,128]{1,0:T(8,128)S(1)}, u32[]{:S(2)}, u32[]{:S(2)}) collective-permute-start(f32[8,128]{1,0:T(8,128)S(1)} %get-tuple-element.55.weight_a), channel_id=1, source_target_pairs={{0,1},{1,0},{2,3},{3,2},{4,5},{5,4},{6,7},{7,6},{8,9},{9,8},{10,11... | collective-permute-start | bytes 12296 | tf_op jit(solution)/shard_map/ppermute | solution.py:229

commit v5 on v4

--- a/solution.py
+++ b/solution.py
@@ -22,6 +22,10 @@
 ORDER = ((1, 2), (2, 1))
 
 
+def in_hbm(x):
+    return pltpu.with_memory_space_constraint(x, pltpu.HBM)
+
+
 def call(kernel, name, outs, out_specs, in_specs, args, flops, moved, scratch=(), mib=8):
     return pl.pallas_call(
         kernel, out_shape=outs, in_specs=in_specs, out_specs=out_specs, scratch_shapes=scratch, name=name,
@@ -50,23 +54,24 @@
     parts = 4
     step = rows // parts
 
-    def kernel(coef_ref, full_ref, wave_ref, weight_ref, sems):
+    def kernel(coef_ref, wave_ref, weight_ref, buf, sems):
         copies = []
         for p in range(parts):
             at = pl.ds(p * step, step)
-            copies.append(pltpu.make_async_copy(coef_ref.at[at], full_ref.at[at], sems.at[p]))
+            copies.append(pltpu.make_async_copy(coef_ref.at[at], buf.at[at], sems.at[p]))
             copies[-1].start()
         weight = jnp.zeros((8, cols), F32)
         for p in range(parts):
             copies[p].wait()
             for r in range(p * step, (p + 1) * step, BLOCK):
-                block = full_ref[r:r + BLOCK, :]
+                block = buf[r:r + BLOCK, :]
                 wave_ref[r:r + BLOCK, :] = block.astype(BF16)
                 weight = weight + folded(block * block)
         put(weight_ref, weight)
 
-    return call(kernel, "open_vector", (SDS((rows, cols), F32), SDS((rows, cols), BF16), ONE), (VMEM, VMEM, VMEM),
-                [ANY], (coef,), 3 * rows * cols, 8 * rows * cols, [pltpu.SemaphoreType.DMA((parts,))])
+    return call(kernel, "open_vector", (SDS((rows, cols), BF16), ONE), (VMEM, VMEM), [ANY], (in_hbm(coef),),
+                3 * rows * cols, 8 * rows * cols,
+                [pltpu.VMEM((rows, cols), F32), pltpu.SemaphoreType.DMA((parts,))], mib=12)
 
 
 def first_half():
@@ -77,29 +82,40 @@
     return 1 - bit
 
 
-def masked_half(left, mask, blocks, sent):
+def operators(left, right, mask, blocks):
     pairs, width, _ = left.shape
     half, inside = width // 2, width // blocks
-
-    def kernel(mask_ref, left_ref, out_ref, buf, sems):
-        h = first_half() if sent else 1 - first_half()
-        copies = []
+    strips = half // inside
+
+    def kernel(mask_ref, left_ref, right_ref, sent_ref, kept_ref, held_ref, buf, sems, right_sems):
+        first = first_half()
+        order = [(o, k, i) for o in range(2) for k in range(pairs) for i in range(strips)]
+        copies, rights = [], []
         for k in range(pairs):
+            rights.append(pltpu.make_async_copy(right_ref.at[k], held_ref.at[k], right_sems.at[k]))
+        for n, (o, k, i) in enumerate(order):
+            h = first if o == 0 else 1 - first
             copies.append(pltpu.make_async_copy(
-                left_ref.at[k, pl.ds(pl.multiple_of(h * half, half), half)], buf.at[k], sems.at[k]))
-            copies[-1].start()
-        for k in range(pairs):
-            copies[k].wait()
-            for i in range(half // inside):
-                for j in range(blocks):
-                    keep = mask_ref[(k * blocks + h * (half // inside) + i) * blocks + j]
-                    block = buf[k, i * inside:(i + 1) * inside, j * inside:(j + 1) * inside]
-                    out_ref[i * inside:(i + 1) * inside, k * width + j * inside:k * width + (j + 1) * inside] = (
-                        jnp.where(keep != 0, block, jnp.zeros_like(block)))
-
-    return call(kernel, "masked_sent" if sent else "masked_kept", SDS((half, pairs * width), BF16), VMEM,
-                [SMEM, ANY], (mask, left), left.size, 2 * left.size,
-                [pltpu.VMEM((pairs, half, width), BF16), pltpu.SemaphoreType.DMA((pairs,))])
+                left_ref.at[k, pl.ds(pl.multiple_of(h * half + i * inside, inside), inside)], buf.at[n], sems.at[n]))
+        for copy in copies + rights:
+            copy.start()
+        for n, (o, k, i) in enumerate(order):
+            h, out_ref = (first, sent_ref) if o == 0 else (1 - first, kept_ref)
+            copies[n].wait()
+            for j in range(blocks):
+                keep = mask_ref[(k * blocks + h * strips + i) * blocks + j]
+                block = buf[n, :, j * inside:(j + 1) * inside]
+                out_ref[i * inside:(i + 1) * inside, k * width + j * inside:k * width + (j + 1) * inside] = (
+                    jnp.where(keep != 0, block, jnp.zeros_like(block)))
+        for copy in rights:
+            copy.wait()
+
+    count = 2 * pairs * strips
+    half_out = SDS((half, pairs * width), BF16)
+    return call(kernel, "operators", (half_out, half_out, SDS(right.shape, BF16)), (VMEM,) * 3, [SMEM, ANY, ANY],
+                (mask, in_hbm(left), in_hbm(right)), left.size, 4 * left.size,
+                [pltpu.VMEM((count, inside, width), BF16), pltpu.SemaphoreType.DMA((count,)),
+                 pltpu.SemaphoreType.DMA((pairs,))], mib=12)
 
 
 def product(out_ref, at, scale, left_ref, right_ref, parts=4):
@@ -228,18 +244,21 @@
     def across(x):
         return lax.ppermute(x, "col", [(c, c ^ 1) for c in range(cols)])
 
-    me, core = lax.axis_index("op"), lax.axis_index("col")
-    low, high = me % 2, (me // 2) % 2
+    me, core = lax.axis_index("op").astype(jnp.uint32), lax.axis_index("col").astype(jnp.uint32)
+    low, high = me & 1, (me >> 1) & 1
     bit0, bit1 = jnp.where(core == 0, low, high), jnp.where(core == 0, high, low)
-    zero = jnp.zeros((), jnp.int32)
+    low_near, low_half, zero = bit1 == 0, bit0 == 0, jnp.zeros((), jnp.uint32)
+    keep_at, send_at = bit1 * quarter, (1 - bit1) * quarter
+    wave_coef, keep_at, send_at, low_near, low_half = lax.optimization_barrier(
+        (wave_coef, keep_at, send_at, low_near, low_half))
 
     def begin(send):
         return swap(send.astype(F16), 0)
 
     def halve(keep, got):
         keep = keep + got.astype(F32)
-        send = lax.dynamic_slice(keep, ((1 - bit1) * quarter, zero), (quarter, size)).astype(F16)
-        return send, lax.dynamic_slice(keep, (bit1 * quarter, zero), (quarter, size))
+        send = lax.dynamic_slice(keep, (send_at, zero), (quarter, size)).astype(F16)
+        return send, lax.dynamic_slice(keep, (keep_at, zero), (quarter, size))
 
     def finish(keep, got):
         keep = keep + got.astype(F32)
@@ -251,15 +270,16 @@
     def gathered(piece):
         p1, p2 = swap(piece, 1), swap(piece, 0)
         p3 = swap(p1, 0)
-        near0, near1 = jnp.where(bit1 == 0, piece, p1), jnp.where(bit1 == 0, p1, piece)
-        far0, far1 = jnp.where(bit1 == 0, p2, p3), jnp.where(bit1 == 0, p3, p2)
+        near0, near1 = jnp.where(low_near, piece, p1), jnp.where(low_near, p1, piece)
+        far0, far1 = jnp.where(low_near, p2, p3), jnp.where(low_near, p3, p2)
         return jnp.concatenate([
-            jnp.where(bit0 == 0, near0, far0), jnp.where(bit0 == 0, near1, far1),
-            jnp.where(bit0 == 0, far0, near0), jnp.where(bit0 == 0, far1, near1)], axis=0).astype(F32)
-
-    vector, own, weight = open_vector(wave_coef)
+            jnp.where(low_half, near0, far0), jnp.where(low_half, near1, far1),
+            jnp.where(low_half, far0, near0), jnp.where(low_half, far1, near1)], axis=0).astype(F32)
+
+    vector = wave_coef
+    own, weight = open_vector(wave_coef)
     mask = block_mask.reshape(-1)
-    sent, kept = masked_half(left, mask, blocks, True), masked_half(left, mask, blocks, False)
+    sent, kept, right = operators(left, right, mask, blocks)
     for step in range(STEPS):
         other = across(own)
         weights = (weight, across(weight))

time: 107 us -> 99.7 us (0.932)
  local copies, waits for them, and re-layouts: 9.61 us -> 0.14 us
  Pallas kernels: 18.4 us -> 20.8 us
  waiting for transfers between devices: 42.9 us -> 44.9 us
    unnamed x34 -> x6, local copies, waits for them, and re-layouts: 9.53 us -> 0.05 us
    pallas_call x16 -> x15, Pallas kernels: 18.4 us -> 20.8 us  [call(): pl.pallas_call(kernel, out_shape=outs, in_specs=in_specs, out_specs=out_s...]
    ppermute x24, waiting for transfers between devices: 37.4 us -> 39.4 us  [swap(): return lax.ppermute(x, BOTH, pairing)]
  transfers between devices with their start and end apart: 31 -> 31, of which waited for: 24 -> 25; matrix products, arithmetic and copies ran while one was open for 2% -> 2% of each run, Pallas kernels for 9% -> 10%
where the time goes in v5:
time: 99.7 us; the launch traced here: 99.6 us
  waiting for transfers between devices  44.9 us (45%)
  starting transfers between devices  31.1 us (31%)
  Pallas kernels  20.8 us (21%)
  other arithmetic  2.16 us (2%)
    ppermute x24, waiting for transfers between devices, swap(): return lax.ppermute(x, BOTH, pairing)  39.4 us
    ppermute x24, starting transfers between devices, swap(): return lax.ppermute(x, BOTH, pairing)  29.6 us
    pallas_call x15, Pallas kernels, call(): pl.pallas_call(kernel, out_shape=outs, in_specs=in_specs, out_specs=out_s...  20.8 us
    ppermute x7, waiting for transfers between devices, across(): return lax.ppermute(x, 'col', [(c, c ^ 1) for c in range(cols)])  5.47 us
  transfers between devices with their start and end apart: 31, of which 25 were waited for; matrix products, arithmetic and copies ran while one was open for 2% of the time, Pallas kernels for 10%

profile of v5, /device:TPU:0, one launch (start us, length us, event | category | flops | bytes accessed | tf_op | source)
XLA Modules:
  0.0 99.6 jit_solution(7916468072668803513)
XLA Ops:
  0.0 1.7 %open_vector.1 = (bf16[1024,512]{1,0:T(8,128)(2,1)S(1)}, f32[8,128]{1,0:T(8,128)S(1)}) custom-call(f32[1024,512]{1,0:T(8,128)} %vector_ref.1), custom_call_target="tpu_custom_call" | custom-call | flops 1572864 | bytes 4194304 | tf_op jit(solution)/shard_map/open_vector/pallas_call | solution.py:30
  1.7 0.5 collective-permute-start.1
  2.4 3.5 %operators.1 = (bf16[512,2048]{1,0:T(8,128)(2,1)S(1)}, bf16[512,2048]{1,0:T(8,128)(2,1)S(1)}, bf16[2,1024,512]{2,1,0:T(8,128)(2,1)S(1)}) custom-call(s32[128]{0:T(128)S(1)} %reshape.3.mask_ref, bf16[2,1024,1024]{2,1,0:T(8,128)(2,1)} %left_ref.1, bf16[2,1024,512]{2,1,0:T(8,128)(2,1)} %right_ref.1), custom_call_target="tpu_custom_call" | custom-call | flops 2097152 | bytes 8388608 | tf_op jit(solution)/shard_map/operators/pallas_call | solution.py:30
  6.0 1.8 %sent_half_0.2 = (bf16[2048,256]{1,0:T(8,128)(2,1)S(1)}, f32[512,256]{1,0:T(8,128)S(1)}) custom-call(f32[8,128]{1,0:T(8,128)S(1)} %get-tuple-element.41.a_ref.weight_a, f32[8,128]{1,0:T(8,128)S(1)} %collective-permute-done.b_ref.weight_b, bf16[1024,512]{1,0:T(8,128)(2,1)S(1)} %get-tuple-element.46.own_ref, ...), custom_call_target="tpu_custom_call" | custom-call | flops 1610612736 | bytes 1048576 | tf_op jit(solution)/shard_map/sent_half_0/pallas_call | solution.py:30
  7.9 3.0 %collective-permute-start.2 = (f16[512,256]{1,0:T(8,128)(2,1)S(1)}, f16[512,256]{1,0:T(8,128)(2,1)S(1)}, u32[]{:S(2)}, u32[]{:S(2)}) collective-permute-start(f16[512,256]{1,0:T(8,128)(2,1)S(1)} %convert_element_type.116), channel_id=1, source_target_pairs={{0,2},{1,5},{2,0},{3,7},{4,6},{5,1},{6,4},{7,3},{8,10},{9,13},{10,... | collective-permute-start | bytes 786440 | tf_op jit(solution)/shard_map/ppermute | solution.py:242
  10.9 1.8 %sent_half_1.2 = (bf16[2048,256]{1,0:T(8,128)(2,1)S(1)}, f32[512,256]{1,0:T(8,128)S(1)}) custom-call(f32[8,128]{1,0:T(8,128)S(1)} %get-tuple-element.41.a_ref.weight_a, f32[8,128]{1,0:T(8,128)S(1)} %collective-permute-done.b_ref.weight_b, bf16[1024,512]{1,0:T(8,128)(2,1)S(1)} %get-tuple-element.46.own_ref, ...), custom_call_target="tpu_custom_call" | custom-call | flops 1610612736 | bytes 1048576 | tf_op jit(solution)/shard_map/sent_half_1/pallas_call | solution.py:30
  12.8 0.7 kept_half.4
  13.6 1.7 %collective-permute-done.2 = f16[512,256]{1,0:T(8,128)(2,1)S(1)} collective-permute-done((f16[512,256]{1,0:T(8,128)(2,1)S(1)}, f16[512,256]{1,0:T(8,128)(2,1)S(1)}, u32[]{:S(2)}, u32[]{:S(2)}) %collective-permute-start.2) | collective-permute-done | bytes 262176 | tf_op jit(solution)/shard_map/ppermute | solution.py:242
  15.4 2.1 %collective-permute-start.3 = (f16[256,256]{1,0:T(8,128)(2,1)S(1)}, f16[256,256]{1,0:T(8,128)(2,1)S(1)}, u32[]{:S(2)}, u32[]{:S(2)}) collective-permute-start(f16[256,256]{1,0:T(8,128)(2,1)S(1)} %dynamic-slice_convert_fusion.3), channel_id=1, source_target_pairs={{0,4},{1,3},{2,6},{3,1},{4,0},{5,7},{6,2},{7,5},{8,12},{9,11},{10,... | collective-permute-start | bytes 393224 | tf_op jit(solution)/shard_map/ppermute | solution.py:242
  17.5 0.7 kept_half.5
  18.2 2.4 %collective-permute-done.8 = f16[512,256]{1,0:T(8,128)(2,1)S(1)} collective-permute-done((f16[512,256]{1,0:T(8,128)(2,1)S(1)}, f16[512,256]{1,0:T(8,128)(2,1)S(1)}, u32[]{:S(2)}, u32[]{:S(2)}) %collective-permute-start.8) | collective-permute-done | bytes 262176 | tf_op jit(solution)/shard_map/ppermute | solution.py:242
  20.7 1.6 %collective-permute-start.9 = (f16[256,256]{1,0:T(8,128)(2,1)S(1)}, f16[256,256]{1,0:T(8,128)(2,1)S(1)}, u32[]{:S(2)}, u32[]{:S(2)}) collective-permute-start(f16[256,256]{1,0:T(8,128)(2,1)S(1)} %dynamic-slice_convert_fusion.2), channel_id=1, source_target_pairs={{0,4},{1,3},{2,6},{3,1},{4,0},{5,7},{6,2},{7,5},{8,12},{9,11},{10,... | collective-permute-start | bytes 393224 | tf_op jit(solution)/shard_map/ppermute | solution.py:242
  22.4 2.6 %collective-permute-start.4 = (f16[256,256]{1,0:T(8,128)(2,1)S(1)}, f16[256,256]{1,0:T(8,128)(2,1)S(1)}, u32[]{:S(2)}, u32[]{:S(2)}) collective-permute-start(f16[256,256]{1,0:T(8,128)(2,1)S(1)} %add_convert_fusion.7), channel_id=1, source_target_pairs={{0,8},{1,9},{2,10},{3,11},{4,12},{5,13},{6,14},{7,15},{8,0},{9,1},... | collective-permute-start | bytes 393224 | tf_op jit(solution)/shard_map/ppermute | solution.py:242
  25.1 2.1 %collective-permute-done.9 = f16[256,256]{1,0:T(8,128)(2,1)S(1)} collective-permute-done((f16[256,256]{1,0:T(8,128)(2,1)S(1)}, f16[256,256]{1,0:T(8,128)(2,1)S(1)}, u32[]{:S(2)}, u32[]{:S(2)}) %collective-permute-start.9) | collective-permute-done | bytes 131104 | tf_op jit(solution)/shard_map/ppermute | solution.py:242
  27.3 2.0 %collective-permute-start.10 = (f16[256,256]{1,0:T(8,128)(2,1)S(1)}, f16[256,256]{1,0:T(8,128)(2,1)S(1)}, u32[]{:S(2)}, u32[]{:S(2)}) collective-permute-start(f16[256,256]{1,0:T(8,128)(2,1)S(1)} %add_convert_fusion.5), channel_id=1, source_target_pairs={{0,8},{1,9},{2,10},{3,11},{4,12},{5,13},{6,14},{7,15},{8,0},{9,1},... | collective-permute-start | bytes 393224 | tf_op jit(solution)/shard_map/ppermute | solution.py:242
  29.3 3.5 %collective-permute-done.4 = f16[256,256]{1,0:T(8,128)(2,1)S(1)} collective-permute-done((f16[256,256]{1,0:T(8,128)(2,1)S(1)}, f16[256,256]{1,0:T(8,128)(2,1)S(1)}, u32[]{:S(2)}, u32[]{:S(2)}) %collective-permute-start.4) | collective-permute-done | bytes 131104 | tf_op jit(solution)/shard_map/ppermute | solution.py:242
  32.8 1.6 %collective-permute-start.5 = (f16[256,256]{1,0:T(8,128)(2,1)S(1)}, f16[256,256]{1,0:T(8,128)(2,1)S(1)}, u32[]{:S(2)}, u32[]{:S(2)}) collective-permute-start(f16[256,256]{1,0:T(8,128)(2,1)S(1)} %add_convert_fusion.6), channel_id=1, source_target_pairs={{0,4},{1,3},{2,6},{3,1},{4,0},{5,7},{6,2},{7,5},{8,12},{9,11},{10,... | collective-permute-start | bytes 393224 | tf_op jit(solution)/shard_map/ppermute | solution.py:242
  34.4 1.1 %collective-permute-done.10 = f16[256,256]{1,0:T(8,128)(2,1)S(1)} collective-permute-done((f16[256,256]{1,0:T(8,128)(2,1)S(1)}, f16[256,256]{1,0:T(8,128)(2,1)S(1)}, u32[]{:S(2)}, u32[]{:S(2)}) %collective-permute-start.10) | collective-permute-done | bytes 131104 | tf_op jit(solution)/shard_map/ppermute | solution.py:242
  35.6 0.8 collective-permute-start.11
  36.4 0.8 collective-permute-start.6
  37.3 0.5 collective-permute-done.5
  37.8 3.6 %collective-permute-start.7 = (f16[256,256]{1,0:T(8,128)(2,1)S(1)}, f16[256,256]{1,0:T(8,128)(2,1)S(1)}, u32[]{:S(2)}, u32[]{:S(2)}) collective-permute-start(f16[256,256]{1,0:T(8,128)(2,1)S(1)} %collective-permute-done.5), channel_id=1, source_target_pairs={{0,2},{1,5},{2,0},{3,7},{4,6},{5,1},{6,4},{7,3},{8,10},{9,13},{10,... | collective-permute-start | bytes 393224 | tf_op jit(solution)/shard_map/ppermute | solution.py:242
  41.4 0.6 collective-permute-done.11
  42.1 2.2 %collective-permute-start.13 = (f16[256,256]{1,0:T(8,128)(2,1)S(1)}, f16[256,256]{1,0:T(8,128)(2,1)S(1)}, u32[]{:S(2)}, u32[]{:S(2)}) collective-permute-start(f16[256,256]{1,0:T(8,128)(2,1)S(1)} %collective-permute-done.11), channel_id=1, source_target_pairs={{0,2},{1,5},{2,0},{3,7},{4,6},{5,1},{6,4},{7,3},{8,10},{9,13},{10,... | collective-permute-start | bytes 393224 | tf_op jit(solution)/shard_map/ppermute | solution.py:242
  44.5 1.8 %collective-permute-done.12 = f16[256,256]{1,0:T(8,128)(2,1)S(1)} collective-permute-done((f16[256,256]{1,0:T(8,128)(2,1)S(1)}, f16[256,256]{1,0:T(8,128)(2,1)S(1)}, u32[]{:S(2)}, u32[]{:S(2)}) %collective-permute-start.12) | collective-permute-done | bytes 131104 | tf_op jit(solution)/shard_map/ppermute | solution.py:242
  46.4 1.4 %collective-permute-done.13 = f16[256,256]{1,0:T(8,128)(2,1)S(1)} collective-permute-done((f16[256,256]{1,0:T(8,128)(2,1)S(1)}, f16[256,256]{1,0:T(8,128)(2,1)S(1)}, u32[]{:S(2)}, u32[]{:S(2)}) %collective-permute-start.13) | collective-permute-done | bytes 131104 | tf_op jit(solution)/shard_map/ppermute | solution.py:242
  47.8 0.2 broadcast_select_fusion.27
  47.9 0.2 maximum_convert_fusion
  48.2 0.3 correlate.2.corr_a
  48.6 1.2 %collective-permute-done.14.corr_b = f32[8,128]{1,0:T(8,128)S(1)} collective-permute-done((f32[8,128]{1,0:T(8,128)S(1)}, f32[8,128]{1,0:T(8,128)S(1)}, u32[]{:S(2)}, u32[]{:S(2)}) %collective-permute-start.14) | collective-permute-done | bytes 4128 | tf_op jit(solution)/shard_map/ppermute | solution.py:245
  49.8 1.0 %correct.2 = (f32[1024,512]{1,0:T(8,128)S(1)}, bf16[1024,512]{1,0:T(8,128)(2,1)S(1)}, f32[8,128]{1,0:T(8,128)S(1)}) custom-call(f32[8,128]{1,0:T(8,128)S(1)} %correlate.2.corr_a, f32[8,128]{1,0:T(8,128)S(1)} %collective-permute-done.14.corr_b, f32[8,128]{1,0:T(8,128)S(1)} %get-tuple-element.41.a_ref.weight_a, ...), custom_call_target="tpu_custom_call" | custom-call | flops 6291456 | bytes 1048576 | tf_op jit(solution)/shard_map/correct/pallas_call | solution.py:30
  50.8 0.2 collective-permute-start.16
  51.0 0.4 collective-permute-start.15
  51.4 2.2 %collective-permute-done.15.b_ref.weight_b = f32[8,128]{1,0:T(8,128)S(1)} collective-permute-done((f32[8,128]{1,0:T(8,128)S(1)}, f32[8,128]{1,0:T(8,128)S(1)}, u32[]{:S(2)}, u32[]{:S(2)}) %collective-permute-start.15) | collective-permute-done | bytes 4128 | tf_op jit(solution)/shard_map/ppermute | solution.py:245
  53.6 1.8 %sent_half_0.3 = (bf16[2048,256]{1,0:T(8,128)(2,1)S(1)}, f32[512,256]{1,0:T(8,128)S(1)}) custom-call(f32[8,128]{1,0:T(8,128)S(1)} %get-tuple-element.58.a_ref.weight_a, f32[8,128]{1,0:T(8,128)S(1)} %collective-permute-done.15.b_ref.weight_b, bf16[1024,512]{1,0:T(8,128)(2,1)S(1)} %get-tuple-element.61.own_ref, ...), custom_call_target="tpu_custom_call" | custom-call | flops 1610612736 | bytes 1048576 | tf_op jit(solution)/shard_map/sent_half_0/pallas_call | solution.py:30
  55.4 1.5 %collective-permute-start.17 = (f16[512,256]{1,0:T(8,128)(2,1)S(1)}, f16[512,256]{1,0:T(8,128)(2,1)S(1)}, u32[]{:S(2)}, u32[]{:S(2)}) collective-permute-start(f16[512,256]{1,0:T(8,128)(2,1)S(1)} %convert_element_type.134), channel_id=1, source_target_pairs={{0,2},{1,5},{2,0},{3,7},{4,6},{5,1},{6,4},{7,3},{8,10},{9,13},{10,... | collective-permute-start | bytes 786440 | tf_op jit(solution)/shard_map/ppermute | solution.py:242
  56.9 1.8 %sent_half_1.3 = (bf16[2048,256]{1,0:T(8,128)(2,1)S(1)}, f32[512,256]{1,0:T(8,128)S(1)}) custom-call(f32[8,128]{1,0:T(8,128)S(1)} %get-tuple-element.58.a_ref.weight_a, f32[8,128]{1,0:T(8,128)S(1)} %collective-permute-done.15.b_ref.weight_b, bf16[1024,512]{1,0:T(8,128)(2,1)S(1)} %get-tuple-element.61.own_ref, ...), custom_call_target="tpu_custom_call" | custom-call | flops 1610612736 | bytes 1048576 | tf_op jit(solution)/shard_map/sent_half_1/pallas_call | solution.py:30
  58.8 0.7 collective-permute-start.23
  59.5 0.7 kept_half.6
  60.2 1.7 %collective-permute-done.17 = f16[512,256]{1,0:T(8,128)(2,1)S(1)} collective-permute-done((f16[512,256]{1,0:T(8,128)(2,1)S(1)}, f16[512,256]{1,0:T(8,128)(2,1)S(1)}, u32[]{:S(2)}, u32[]{:S(2)}) %collective-permute-start.17) | collective-permute-done | bytes 262176 | tf_op jit(solution)/shard_map/ppermute | solution.py:242
  62.1 0.9 kept_half.7
  63.0 3.4 %collective-permute-done.23 = f16[512,256]{1,0:T(8,128)(2,1)S(1)} collective-permute-done((f16[512,256]{1,0:T(8,128)(2,1)S(1)}, f16[512,256]{1,0:T(8,128)(2,1)S(1)}, u32[]{:S(2)}, u32[]{:S(2)}) %collective-permute-start.23) | collective-permute-done | bytes 262176 | tf_op jit(solution)/shard_map/ppermute | solution.py:242
  66.6 0.4 collective-permute-done.18
  67.1 1.9 %collective-permute-start.19 = (f16[256,256]{1,0:T(8,128)(2,1)S(1)}, f16[256,256]{1,0:T(8,128)(2,1)S(1)}, u32[]{:S(2)}, u32[]{:S(2)}) collective-permute-start(f16[256,256]{1,0:T(8,128)(2,1)S(1)} %add_convert_fusion.3), channel_id=1, source_target_pairs={{0,8},{1,9},{2,10},{3,11},{4,12},{5,13},{6,14},{7,15},{8,0},{9,1},... | collective-permute-start | bytes 393224 | tf_op jit(solution)/shard_map/ppermute | solution.py:242
  69.0 3.7 %collective-permute-done.24 = f16[256,256]{1,0:T(8,128)(2,1)S(1)} collective-permute-done((f16[256,256]{1,0:T(8,128)(2,1)S(1)}, f16[256,256]{1,0:T(8,128)(2,1)S(1)}, u32[]{:S(2)}, u32[]{:S(2)}) %collective-permute-start.24) | collective-permute-done | bytes 131104 | tf_op jit(solution)/shard_map/ppermute | solution.py:242
  72.8 0.5 collective-permute-start.25
  73.3 6.0 %collective-permute-done.19 = f16[256,256]{1,0:T(8,128)(2,1)S(1)} collective-permute-done((f16[256,256]{1,0:T(8,128)(2,1)S(1)}, f16[256,256]{1,0:T(8,128)(2,1)S(1)}, u32[]{:S(2)}, u32[]{:S(2)}) %collective-permute-start.19) | collective-permute-done | bytes 131104 | tf_op jit(solution)/shard_map/ppermute | solution.py:242
  79.4 2.0 %collective-permute-done.25 = f16[256,256]{1,0:T(8,128)(2,1)S(1)} collective-permute-done((f16[256,256]{1,0:T(8,128)(2,1)S(1)}, f16[256,256]{1,0:T(8,128)(2,1)S(1)}, u32[]{:S(2)}, u32[]{:S(2)}) %collective-permute-start.25) | collective-permute-done | bytes 131104 | tf_op jit(solution)/shard_map/ppermute | solution.py:242
  81.5 1.2 %collective-permute-start.21 = (f16[256,256]{1,0:T(8,128)(2,1)S(1)}, f16[256,256]{1,0:T(8,128)(2,1)S(1)}, u32[]{:S(2)}, u32[]{:S(2)}) collective-permute-start(f16[256,256]{1,0:T(8,128)(2,1)S(1)} %add_convert_fusion.2), channel_id=1, source_target_pairs={{0,2},{1,5},{2,0},{3,7},{4,6},{5,1},{6,4},{7,3},{8,10},{9,13},{10,... | collective-permute-start | bytes 393224 | tf_op jit(solution)/shard_map/ppermute | solution.py:242
  82.7 2.0 %collective-permute-done.20 = f16[256,256]{1,0:T(8,128)(2,1)S(1)} collective-permute-done((f16[256,256]{1,0:T(8,128)(2,1)S(1)}, f16[256,256]{1,0:T(8,128)(2,1)S(1)}, u32[]{:S(2)}, u32[]{:S(2)}) %collective-permute-start.20) | collective-permute-done | bytes 131104 | tf_op jit(solution)/shard_map/ppermute | solution.py:242
  84.7 1.1 %collective-permute-start.22 = (f16[256,256]{1,0:T(8,128)(2,1)S(1)}, f16[256,256]{1,0:T(8,128)(2,1)S(1)}, u32[]{:S(2)}, u32[]{:S(2)}) collective-permute-start(f16[256,256]{1,0:T(8,128)(2,1)S(1)} %collective-permute-done.20), channel_id=1, source_target_pairs={{0,2},{1,5},{2,0},{3,7},{4,6},{5,1},{6,4},{7,3},{8,10},{9,13},{10,... | collective-permute-start | bytes 393224 | tf_op jit(solution)/shard_map/ppermute | solution.py:242
  85.7 1.0 collective-permute-start.27
  86.7 1.2 %collective-permute-done.26 = f16[256,256]{1,0:T(8,128)(2,1)S(1)} collective-permute-done((f16[256,256]{1,0:T(8,128)(2,1)S(1)}, f16[256,256]{1,0:T(8,128)(2,1)S(1)}, u32[]{:S(2)}, u32[]{:S(2)}) %collective-permute-start.26) | collective-permute-done | bytes 131104 | tf_op jit(solution)/shard_map/ppermute | solution.py:242
  87.9 0.9 collective-permute-start.28
  88.8 0.8 collective-permute-done.22
  89.6 0.2 broadcast_select_fusion.23
  89.9 1.1 %collective-permute-done.27 = f16[256,256]{1,0:T(8,128)(2,1)S(1)} collective-permute-done((f16[256,256]{1,0:T(8,128)(2,1)S(1)}, f16[256,256]{1,0:T(8,128)(2,1)S(1)}, u32[]{:S(2)}, u32[]{:S(2)}) %collective-permute-start.27) | collective-permute-done | bytes 131104 | tf_op jit(solution)/shard_map/ppermute | solution.py:242
  91.0 1.8 %collective-permute-done.28 = f16[256,256]{1,0:T(8,128)(2,1)S(1)} collective-permute-done((f16[256,256]{1,0:T(8,128)(2,1)S(1)}, f16[256,256]{1,0:T(8,128)(2,1)S(1)}, u32[]{:S(2)}, u32[]{:S(2)}) %collective-permute-start.28) | collective-permute-done | bytes 131104 | tf_op jit(solution)/shard_map/ppermute | solution.py:242
  93.1 0.5 correlate.3.corr_a
  93.7 1.2 %collective-permute-done.29.corr_b = f32[8,128]{1,0:T(8,128)S(1)} collective-permute-done((f32[8,128]{1,0:T(8,128)S(1)}, f32[8,128]{1,0:T(8,128)S(1)}, u32[]{:S(2)}, u32[]{:S(2)}) %collective-permute-start.29) | collective-permute-done | bytes 4128 | tf_op jit(solution)/shard_map/ppermute | solution.py:245
  94.8 2.0 %correct.3 = (f32[1024,512]{1,0:T(8,128)S(1)}, bf16[1024,512]{1,0:T(8,128)(2,1)}, f32[8,128]{1,0:T(8,128)S(1)}) custom-call(f32[8,128]{1,0:T(8,128)S(1)} %correlate.3.corr_a, f32[8,128]{1,0:T(8,128)S(1)} %collective-permute-done.29.corr_b, f32[8,128]{1,0:T(8,128)S(1)} %get-tuple-element.58.a_ref.weight_a, ...), custom_call_target="tpu_custom_call" | custom-call | flops 6291456 | bytes 1048576 | tf_op jit(solution)/shard_map/correct/pallas_call | solution.py:30
  96.8 0.2 collective-permute-start.30
  97.0 1.0 %collective-permute-done.30.weight_b = f32[8,128]{1,0:T(8,128)S(1)} collective-permute-done((f32[8,128]{1,0:T(8,128)S(1)}, f32[8,128]{1,0:T(8,128)S(1)}, u32[]{:S(2)}, u32[]{:S(2)}) %collective-permute-start.30) | collective-permute-done | bytes 4128 | tf_op jit(solution)/shard_map/ppermute | solution.py:245
  98.0 1.4 %normalise.1 = f32[1024,512]{1,0:T(8,128)} custom-call(f32[8,128]{1,0:T(8,128)S(1)} %get-tuple-element.69.weight_a, f32[8,128]{1,0:T(8,128)S(1)} %collective-permute-done.30.weight_b, f32[1024,512]{1,0:T(8,128)S(1)} %get-tuple-element.70.vector_ref), custom_call_target="tpu_custom_call" | custom-call | flops 524288 | bytes 4194304 | tf_op jit(solution)/shard_map/normalise/pallas_call | solution.py:30
  (47 shorter events, 2.5 us)
Async XLA Ops:
  0.0 2.3 %copy-start.2 = (s32[2,8,8]{2,1,0:T(8,128)S(1)}, s32[2,8,8]{2,1,0:T(8,128)}, u32[]{:S(2)}) copy-start(s32[2,8,8]{2,1,0:T(8,128)} %param.9) | copy-start | bytes 1540
  1.7 4.2 %collective-permute-start.1 = (bf16[1024,512]{1,0:T(8,128)(2,1)S(1)}, bf16[1024,512]{1,0:T(8,128)(2,1)S(1)}, u32[]{:S(2)}, u32[]{:S(2)}) collective-permute-start(bf16[1024,512]{1,0:T(8,128)(2,1)S(1)} %get-tuple-element.46.own_ref), channel_id=1, source_target_pairs={{0,1},{1,0},{2,3},{3,2},{4,5},{5,4},{6,7},{7,6},{8,9},{9,8},{10,11... | collective-permute-start | bytes 3145736 | tf_op jit(solution)/shard_map/ppermute | solution.py:245
  2.3 3.7 %collective-permute-start = (f32[8,128]{1,0:T(8,128)S(1)}, f32[8,128]{1,0:T(8,128)S(1)}, u32[]{:S(2)}, u32[]{:S(2)}) collective-permute-start(f32[8,128]{1,0:T(8,128)S(1)} %get-tuple-element.41.a_ref.weight_a), channel_id=1, source_target_pairs={{0,1},{1,0},{2,3},{3,2},{4,5},{5,4},{6,7},{7,6},{8,9},{9,8},{10,11... | collective-permute-start | bytes 12296 | tf_op jit(solution)/shard_map/ppermute | solution.py:245
  7.9 7.4 %collective-permute-start.2 = (f16[512,256]{1,0:T(8,128)(2,1)S(1)}, f16[512,256]{1,0:T(8,128)(2,1)S(1)}, u32[]{:S(2)}, u32[]{:S(2)}) collective-permute-start(f16[512,256]{1,0:T(8,128)(2,1)S(1)} %convert_element_type.116), channel_id=1, source_target_pairs={{0,2},{1,5},{2,0},{3,7},{4,6},{5,1},{6,4},{7,3},{8,10},{9,13},{10,... | collective-permute-start | bytes 786440 | tf_op jit(solution)/shard_map/ppermute | solution.py:242
  12.8 7.8 %collective-permute-start.8 = (f16[512,256]{1,0:T(8,128)(2,1)S(1)}, f16[512,256]{1,0:T(8,128)(2,1)S(1)}, u32[]{:S(2)}, u32[]{:S(2)}) collective-permute-start(f16[512,256]{1,0:T(8,128)(2,1)S(1)} %convert_element_type.125), channel_id=1, source_target_pairs={{0,2},{1,5},{2,0},{3,7},{4,6},{5,1},{6,4},{7,3},{8,10},{9,13},{10,... | collective-permute-start | bytes 786440 | tf_op jit(solution)/shard_map/ppermute | solution.py:242
  15.4 7.0 %collective-permute-start.3 = (f16[256,256]{1,0:T(8,128)(2,1)S(1)}, f16[256,256]{1,0:T(8,128)(2,1)S(1)}, u32[]{:S(2)}, u32[]{:S(2)}) collective-permute-start(f16[256,256]{1,0:T(8,128)(2,1)S(1)} %dynamic-slice_convert_fusion.3), channel_id=1, source_target_pairs={{0,4},{1,3},{2,6},{3,1},{4,0},{5,7},{6,2},{7,5},{8,12},{9,11},{10,... | collective-permute-start | bytes 393224 | tf_op jit(solution)/shard_map/ppermute | solution.py:242
  20.7 6.5 %collective-permute-start.9 = (f16[256,256]{1,0:T(8,128)(2,1)S(1)}, f16[256,256]{1,0:T(8,128)(2,1)S(1)}, u32[]{:S(2)}, u32[]{:S(2)}) collective-permute-start(f16[256,256]{1,0:T(8,128)(2,1)S(1)} %dynamic-slice_convert_fusion.2), channel_id=1, source_target_pairs={{0,4},{1,3},{2,6},{3,1},{4,0},{5,7},{6,2},{7,5},{8,12},{9,11},{10,... | collective-permute-start | bytes 393224 | tf_op jit(solution)/shard_map/ppermute | solution.py:242
  22.4 10.3 %collective-permute-start.4 = (f16[256,256]{1,0:T(8,128)(2,1)S(1)}, f16[256,256]{1,0:T(8,128)(2,1)S(1)}, u32[]{:S(2)}, u32[]{:S(2)}) collective-permute-start(f16[256,256]{1,0:T(8,128)(2,1)S(1)} %add_convert_fusion.7), channel_id=1, source_target_pairs={{0,8},{1,9},{2,10},{3,11},{4,12},{5,13},{6,14},{7,15},{8,0},{9,1},... | collective-permute-start | bytes 393224 | tf_op jit(solution)/shard_map/ppermute | solution.py:242
  27.3 8.2 %collective-permute-start.10 = (f16[256,256]{1,0:T(8,128)(2,1)S(1)}, f16[256,256]{1,0:T(8,128)(2,1)S(1)}, u32[]{:S(2)}, u32[]{:S(2)}) collective-permute-start(f16[256,256]{1,0:T(8,128)(2,1)S(1)} %add_convert_fusion.5), channel_id=1, source_target_pairs={{0,8},{1,9},{2,10},{3,11},{4,12},{5,13},{6,14},{7,15},{8,0},{9,1},... | collective-permute-start | bytes 393224 | tf_op jit(solution)/shard_map/ppermute | solution.py:242
  32.8 5.0 %collective-permute-start.5 = (f16[256,256]{1,0:T(8,128)(2,1)S(1)}, f16[256,256]{1,0:T(8,128)(2,1)S(1)}, u32[]{:S(2)}, u32[]{:S(2)}) collective-permute-start(f16[256,256]{1,0:T(8,128)(2,1)S(1)} %add_convert_fusion.6), channel_id=1, source_target_pairs={{0,4},{1,3},{2,6},{3,1},{4,0},{5,7},{6,2},{7,5},{8,12},{9,11},{10,... | collective-permute-start | bytes 393224 | tf_op jit(solution)/shard_map/ppermute | solution.py:242
  35.6 6.5 %collective-permute-start.11 = (f16[256,256]{1,0:T(8,128)(2,1)S(1)}, f16[256,256]{1,0:T(8,128)(2,1)S(1)}, u32[]{:S(2)}, u32[]{:S(2)}) collective-permute-start(f16[256,256]{1,0:T(8,128)(2,1)S(1)} %add_convert_fusion.4), channel_id=1, source_target_pairs={{0,4},{1,3},{2,6},{3,1},{4,0},{5,7},{6,2},{7,5},{8,12},{9,11},{10,... | collective-permute-start | bytes 393224 | tf_op jit(solution)/shard_map/ppermute | solution.py:242
  36.4 7.8 %collective-permute-start.6 = (f16[256,256]{1,0:T(8,128)(2,1)S(1)}, f16[256,256]{1,0:T(8,128)(2,1)S(1)}, u32[]{:S(2)}, u32[]{:S(2)}) collective-permute-start(f16[256,256]{1,0:T(8,128)(2,1)S(1)} %add_convert_fusion.6), channel_id=1, source_target_pairs={{0,2},{1,5},{2,0},{3,7},{4,6},{5,1},{6,4},{7,3},{8,10},{9,13},{10,... | collective-permute-start | bytes 393224 | tf_op jit(solution)/shard_map/ppermute | solution.py:242
  37.8 6.6 %collective-permute-start.7 = (f16[256,256]{1,0:T(8,128)(2,1)S(1)}, f16[256,256]{1,0:T(8,128)(2,1)S(1)}, u32[]{:S(2)}, u32[]{:S(2)}) collective-permute-start(f16[256,256]{1,0:T(8,128)(2,1)S(1)} %collective-permute-done.5), channel_id=1, source_target_pairs={{0,2},{1,5},{2,0},{3,7},{4,6},{5,1},{6,4},{7,3},{8,10},{9,13},{10,... | collective-permute-start | bytes 393224 | tf_op jit(solution)/shard_map/ppermute | solution.py:242
  41.4 5.0 %collective-permute-start.12 = (f16[256,256]{1,0:T(8,128)(2,1)S(1)}, f16[256,256]{1,0:T(8,128)(2,1)S(1)}, u32[]{:S(2)}, u32[]{:S(2)}) collective-permute-start(f16[256,256]{1,0:T(8,128)(2,1)S(1)} %add_convert_fusion.4), channel_id=1, source_target_pairs={{0,2},{1,5},{2,0},{3,7},{4,6},{5,1},{6,4},{7,3},{8,10},{9,13},{10,... | collective-permute-start | bytes 393224 | tf_op jit(solution)/shard_map/ppermute | solution.py:242
  42.1 5.7 %collective-permute-start.13 = (f16[256,256]{1,0:T(8,128)(2,1)S(1)}, f16[256,256]{1,0:T(8,128)(2,1)S(1)}, u32[]{:S(2)}, u32[]{:S(2)}) collective-permute-start(f16[256,256]{1,0:T(8,128)(2,1)S(1)} %collective-permute-done.11), channel_id=1, source_target_pairs={{0,2},{1,5},{2,0},{3,7},{4,6},{5,1},{6,4},{7,3},{8,10},{9,13},{10,... | collective-permute-start | bytes 393224 | tf_op jit(solution)/shard_map/ppermute | solution.py:242
  44.5 3.7 %copy-start = (f32[1024,512]{1,0:T(8,128)S(1)}, f32[1024,512]{1,0:T(8,128)}, u32[]{:S(2)}) copy-start(f32[1024,512]{1,0:T(8,128)} %vector_ref.1) | copy-start | bytes 6291460
  48.2 1.6 %copy-start.1 = (f32[1024,512]{1,0:T(8,128)S(1)}, f32[1024,512]{1,0:T(8,128)}, u32[]{:S(2)}) copy-start(f32[1024,512]{1,0:T(8,128)} %diag_ref.3) | copy-start | bytes 6291460
  48.5 1.2 %collective-permute-start.14 = (f32[8,128]{1,0:T(8,128)S(1)}, f32[8,128]{1,0:T(8,128)S(1)}, u32[]{:S(2)}, u32[]{:S(2)}) collective-permute-start(f32[8,128]{1,0:T(8,128)S(1)} %correlate.2.corr_a), channel_id=1, source_target_pairs={{0,1},{1,0},{2,3},{3,2},{4,5},{5,4},{6,7},{7,6},{8,9},{9,8},{10,11... | collective-permute-start | bytes 12296 | tf_op jit(solution)/shard_map/ppermute | solution.py:245
  50.8 2.7 %collective-permute-start.16 = (bf16[1024,512]{1,0:T(8,128)(2,1)S(1)}, bf16[1024,512]{1,0:T(8,128)(2,1)S(1)}, u32[]{:S(2)}, u32[]{:S(2)}) collective-permute-start(bf16[1024,512]{1,0:T(8,128)(2,1)S(1)} %get-tuple-element.61.own_ref), channel_id=1, source_target_pairs={{0,1},{1,0},{2,3},{3,2},{4,5},{5,4},{6,7},{7,6},{8,9},{9,8},{10,11... | collective-permute-start | bytes 3145736 | tf_op jit(solution)/shard_map/ppermute | solution.py:245
  51.0 2.5 %collective-permute-start.15 = (f32[8,128]{1,0:T(8,128)S(1)}, f32[8,128]{1,0:T(8,128)S(1)}, u32[]{:S(2)}, u32[]{:S(2)}) collective-permute-start(f32[8,128]{1,0:T(8,128)S(1)} %get-tuple-element.58.a_ref.weight_a), channel_id=1, source_target_pairs={{0,1},{1,0},{2,3},{3,2},{4,5},{5,4},{6,7},{7,6},{8,9},{9,8},{10,11... | collective-permute-start | bytes 12296 | tf_op jit(solution)/shard_map/ppermute | solution.py:245
  55.4 6.4 %collective-permute-start.17 = (f16[512,256]{1,0:T(8,128)(2,1)S(1)}, f16[512,256]{1,0:T(8,128)(2,1)S(1)}, u32[]{:S(2)}, u32[]{:S(2)}) collective-permute-start(f16[512,256]{1,0:T(8,128)(2,1)S(1)} %convert_element_type.134), channel_id=1, source_target_pairs={{0,2},{1,5},{2,0},{3,7},{4,6},{5,1},{6,4},{7,3},{8,10},{9,13},{10,... | collective-permute-start | bytes 786440 | tf_op jit(solution)/shard_map/ppermute | solution.py:242
  58.8 7.6 %collective-permute-start.23 = (f16[512,256]{1,0:T(8,128)(2,1)S(1)}, f16[512,256]{1,0:T(8,128)(2,1)S(1)}, u32[]{:S(2)}, u32[]{:S(2)}) collective-permute-start(f16[512,256]{1,0:T(8,128)(2,1)S(1)} %convert_element_type.143), channel_id=1, source_target_pairs={{0,2},{1,5},{2,0},{3,7},{4,6},{5,1},{6,4},{7,3},{8,10},{9,13},{10,... | collective-permute-start | bytes 786440 | tf_op jit(solution)/shard_map/ppermute | solution.py:242
  62.0 5.0 %collective-permute-start.18 = (f16[256,256]{1,0:T(8,128)(2,1)S(1)}, f16[256,256]{1,0:T(8,128)(2,1)S(1)}, u32[]{:S(2)}, u32[]{:S(2)}) collective-permute-start(f16[256,256]{1,0:T(8,128)(2,1)S(1)} %dynamic-slice_convert_fusion.1), channel_id=1, source_target_pairs={{0,4},{1,3},{2,6},{3,1},{4,0},{5,7},{6,2},{7,5},{8,12},{9,11},{10,... | collective-permute-start | bytes 393224 | tf_op jit(solution)/shard_map/ppermute | solution.py:242
  66.5 6.2 %collective-permute-start.24 = (f16[256,256]{1,0:T(8,128)(2,1)S(1)}, f16[256,256]{1,0:T(8,128)(2,1)S(1)}, u32[]{:S(2)}, u32[]{:S(2)}) collective-permute-start(f16[256,256]{1,0:T(8,128)(2,1)S(1)} %dynamic-slice_convert_fusion), channel_id=1, source_target_pairs={{0,4},{1,3},{2,6},{3,1},{4,0},{5,7},{6,2},{7,5},{8,12},{9,11},{10,... | collective-permute-start | bytes 393224 | tf_op jit(solution)/shard_map/ppermute | solution.py:242
  67.1 12.2 %collective-permute-start.19 = (f16[256,256]{1,0:T(8,128)(2,1)S(1)}, f16[256,256]{1,0:T(8,128)(2,1)S(1)}, u32[]{:S(2)}, u32[]{:S(2)}) collective-permute-start(f16[256,256]{1,0:T(8,128)(2,1)S(1)} %add_convert_fusion.3), channel_id=1, source_target_pairs={{0,8},{1,9},{2,10},{3,11},{4,12},{5,13},{6,14},{7,15},{8,0},{9,1},... | collective-permute-start | bytes 393224 | tf_op jit(solution)/shard_map/ppermute | solution.py:242
  72.8 8.6 %collective-permute-start.25 = (f16[256,256]{1,0:T(8,128)(2,1)S(1)}, f16[256,256]{1,0:T(8,128)(2,1)S(1)}, u32[]{:S(2)}, u32[]{:S(2)}) collective-permute-start(f16[256,256]{1,0:T(8,128)(2,1)S(1)} %add_convert_fusion.1), channel_id=1, source_target_pairs={{0,8},{1,9},{2,10},{3,11},{4,12},{5,13},{6,14},{7,15},{8,0},{9,1},... | collective-permute-start | bytes 393224 | tf_op jit(solution)/shard_map/ppermute | solution.py:242
  79.3 5.4 %collective-permute-start.20 = (f16[256,256]{1,0:T(8,128)(2,1)S(1)}, f16[256,256]{1,0:T(8,128)(2,1)S(1)}, u32[]{:S(2)}, u32[]{:S(2)}) collective-permute-start(f16[256,256]{1,0:T(8,128)(2,1)S(1)} %add_convert_fusion.2), channel_id=1, source_target_pairs={{0,4},{1,3},{2,6},{3,1},{4,0},{5,7},{6,2},{7,5},{8,12},{9,11},{10,... | collective-permute-start | bytes 393224 | tf_op jit(solution)/shard_map/ppermute | solution.py:242
  81.4 6.4 %collective-permute-start.26 = (f16[256,256]{1,0:T(8,128)(2,1)S(1)}, f16[256,256]{1,0:T(8,128)(2,1)S(1)}, u32[]{:S(2)}, u32[]{:S(2)}) collective-permute-start(f16[256,256]{1,0:T(8,128)(2,1)S(1)} %add_convert_fusion), channel_id=1, source_target_pairs={{0,4},{1,3},{2,6},{3,1},{4,0},{5,7},{6,2},{7,5},{8,12},{9,11},{10,... | collective-permute-start | bytes 393224 | tf_op jit(solution)/shard_map/ppermute | solution.py:242
  81.5 7.3 %collective-permute-start.21 = (f16[256,256]{1,0:T(8,128)(2,1)S(1)}, f16[256,256]{1,0:T(8,128)(2,1)S(1)}, u32[]{:S(2)}, u32[]{:S(2)}) collective-permute-start(f16[256,256]{1,0:T(8,128)(2,1)S(1)} %add_convert_fusion.2), channel_id=1, source_target_pairs={{0,2},{1,5},{2,0},{3,7},{4,6},{5,1},{6,4},{7,3},{8,10},{9,13},{10,... | collective-permute-start | bytes 393224 | tf_op jit(solution)/shard_map/ppermute | solution.py:242
  84.7 5.0 %collective-permute-start.22 = (f16[256,256]{1,0:T(8,128)(2,1)S(1)}, f16[256,256]{1,0:T(8,128)(2,1)S(1)}, u32[]{:S(2)}, u32[]{:S(2)}) collective-permute-start(f16[256,256]{1,0:T(8,128)(2,1)S(1)} %collective-permute-done.20), channel_id=1, source_target_pairs={{0,2},{1,5},{2,0},{3,7},{4,6},{5,1},{6,4},{7,3},{8,10},{9,13},{10,... | collective-permute-start | bytes 393224 | tf_op jit(solution)/shard_map/ppermute | solution.py:242
  85.7 5.3 %collective-permute-start.27 = (f16[256,256]{1,0:T(8,128)(2,1)S(1)}, f16[256,256]{1,0:T(8,128)(2,1)S(1)}, u32[]{:S(2)}, u32[]{:S(2)}) collective-permute-start(f16[256,256]{1,0:T(8,128)(2,1)S(1)} %add_convert_fusion), channel_id=1, source_target_pairs={{0,2},{1,5},{2,0},{3,7},{4,6},{5,1},{6,4},{7,3},{8,10},{9,13},{10,... | collective-permute-start | bytes 393224 | tf_op jit(solution)/shard_map/ppermute | solution.py:242
  87.9 5.0 %collective-permute-start.28 = (f16[256,256]{1,0:T(8,128)(2,1)S(1)}, f16[256,256]{1,0:T(8,128)(2,1)S(1)}, u32[]{:S(2)}, u32[]{:S(2)}) collective-permute-start(f16[256,256]{1,0:T(8,128)(2,1)S(1)} %collective-permute-done.26), channel_id=1, source_target_pairs={{0,2},{1,5},{2,0},{3,7},{4,6},{5,1},{6,4},{7,3},{8,10},{9,13},{10,... | collective-permute-start | bytes 393224 | tf_op jit(solution)/shard_map/ppermute | solution.py:242
  93.6 1.2 %collective-permute-start.29 = (f32[8,128]{1,0:T(8,128)S(1)}, f32[8,128]{1,0:T(8,128)S(1)}, u32[]{:S(2)}, u32[]{:S(2)}) collective-permute-start(f32[8,128]{1,0:T(8,128)S(1)} %correlate.3.corr_a), channel_id=1, source_target_pairs={{0,1},{1,0},{2,3},{3,2},{4,5},{5,4},{6,7},{7,6},{8,9},{9,8},{10,11... | collective-permute-start | bytes 12296 | tf_op jit(solution)/shard_map/ppermute | solution.py:245
  96.8 1.2 %collective-permute-start.30 = (f32[8,128]{1,0:T(8,128)S(1)}, f32[8,128]{1,0:T(8,128)S(1)}, u32[]{:S(2)}, u32[]{:S(2)}) collective-permute-start(f32[8,128]{1,0:T(8,128)S(1)} %get-tuple-element.69.weight_a), channel_id=1, source_target_pairs={{0,1},{1,0},{2,3},{3,2},{4,5},{5,4},{6,7},{7,6},{8,9},{9,8},{10,11... | collective-permute-start | bytes 12296 | tf_op jit(solution)/shard_map/ppermute | solution.py:245

commit v6 on v5

--- a/solution.py
+++ b/solution.py
@@ -82,25 +82,27 @@
     return 1 - bit
 
 
-def operators(left, right, mask, blocks):
+def operators(left, right, mask, blocks, sent):
     pairs, width, _ = left.shape
     half, inside = width // 2, width // blocks
     strips = half // inside
 
-    def kernel(mask_ref, left_ref, right_ref, sent_ref, kept_ref, held_ref, buf, sems, right_sems):
-        first = first_half()
-        order = [(o, k, i) for o in range(2) for k in range(pairs) for i in range(strips)]
-        copies, rights = [], []
-        for k in range(pairs):
-            rights.append(pltpu.make_async_copy(right_ref.at[k], held_ref.at[k], right_sems.at[k]))
-        for n, (o, k, i) in enumerate(order):
-            h = first if o == 0 else 1 - first
+    def kernel(mask_ref, left_ref, *refs):
+        if sent:
+            right_ref, out_ref, held_ref, buf, sems, right_sems = refs
+        else:
+            out_ref, buf, sems = refs
+        h = first_half() if sent else 1 - first_half()
+        order = [(k, i) for k in range(pairs) for i in range(strips)]
+        copies = []
+        for n, (k, i) in enumerate(order):
             copies.append(pltpu.make_async_copy(
                 left_ref.at[k, pl.ds(pl.multiple_of(h * half + i * inside, inside), inside)], buf.at[n], sems.at[n]))
+        rights = [pltpu.make_async_copy(right_ref.at[k], held_ref.at[k], right_sems.at[k])
+                  for k in range(pairs)] if sent else []
         for copy in copies + rights:
             copy.start()
-        for n, (o, k, i) in enumerate(order):
-            h, out_ref = (first, sent_ref) if o == 0 else (1 - first, kept_ref)
+        for n, (k, i) in enumerate(order):
             copies[n].wait()
             for j in range(blocks):
                 keep = mask_ref[(k * blocks + h * strips + i) * blocks + j]
@@ -110,19 +112,21 @@
         for copy in rights:
             copy.wait()
 
-    count = 2 * pairs * strips
-    half_out = SDS((half, pairs * width), BF16)
-    return call(kernel, "operators", (half_out, half_out, SDS(right.shape, BF16)), (VMEM,) * 3, [SMEM, ANY, ANY],
-                (mask, in_hbm(left), in_hbm(right)), left.size, 4 * left.size,
-                [pltpu.VMEM((count, inside, width), BF16), pltpu.SemaphoreType.DMA((count,)),
-                 pltpu.SemaphoreType.DMA((pairs,))], mib=12)
-
-
-def product(out_ref, at, scale, left_ref, right_ref, parts=4):
+    count = pairs * strips
+    out, args = SDS((half, pairs * width), BF16), (mask, in_hbm(left))
+    scratch = [pltpu.VMEM((count, inside, width), BF16), pltpu.SemaphoreType.DMA((count,))]
+    if sent:
+        return call(kernel, "sent_operators", (out, SDS(right.shape, BF16)), (VMEM, VMEM), [SMEM, ANY, ANY],
+                    args + (in_hbm(right),), left.size, 4 * left.size,
+                    scratch + [pltpu.SemaphoreType.DMA((pairs,))], mib=12)
+    return call(kernel, "kept_operators", out, VMEM, [SMEM, ANY], args, left.size, 2 * left.size, scratch, mib=12)
+
+
+def product(out_ref, scale, left_ref, right_ref, parts):
     step = left_ref.shape[0] // parts
     for p in range(parts):
         rows = slice(p * step, (p + 1) * step)
-        out_ref[rows, at] = scale * jnp.dot(left_ref[rows, :], right_ref[...], preferred_element_type=F32)
+        out_ref[rows, :] = scale * jnp.dot(left_ref[rows, :], right_ref[...], preferred_element_type=F32)
 
 
 def sent_half(chunk, reach, weights, own, other, right, masked):
@@ -142,7 +146,7 @@
                 inner_ref[k * width + r:k * width + r + step, :] = (
                     jnp.dot(own_ref[r:r + step, :], near, preferred_element_type=F32)
                     + jnp.dot(other_ref[r:r + step, :], far, preferred_element_type=F32)).astype(BF16)
-        product(send_ref, slice(None), scale, masked_ref, inner_ref, 2)
+        product(send_ref, scale, masked_ref, inner_ref, 2)
 
     return call(kernel, "sent_half_%d" % chunk, (SDS((pairs * width, size), BF16), SDS((half, size), F32)),
                 (VMEM, VMEM), [VMEM] * 6, (*weights, own, other, right, masked),
@@ -154,7 +158,7 @@
     size = inner.shape[1]
 
     def kernel(a_ref, b_ref, inner_ref, masked_ref, keep_ref):
-        product(keep_ref, slice(None), scale_of(reach, total(a_ref, b_ref)), masked_ref, inner_ref, 2)
+        product(keep_ref, scale_of(reach, total(a_ref, b_ref)), masked_ref, inner_ref, 2)
 
     return call(kernel, "kept_half", SDS((half, size), F32), VMEM, [VMEM] * 4,
                 (*weights, inner, masked), 2 * half * depth * size, 2 ** 20)
@@ -174,12 +178,12 @@
     return call(kernel, "correlate", ONE, VMEM, [VMEM] * (1 + len(sigmas)), (vector, *sigmas), 2 * rows * cols, 2 ** 20)
 
 
-def correct(first, reach, cells, vector, sigmas, diag, corr, weights):
+def correct(first, last, reach, cells, vector, sigmas, diag, corr, weights):
     rows, cols = vector.shape
     size = cols // len(sigmas)
 
     def kernel(corr_a, corr_b, weight_a, weight_b, vector_ref, diag_ref, *refs):
-        sigma_refs, (moved_ref, wave_ref, square_ref) = refs[:-3], refs[-3:]
+        sigma_refs, (moved_ref, square_ref) = refs[:len(sigmas)], refs[len(sigmas):len(sigmas) + 2]
         weight = total(weight_a, weight_b)
         scale = scale_of(reach, weight)
         norm = jnp.ones((1, 1), F32) if first else lax.rsqrt(weight / cells + EPS)
@@ -195,12 +199,14 @@
                 slope = spacing / jnp.maximum(spacing * spacing, 1.0)
                 moved = coef - (sigma_ref[r:r + BLOCK, :] * unit - theta * coef) * slope
                 moved_ref[at] = moved
-                wave_ref[at] = moved.astype(BF16)
+                if not last:
+                    refs[-1][at] = moved.astype(BF16)
                 out = out + folded(moved * moved)
         put(square_ref, out)
 
-    return call(kernel, "correct", (SDS((rows, cols), F32), SDS((rows, cols), BF16), ONE), (VMEM, VMEM, VMEM),
-                [VMEM] * (6 + len(sigmas)), (*corr, *weights, vector, diag, *sigmas), 12 * rows * cols, 2 ** 20)
+    outs = (SDS((rows, cols), F32), ONE) + ((() if last else (SDS((rows, cols), BF16),)))
+    return call(kernel, "correct", outs, (VMEM,) * len(outs), [VMEM] * (6 + len(sigmas)),
+                (*corr, *weights, vector, diag, *sigmas), 12 * rows * cols, 2 ** 20)
 
 
 def normalise(cells, vector, weights):
@@ -269,7 +275,7 @@
 
     def gathered(piece):
         p1, p2 = swap(piece, 1), swap(piece, 0)
-        p3 = swap(p1, 0)
+        p3 = lax.ppermute(piece, BOTH, [(o * cols + c, (o ^ 3) * cols + c) for o in range(ops) for c in range(cols)])
         near0, near1 = jnp.where(low_near, piece, p1), jnp.where(low_near, p1, piece)
         far0, far1 = jnp.where(low_near, p2, p3), jnp.where(low_near, p3, p2)
         return jnp.concatenate([
@@ -279,7 +285,7 @@
     vector = wave_coef
     own, weight = open_vector(wave_coef)
     mask = block_mask.reshape(-1)
-    sent, kept, right = operators(left, right, mask, blocks)
+    sent, right = operators(left, right, mask, blocks, True)
     for step in range(STEPS):
         other = across(own)
         weights = (weight, across(weight))
@@ -289,7 +295,9 @@
             gots.append(begin(send))
             inners.append(inner)
             own, other = lax.optimization_barrier((own, other, inner))[:2]
-        inners[0] = lax.optimization_barrier((inners[0], inners[-1]))[0]
+        inners[0], mask = lax.optimization_barrier((inners[0], mask, inners[-1]))[:2]
+        if step == 0:
+            kept = operators(left, right, mask, blocks, False)
         sigmas = []
         for c in range(CHUNKS):
             keep = kept_half(reach, weights, inners[c], kept)
@@ -298,8 +306,9 @@
                 send, inners[c + 1] = lax.optimization_barrier((send, inners[c + 1]))
             sigmas.append(gathered(finish(keep, swap(send, 1))))
         corr = correlate(vector, sigmas)
-        vector, own, weight = correct(
-            step == 0, reach, cells, vector, sigmas, diag_energy, (corr, across(corr)), weights)
+        vector, weight, *own = correct(
+            step == 0, step == STEPS - 1, reach, cells, vector, sigmas, diag_energy, (corr, across(corr)), weights)
+        own = own[0] if own else None
     return normalise(cells, vector, (weight, across(weight)))
 
 

time: 99.7 us -> 96.6 us (0.969)
  waiting for transfers between devices: 44.9 us -> 41.7 us
    ppermute x24 -> x20, waiting for transfers between devices: 39.4 us -> 29 us  [swap(): return lax.ppermute(x, BOTH, pairing)]
    ppermute x0 -> x4, waiting for transfers between devices: none -> 7.17 us  [gathered(): lax.ppermute(piece, BOTH, [(o * cols + c, (o ^ 3) * cols + c) for o in ra...]
    ppermute x24 -> x20, starting transfers between devices: 29.6 us -> 27.1 us  [swap(): return lax.ppermute(x, BOTH, pairing)]
    ppermute x0 -> x4, starting transfers between devices: none -> 1.87 us  [gathered(): lax.ppermute(piece, BOTH, [(o * cols + c, (o ^ 3) * cols + c) for o in ra...]
    pallas_call x15 -> x16, Pallas kernels: 20.8 us -> 21.4 us  [call(): pl.pallas_call(kernel, out_shape=outs, in_specs=in_specs, out_specs=out_s...]
  transfers between devices with their start and end apart: 31 -> 31, of which waited for: 25 -> 23; matrix products, arithmetic and copies ran while one was open for 2% -> 2% of each run, Pallas kernels for 10% -> 12%
where the time goes in v6:
time: 96.6 us; the launch traced here: 96.4 us
  waiting for transfers between devices  41.7 us (43%)
  starting transfers between devices  30.5 us (32%)
  Pallas kernels  21.4 us (22%)
  other arithmetic  2.17 us (2%)
    ppermute x20, waiting for transfers between devices, swap(): return lax.ppermute(x, BOTH, pairing)  29 us
    ppermute x20, starting transfers between devices, swap(): return lax.ppermute(x, BOTH, pairing)  27.1 us
    pallas_call x16, Pallas kernels, call(): pl.pallas_call(kernel, out_shape=outs, in_specs=in_specs, out_specs=out_s...  21.4 us
    ppermute x4, waiting for transfers between devices, gathered(): lax.ppermute(piece, BOTH, [(o * cols + c, (o ^ 3) * cols + c) for o in ra...  7.17 us
    ppermute x7, waiting for transfers between devices, across(): return lax.ppermute(x, 'col', [(c, c ^ 1) for c in range(cols)])  5.47 us
  transfers between devices with their start and end apart: 31, of which 23 were waited for; matrix products, arithmetic and copies ran while one was open for 2% of the time, Pallas kernels for 12%

profile of v6, /device:TPU:0, one launch (start us, length us, event | category | flops | bytes accessed | tf_op | source)
XLA Modules:
  0.0 96.4 jit_solution(6845027456591987904)
XLA Ops:
  0.0 1.7 %open_vector.1 = (bf16[1024,512]{1,0:T(8,128)(2,1)S(1)}, f32[8,128]{1,0:T(8,128)S(1)}) custom-call(f32[1024,512]{1,0:T(8,128)} %vector_ref.1), custom_call_target="tpu_custom_call" | custom-call | flops 1572864 | bytes 4194304 | tf_op jit(solution)/shard_map/open_vector/pallas_call | solution.py:30
  1.7 0.5 collective-permute-start.1
  2.4 2.9 %sent_operators.1 = (bf16[512,2048]{1,0:T(8,128)(2,1)S(1)}, bf16[2,1024,512]{2,1,0:T(8,128)(2,1)S(1)}) custom-call(s32[128]{0:T(128)S(1)} %reshape.3.mask_ref, bf16[2,1024,1024]{2,1,0:T(8,128)(2,1)} %left_ref.3, bf16[2,1024,512]{2,1,0:T(8,128)(2,1)} %refs_0_.1), custom_call_target="tpu_custom_call" | custom-call | flops 2097152 | bytes 8388608 | tf_op jit(solution)/shard_map/sent_operators/pallas_call | solution.py:30
  5.3 1.8 %sent_half_0.2 = (bf16[2048,256]{1,0:T(8,128)(2,1)S(1)}, f32[512,256]{1,0:T(8,128)S(1)}) custom-call(f32[8,128]{1,0:T(8,128)S(1)} %get-tuple-element.41.a_ref.weight_a, f32[8,128]{1,0:T(8,128)S(1)} %collective-permute-done.b_ref.weight_b, bf16[1024,512]{1,0:T(8,128)(2,1)S(1)} %get-tuple-element.46.own_ref, ...), custom_call_target="tpu_custom_call" | custom-call | flops 1610612736 | bytes 1048576 | tf_op jit(solution)/shard_map/sent_half_0/pallas_call | solution.py:30
  7.2 3.0 %collective-permute-start.2 = (f16[512,256]{1,0:T(8,128)(2,1)S(1)}, f16[512,256]{1,0:T(8,128)(2,1)S(1)}, u32[]{:S(2)}, u32[]{:S(2)}) collective-permute-start(f16[512,256]{1,0:T(8,128)(2,1)S(1)} %convert_element_type.116), channel_id=1, source_target_pairs={{0,2},{1,5},{2,0},{3,7},{4,6},{5,1},{6,4},{7,3},{8,10},{9,13},{10,... | collective-permute-start | bytes 786440 | tf_op jit(solution)/shard_map/ppermute | solution.py:248
  10.2 1.8 %sent_half_1.2 = (bf16[2048,256]{1,0:T(8,128)(2,1)S(1)}, f32[512,256]{1,0:T(8,128)S(1)}) custom-call(f32[8,128]{1,0:T(8,128)S(1)} %get-tuple-element.41.a_ref.weight_a, f32[8,128]{1,0:T(8,128)S(1)} %collective-permute-done.b_ref.weight_b, bf16[1024,512]{1,0:T(8,128)(2,1)S(1)} %get-tuple-element.46.own_ref, ...), custom_call_target="tpu_custom_call" | custom-call | flops 1610612736 | bytes 1048576 | tf_op jit(solution)/shard_map/sent_half_1/pallas_call | solution.py:30
  12.2 2.2 %kept_operators.1.masked_ref = bf16[512,2048]{1,0:T(8,128)(2,1)S(1)} custom-call(s32[128]{0:T(128)S(1)} %reshape.3.mask_ref, bf16[2,1024,1024]{2,1,0:T(8,128)(2,1)} %left_ref.3), custom_call_target="tpu_custom_call" | custom-call | flops 2097152 | bytes 4194304 | tf_op jit(solution)/shard_map/kept_operators/pallas_call | solution.py:30
  14.4 0.7 kept_half.4
  15.2 2.1 %collective-permute-start.3 = (f16[256,256]{1,0:T(8,128)(2,1)S(1)}, f16[256,256]{1,0:T(8,128)(2,1)S(1)}, u32[]{:S(2)}, u32[]{:S(2)}) collective-permute-start(f16[256,256]{1,0:T(8,128)(2,1)S(1)} %dynamic-slice_convert_fusion.3), channel_id=1, source_target_pairs={{0,4},{1,3},{2,6},{3,1},{4,0},{5,7},{6,2},{7,5},{8,12},{9,11},{10,... | collective-permute-start | bytes 393224 | tf_op jit(solution)/shard_map/ppermute | solution.py:248
  17.4 0.7 kept_half.5
  18.1 1.1 %collective-permute-done.8 = f16[512,256]{1,0:T(8,128)(2,1)S(1)} collective-permute-done((f16[512,256]{1,0:T(8,128)(2,1)S(1)}, f16[512,256]{1,0:T(8,128)(2,1)S(1)}, u32[]{:S(2)}, u32[]{:S(2)}) %collective-permute-start.8) | collective-permute-done | bytes 262176 | tf_op jit(solution)/shard_map/ppermute | solution.py:248
  19.3 1.5 %collective-permute-start.9 = (f16[256,256]{1,0:T(8,128)(2,1)S(1)}, f16[256,256]{1,0:T(8,128)(2,1)S(1)}, u32[]{:S(2)}, u32[]{:S(2)}) collective-permute-start(f16[256,256]{1,0:T(8,128)(2,1)S(1)} %dynamic-slice_convert_fusion.2), channel_id=1, source_target_pairs={{0,4},{1,3},{2,6},{3,1},{4,0},{5,7},{6,2},{7,5},{8,12},{9,11},{10,... | collective-permute-start | bytes 393224 | tf_op jit(solution)/shard_map/ppermute | solution.py:248
  20.9 2.6 %collective-permute-start.4 = (f16[256,256]{1,0:T(8,128)(2,1)S(1)}, f16[256,256]{1,0:T(8,128)(2,1)S(1)}, u32[]{:S(2)}, u32[]{:S(2)}) collective-permute-start(f16[256,256]{1,0:T(8,128)(2,1)S(1)} %add_convert_fusion.7), channel_id=1, source_target_pairs={{0,8},{1,9},{2,10},{3,11},{4,12},{5,13},{6,14},{7,15},{8,0},{9,1},... | collective-permute-start | bytes 393224 | tf_op jit(solution)/shard_map/ppermute | solution.py:248
  23.5 2.3 %collective-permute-done.9 = f16[256,256]{1,0:T(8,128)(2,1)S(1)} collective-permute-done((f16[256,256]{1,0:T(8,128)(2,1)S(1)}, f16[256,256]{1,0:T(8,128)(2,1)S(1)}, u32[]{:S(2)}, u32[]{:S(2)}) %collective-permute-start.9) | collective-permute-done | bytes 131104 | tf_op jit(solution)/shard_map/ppermute | solution.py:248
  25.9 2.4 %collective-permute-start.10 = (f16[256,256]{1,0:T(8,128)(2,1)S(1)}, f16[256,256]{1,0:T(8,128)(2,1)S(1)}, u32[]{:S(2)}, u32[]{:S(2)}) collective-permute-start(f16[256,256]{1,0:T(8,128)(2,1)S(1)} %add_convert_fusion.5), channel_id=1, source_target_pairs={{0,8},{1,9},{2,10},{3,11},{4,12},{5,13},{6,14},{7,15},{8,0},{9,1},... | collective-permute-start | bytes 393224 | tf_op jit(solution)/shard_map/ppermute | solution.py:248
  28.3 5.1 %collective-permute-done.4 = f16[256,256]{1,0:T(8,128)(2,1)S(1)} collective-permute-done((f16[256,256]{1,0:T(8,128)(2,1)S(1)}, f16[256,256]{1,0:T(8,128)(2,1)S(1)}, u32[]{:S(2)}, u32[]{:S(2)}) %collective-permute-start.4) | collective-permute-done | bytes 131104 | tf_op jit(solution)/shard_map/ppermute | solution.py:248
  33.5 0.6 collective-permute-start.7
  34.1 0.9 collective-permute-start.6
  34.9 2.1 %collective-permute-start.5 = (f16[256,256]{1,0:T(8,128)(2,1)S(1)}, f16[256,256]{1,0:T(8,128)(2,1)S(1)}, u32[]{:S(2)}, u32[]{:S(2)}) collective-permute-start(f16[256,256]{1,0:T(8,128)(2,1)S(1)} %add_convert_fusion.6), channel_id=1, source_target_pairs={{0,4},{1,3},{2,6},{3,1},{4,0},{5,7},{6,2},{7,5},{8,12},{9,11},{10,... | collective-permute-start | bytes 393224 | tf_op jit(solution)/shard_map/ppermute | solution.py:248
  37.1 0.6 collective-permute-start.13
  37.7 0.9 collective-permute-start.12
  38.6 2.3 %collective-permute-done.7 = f16[256,256]{1,0:T(8,128)(2,1)S(1)} collective-permute-done((f16[256,256]{1,0:T(8,128)(2,1)S(1)}, f16[256,256]{1,0:T(8,128)(2,1)S(1)}, u32[]{:S(2)}, u32[]{:S(2)}) %collective-permute-start.7) | collective-permute-done | bytes 131104 | tf_op jit(solution)/shard_map/ppermute | solution.py:278
  40.9 2.2 %collective-permute-done.6 = f16[256,256]{1,0:T(8,128)(2,1)S(1)} collective-permute-done((f16[256,256]{1,0:T(8,128)(2,1)S(1)}, f16[256,256]{1,0:T(8,128)(2,1)S(1)}, u32[]{:S(2)}, u32[]{:S(2)}) %collective-permute-start.6) | collective-permute-done | bytes 131104 | tf_op jit(solution)/shard_map/ppermute | solution.py:248
  43.1 0.2 collective-permute-done.5
  43.5 1.3 %collective-permute-done.13 = f16[256,256]{1,0:T(8,128)(2,1)S(1)} collective-permute-done((f16[256,256]{1,0:T(8,128)(2,1)S(1)}, f16[256,256]{1,0:T(8,128)(2,1)S(1)}, u32[]{:S(2)}, u32[]{:S(2)}) %collective-permute-start.13) | collective-permute-done | bytes 131104 | tf_op jit(solution)/shard_map/ppermute | solution.py:278
  44.8 1.3 %collective-permute-done.12 = f16[256,256]{1,0:T(8,128)(2,1)S(1)} collective-permute-done((f16[256,256]{1,0:T(8,128)(2,1)S(1)}, f16[256,256]{1,0:T(8,128)(2,1)S(1)}, u32[]{:S(2)}, u32[]{:S(2)}) %collective-permute-start.12) | collective-permute-done | bytes 131104 | tf_op jit(solution)/shard_map/ppermute | solution.py:248
  46.0 0.2 collective-permute-done.11
  46.4 0.2 maximum_convert_fusion
  46.7 0.3 correlate.2.corr_a
  47.1 1.2 %collective-permute-done.14.corr_b = f32[8,128]{1,0:T(8,128)S(1)} collective-permute-done((f32[8,128]{1,0:T(8,128)S(1)}, f32[8,128]{1,0:T(8,128)S(1)}, u32[]{:S(2)}, u32[]{:S(2)}) %collective-permute-start.14) | collective-permute-done | bytes 4128 | tf_op jit(solution)/shard_map/ppermute | solution.py:251
  48.3 1.0 %correct.2 = (f32[1024,512]{1,0:T(8,128)S(1)}, f32[8,128]{1,0:T(8,128)S(1)}, bf16[1024,512]{1,0:T(8,128)(2,1)S(1)}) custom-call(f32[8,128]{1,0:T(8,128)S(1)} %correlate.2.corr_a, f32[8,128]{1,0:T(8,128)S(1)} %collective-permute-done.14.corr_b, f32[8,128]{1,0:T(8,128)S(1)} %get-tuple-element.41.a_ref.weight_a, ...), custom_call_target="tpu_custom_call" | custom-call | flops 6291456 | bytes 1048576 | tf_op jit(solution)/shard_map/correct/pallas_call | solution.py:30
  49.3 0.2 collective-permute-start.16
  49.5 0.4 collective-permute-start.15
  49.9 2.2 %collective-permute-done.15.b_ref.weight_b = f32[8,128]{1,0:T(8,128)S(1)} collective-permute-done((f32[8,128]{1,0:T(8,128)S(1)}, f32[8,128]{1,0:T(8,128)S(1)}, u32[]{:S(2)}, u32[]{:S(2)}) %collective-permute-start.15) | collective-permute-done | bytes 4128 | tf_op jit(solution)/shard_map/ppermute | solution.py:251
  52.0 1.8 %sent_half_0.3 = (bf16[2048,256]{1,0:T(8,128)(2,1)S(1)}, f32[512,256]{1,0:T(8,128)S(1)}) custom-call(f32[8,128]{1,0:T(8,128)S(1)} %get-tuple-element.58.a_ref.weight_a, f32[8,128]{1,0:T(8,128)S(1)} %collective-permute-done.15.b_ref.weight_b, bf16[1024,512]{1,0:T(8,128)(2,1)S(1)} %get-tuple-element.61.own_ref, ...), custom_call_target="tpu_custom_call" | custom-call | flops 1610612736 | bytes 1048576 | tf_op jit(solution)/shard_map/sent_half_0/pallas_call | solution.py:30
  53.9 0.8 collective-permute-start.17
  54.7 1.8 %sent_half_1.3 = (bf16[2048,256]{1,0:T(8,128)(2,1)S(1)}, f32[512,256]{1,0:T(8,128)S(1)}) custom-call(f32[8,128]{1,0:T(8,128)S(1)} %get-tuple-element.58.a_ref.weight_a, f32[8,128]{1,0:T(8,128)S(1)} %collective-permute-done.15.b_ref.weight_b, bf16[1024,512]{1,0:T(8,128)(2,1)S(1)} %get-tuple-element.61.own_ref, ...), custom_call_target="tpu_custom_call" | custom-call | flops 1610612736 | bytes 1048576 | tf_op jit(solution)/shard_map/sent_half_1/pallas_call | solution.py:30
  56.5 1.4 %collective-permute-start.23 = (f16[512,256]{1,0:T(8,128)(2,1)S(1)}, f16[512,256]{1,0:T(8,128)(2,1)S(1)}, u32[]{:S(2)}, u32[]{:S(2)}) collective-permute-start(f16[512,256]{1,0:T(8,128)(2,1)S(1)} %convert_element_type.143), channel_id=1, source_target_pairs={{0,2},{1,5},{2,0},{3,7},{4,6},{5,1},{6,4},{7,3},{8,10},{9,13},{10,... | collective-permute-start | bytes 786440 | tf_op jit(solution)/shard_map/ppermute | solution.py:248
  57.9 0.7 kept_half.6
  58.6 1.7 %collective-permute-done.17 = f16[512,256]{1,0:T(8,128)(2,1)S(1)} collective-permute-done((f16[512,256]{1,0:T(8,128)(2,1)S(1)}, f16[512,256]{1,0:T(8,128)(2,1)S(1)}, u32[]{:S(2)}, u32[]{:S(2)}) %collective-permute-start.17) | collective-permute-done | bytes 262176 | tf_op jit(solution)/shard_map/ppermute | solution.py:248
  60.5 0.2 collective-permute-start.18
  60.7 0.9 kept_half.7
  61.6 2.2 %collective-permute-done.23 = f16[512,256]{1,0:T(8,128)(2,1)S(1)} collective-permute-done((f16[512,256]{1,0:T(8,128)(2,1)S(1)}, f16[512,256]{1,0:T(8,128)(2,1)S(1)}, u32[]{:S(2)}, u32[]{:S(2)}) %collective-permute-start.23) | collective-permute-done | bytes 262176 | tf_op jit(solution)/shard_map/ppermute | solution.py:248
  64.1 1.4 %collective-permute-done.18 = f16[256,256]{1,0:T(8,128)(2,1)S(1)} collective-permute-done((f16[256,256]{1,0:T(8,128)(2,1)S(1)}, f16[256,256]{1,0:T(8,128)(2,1)S(1)}, u32[]{:S(2)}, u32[]{:S(2)}) %collective-permute-start.18) | collective-permute-done | bytes 131104 | tf_op jit(solution)/shard_map/ppermute | solution.py:248
  65.6 2.6 %collective-permute-start.19 = (f16[256,256]{1,0:T(8,128)(2,1)S(1)}, f16[256,256]{1,0:T(8,128)(2,1)S(1)}, u32[]{:S(2)}, u32[]{:S(2)}) collective-permute-start(f16[256,256]{1,0:T(8,128)(2,1)S(1)} %add_convert_fusion.3), channel_id=1, source_target_pairs={{0,8},{1,9},{2,10},{3,11},{4,12},{5,13},{6,14},{7,15},{8,0},{9,1},... | collective-permute-start | bytes 393224 | tf_op jit(solution)/shard_map/ppermute | solution.py:248
  68.2 2.3 %collective-permute-done.24 = f16[256,256]{1,0:T(8,128)(2,1)S(1)} collective-permute-done((f16[256,256]{1,0:T(8,128)(2,1)S(1)}, f16[256,256]{1,0:T(8,128)(2,1)S(1)}, u32[]{:S(2)}, u32[]{:S(2)}) %collective-permute-start.24) | collective-permute-done | bytes 131104 | tf_op jit(solution)/shard_map/ppermute | solution.py:248
  70.6 1.9 %collective-permute-start.25 = (f16[256,256]{1,0:T(8,128)(2,1)S(1)}, f16[256,256]{1,0:T(8,128)(2,1)S(1)}, u32[]{:S(2)}, u32[]{:S(2)}) collective-permute-start(f16[256,256]{1,0:T(8,128)(2,1)S(1)} %add_convert_fusion.1), channel_id=1, source_target_pairs={{0,8},{1,9},{2,10},{3,11},{4,12},{5,13},{6,14},{7,15},{8,0},{9,1},... | collective-permute-start | bytes 393224 | tf_op jit(solution)/shard_map/ppermute | solution.py:248
  72.4 5.7 %collective-permute-done.19 = f16[256,256]{1,0:T(8,128)(2,1)S(1)} collective-permute-done((f16[256,256]{1,0:T(8,128)(2,1)S(1)}, f16[256,256]{1,0:T(8,128)(2,1)S(1)}, u32[]{:S(2)}, u32[]{:S(2)}) %collective-permute-start.19) | collective-permute-done | bytes 131104 | tf_op jit(solution)/shard_map/ppermute | solution.py:248
  78.3 1.2 %collective-permute-start.21 = (f16[256,256]{1,0:T(8,128)(2,1)S(1)}, f16[256,256]{1,0:T(8,128)(2,1)S(1)}, u32[]{:S(2)}, u32[]{:S(2)}) collective-permute-start(f16[256,256]{1,0:T(8,128)(2,1)S(1)} %add_convert_fusion.2), channel_id=1, source_target_pairs={{0,2},{1,5},{2,0},{3,7},{4,6},{5,1},{6,4},{7,3},{8,10},{9,13},{10,... | collective-permute-start | bytes 393224 | tf_op jit(solution)/shard_map/ppermute | solution.py:248
  79.4 2.3 %collective-permute-start.20 = (f16[256,256]{1,0:T(8,128)(2,1)S(1)}, f16[256,256]{1,0:T(8,128)(2,1)S(1)}, u32[]{:S(2)}, u32[]{:S(2)}) collective-permute-start(f16[256,256]{1,0:T(8,128)(2,1)S(1)} %add_convert_fusion.2), channel_id=1, source_target_pairs={{0,4},{1,3},{2,6},{3,1},{4,0},{5,7},{6,2},{7,5},{8,12},{9,11},{10,... | collective-permute-start | bytes 393224 | tf_op jit(solution)/shard_map/ppermute | solution.py:248
  81.8 0.6 collective-permute-start.28
  82.4 0.9 collective-permute-start.27
  83.3 2.2 %collective-permute-done.22 = f16[256,256]{1,0:T(8,128)(2,1)S(1)} collective-permute-done((f16[256,256]{1,0:T(8,128)(2,1)S(1)}, f16[256,256]{1,0:T(8,128)(2,1)S(1)}, u32[]{:S(2)}, u32[]{:S(2)}) %collective-permute-start.22) | collective-permute-done | bytes 131104 | tf_op jit(solution)/shard_map/ppermute | solution.py:278
  85.5 1.8 %collective-permute-done.21 = f16[256,256]{1,0:T(8,128)(2,1)S(1)} collective-permute-done((f16[256,256]{1,0:T(8,128)(2,1)S(1)}, f16[256,256]{1,0:T(8,128)(2,1)S(1)}, u32[]{:S(2)}, u32[]{:S(2)}) %collective-permute-start.21) | collective-permute-done | bytes 131104 | tf_op jit(solution)/shard_map/ppermute | solution.py:248
  87.6 1.4 %collective-permute-done.28 = f16[256,256]{1,0:T(8,128)(2,1)S(1)} collective-permute-done((f16[256,256]{1,0:T(8,128)(2,1)S(1)}, f16[256,256]{1,0:T(8,128)(2,1)S(1)}, u32[]{:S(2)}, u32[]{:S(2)}) %collective-permute-start.28) | collective-permute-done | bytes 131104 | tf_op jit(solution)/shard_map/ppermute | solution.py:278
  89.0 1.3 %collective-permute-done.27 = f16[256,256]{1,0:T(8,128)(2,1)S(1)} collective-permute-done((f16[256,256]{1,0:T(8,128)(2,1)S(1)}, f16[256,256]{1,0:T(8,128)(2,1)S(1)}, u32[]{:S(2)}, u32[]{:S(2)}) %collective-permute-start.27) | collective-permute-done | bytes 131104 | tf_op jit(solution)/shard_map/ppermute | solution.py:248
  90.3 0.3 collective-permute-done.26
  90.5 0.2 broadcast_select_fusion.19
  90.8 0.5 correlate.3.corr_a
  91.4 1.2 %collective-permute-done.29.corr_b = f32[8,128]{1,0:T(8,128)S(1)} collective-permute-done((f32[8,128]{1,0:T(8,128)S(1)}, f32[8,128]{1,0:T(8,128)S(1)}, u32[]{:S(2)}, u32[]{:S(2)}) %collective-permute-start.29) | collective-permute-done | bytes 4128 | tf_op jit(solution)/shard_map/ppermute | solution.py:251
  92.5 1.1 %correct.3 = (f32[1024,512]{1,0:T(8,128)S(1)}, f32[8,128]{1,0:T(8,128)S(1)}) custom-call(f32[8,128]{1,0:T(8,128)S(1)} %correlate.3.corr_a, f32[8,128]{1,0:T(8,128)S(1)} %collective-permute-done.29.corr_b, f32[8,128]{1,0:T(8,128)S(1)} %get-tuple-element.58.a_ref.weight_a, f32[8,128]{1,0:T(8,128)S(1)} %collective-permute-done.15.b_ref.weight_b, ...), custom_call_target="tpu_custom_call" | custom-call | flops 6291456 | bytes 1048576 | tf_op jit(solution)/shard_map/correct/pallas_call | solution.py:30
  93.6 0.2 collective-permute-start.30
  93.8 1.0 %collective-permute-done.30.weight_b = f32[8,128]{1,0:T(8,128)S(1)} collective-permute-done((f32[8,128]{1,0:T(8,128)S(1)}, f32[8,128]{1,0:T(8,128)S(1)}, u32[]{:S(2)}, u32[]{:S(2)}) %collective-permute-start.30) | collective-permute-done | bytes 4128 | tf_op jit(solution)/shard_map/ppermute | solution.py:251
  94.8 1.4 %normalise.1 = f32[1024,512]{1,0:T(8,128)} custom-call(f32[8,128]{1,0:T(8,128)S(1)} %get-tuple-element.69.weight_a, f32[8,128]{1,0:T(8,128)S(1)} %collective-permute-done.30.weight_b, f32[1024,512]{1,0:T(8,128)S(1)} %get-tuple-element.70.vector_ref), custom_call_target="tpu_custom_call" | custom-call | flops 524288 | bytes 4194304 | tf_op jit(solution)/shard_map/normalise/pallas_call | solution.py:30
  (48 shorter events, 2.5 us)
Async XLA Ops:
  0.0 2.3 %copy-start.2 = (s32[2,8,8]{2,1,0:T(8,128)S(1)}, s32[2,8,8]{2,1,0:T(8,128)}, u32[]{:S(2)}) copy-start(s32[2,8,8]{2,1,0:T(8,128)} %param.9) | copy-start | bytes 1540
  1.7 3.6 %collective-permute-start.1 = (bf16[1024,512]{1,0:T(8,128)(2,1)S(1)}, bf16[1024,512]{1,0:T(8,128)(2,1)S(1)}, u32[]{:S(2)}, u32[]{:S(2)}) collective-permute-start(bf16[1024,512]{1,0:T(8,128)(2,1)S(1)} %get-tuple-element.46.own_ref), channel_id=1, source_target_pairs={{0,1},{1,0},{2,3},{3,2},{4,5},{5,4},{6,7},{7,6},{8,9},{9,8},{10,11... | collective-permute-start | bytes 3145736 | tf_op jit(solution)/shard_map/ppermute | solution.py:251
  2.3 3.0 %collective-permute-start = (f32[8,128]{1,0:T(8,128)S(1)}, f32[8,128]{1,0:T(8,128)S(1)}, u32[]{:S(2)}, u32[]{:S(2)}) collective-permute-start(f32[8,128]{1,0:T(8,128)S(1)} %get-tuple-element.41.a_ref.weight_a), channel_id=1, source_target_pairs={{0,1},{1,0},{2,3},{3,2},{4,5},{5,4},{6,7},{7,6},{8,9},{9,8},{10,11... | collective-permute-start | bytes 12296 | tf_op jit(solution)/shard_map/ppermute | solution.py:251
  7.2 7.9 %collective-permute-start.2 = (f16[512,256]{1,0:T(8,128)(2,1)S(1)}, f16[512,256]{1,0:T(8,128)(2,1)S(1)}, u32[]{:S(2)}, u32[]{:S(2)}) collective-permute-start(f16[512,256]{1,0:T(8,128)(2,1)S(1)} %convert_element_type.116), channel_id=1, source_target_pairs={{0,2},{1,5},{2,0},{3,7},{4,6},{5,1},{6,4},{7,3},{8,10},{9,13},{10,... | collective-permute-start | bytes 786440 | tf_op jit(solution)/shard_map/ppermute | solution.py:248
  12.1 7.1 %collective-permute-start.8 = (f16[512,256]{1,0:T(8,128)(2,1)S(1)}, f16[512,256]{1,0:T(8,128)(2,1)S(1)}, u32[]{:S(2)}, u32[]{:S(2)}) collective-permute-start(f16[512,256]{1,0:T(8,128)(2,1)S(1)} %convert_element_type.125), channel_id=1, source_target_pairs={{0,2},{1,5},{2,0},{3,7},{4,6},{5,1},{6,4},{7,3},{8,10},{9,13},{10,... | collective-permute-start | bytes 786440 | tf_op jit(solution)/shard_map/ppermute | solution.py:248
  15.2 5.6 %collective-permute-start.3 = (f16[256,256]{1,0:T(8,128)(2,1)S(1)}, f16[256,256]{1,0:T(8,128)(2,1)S(1)}, u32[]{:S(2)}, u32[]{:S(2)}) collective-permute-start(f16[256,256]{1,0:T(8,128)(2,1)S(1)} %dynamic-slice_convert_fusion.3), channel_id=1, source_target_pairs={{0,4},{1,3},{2,6},{3,1},{4,0},{5,7},{6,2},{7,5},{8,12},{9,11},{10,... | collective-permute-start | bytes 393224 | tf_op jit(solution)/shard_map/ppermute | solution.py:248
  19.3 6.5 %collective-permute-start.9 = (f16[256,256]{1,0:T(8,128)(2,1)S(1)}, f16[256,256]{1,0:T(8,128)(2,1)S(1)}, u32[]{:S(2)}, u32[]{:S(2)}) collective-permute-start(f16[256,256]{1,0:T(8,128)(2,1)S(1)} %dynamic-slice_convert_fusion.2), channel_id=1, source_target_pairs={{0,4},{1,3},{2,6},{3,1},{4,0},{5,7},{6,2},{7,5},{8,12},{9,11},{10,... | collective-permute-start | bytes 393224 | tf_op jit(solution)/shard_map/ppermute | solution.py:248
  20.9 12.5 %collective-permute-start.4 = (f16[256,256]{1,0:T(8,128)(2,1)S(1)}, f16[256,256]{1,0:T(8,128)(2,1)S(1)}, u32[]{:S(2)}, u32[]{:S(2)}) collective-permute-start(f16[256,256]{1,0:T(8,128)(2,1)S(1)} %add_convert_fusion.7), channel_id=1, source_target_pairs={{0,8},{1,9},{2,10},{3,11},{4,12},{5,13},{6,14},{7,15},{8,0},{9,1},... | collective-permute-start | bytes 393224 | tf_op jit(solution)/shard_map/ppermute | solution.py:248
  25.9 11.1 %collective-permute-start.10 = (f16[256,256]{1,0:T(8,128)(2,1)S(1)}, f16[256,256]{1,0:T(8,128)(2,1)S(1)}, u32[]{:S(2)}, u32[]{:S(2)}) collective-permute-start(f16[256,256]{1,0:T(8,128)(2,1)S(1)} %add_convert_fusion.5), channel_id=1, source_target_pairs={{0,8},{1,9},{2,10},{3,11},{4,12},{5,13},{6,14},{7,15},{8,0},{9,1},... | collective-permute-start | bytes 393224 | tf_op jit(solution)/shard_map/ppermute | solution.py:248
  33.5 7.4 %collective-permute-start.7 = (f16[256,256]{1,0:T(8,128)(2,1)S(1)}, f16[256,256]{1,0:T(8,128)(2,1)S(1)}, u32[]{:S(2)}, u32[]{:S(2)}) collective-permute-start(f16[256,256]{1,0:T(8,128)(2,1)S(1)} %add_convert_fusion.6), channel_id=1, source_target_pairs={{0,6},{1,7},{2,4},{3,5},{4,2},{5,3},{6,0},{7,1},{8,14},{9,15},{10,... | collective-permute-start | bytes 393224 | tf_op jit(solution)/shard_map/ppermute | solution.py:278
  34.1 9.1 %collective-permute-start.6 = (f16[256,256]{1,0:T(8,128)(2,1)S(1)}, f16[256,256]{1,0:T(8,128)(2,1)S(1)}, u32[]{:S(2)}, u32[]{:S(2)}) collective-permute-start(f16[256,256]{1,0:T(8,128)(2,1)S(1)} %add_convert_fusion.6), channel_id=1, source_target_pairs={{0,2},{1,5},{2,0},{3,7},{4,6},{5,1},{6,4},{7,3},{8,10},{9,13},{10,... | collective-permute-start | bytes 393224 | tf_op jit(solution)/shard_map/ppermute | solution.py:248
  34.9 8.3 %collective-permute-start.5 = (f16[256,256]{1,0:T(8,128)(2,1)S(1)}, f16[256,256]{1,0:T(8,128)(2,1)S(1)}, u32[]{:S(2)}, u32[]{:S(2)}) collective-permute-start(f16[256,256]{1,0:T(8,128)(2,1)S(1)} %add_convert_fusion.6), channel_id=1, source_target_pairs={{0,4},{1,3},{2,6},{3,1},{4,0},{5,7},{6,2},{7,5},{8,12},{9,11},{10,... | collective-permute-start | bytes 393224 | tf_op jit(solution)/shard_map/ppermute | solution.py:248
  37.1 7.7 %collective-permute-start.13 = (f16[256,256]{1,0:T(8,128)(2,1)S(1)}, f16[256,256]{1,0:T(8,128)(2,1)S(1)}, u32[]{:S(2)}, u32[]{:S(2)}) collective-permute-start(f16[256,256]{1,0:T(8,128)(2,1)S(1)} %add_convert_fusion.4), channel_id=1, source_target_pairs={{0,6},{1,7},{2,4},{3,5},{4,2},{5,3},{6,0},{7,1},{8,14},{9,15},{10,... | collective-permute-start | bytes 393224 | tf_op jit(solution)/shard_map/ppermute | solution.py:278
  37.7 8.3 %collective-permute-start.12 = (f16[256,256]{1,0:T(8,128)(2,1)S(1)}, f16[256,256]{1,0:T(8,128)(2,1)S(1)}, u32[]{:S(2)}, u32[]{:S(2)}) collective-permute-start(f16[256,256]{1,0:T(8,128)(2,1)S(1)} %add_convert_fusion.4), channel_id=1, source_target_pairs={{0,2},{1,5},{2,0},{3,7},{4,6},{5,1},{6,4},{7,3},{8,10},{9,13},{10,... | collective-permute-start | bytes 393224 | tf_op jit(solution)/shard_map/ppermute | solution.py:248
  40.9 5.3 %collective-permute-start.11 = (f16[256,256]{1,0:T(8,128)(2,1)S(1)}, f16[256,256]{1,0:T(8,128)(2,1)S(1)}, u32[]{:S(2)}, u32[]{:S(2)}) collective-permute-start(f16[256,256]{1,0:T(8,128)(2,1)S(1)} %add_convert_fusion.4), channel_id=1, source_target_pairs={{0,4},{1,3},{2,6},{3,1},{4,0},{5,7},{6,2},{7,5},{8,12},{9,11},{10,... | collective-permute-start | bytes 393224 | tf_op jit(solution)/shard_map/ppermute | solution.py:248
  43.5 3.2 %copy-start = (f32[1024,512]{1,0:T(8,128)S(1)}, f32[1024,512]{1,0:T(8,128)}, u32[]{:S(2)}) copy-start(f32[1024,512]{1,0:T(8,128)} %vector_ref.1) | copy-start | bytes 6291460
  46.7 1.6 %copy-start.1 = (f32[1024,512]{1,0:T(8,128)S(1)}, f32[1024,512]{1,0:T(8,128)}, u32[]{:S(2)}) copy-start(f32[1024,512]{1,0:T(8,128)} %diag_ref.3) | copy-start | bytes 6291460
  47.0 1.2 %collective-permute-start.14 = (f32[8,128]{1,0:T(8,128)S(1)}, f32[8,128]{1,0:T(8,128)S(1)}, u32[]{:S(2)}, u32[]{:S(2)}) collective-permute-start(f32[8,128]{1,0:T(8,128)S(1)} %correlate.2.corr_a), channel_id=1, source_target_pairs={{0,1},{1,0},{2,3},{3,2},{4,5},{5,4},{6,7},{7,6},{8,9},{9,8},{10,11... | collective-permute-start | bytes 12296 | tf_op jit(solution)/shard_map/ppermute | solution.py:251
  49.3 2.7 %collective-permute-start.16 = (bf16[1024,512]{1,0:T(8,128)(2,1)S(1)}, bf16[1024,512]{1,0:T(8,128)(2,1)S(1)}, u32[]{:S(2)}, u32[]{:S(2)}) collective-permute-start(bf16[1024,512]{1,0:T(8,128)(2,1)S(1)} %get-tuple-element.61.own_ref), channel_id=1, source_target_pairs={{0,1},{1,0},{2,3},{3,2},{4,5},{5,4},{6,7},{7,6},{8,9},{9,8},{10,11... | collective-permute-start | bytes 3145736 | tf_op jit(solution)/shard_map/ppermute | solution.py:251
  49.5 2.5 %collective-permute-start.15 = (f32[8,128]{1,0:T(8,128)S(1)}, f32[8,128]{1,0:T(8,128)S(1)}, u32[]{:S(2)}, u32[]{:S(2)}) collective-permute-start(f32[8,128]{1,0:T(8,128)S(1)} %get-tuple-element.58.a_ref.weight_a), channel_id=1, source_target_pairs={{0,1},{1,0},{2,3},{3,2},{4,5},{5,4},{6,7},{7,6},{8,9},{9,8},{10,11... | collective-permute-start | bytes 12296 | tf_op jit(solution)/shard_map/ppermute | solution.py:251
  53.9 6.4 %collective-permute-start.17 = (f16[512,256]{1,0:T(8,128)(2,1)S(1)}, f16[512,256]{1,0:T(8,128)(2,1)S(1)}, u32[]{:S(2)}, u32[]{:S(2)}) collective-permute-start(f16[512,256]{1,0:T(8,128)(2,1)S(1)} %convert_element_type.134), channel_id=1, source_target_pairs={{0,2},{1,5},{2,0},{3,7},{4,6},{5,1},{6,4},{7,3},{8,10},{9,13},{10,... | collective-permute-start | bytes 786440 | tf_op jit(solution)/shard_map/ppermute | solution.py:248
  56.5 7.3 %collective-permute-start.23 = (f16[512,256]{1,0:T(8,128)(2,1)S(1)}, f16[512,256]{1,0:T(8,128)(2,1)S(1)}, u32[]{:S(2)}, u32[]{:S(2)}) collective-permute-start(f16[512,256]{1,0:T(8,128)(2,1)S(1)} %convert_element_type.143), channel_id=1, source_target_pairs={{0,2},{1,5},{2,0},{3,7},{4,6},{5,1},{6,4},{7,3},{8,10},{9,13},{10,... | collective-permute-start | bytes 786440 | tf_op jit(solution)/shard_map/ppermute | solution.py:248
  60.5 5.0 %collective-permute-start.18 = (f16[256,256]{1,0:T(8,128)(2,1)S(1)}, f16[256,256]{1,0:T(8,128)(2,1)S(1)}, u32[]{:S(2)}, u32[]{:S(2)}) collective-permute-start(f16[256,256]{1,0:T(8,128)(2,1)S(1)} %dynamic-slice_convert_fusion.1), channel_id=1, source_target_pairs={{0,4},{1,3},{2,6},{3,1},{4,0},{5,7},{6,2},{7,5},{8,12},{9,11},{10,... | collective-permute-start | bytes 393224 | tf_op jit(solution)/shard_map/ppermute | solution.py:248
  63.9 6.6 %collective-permute-start.24 = (f16[256,256]{1,0:T(8,128)(2,1)S(1)}, f16[256,256]{1,0:T(8,128)(2,1)S(1)}, u32[]{:S(2)}, u32[]{:S(2)}) collective-permute-start(f16[256,256]{1,0:T(8,128)(2,1)S(1)} %dynamic-slice_convert_fusion), channel_id=1, source_target_pairs={{0,4},{1,3},{2,6},{3,1},{4,0},{5,7},{6,2},{7,5},{8,12},{9,11},{10,... | collective-permute-start | bytes 393224 | tf_op jit(solution)/shard_map/ppermute | solution.py:248
  65.6 12.6 %collective-permute-start.19 = (f16[256,256]{1,0:T(8,128)(2,1)S(1)}, f16[256,256]{1,0:T(8,128)(2,1)S(1)}, u32[]{:S(2)}, u32[]{:S(2)}) collective-permute-start(f16[256,256]{1,0:T(8,128)(2,1)S(1)} %add_convert_fusion.3), channel_id=1, source_target_pairs={{0,8},{1,9},{2,10},{3,11},{4,12},{5,13},{6,14},{7,15},{8,0},{9,1},... | collective-permute-start | bytes 393224 | tf_op jit(solution)/shard_map/ppermute | solution.py:248
  70.6 11.2 %collective-permute-start.25 = (f16[256,256]{1,0:T(8,128)(2,1)S(1)}, f16[256,256]{1,0:T(8,128)(2,1)S(1)}, u32[]{:S(2)}, u32[]{:S(2)}) collective-permute-start(f16[256,256]{1,0:T(8,128)(2,1)S(1)} %add_convert_fusion.1), channel_id=1, source_target_pairs={{0,8},{1,9},{2,10},{3,11},{4,12},{5,13},{6,14},{7,15},{8,0},{9,1},... | collective-permute-start | bytes 393224 | tf_op jit(solution)/shard_map/ppermute | solution.py:248
  78.2 7.4 %collective-permute-start.22 = (f16[256,256]{1,0:T(8,128)(2,1)S(1)}, f16[256,256]{1,0:T(8,128)(2,1)S(1)}, u32[]{:S(2)}, u32[]{:S(2)}) collective-permute-start(f16[256,256]{1,0:T(8,128)(2,1)S(1)} %add_convert_fusion.2), channel_id=1, source_target_pairs={{0,6},{1,7},{2,4},{3,5},{4,2},{5,3},{6,0},{7,1},{8,14},{9,15},{10,... | collective-permute-start | bytes 393224 | tf_op jit(solution)/shard_map/ppermute | solution.py:278
  78.3 9.1 %collective-permute-start.21 = (f16[256,256]{1,0:T(8,128)(2,1)S(1)}, f16[256,256]{1,0:T(8,128)(2,1)S(1)}, u32[]{:S(2)}, u32[]{:S(2)}) collective-permute-start(f16[256,256]{1,0:T(8,128)(2,1)S(1)} %add_convert_fusion.2), channel_id=1, source_target_pairs={{0,2},{1,5},{2,0},{3,7},{4,6},{5,1},{6,4},{7,3},{8,10},{9,13},{10,... | collective-permute-start | bytes 393224 | tf_op jit(solution)/shard_map/ppermute | solution.py:248
  79.4 7.9 %collective-permute-start.20 = (f16[256,256]{1,0:T(8,128)(2,1)S(1)}, f16[256,256]{1,0:T(8,128)(2,1)S(1)}, u32[]{:S(2)}, u32[]{:S(2)}) collective-permute-start(f16[256,256]{1,0:T(8,128)(2,1)S(1)} %add_convert_fusion.2), channel_id=1, source_target_pairs={{0,4},{1,3},{2,6},{3,1},{4,0},{5,7},{6,2},{7,5},{8,12},{9,11},{10,... | collective-permute-start | bytes 393224 | tf_op jit(solution)/shard_map/ppermute | solution.py:248
  81.8 7.2 %collective-permute-start.28 = (f16[256,256]{1,0:T(8,128)(2,1)S(1)}, f16[256,256]{1,0:T(8,128)(2,1)S(1)}, u32[]{:S(2)}, u32[]{:S(2)}) collective-permute-start(f16[256,256]{1,0:T(8,128)(2,1)S(1)} %add_convert_fusion), channel_id=1, source_target_pairs={{0,6},{1,7},{2,4},{3,5},{4,2},{5,3},{6,0},{7,1},{8,14},{9,15},{10,... | collective-permute-start | bytes 393224 | tf_op jit(solution)/shard_map/ppermute | solution.py:278
  82.4 7.9 %collective-permute-start.27 = (f16[256,256]{1,0:T(8,128)(2,1)S(1)}, f16[256,256]{1,0:T(8,128)(2,1)S(1)}, u32[]{:S(2)}, u32[]{:S(2)}) collective-permute-start(f16[256,256]{1,0:T(8,128)(2,1)S(1)} %add_convert_fusion), channel_id=1, source_target_pairs={{0,2},{1,5},{2,0},{3,7},{4,6},{5,1},{6,4},{7,3},{8,10},{9,13},{10,... | collective-permute-start | bytes 393224 | tf_op jit(solution)/shard_map/ppermute | solution.py:248
  85.5 5.0 %collective-permute-start.26 = (f16[256,256]{1,0:T(8,128)(2,1)S(1)}, f16[256,256]{1,0:T(8,128)(2,1)S(1)}, u32[]{:S(2)}, u32[]{:S(2)}) collective-permute-start(f16[256,256]{1,0:T(8,128)(2,1)S(1)} %add_convert_fusion), channel_id=1, source_target_pairs={{0,4},{1,3},{2,6},{3,1},{4,0},{5,7},{6,2},{7,5},{8,12},{9,11},{10,... | collective-permute-start | bytes 393224 | tf_op jit(solution)/shard_map/ppermute | solution.py:248
  91.3 1.2 %collective-permute-start.29 = (f32[8,128]{1,0:T(8,128)S(1)}, f32[8,128]{1,0:T(8,128)S(1)}, u32[]{:S(2)}, u32[]{:S(2)}) collective-permute-start(f32[8,128]{1,0:T(8,128)S(1)} %correlate.3.corr_a), channel_id=1, source_target_pairs={{0,1},{1,0},{2,3},{3,2},{4,5},{5,4},{6,7},{7,6},{8,9},{9,8},{10,11... | collective-permute-start | bytes 12296 | tf_op jit(solution)/shard_map/ppermute | solution.py:251
  93.6 1.2 %collective-permute-start.30 = (f32[8,128]{1,0:T(8,128)S(1)}, f32[8,128]{1,0:T(8,128)S(1)}, u32[]{:S(2)}, u32[]{:S(2)}) collective-permute-start(f32[8,128]{1,0:T(8,128)S(1)} %get-tuple-element.69.weight_a), channel_id=1, source_target_pairs={{0,1},{1,0},{2,3},{3,2},{4,5},{5,4},{6,7},{7,6},{8,9},{9,8},{10,11... | collective-permute-start | bytes 12296 | tf_op jit(solution)/shard_map/ppermute | solution.py:251

commit v7 on v6

--- a/solution.py
+++ b/solution.py
@@ -51,7 +51,7 @@
 
 def open_vector(coef):
     rows, cols = coef.shape
-    parts = 4
+    parts = 8
     step = rows // parts
 
     def kernel(coef_ref, wave_ref, weight_ref, buf, sems):
@@ -82,26 +82,19 @@
     return 1 - bit
 
 
-def operators(left, right, mask, blocks, sent):
+def operators(left, mask, blocks, sent):
     pairs, width, _ = left.shape
     half, inside = width // 2, width // blocks
     strips = half // inside
 
-    def kernel(mask_ref, left_ref, *refs):
-        if sent:
-            right_ref, out_ref, held_ref, buf, sems, right_sems = refs
-        else:
-            out_ref, buf, sems = refs
+    def kernel(mask_ref, left_ref, out_ref, buf, sems):
         h = first_half() if sent else 1 - first_half()
         order = [(k, i) for k in range(pairs) for i in range(strips)]
         copies = []
         for n, (k, i) in enumerate(order):
             copies.append(pltpu.make_async_copy(
                 left_ref.at[k, pl.ds(pl.multiple_of(h * half + i * inside, inside), inside)], buf.at[n], sems.at[n]))
-        rights = [pltpu.make_async_copy(right_ref.at[k], held_ref.at[k], right_sems.at[k])
-                  for k in range(pairs)] if sent else []
-        for copy in copies + rights:
-            copy.start()
+            copies[-1].start()
         for n, (k, i) in enumerate(order):
             copies[n].wait()
             for j in range(blocks):
@@ -109,17 +102,11 @@
                 block = buf[n, :, j * inside:(j + 1) * inside]
                 out_ref[i * inside:(i + 1) * inside, k * width + j * inside:k * width + (j + 1) * inside] = (
                     jnp.where(keep != 0, block, jnp.zeros_like(block)))
-        for copy in rights:
-            copy.wait()
 
     count = pairs * strips
-    out, args = SDS((half, pairs * width), BF16), (mask, in_hbm(left))
-    scratch = [pltpu.VMEM((count, inside, width), BF16), pltpu.SemaphoreType.DMA((count,))]
-    if sent:
-        return call(kernel, "sent_operators", (out, SDS(right.shape, BF16)), (VMEM, VMEM), [SMEM, ANY, ANY],
-                    args + (in_hbm(right),), left.size, 4 * left.size,
-                    scratch + [pltpu.SemaphoreType.DMA((pairs,))], mib=12)
-    return call(kernel, "kept_operators", out, VMEM, [SMEM, ANY], args, left.size, 2 * left.size, scratch, mib=12)
+    return call(kernel, "sent_operators" if sent else "kept_operators", SDS((half, pairs * width), BF16), VMEM,
+                [SMEM, ANY], (mask, in_hbm(left)), left.size, 2 * left.size,
+                [pltpu.VMEM((count, inside, width), BF16), pltpu.SemaphoreType.DMA((count,))], mib=12)
 
 
 def product(out_ref, scale, left_ref, right_ref, parts):
@@ -211,7 +198,7 @@
 
 def normalise(cells, vector, weights):
     rows, cols = vector.shape
-    parts = 4
+    parts = 8
     step = rows // parts
 
     def kernel(weight_a, weight_b, vector_ref, out_ref, buf, sems):
@@ -274,8 +261,8 @@
         return keep.astype(F16)
 
     def gathered(piece):
+        p3 = lax.ppermute(piece, BOTH, [(o * cols + c, (o ^ 3) * cols + c) for o in range(ops) for c in range(cols)])
         p1, p2 = swap(piece, 1), swap(piece, 0)
-        p3 = lax.ppermute(piece, BOTH, [(o * cols + c, (o ^ 3) * cols + c) for o in range(ops) for c in range(cols)])
         near0, near1 = jnp.where(low_near, piece, p1), jnp.where(low_near, p1, piece)
         far0, far1 = jnp.where(low_near, p2, p3), jnp.where(low_near, p3, p2)
         return jnp.concatenate([
@@ -285,7 +272,7 @@
     vector = wave_coef
     own, weight = open_vector(wave_coef)
     mask = block_mask.reshape(-1)
-    sent, right = operators(left, right, mask, blocks, True)
+    sent = operators(left, mask, blocks, True)
     for step in range(STEPS):
         other = across(own)
         weights = (weight, across(weight))
@@ -297,7 +284,7 @@
             own, other = lax.optimization_barrier((own, other, inner))[:2]
         inners[0], mask = lax.optimization_barrier((inners[0], mask, inners[-1]))[:2]
         if step == 0:
-            kept = operators(left, right, mask, blocks, False)
+            kept = operators(left, mask, blocks, False)
         sigmas = []
         for c in range(CHUNKS):
             keep = kept_half(reach, weights, inners[c], kept)

time: 96.6 us -> 96.1 us (level)
  transfers between devices with their start and end apart: 31 -> 31, of which waited for: 23 -> 23; matrix products, arithmetic and copies ran while one was open for 2% -> 1% of each run, Pallas kernels for 12% -> 12%
where the time goes in v7:
time: 96.1 us; the launch traced here: 95.9 us
  waiting for transfers between devices  41.7 us (43%)
  starting transfers between devices  30.5 us (32%)
  Pallas kernels  20.9 us (22%)
  other arithmetic  2.11 us (2%)
    ppermute x20, waiting for transfers between devices, swap(): return lax.ppermute(x, BOTH, pairing)  29.1 us
    ppermute x20, starting transfers between devices, swap(): return lax.ppermute(x, BOTH, pairing)  27.1 us
    pallas_call x16, Pallas kernels, call(): pl.pallas_call(kernel, out_shape=outs, in_specs=in_specs, out_specs=out_s...  20.9 us
    ppermute x4, waiting for transfers between devices, gathered(): lax.ppermute(piece, BOTH, [(o * cols + c, (o ^ 3) * cols + c) for o in ra...  7.18 us
    ppermute x7, waiting for transfers between devices, across(): return lax.ppermute(x, 'col', [(c, c ^ 1) for c in range(cols)])  5.47 us
  transfers between devices with their start and end apart: 31, of which 23 were waited for; matrix products, arithmetic and copies ran while one was open for 1% of the time, Pallas kernels for 12%

profile of v7, /device:TPU:0, one launch (start us, length us, event | category | flops | bytes accessed | tf_op | source)
XLA Modules:
  0.0 95.9 jit_solution(3839119553306208382)
XLA Ops:
  0.0 1.7 %open_vector.1 = (bf16[1024,512]{1,0:T(8,128)(2,1)S(1)}, f32[8,128]{1,0:T(8,128)S(1)}) custom-call(f32[1024,512]{1,0:T(8,128)} %vector_ref.1), custom_call_target="tpu_custom_call" | custom-call | flops 1572864 | bytes 4194304 | tf_op jit(solution)/shard_map/open_vector/pallas_call | solution.py:30
  1.7 0.5 collective-permute-start.1
  2.4 2.3 %sent_operators.1.masked_ref = bf16[512,2048]{1,0:T(8,128)(2,1)S(1)} custom-call(s32[128]{0:T(128)S(1)} %reshape.3.mask_ref, bf16[2,1024,1024]{2,1,0:T(8,128)(2,1)} %left_ref.3), custom_call_target="tpu_custom_call" | custom-call | flops 2097152 | bytes 4194304 | tf_op jit(solution)/shard_map/sent_operators/pallas_call | solution.py:30
  4.7 1.8 %sent_half_0.2 = (bf16[2048,256]{1,0:T(8,128)(2,1)S(1)}, f32[512,256]{1,0:T(8,128)S(1)}) custom-call(f32[8,128]{1,0:T(8,128)S(1)} %get-tuple-element.39.a_ref.weight_a, f32[8,128]{1,0:T(8,128)S(1)} %collective-permute-done.b_ref.weight_b, bf16[1024,512]{1,0:T(8,128)(2,1)S(1)} %get-tuple-element.42.own_ref, ...), custom_call_target="tpu_custom_call" | custom-call | flops 1610612736 | bytes 1048576 | tf_op jit(solution)/shard_map/sent_half_0/pallas_call | solution.py:30
  6.6 3.0 %collective-permute-start.2 = (f16[512,256]{1,0:T(8,128)(2,1)S(1)}, f16[512,256]{1,0:T(8,128)(2,1)S(1)}, u32[]{:S(2)}, u32[]{:S(2)}) collective-permute-start(f16[512,256]{1,0:T(8,128)(2,1)S(1)} %convert_element_type.116), channel_id=1, source_target_pairs={{0,2},{1,5},{2,0},{3,7},{4,6},{5,1},{6,4},{7,3},{8,10},{9,13},{10,... | collective-permute-start | bytes 786440 | tf_op jit(solution)/shard_map/ppermute | solution.py:235
  9.6 1.8 %sent_half_1.2 = (bf16[2048,256]{1,0:T(8,128)(2,1)S(1)}, f32[512,256]{1,0:T(8,128)S(1)}) custom-call(f32[8,128]{1,0:T(8,128)S(1)} %get-tuple-element.39.a_ref.weight_a, f32[8,128]{1,0:T(8,128)S(1)} %collective-permute-done.b_ref.weight_b, bf16[1024,512]{1,0:T(8,128)(2,1)S(1)} %get-tuple-element.42.own_ref, ...), custom_call_target="tpu_custom_call" | custom-call | flops 1610612736 | bytes 1048576 | tf_op jit(solution)/shard_map/sent_half_1/pallas_call | solution.py:30
  11.6 2.2 %kept_operators.1.masked_ref = bf16[512,2048]{1,0:T(8,128)(2,1)S(1)} custom-call(s32[128]{0:T(128)S(1)} %reshape.3.mask_ref, bf16[2,1024,1024]{2,1,0:T(8,128)(2,1)} %left_ref.3), custom_call_target="tpu_custom_call" | custom-call | flops 2097152 | bytes 4194304 | tf_op jit(solution)/shard_map/kept_operators/pallas_call | solution.py:30
  13.8 0.7 kept_half.4
  14.7 2.1 %collective-permute-start.3 = (f16[256,256]{1,0:T(8,128)(2,1)S(1)}, f16[256,256]{1,0:T(8,128)(2,1)S(1)}, u32[]{:S(2)}, u32[]{:S(2)}) collective-permute-start(f16[256,256]{1,0:T(8,128)(2,1)S(1)} %dynamic-slice_convert_fusion.3), channel_id=1, source_target_pairs={{0,4},{1,3},{2,6},{3,1},{4,0},{5,7},{6,2},{7,5},{8,12},{9,11},{10,... | collective-permute-start | bytes 393224 | tf_op jit(solution)/shard_map/ppermute | solution.py:235
  16.8 0.7 kept_half.5
  17.5 1.1 %collective-permute-done.8 = f16[512,256]{1,0:T(8,128)(2,1)S(1)} collective-permute-done((f16[512,256]{1,0:T(8,128)(2,1)S(1)}, f16[512,256]{1,0:T(8,128)(2,1)S(1)}, u32[]{:S(2)}, u32[]{:S(2)}) %collective-permute-start.8) | collective-permute-done | bytes 262176 | tf_op jit(solution)/shard_map/ppermute | solution.py:235
  18.8 1.5 %collective-permute-start.9 = (f16[256,256]{1,0:T(8,128)(2,1)S(1)}, f16[256,256]{1,0:T(8,128)(2,1)S(1)}, u32[]{:S(2)}, u32[]{:S(2)}) collective-permute-start(f16[256,256]{1,0:T(8,128)(2,1)S(1)} %dynamic-slice_convert_fusion.2), channel_id=1, source_target_pairs={{0,4},{1,3},{2,6},{3,1},{4,0},{5,7},{6,2},{7,5},{8,12},{9,11},{10,... | collective-permute-start | bytes 393224 | tf_op jit(solution)/shard_map/ppermute | solution.py:235
  20.3 2.7 %collective-permute-start.4 = (f16[256,256]{1,0:T(8,128)(2,1)S(1)}, f16[256,256]{1,0:T(8,128)(2,1)S(1)}, u32[]{:S(2)}, u32[]{:S(2)}) collective-permute-start(f16[256,256]{1,0:T(8,128)(2,1)S(1)} %add_convert_fusion.7), channel_id=1, source_target_pairs={{0,8},{1,9},{2,10},{3,11},{4,12},{5,13},{6,14},{7,15},{8,0},{9,1},... | collective-permute-start | bytes 393224 | tf_op jit(solution)/shard_map/ppermute | solution.py:235
  23.0 2.3 %collective-permute-done.9 = f16[256,256]{1,0:T(8,128)(2,1)S(1)} collective-permute-done((f16[256,256]{1,0:T(8,128)(2,1)S(1)}, f16[256,256]{1,0:T(8,128)(2,1)S(1)}, u32[]{:S(2)}, u32[]{:S(2)}) %collective-permute-start.9) | collective-permute-done | bytes 131104 | tf_op jit(solution)/shard_map/ppermute | solution.py:235
  25.3 2.5 %collective-permute-start.10 = (f16[256,256]{1,0:T(8,128)(2,1)S(1)}, f16[256,256]{1,0:T(8,128)(2,1)S(1)}, u32[]{:S(2)}, u32[]{:S(2)}) collective-permute-start(f16[256,256]{1,0:T(8,128)(2,1)S(1)} %add_convert_fusion.5), channel_id=1, source_target_pairs={{0,8},{1,9},{2,10},{3,11},{4,12},{5,13},{6,14},{7,15},{8,0},{9,1},... | collective-permute-start | bytes 393224 | tf_op jit(solution)/shard_map/ppermute | solution.py:235
  27.8 5.1 %collective-permute-done.4 = f16[256,256]{1,0:T(8,128)(2,1)S(1)} collective-permute-done((f16[256,256]{1,0:T(8,128)(2,1)S(1)}, f16[256,256]{1,0:T(8,128)(2,1)S(1)}, u32[]{:S(2)}, u32[]{:S(2)}) %collective-permute-start.4) | collective-permute-done | bytes 131104 | tf_op jit(solution)/shard_map/ppermute | solution.py:235
  32.9 0.6 collective-permute-start.7
  33.5 0.9 collective-permute-start.6
  34.4 2.1 %collective-permute-start.5 = (f16[256,256]{1,0:T(8,128)(2,1)S(1)}, f16[256,256]{1,0:T(8,128)(2,1)S(1)}, u32[]{:S(2)}, u32[]{:S(2)}) collective-permute-start(f16[256,256]{1,0:T(8,128)(2,1)S(1)} %add_convert_fusion.6), channel_id=1, source_target_pairs={{0,4},{1,3},{2,6},{3,1},{4,0},{5,7},{6,2},{7,5},{8,12},{9,11},{10,... | collective-permute-start | bytes 393224 | tf_op jit(solution)/shard_map/ppermute | solution.py:235
  36.5 0.6 collective-permute-start.13
  37.1 1.0 %collective-permute-start.12 = (f16[256,256]{1,0:T(8,128)(2,1)S(1)}, f16[256,256]{1,0:T(8,128)(2,1)S(1)}, u32[]{:S(2)}, u32[]{:S(2)}) collective-permute-start(f16[256,256]{1,0:T(8,128)(2,1)S(1)} %add_convert_fusion.4), channel_id=1, source_target_pairs={{0,2},{1,5},{2,0},{3,7},{4,6},{5,1},{6,4},{7,3},{8,10},{9,13},{10,... | collective-permute-start | bytes 393224 | tf_op jit(solution)/shard_map/ppermute | solution.py:235
  38.1 2.3 %collective-permute-done.7 = f16[256,256]{1,0:T(8,128)(2,1)S(1)} collective-permute-done((f16[256,256]{1,0:T(8,128)(2,1)S(1)}, f16[256,256]{1,0:T(8,128)(2,1)S(1)}, u32[]{:S(2)}, u32[]{:S(2)}) %collective-permute-start.7) | collective-permute-done | bytes 131104 | tf_op jit(solution)/shard_map/ppermute | solution.py:264
  40.4 2.2 %collective-permute-done.6 = f16[256,256]{1,0:T(8,128)(2,1)S(1)} collective-permute-done((f16[256,256]{1,0:T(8,128)(2,1)S(1)}, f16[256,256]{1,0:T(8,128)(2,1)S(1)}, u32[]{:S(2)}, u32[]{:S(2)}) %collective-permute-start.6) | collective-permute-done | bytes 131104 | tf_op jit(solution)/shard_map/ppermute | solution.py:235
  42.6 0.2 collective-permute-done.5
  42.9 1.3 %collective-permute-done.13 = f16[256,256]{1,0:T(8,128)(2,1)S(1)} collective-permute-done((f16[256,256]{1,0:T(8,128)(2,1)S(1)}, f16[256,256]{1,0:T(8,128)(2,1)S(1)}, u32[]{:S(2)}, u32[]{:S(2)}) %collective-permute-start.13) | collective-permute-done | bytes 131104 | tf_op jit(solution)/shard_map/ppermute | solution.py:264
  44.2 1.3 %collective-permute-done.12 = f16[256,256]{1,0:T(8,128)(2,1)S(1)} collective-permute-done((f16[256,256]{1,0:T(8,128)(2,1)S(1)}, f16[256,256]{1,0:T(8,128)(2,1)S(1)}, u32[]{:S(2)}, u32[]{:S(2)}) %collective-permute-start.12) | collective-permute-done | bytes 131104 | tf_op jit(solution)/shard_map/ppermute | solution.py:235
  45.5 0.2 collective-permute-done.11
  45.7 0.2 broadcast_select_fusion.27
  45.9 0.2 maximum_convert_fusion
  46.1 0.3 correlate.2.corr_a
  46.5 1.2 %collective-permute-done.14.corr_b = f32[8,128]{1,0:T(8,128)S(1)} collective-permute-done((f32[8,128]{1,0:T(8,128)S(1)}, f32[8,128]{1,0:T(8,128)S(1)}, u32[]{:S(2)}, u32[]{:S(2)}) %collective-permute-start.14) | collective-permute-done | bytes 4128 | tf_op jit(solution)/shard_map/ppermute | solution.py:238
  47.7 1.0 %correct.2 = (f32[1024,512]{1,0:T(8,128)S(1)}, f32[8,128]{1,0:T(8,128)S(1)}, bf16[1024,512]{1,0:T(8,128)(2,1)S(1)}) custom-call(f32[8,128]{1,0:T(8,128)S(1)} %correlate.2.corr_a, f32[8,128]{1,0:T(8,128)S(1)} %collective-permute-done.14.corr_b, f32[8,128]{1,0:T(8,128)S(1)} %get-tuple-element.39.a_ref.weight_a, ...), custom_call_target="tpu_custom_call" | custom-call | flops 6291456 | bytes 1048576 | tf_op jit(solution)/shard_map/correct/pallas_call | solution.py:30
  48.8 0.2 collective-permute-start.16
  48.9 0.4 collective-permute-start.15
  49.3 2.2 %collective-permute-done.15.b_ref.weight_b = f32[8,128]{1,0:T(8,128)S(1)} collective-permute-done((f32[8,128]{1,0:T(8,128)S(1)}, f32[8,128]{1,0:T(8,128)S(1)}, u32[]{:S(2)}, u32[]{:S(2)}) %collective-permute-start.15) | collective-permute-done | bytes 4128 | tf_op jit(solution)/shard_map/ppermute | solution.py:238
  51.5 1.8 %sent_half_0.3 = (bf16[2048,256]{1,0:T(8,128)(2,1)S(1)}, f32[512,256]{1,0:T(8,128)S(1)}) custom-call(f32[8,128]{1,0:T(8,128)S(1)} %get-tuple-element.54.a_ref.weight_a, f32[8,128]{1,0:T(8,128)S(1)} %collective-permute-done.15.b_ref.weight_b, bf16[1024,512]{1,0:T(8,128)(2,1)S(1)} %get-tuple-element.57.own_ref, ...), custom_call_target="tpu_custom_call" | custom-call | flops 1610612736 | bytes 1048576 | tf_op jit(solution)/shard_map/sent_half_0/pallas_call | solution.py:30
  53.4 0.8 collective-permute-start.17
  54.1 1.8 %sent_half_1.3 = (bf16[2048,256]{1,0:T(8,128)(2,1)S(1)}, f32[512,256]{1,0:T(8,128)S(1)}) custom-call(f32[8,128]{1,0:T(8,128)S(1)} %get-tuple-element.54.a_ref.weight_a, f32[8,128]{1,0:T(8,128)S(1)} %collective-permute-done.15.b_ref.weight_b, bf16[1024,512]{1,0:T(8,128)(2,1)S(1)} %get-tuple-element.57.own_ref, ...), custom_call_target="tpu_custom_call" | custom-call | flops 1610612736 | bytes 1048576 | tf_op jit(solution)/shard_map/sent_half_1/pallas_call | solution.py:30
  56.0 1.4 %collective-permute-start.23 = (f16[512,256]{1,0:T(8,128)(2,1)S(1)}, f16[512,256]{1,0:T(8,128)(2,1)S(1)}, u32[]{:S(2)}, u32[]{:S(2)}) collective-permute-start(f16[512,256]{1,0:T(8,128)(2,1)S(1)} %convert_element_type.143), channel_id=1, source_target_pairs={{0,2},{1,5},{2,0},{3,7},{4,6},{5,1},{6,4},{7,3},{8,10},{9,13},{10,... | collective-permute-start | bytes 786440 | tf_op jit(solution)/shard_map/ppermute | solution.py:235
  57.4 0.7 kept_half.6
  58.1 1.7 %collective-permute-done.17 = f16[512,256]{1,0:T(8,128)(2,1)S(1)} collective-permute-done((f16[512,256]{1,0:T(8,128)(2,1)S(1)}, f16[512,256]{1,0:T(8,128)(2,1)S(1)}, u32[]{:S(2)}, u32[]{:S(2)}) %collective-permute-start.17) | collective-permute-done | bytes 262176 | tf_op jit(solution)/shard_map/ppermute | solution.py:235
  60.1 0.9 kept_half.7
  61.0 2.3 %collective-permute-done.23 = f16[512,256]{1,0:T(8,128)(2,1)S(1)} collective-permute-done((f16[512,256]{1,0:T(8,128)(2,1)S(1)}, f16[512,256]{1,0:T(8,128)(2,1)S(1)}, u32[]{:S(2)}, u32[]{:S(2)}) %collective-permute-start.23) | collective-permute-done | bytes 262176 | tf_op jit(solution)/shard_map/ppermute | solution.py:235
  63.5 1.4 %collective-permute-done.18 = f16[256,256]{1,0:T(8,128)(2,1)S(1)} collective-permute-done((f16[256,256]{1,0:T(8,128)(2,1)S(1)}, f16[256,256]{1,0:T(8,128)(2,1)S(1)}, u32[]{:S(2)}, u32[]{:S(2)}) %collective-permute-start.18) | collective-permute-done | bytes 131104 | tf_op jit(solution)/shard_map/ppermute | solution.py:235
  65.0 2.6 %collective-permute-start.19 = (f16[256,256]{1,0:T(8,128)(2,1)S(1)}, f16[256,256]{1,0:T(8,128)(2,1)S(1)}, u32[]{:S(2)}, u32[]{:S(2)}) collective-permute-start(f16[256,256]{1,0:T(8,128)(2,1)S(1)} %add_convert_fusion.3), channel_id=1, source_target_pairs={{0,8},{1,9},{2,10},{3,11},{4,12},{5,13},{6,14},{7,15},{8,0},{9,1},... | collective-permute-start | bytes 393224 | tf_op jit(solution)/shard_map/ppermute | solution.py:235
  67.6 2.3 %collective-permute-done.24 = f16[256,256]{1,0:T(8,128)(2,1)S(1)} collective-permute-done((f16[256,256]{1,0:T(8,128)(2,1)S(1)}, f16[256,256]{1,0:T(8,128)(2,1)S(1)}, u32[]{:S(2)}, u32[]{:S(2)}) %collective-permute-start.24) | collective-permute-done | bytes 131104 | tf_op jit(solution)/shard_map/ppermute | solution.py:235
  70.0 1.9 %collective-permute-start.25 = (f16[256,256]{1,0:T(8,128)(2,1)S(1)}, f16[256,256]{1,0:T(8,128)(2,1)S(1)}, u32[]{:S(2)}, u32[]{:S(2)}) collective-permute-start(f16[256,256]{1,0:T(8,128)(2,1)S(1)} %add_convert_fusion.1), channel_id=1, source_target_pairs={{0,8},{1,9},{2,10},{3,11},{4,12},{5,13},{6,14},{7,15},{8,0},{9,1},... | collective-permute-start | bytes 393224 | tf_op jit(solution)/shard_map/ppermute | solution.py:235
  71.9 5.7 %collective-permute-done.19 = f16[256,256]{1,0:T(8,128)(2,1)S(1)} collective-permute-done((f16[256,256]{1,0:T(8,128)(2,1)S(1)}, f16[256,256]{1,0:T(8,128)(2,1)S(1)}, u32[]{:S(2)}, u32[]{:S(2)}) %collective-permute-start.19) | collective-permute-done | bytes 131104 | tf_op jit(solution)/shard_map/ppermute | solution.py:235
  77.7 1.2 %collective-permute-start.21 = (f16[256,256]{1,0:T(8,128)(2,1)S(1)}, f16[256,256]{1,0:T(8,128)(2,1)S(1)}, u32[]{:S(2)}, u32[]{:S(2)}) collective-permute-start(f16[256,256]{1,0:T(8,128)(2,1)S(1)} %add_convert_fusion.2), channel_id=1, source_target_pairs={{0,2},{1,5},{2,0},{3,7},{4,6},{5,1},{6,4},{7,3},{8,10},{9,13},{10,... | collective-permute-start | bytes 393224 | tf_op jit(solution)/shard_map/ppermute | solution.py:235
  78.9 2.3 %collective-permute-start.20 = (f16[256,256]{1,0:T(8,128)(2,1)S(1)}, f16[256,256]{1,0:T(8,128)(2,1)S(1)}, u32[]{:S(2)}, u32[]{:S(2)}) collective-permute-start(f16[256,256]{1,0:T(8,128)(2,1)S(1)} %add_convert_fusion.2), channel_id=1, source_target_pairs={{0,4},{1,3},{2,6},{3,1},{4,0},{5,7},{6,2},{7,5},{8,12},{9,11},{10,... | collective-permute-start | bytes 393224 | tf_op jit(solution)/shard_map/ppermute | solution.py:235
  81.2 0.6 collective-permute-start.28
  81.8 0.9 collective-permute-start.27
  82.8 2.2 %collective-permute-done.22 = f16[256,256]{1,0:T(8,128)(2,1)S(1)} collective-permute-done((f16[256,256]{1,0:T(8,128)(2,1)S(1)}, f16[256,256]{1,0:T(8,128)(2,1)S(1)}, u32[]{:S(2)}, u32[]{:S(2)}) %collective-permute-start.22) | collective-permute-done | bytes 131104 | tf_op jit(solution)/shard_map/ppermute | solution.py:264
  85.0 1.8 %collective-permute-done.21 = f16[256,256]{1,0:T(8,128)(2,1)S(1)} collective-permute-done((f16[256,256]{1,0:T(8,128)(2,1)S(1)}, f16[256,256]{1,0:T(8,128)(2,1)S(1)}, u32[]{:S(2)}, u32[]{:S(2)}) %collective-permute-start.21) | collective-permute-done | bytes 131104 | tf_op jit(solution)/shard_map/ppermute | solution.py:235
  87.1 1.4 %collective-permute-done.28 = f16[256,256]{1,0:T(8,128)(2,1)S(1)} collective-permute-done((f16[256,256]{1,0:T(8,128)(2,1)S(1)}, f16[256,256]{1,0:T(8,128)(2,1)S(1)}, u32[]{:S(2)}, u32[]{:S(2)}) %collective-permute-start.28) | collective-permute-done | bytes 131104 | tf_op jit(solution)/shard_map/ppermute | solution.py:264
  88.5 1.3 %collective-permute-done.27 = f16[256,256]{1,0:T(8,128)(2,1)S(1)} collective-permute-done((f16[256,256]{1,0:T(8,128)(2,1)S(1)}, f16[256,256]{1,0:T(8,128)(2,1)S(1)}, u32[]{:S(2)}, u32[]{:S(2)}) %collective-permute-start.27) | collective-permute-done | bytes 131104 | tf_op jit(solution)/shard_map/ppermute | solution.py:235
  89.7 0.2 collective-permute-done.26
  90.0 0.2 broadcast_select_fusion.19
  90.2 0.5 correlate.3.corr_a
  90.8 1.2 %collective-permute-done.29.corr_b = f32[8,128]{1,0:T(8,128)S(1)} collective-permute-done((f32[8,128]{1,0:T(8,128)S(1)}, f32[8,128]{1,0:T(8,128)S(1)}, u32[]{:S(2)}, u32[]{:S(2)}) %collective-permute-start.29) | collective-permute-done | bytes 4128 | tf_op jit(solution)/shard_map/ppermute | solution.py:238
  91.9 1.1 %correct.3 = (f32[1024,512]{1,0:T(8,128)S(1)}, f32[8,128]{1,0:T(8,128)S(1)}) custom-call(f32[8,128]{1,0:T(8,128)S(1)} %correlate.3.corr_a, f32[8,128]{1,0:T(8,128)S(1)} %collective-permute-done.29.corr_b, f32[8,128]{1,0:T(8,128)S(1)} %get-tuple-element.54.a_ref.weight_a, f32[8,128]{1,0:T(8,128)S(1)} %collective-permute-done.15.b_ref.weight_b, ...), custom_call_target="tpu_custom_call" | custom-call | flops 6291456 | bytes 1048576 | tf_op jit(solution)/shard_map/correct/pallas_call | solution.py:30
  93.0 0.2 collective-permute-start.30
  93.3 1.0 %collective-permute-done.30.weight_b = f32[8,128]{1,0:T(8,128)S(1)} collective-permute-done((f32[8,128]{1,0:T(8,128)S(1)}, f32[8,128]{1,0:T(8,128)S(1)}, u32[]{:S(2)}, u32[]{:S(2)}) %collective-permute-start.30) | collective-permute-done | bytes 4128 | tf_op jit(solution)/shard_map/ppermute | solution.py:238
  94.3 1.4 %normalise.1 = f32[1024,512]{1,0:T(8,128)} custom-call(f32[8,128]{1,0:T(8,128)S(1)} %get-tuple-element.65.weight_a, f32[8,128]{1,0:T(8,128)S(1)} %collective-permute-done.30.weight_b, f32[1024,512]{1,0:T(8,128)S(1)} %get-tuple-element.66.vector_ref), custom_call_target="tpu_custom_call" | custom-call | flops 524288 | bytes 4194304 | tf_op jit(solution)/shard_map/normalise/pallas_call | solution.py:30
  (50 shorter events, 2.4 us)
Async XLA Ops:
  0.0 2.3 %copy-start.3 = (s32[2,8,8]{2,1,0:T(8,128)S(1)}, s32[2,8,8]{2,1,0:T(8,128)}, u32[]{:S(2)}) copy-start(s32[2,8,8]{2,1,0:T(8,128)} %param.9) | copy-start | bytes 1540
  1.7 3.0 %collective-permute-start.1 = (bf16[1024,512]{1,0:T(8,128)(2,1)S(1)}, bf16[1024,512]{1,0:T(8,128)(2,1)S(1)}, u32[]{:S(2)}, u32[]{:S(2)}) collective-permute-start(bf16[1024,512]{1,0:T(8,128)(2,1)S(1)} %get-tuple-element.42.own_ref), channel_id=1, source_target_pairs={{0,1},{1,0},{2,3},{3,2},{4,5},{5,4},{6,7},{7,6},{8,9},{9,8},{10,11... | collective-permute-start | bytes 3145736 | tf_op jit(solution)/shard_map/ppermute | solution.py:238
  2.3 2.5 %collective-permute-start = (f32[8,128]{1,0:T(8,128)S(1)}, f32[8,128]{1,0:T(8,128)S(1)}, u32[]{:S(2)}, u32[]{:S(2)}) collective-permute-start(f32[8,128]{1,0:T(8,128)S(1)} %get-tuple-element.39.a_ref.weight_a), channel_id=1, source_target_pairs={{0,1},{1,0},{2,3},{3,2},{4,5},{5,4},{6,7},{7,6},{8,9},{9,8},{10,11... | collective-permute-start | bytes 12296 | tf_op jit(solution)/shard_map/ppermute | solution.py:238
  2.4 2.3 %copy-start = (bf16[2,1024,512]{2,1,0:T(8,128)(2,1)S(1)}, bf16[2,1024,512]{2,1,0:T(8,128)(2,1)}, u32[]{:S(2)}) copy-start(bf16[2,1024,512]{2,1,0:T(8,128)(2,1)} %right_ref.7) | copy-start | bytes 6291460
  6.6 7.9 %collective-permute-start.2 = (f16[512,256]{1,0:T(8,128)(2,1)S(1)}, f16[512,256]{1,0:T(8,128)(2,1)S(1)}, u32[]{:S(2)}, u32[]{:S(2)}) collective-permute-start(f16[512,256]{1,0:T(8,128)(2,1)S(1)} %convert_element_type.116), channel_id=1, source_target_pairs={{0,2},{1,5},{2,0},{3,7},{4,6},{5,1},{6,4},{7,3},{8,10},{9,13},{10,... | collective-permute-start | bytes 786440 | tf_op jit(solution)/shard_map/ppermute | solution.py:235
  11.5 7.1 %collective-permute-start.8 = (f16[512,256]{1,0:T(8,128)(2,1)S(1)}, f16[512,256]{1,0:T(8,128)(2,1)S(1)}, u32[]{:S(2)}, u32[]{:S(2)}) collective-permute-start(f16[512,256]{1,0:T(8,128)(2,1)S(1)} %convert_element_type.125), channel_id=1, source_target_pairs={{0,2},{1,5},{2,0},{3,7},{4,6},{5,1},{6,4},{7,3},{8,10},{9,13},{10,... | collective-permute-start | bytes 786440 | tf_op jit(solution)/shard_map/ppermute | solution.py:235
  14.7 5.6 %collective-permute-start.3 = (f16[256,256]{1,0:T(8,128)(2,1)S(1)}, f16[256,256]{1,0:T(8,128)(2,1)S(1)}, u32[]{:S(2)}, u32[]{:S(2)}) collective-permute-start(f16[256,256]{1,0:T(8,128)(2,1)S(1)} %dynamic-slice_convert_fusion.3), channel_id=1, source_target_pairs={{0,4},{1,3},{2,6},{3,1},{4,0},{5,7},{6,2},{7,5},{8,12},{9,11},{10,... | collective-permute-start | bytes 393224 | tf_op jit(solution)/shard_map/ppermute | solution.py:235
  18.8 6.5 %collective-permute-start.9 = (f16[256,256]{1,0:T(8,128)(2,1)S(1)}, f16[256,256]{1,0:T(8,128)(2,1)S(1)}, u32[]{:S(2)}, u32[]{:S(2)}) collective-permute-start(f16[256,256]{1,0:T(8,128)(2,1)S(1)} %dynamic-slice_convert_fusion.2), channel_id=1, source_target_pairs={{0,4},{1,3},{2,6},{3,1},{4,0},{5,7},{6,2},{7,5},{8,12},{9,11},{10,... | collective-permute-start | bytes 393224 | tf_op jit(solution)/shard_map/ppermute | solution.py:235
  20.3 12.6 %collective-permute-start.4 = (f16[256,256]{1,0:T(8,128)(2,1)S(1)}, f16[256,256]{1,0:T(8,128)(2,1)S(1)}, u32[]{:S(2)}, u32[]{:S(2)}) collective-permute-start(f16[256,256]{1,0:T(8,128)(2,1)S(1)} %add_convert_fusion.7), channel_id=1, source_target_pairs={{0,8},{1,9},{2,10},{3,11},{4,12},{5,13},{6,14},{7,15},{8,0},{9,1},... | collective-permute-start | bytes 393224 | tf_op jit(solution)/shard_map/ppermute | solution.py:235
  25.3 11.2 %collective-permute-start.10 = (f16[256,256]{1,0:T(8,128)(2,1)S(1)}, f16[256,256]{1,0:T(8,128)(2,1)S(1)}, u32[]{:S(2)}, u32[]{:S(2)}) collective-permute-start(f16[256,256]{1,0:T(8,128)(2,1)S(1)} %add_convert_fusion.5), channel_id=1, source_target_pairs={{0,8},{1,9},{2,10},{3,11},{4,12},{5,13},{6,14},{7,15},{8,0},{9,1},... | collective-permute-start | bytes 393224 | tf_op jit(solution)/shard_map/ppermute | solution.py:235
  32.9 7.4 %collective-permute-start.7 = (f16[256,256]{1,0:T(8,128)(2,1)S(1)}, f16[256,256]{1,0:T(8,128)(2,1)S(1)}, u32[]{:S(2)}, u32[]{:S(2)}) collective-permute-start(f16[256,256]{1,0:T(8,128)(2,1)S(1)} %add_convert_fusion.6), channel_id=1, source_target_pairs={{0,6},{1,7},{2,4},{3,5},{4,2},{5,3},{6,0},{7,1},{8,14},{9,15},{10,... | collective-permute-start | bytes 393224 | tf_op jit(solution)/shard_map/ppermute | solution.py:264
  33.5 9.1 %collective-permute-start.6 = (f16[256,256]{1,0:T(8,128)(2,1)S(1)}, f16[256,256]{1,0:T(8,128)(2,1)S(1)}, u32[]{:S(2)}, u32[]{:S(2)}) collective-permute-start(f16[256,256]{1,0:T(8,128)(2,1)S(1)} %add_convert_fusion.6), channel_id=1, source_target_pairs={{0,2},{1,5},{2,0},{3,7},{4,6},{5,1},{6,4},{7,3},{8,10},{9,13},{10,... | collective-permute-start | bytes 393224 | tf_op jit(solution)/shard_map/ppermute | solution.py:235
  34.4 8.4 %collective-permute-start.5 = (f16[256,256]{1,0:T(8,128)(2,1)S(1)}, f16[256,256]{1,0:T(8,128)(2,1)S(1)}, u32[]{:S(2)}, u32[]{:S(2)}) collective-permute-start(f16[256,256]{1,0:T(8,128)(2,1)S(1)} %add_convert_fusion.6), channel_id=1, source_target_pairs={{0,4},{1,3},{2,6},{3,1},{4,0},{5,7},{6,2},{7,5},{8,12},{9,11},{10,... | collective-permute-start | bytes 393224 | tf_op jit(solution)/shard_map/ppermute | solution.py:235
  36.5 7.7 %collective-permute-start.13 = (f16[256,256]{1,0:T(8,128)(2,1)S(1)}, f16[256,256]{1,0:T(8,128)(2,1)S(1)}, u32[]{:S(2)}, u32[]{:S(2)}) collective-permute-start(f16[256,256]{1,0:T(8,128)(2,1)S(1)} %add_convert_fusion.4), channel_id=1, source_target_pairs={{0,6},{1,7},{2,4},{3,5},{4,2},{5,3},{6,0},{7,1},{8,14},{9,15},{10,... | collective-permute-start | bytes 393224 | tf_op jit(solution)/shard_map/ppermute | solution.py:264
  37.1 8.4 %collective-permute-start.12 = (f16[256,256]{1,0:T(8,128)(2,1)S(1)}, f16[256,256]{1,0:T(8,128)(2,1)S(1)}, u32[]{:S(2)}, u32[]{:S(2)}) collective-permute-start(f16[256,256]{1,0:T(8,128)(2,1)S(1)} %add_convert_fusion.4), channel_id=1, source_target_pairs={{0,2},{1,5},{2,0},{3,7},{4,6},{5,1},{6,4},{7,3},{8,10},{9,13},{10,... | collective-permute-start | bytes 393224 | tf_op jit(solution)/shard_map/ppermute | solution.py:235
  40.4 5.3 %collective-permute-start.11 = (f16[256,256]{1,0:T(8,128)(2,1)S(1)}, f16[256,256]{1,0:T(8,128)(2,1)S(1)}, u32[]{:S(2)}, u32[]{:S(2)}) collective-permute-start(f16[256,256]{1,0:T(8,128)(2,1)S(1)} %add_convert_fusion.4), channel_id=1, source_target_pairs={{0,4},{1,3},{2,6},{3,1},{4,0},{5,7},{6,2},{7,5},{8,12},{9,11},{10,... | collective-permute-start | bytes 393224 | tf_op jit(solution)/shard_map/ppermute | solution.py:235
  42.9 3.2 %copy-start.1 = (f32[1024,512]{1,0:T(8,128)S(1)}, f32[1024,512]{1,0:T(8,128)}, u32[]{:S(2)}) copy-start(f32[1024,512]{1,0:T(8,128)} %vector_ref.1) | copy-start | bytes 6291460
  46.1 1.6 %copy-start.2 = (f32[1024,512]{1,0:T(8,128)S(1)}, f32[1024,512]{1,0:T(8,128)}, u32[]{:S(2)}) copy-start(f32[1024,512]{1,0:T(8,128)} %diag_ref.3) | copy-start | bytes 6291460
  46.4 1.2 %collective-permute-start.14 = (f32[8,128]{1,0:T(8,128)S(1)}, f32[8,128]{1,0:T(8,128)S(1)}, u32[]{:S(2)}, u32[]{:S(2)}) collective-permute-start(f32[8,128]{1,0:T(8,128)S(1)} %correlate.2.corr_a), channel_id=1, source_target_pairs={{0,1},{1,0},{2,3},{3,2},{4,5},{5,4},{6,7},{7,6},{8,9},{9,8},{10,11... | collective-permute-start | bytes 12296 | tf_op jit(solution)/shard_map/ppermute | solution.py:238
  48.8 2.7 %collective-permute-start.16 = (bf16[1024,512]{1,0:T(8,128)(2,1)S(1)}, bf16[1024,512]{1,0:T(8,128)(2,1)S(1)}, u32[]{:S(2)}, u32[]{:S(2)}) collective-permute-start(bf16[1024,512]{1,0:T(8,128)(2,1)S(1)} %get-tuple-element.57.own_ref), channel_id=1, source_target_pairs={{0,1},{1,0},{2,3},{3,2},{4,5},{5,4},{6,7},{7,6},{8,9},{9,8},{10,11... | collective-permute-start | bytes 3145736 | tf_op jit(solution)/shard_map/ppermute | solution.py:238
  48.9 2.5 %collective-permute-start.15 = (f32[8,128]{1,0:T(8,128)S(1)}, f32[8,128]{1,0:T(8,128)S(1)}, u32[]{:S(2)}, u32[]{:S(2)}) collective-permute-start(f32[8,128]{1,0:T(8,128)S(1)} %get-tuple-element.54.a_ref.weight_a), channel_id=1, source_target_pairs={{0,1},{1,0},{2,3},{3,2},{4,5},{5,4},{6,7},{7,6},{8,9},{9,8},{10,11... | collective-permute-start | bytes 12296 | tf_op jit(solution)/shard_map/ppermute | solution.py:238
  53.4 6.4 %collective-permute-start.17 = (f16[512,256]{1,0:T(8,128)(2,1)S(1)}, f16[512,256]{1,0:T(8,128)(2,1)S(1)}, u32[]{:S(2)}, u32[]{:S(2)}) collective-permute-start(f16[512,256]{1,0:T(8,128)(2,1)S(1)} %convert_element_type.134), channel_id=1, source_target_pairs={{0,2},{1,5},{2,0},{3,7},{4,6},{5,1},{6,4},{7,3},{8,10},{9,13},{10,... | collective-permute-start | bytes 786440 | tf_op jit(solution)/shard_map/ppermute | solution.py:235
  56.0 7.3 %collective-permute-start.23 = (f16[512,256]{1,0:T(8,128)(2,1)S(1)}, f16[512,256]{1,0:T(8,128)(2,1)S(1)}, u32[]{:S(2)}, u32[]{:S(2)}) collective-permute-start(f16[512,256]{1,0:T(8,128)(2,1)S(1)} %convert_element_type.143), channel_id=1, source_target_pairs={{0,2},{1,5},{2,0},{3,7},{4,6},{5,1},{6,4},{7,3},{8,10},{9,13},{10,... | collective-permute-start | bytes 786440 | tf_op jit(solution)/shard_map/ppermute | solution.py:235
  59.9 5.0 %collective-permute-start.18 = (f16[256,256]{1,0:T(8,128)(2,1)S(1)}, f16[256,256]{1,0:T(8,128)(2,1)S(1)}, u32[]{:S(2)}, u32[]{:S(2)}) collective-permute-start(f16[256,256]{1,0:T(8,128)(2,1)S(1)} %dynamic-slice_convert_fusion.1), channel_id=1, source_target_pairs={{0,4},{1,3},{2,6},{3,1},{4,0},{5,7},{6,2},{7,5},{8,12},{9,11},{10,... | collective-permute-start | bytes 393224 | tf_op jit(solution)/shard_map/ppermute | solution.py:235
  63.4 6.6 %collective-permute-start.24 = (f16[256,256]{1,0:T(8,128)(2,1)S(1)}, f16[256,256]{1,0:T(8,128)(2,1)S(1)}, u32[]{:S(2)}, u32[]{:S(2)}) collective-permute-start(f16[256,256]{1,0:T(8,128)(2,1)S(1)} %dynamic-slice_convert_fusion), channel_id=1, source_target_pairs={{0,4},{1,3},{2,6},{3,1},{4,0},{5,7},{6,2},{7,5},{8,12},{9,11},{10,... | collective-permute-start | bytes 393224 | tf_op jit(solution)/shard_map/ppermute | solution.py:235
  65.0 12.6 %collective-permute-start.19 = (f16[256,256]{1,0:T(8,128)(2,1)S(1)}, f16[256,256]{1,0:T(8,128)(2,1)S(1)}, u32[]{:S(2)}, u32[]{:S(2)}) collective-permute-start(f16[256,256]{1,0:T(8,128)(2,1)S(1)} %add_convert_fusion.3), channel_id=1, source_target_pairs={{0,8},{1,9},{2,10},{3,11},{4,12},{5,13},{6,14},{7,15},{8,0},{9,1},... | collective-permute-start | bytes 393224 | tf_op jit(solution)/shard_map/ppermute | solution.py:235
  70.0 11.2 %collective-permute-start.25 = (f16[256,256]{1,0:T(8,128)(2,1)S(1)}, f16[256,256]{1,0:T(8,128)(2,1)S(1)}, u32[]{:S(2)}, u32[]{:S(2)}) collective-permute-start(f16[256,256]{1,0:T(8,128)(2,1)S(1)} %add_convert_fusion.1), channel_id=1, source_target_pairs={{0,8},{1,9},{2,10},{3,11},{4,12},{5,13},{6,14},{7,15},{8,0},{9,1},... | collective-permute-start | bytes 393224 | tf_op jit(solution)/shard_map/ppermute | solution.py:235
  77.6 7.4 %collective-permute-start.22 = (f16[256,256]{1,0:T(8,128)(2,1)S(1)}, f16[256,256]{1,0:T(8,128)(2,1)S(1)}, u32[]{:S(2)}, u32[]{:S(2)}) collective-permute-start(f16[256,256]{1,0:T(8,128)(2,1)S(1)} %add_convert_fusion.2), channel_id=1, source_target_pairs={{0,6},{1,7},{2,4},{3,5},{4,2},{5,3},{6,0},{7,1},{8,14},{9,15},{10,... | collective-permute-start | bytes 393224 | tf_op jit(solution)/shard_map/ppermute | solution.py:264
  77.7 9.1 %collective-permute-start.21 = (f16[256,256]{1,0:T(8,128)(2,1)S(1)}, f16[256,256]{1,0:T(8,128)(2,1)S(1)}, u32[]{:S(2)}, u32[]{:S(2)}) collective-permute-start(f16[256,256]{1,0:T(8,128)(2,1)S(1)} %add_convert_fusion.2), channel_id=1, source_target_pairs={{0,2},{1,5},{2,0},{3,7},{4,6},{5,1},{6,4},{7,3},{8,10},{9,13},{10,... | collective-permute-start | bytes 393224 | tf_op jit(solution)/shard_map/ppermute | solution.py:235
  78.9 7.9 %collective-permute-start.20 = (f16[256,256]{1,0:T(8,128)(2,1)S(1)}, f16[256,256]{1,0:T(8,128)(2,1)S(1)}, u32[]{:S(2)}, u32[]{:S(2)}) collective-permute-start(f16[256,256]{1,0:T(8,128)(2,1)S(1)} %add_convert_fusion.2), channel_id=1, source_target_pairs={{0,4},{1,3},{2,6},{3,1},{4,0},{5,7},{6,2},{7,5},{8,12},{9,11},{10,... | collective-permute-start | bytes 393224 | tf_op jit(solution)/shard_map/ppermute | solution.py:235
  81.2 7.2 %collective-permute-start.28 = (f16[256,256]{1,0:T(8,128)(2,1)S(1)}, f16[256,256]{1,0:T(8,128)(2,1)S(1)}, u32[]{:S(2)}, u32[]{:S(2)}) collective-permute-start(f16[256,256]{1,0:T(8,128)(2,1)S(1)} %add_convert_fusion), channel_id=1, source_target_pairs={{0,6},{1,7},{2,4},{3,5},{4,2},{5,3},{6,0},{7,1},{8,14},{9,15},{10,... | collective-permute-start | bytes 393224 | tf_op jit(solution)/shard_map/ppermute | solution.py:264
  81.8 7.9 %collective-permute-start.27 = (f16[256,256]{1,0:T(8,128)(2,1)S(1)}, f16[256,256]{1,0:T(8,128)(2,1)S(1)}, u32[]{:S(2)}, u32[]{:S(2)}) collective-permute-start(f16[256,256]{1,0:T(8,128)(2,1)S(1)} %add_convert_fusion), channel_id=1, source_target_pairs={{0,2},{1,5},{2,0},{3,7},{4,6},{5,1},{6,4},{7,3},{8,10},{9,13},{10,... | collective-permute-start | bytes 393224 | tf_op jit(solution)/shard_map/ppermute | solution.py:235
  85.0 5.0 %collective-permute-start.26 = (f16[256,256]{1,0:T(8,128)(2,1)S(1)}, f16[256,256]{1,0:T(8,128)(2,1)S(1)}, u32[]{:S(2)}, u32[]{:S(2)}) collective-permute-start(f16[256,256]{1,0:T(8,128)(2,1)S(1)} %add_convert_fusion), channel_id=1, source_target_pairs={{0,4},{1,3},{2,6},{3,1},{4,0},{5,7},{6,2},{7,5},{8,12},{9,11},{10,... | collective-permute-start | bytes 393224 | tf_op jit(solution)/shard_map/ppermute | solution.py:235
  90.7 1.2 %collective-permute-start.29 = (f32[8,128]{1,0:T(8,128)S(1)}, f32[8,128]{1,0:T(8,128)S(1)}, u32[]{:S(2)}, u32[]{:S(2)}) collective-permute-start(f32[8,128]{1,0:T(8,128)S(1)} %correlate.3.corr_a), channel_id=1, source_target_pairs={{0,1},{1,0},{2,3},{3,2},{4,5},{5,4},{6,7},{7,6},{8,9},{9,8},{10,11... | collective-permute-start | bytes 12296 | tf_op jit(solution)/shard_map/ppermute | solution.py:238
  93.0 1.2 %collective-permute-start.30 = (f32[8,128]{1,0:T(8,128)S(1)}, f32[8,128]{1,0:T(8,128)S(1)}, u32[]{:S(2)}, u32[]{:S(2)}) collective-permute-start(f32[8,128]{1,0:T(8,128)S(1)} %get-tuple-element.65.weight_a), channel_id=1, source_target_pairs={{0,1},{1,0},{2,3},{3,2},{4,5},{5,4},{6,7},{7,6},{8,9},{9,8},{10,11... | collective-permute-start | bytes 12296 | tf_op jit(solution)/shard_map/ppermute | solution.py:238

commit v8 on v7

--- a/solution.py
+++ b/solution.py
@@ -78,7 +78,8 @@
     me, core = lax.axis_index("op"), lax.axis_index("col")
     bit = 0
     for c, (mask, _) in enumerate(ORDER):
-        bit = bit + jnp.where(core == c, (me // mask) % 2, 0)
+        place = me // mask + (me // 4 if mask == 2 else 0)
+        bit = bit + jnp.where(core == c, place % 2, 0)
     return 1 - bit
 
 
@@ -230,7 +231,7 @@
         pairing = []
         for o in range(ops):
             for c in range(cols):
-                bit = ORDER[c % 2][stage] if stage < 2 else 1 << stage
+                bit = (*ORDER[c % 2], 6)[stage] if stage < 3 else 1 << stage
                 pairing.append((o * cols + c, (o ^ bit) * cols + c))
         return lax.ppermute(x, BOTH, pairing)
 
@@ -238,7 +239,7 @@
         return lax.ppermute(x, "col", [(c, c ^ 1) for c in range(cols)])
 
     me, core = lax.axis_index("op").astype(jnp.uint32), lax.axis_index("col").astype(jnp.uint32)
-    low, high = me & 1, (me >> 1) & 1
+    low, high = me & 1, ((me >> 1) ^ (me >> 2)) & 1
     bit0, bit1 = jnp.where(core == 0, low, high), jnp.where(core == 0, high, low)
     low_near, low_half, zero = bit1 == 0, bit0 == 0, jnp.zeros((), jnp.uint32)
     keep_at, send_at = bit1 * quarter, (1 - bit1) * quarter

time: 96.1 us -> 93.9 us (0.977)
  waiting for transfers between devices: 41.7 us -> 20.1 us
  starting transfers between devices: 30.5 us -> 50 us
    ppermute x20, waiting for transfers between devices: 29.1 us -> 12 us  [swap(): return lax.ppermute(x, BOTH, pairing)]
    ppermute x4, starting transfers between devices: 1.81 us -> 13.5 us  [gathered(): lax.ppermute(piece, BOTH, [(o * cols + c, (o ^ 3) * cols + c) for o in ra...]
    ppermute x20, starting transfers between devices: 27.1 us -> 34.9 us  [swap(): return lax.ppermute(x, BOTH, pairing)]
    ppermute x4, waiting for transfers between devices: 7.18 us -> 2.63 us  [gathered(): lax.ppermute(piece, BOTH, [(o * cols + c, (o ^ 3) * cols + c) for o in ra...]
  transfers between devices with their start and end apart: 31 -> 31, of which waited for: 23 -> 15; matrix products, arithmetic and copies ran while one was open for 1% -> 2% of each run, Pallas kernels for 12% -> 12%
where the time goes in v8:
time: 93.9 us; the launch traced here: 93.7 us
  starting transfers between devices  50 us (53%)
  Pallas kernels  20.9 us (22%)
  waiting for transfers between devices  20.1 us (21%)
  other arithmetic  2.11 us (2%)
    ppermute x20, starting transfers between devices, swap(): return lax.ppermute(x, BOTH, pairing)  34.9 us
    pallas_call x16, Pallas kernels, call(): pl.pallas_call(kernel, out_shape=outs, in_specs=in_specs, out_specs=out_s...  20.9 us
    ppermute x4, starting transfers between devices, gathered(): lax.ppermute(piece, BOTH, [(o * cols + c, (o ^ 3) * cols + c) for o in ra...  13.5 us
    ppermute x20, waiting for transfers between devices, swap(): return lax.ppermute(x, BOTH, pairing)  12 us
    ppermute x7, waiting for transfers between devices, across(): return lax.ppermute(x, 'col', [(c, c ^ 1) for c in range(cols)])  5.47 us
    ppermute x4, waiting for transfers between devices, gathered(): lax.ppermute(piece, BOTH, [(o * cols + c, (o ^ 3) * cols + c) for o in ra...  2.63 us
  transfers between devices with their start and end apart: 31, of which 15 were waited for; matrix products, arithmetic and copies ran while one was open for 2% of the time, Pallas kernels for 12%

profile of v8, /device:TPU:0, one launch (start us, length us, event | category | flops | bytes accessed | tf_op | source)
XLA Modules:
  0.0 93.7 jit_solution(767960395481779721)
XLA Ops:
  0.0 1.7 %open_vector.1 = (bf16[1024,512]{1,0:T(8,128)(2,1)S(1)}, f32[8,128]{1,0:T(8,128)S(1)}) custom-call(f32[1024,512]{1,0:T(8,128)} %vector_ref.1), custom_call_target="tpu_custom_call" | custom-call | flops 1572864 | bytes 4194304 | tf_op jit(solution)/shard_map/open_vector/pallas_call | solution.py:30
  1.7 0.5 collective-permute-start.1
  2.4 2.3 %sent_operators.1.masked_ref = bf16[512,2048]{1,0:T(8,128)(2,1)S(1)} custom-call(s32[128]{0:T(128)S(1)} %reshape.3.mask_ref, bf16[2,1024,1024]{2,1,0:T(8,128)(2,1)} %left_ref.3), custom_call_target="tpu_custom_call" | custom-call | flops 2097152 | bytes 4194304 | tf_op jit(solution)/shard_map/sent_operators/pallas_call | solution.py:30
  4.7 1.8 %sent_half_0.2 = (bf16[2048,256]{1,0:T(8,128)(2,1)S(1)}, f32[512,256]{1,0:T(8,128)S(1)}) custom-call(f32[8,128]{1,0:T(8,128)S(1)} %get-tuple-element.39.a_ref.weight_a, f32[8,128]{1,0:T(8,128)S(1)} %collective-permute-done.b_ref.weight_b, bf16[1024,512]{1,0:T(8,128)(2,1)S(1)} %get-tuple-element.42.own_ref, ...), custom_call_target="tpu_custom_call" | custom-call | flops 1610612736 | bytes 1048576 | tf_op jit(solution)/shard_map/sent_half_0/pallas_call | solution.py:30
  6.6 3.0 %collective-permute-start.2 = (f16[512,256]{1,0:T(8,128)(2,1)S(1)}, f16[512,256]{1,0:T(8,128)(2,1)S(1)}, u32[]{:S(2)}, u32[]{:S(2)}) collective-permute-start(f16[512,256]{1,0:T(8,128)(2,1)S(1)} %convert_element_type.116), channel_id=1, source_target_pairs={{0,2},{1,5},{2,0},{3,7},{4,6},{5,1},{6,4},{7,3},{8,10},{9,13},{10,... | collective-permute-start | bytes 786440 | tf_op jit(solution)/shard_map/ppermute | solution.py:236
  9.6 1.8 %sent_half_1.2 = (bf16[2048,256]{1,0:T(8,128)(2,1)S(1)}, f32[512,256]{1,0:T(8,128)S(1)}) custom-call(f32[8,128]{1,0:T(8,128)S(1)} %get-tuple-element.39.a_ref.weight_a, f32[8,128]{1,0:T(8,128)S(1)} %collective-permute-done.b_ref.weight_b, bf16[1024,512]{1,0:T(8,128)(2,1)S(1)} %get-tuple-element.42.own_ref, ...), custom_call_target="tpu_custom_call" | custom-call | flops 1610612736 | bytes 1048576 | tf_op jit(solution)/shard_map/sent_half_1/pallas_call | solution.py:30
  11.5 0.1 collective-permute-start.8
  11.6 2.2 %kept_operators.1.masked_ref = bf16[512,2048]{1,0:T(8,128)(2,1)S(1)} custom-call(s32[128]{0:T(128)S(1)} %reshape.3.mask_ref, bf16[2,1024,1024]{2,1,0:T(8,128)(2,1)} %left_ref.3), custom_call_target="tpu_custom_call" | custom-call | flops 2097152 | bytes 4194304 | tf_op jit(solution)/shard_map/kept_operators/pallas_call | solution.py:30
  13.8 0.7 kept_half.4
  14.7 2.1 %collective-permute-start.3 = (f16[256,256]{1,0:T(8,128)(2,1)S(1)}, f16[256,256]{1,0:T(8,128)(2,1)S(1)}, u32[]{:S(2)}, u32[]{:S(2)}) collective-permute-start(f16[256,256]{1,0:T(8,128)(2,1)S(1)} %dynamic-slice_convert_fusion.3), channel_id=1, source_target_pairs={{0,4},{1,3},{2,6},{3,1},{4,0},{5,7},{6,2},{7,5},{8,12},{9,11},{10,... | collective-permute-start | bytes 393224 | tf_op jit(solution)/shard_map/ppermute | solution.py:236
  16.8 0.7 kept_half.5
  17.5 1.1 %collective-permute-done.8 = f16[512,256]{1,0:T(8,128)(2,1)S(1)} collective-permute-done((f16[512,256]{1,0:T(8,128)(2,1)S(1)}, f16[512,256]{1,0:T(8,128)(2,1)S(1)}, u32[]{:S(2)}, u32[]{:S(2)}) %collective-permute-start.8) | collective-permute-done | bytes 262176 | tf_op jit(solution)/shard_map/ppermute | solution.py:236
  18.8 1.5 %collective-permute-start.9 = (f16[256,256]{1,0:T(8,128)(2,1)S(1)}, f16[256,256]{1,0:T(8,128)(2,1)S(1)}, u32[]{:S(2)}, u32[]{:S(2)}) collective-permute-start(f16[256,256]{1,0:T(8,128)(2,1)S(1)} %dynamic-slice_convert_fusion.2), channel_id=1, source_target_pairs={{0,4},{1,3},{2,6},{3,1},{4,0},{5,7},{6,2},{7,5},{8,12},{9,11},{10,... | collective-permute-start | bytes 393224 | tf_op jit(solution)/shard_map/ppermute | solution.py:236
  20.3 3.6 %collective-permute-start.4 = (f16[256,256]{1,0:T(8,128)(2,1)S(1)}, f16[256,256]{1,0:T(8,128)(2,1)S(1)}, u32[]{:S(2)}, u32[]{:S(2)}) collective-permute-start(f16[256,256]{1,0:T(8,128)(2,1)S(1)} %add_convert_fusion.7), channel_id=1, source_target_pairs={{0,12},{1,13},{2,14},{3,15},{4,8},{5,9},{6,10},{7,11},{8,4},{9,5},... | collective-permute-start | bytes 393224 | tf_op jit(solution)/shard_map/ppermute | solution.py:236
  24.0 3.4 %collective-permute-start.10 = (f16[256,256]{1,0:T(8,128)(2,1)S(1)}, f16[256,256]{1,0:T(8,128)(2,1)S(1)}, u32[]{:S(2)}, u32[]{:S(2)}) collective-permute-start(f16[256,256]{1,0:T(8,128)(2,1)S(1)} %add_convert_fusion.5), channel_id=1, source_target_pairs={{0,12},{1,13},{2,14},{3,15},{4,8},{5,9},{6,10},{7,11},{8,4},{9,5},... | collective-permute-start | bytes 393224 | tf_op jit(solution)/shard_map/ppermute | solution.py:236
  27.4 1.7 %collective-permute-done.4 = f16[256,256]{1,0:T(8,128)(2,1)S(1)} collective-permute-done((f16[256,256]{1,0:T(8,128)(2,1)S(1)}, f16[256,256]{1,0:T(8,128)(2,1)S(1)}, u32[]{:S(2)}, u32[]{:S(2)}) %collective-permute-start.4) | collective-permute-done | bytes 131104 | tf_op jit(solution)/shard_map/ppermute | solution.py:236
  29.1 4.7 %collective-permute-start.7 = (f16[256,256]{1,0:T(8,128)(2,1)S(1)}, f16[256,256]{1,0:T(8,128)(2,1)S(1)}, u32[]{:S(2)}, u32[]{:S(2)}) collective-permute-start(f16[256,256]{1,0:T(8,128)(2,1)S(1)} %add_convert_fusion.6), channel_id=1, source_target_pairs={{0,6},{1,7},{2,4},{3,5},{4,2},{5,3},{6,0},{7,1},{8,14},{9,15},{10,... | collective-permute-start | bytes 393224 | tf_op jit(solution)/shard_map/ppermute | solution.py:265
  33.8 1.2 %collective-permute-start.6 = (f16[256,256]{1,0:T(8,128)(2,1)S(1)}, f16[256,256]{1,0:T(8,128)(2,1)S(1)}, u32[]{:S(2)}, u32[]{:S(2)}) collective-permute-start(f16[256,256]{1,0:T(8,128)(2,1)S(1)} %add_convert_fusion.6), channel_id=1, source_target_pairs={{0,2},{1,5},{2,0},{3,7},{4,6},{5,1},{6,4},{7,3},{8,10},{9,13},{10,... | collective-permute-start | bytes 393224 | tf_op jit(solution)/shard_map/ppermute | solution.py:236
  35.1 2.3 %collective-permute-start.13 = (f16[256,256]{1,0:T(8,128)(2,1)S(1)}, f16[256,256]{1,0:T(8,128)(2,1)S(1)}, u32[]{:S(2)}, u32[]{:S(2)}) collective-permute-start(f16[256,256]{1,0:T(8,128)(2,1)S(1)} %add_convert_fusion.4), channel_id=1, source_target_pairs={{0,6},{1,7},{2,4},{3,5},{4,2},{5,3},{6,0},{7,1},{8,14},{9,15},{10,... | collective-permute-start | bytes 393224 | tf_op jit(solution)/shard_map/ppermute | solution.py:265
  37.4 1.2 %collective-permute-start.12 = (f16[256,256]{1,0:T(8,128)(2,1)S(1)}, f16[256,256]{1,0:T(8,128)(2,1)S(1)}, u32[]{:S(2)}, u32[]{:S(2)}) collective-permute-start(f16[256,256]{1,0:T(8,128)(2,1)S(1)} %add_convert_fusion.4), channel_id=1, source_target_pairs={{0,2},{1,5},{2,0},{3,7},{4,6},{5,1},{6,4},{7,3},{8,10},{9,13},{10,... | collective-permute-start | bytes 393224 | tf_op jit(solution)/shard_map/ppermute | solution.py:236
  38.6 2.2 %collective-permute-start.11 = (f16[256,256]{1,0:T(8,128)(2,1)S(1)}, f16[256,256]{1,0:T(8,128)(2,1)S(1)}, u32[]{:S(2)}, u32[]{:S(2)}) collective-permute-start(f16[256,256]{1,0:T(8,128)(2,1)S(1)} %add_convert_fusion.4), channel_id=1, source_target_pairs={{0,4},{1,3},{2,6},{3,1},{4,0},{5,7},{6,2},{7,5},{8,12},{9,11},{10,... | collective-permute-start | bytes 393224 | tf_op jit(solution)/shard_map/ppermute | solution.py:236
  40.8 0.2 broadcast_select_fusion.31
  41.0 0.7 collective-permute-done.13
  41.7 1.3 %collective-permute-done.12 = f16[256,256]{1,0:T(8,128)(2,1)S(1)} collective-permute-done((f16[256,256]{1,0:T(8,128)(2,1)S(1)}, f16[256,256]{1,0:T(8,128)(2,1)S(1)}, u32[]{:S(2)}, u32[]{:S(2)}) %collective-permute-start.12) | collective-permute-done | bytes 131104 | tf_op jit(solution)/shard_map/ppermute | solution.py:236
  43.0 0.7 collective-permute-done.11
  43.7 0.2 broadcast_select_fusion.27
  43.9 0.2 maximum_convert_fusion
  44.2 0.3 correlate.2.corr_a
  44.5 1.2 %collective-permute-done.14.corr_b = f32[8,128]{1,0:T(8,128)S(1)} collective-permute-done((f32[8,128]{1,0:T(8,128)S(1)}, f32[8,128]{1,0:T(8,128)S(1)}, u32[]{:S(2)}, u32[]{:S(2)}) %collective-permute-start.14) | collective-permute-done | bytes 4128 | tf_op jit(solution)/shard_map/ppermute | solution.py:239
  45.7 1.0 %correct.2 = (f32[1024,512]{1,0:T(8,128)S(1)}, f32[8,128]{1,0:T(8,128)S(1)}, bf16[1024,512]{1,0:T(8,128)(2,1)S(1)}) custom-call(f32[8,128]{1,0:T(8,128)S(1)} %correlate.2.corr_a, f32[8,128]{1,0:T(8,128)S(1)} %collective-permute-done.14.corr_b, f32[8,128]{1,0:T(8,128)S(1)} %get-tuple-element.39.a_ref.weight_a, ...), custom_call_target="tpu_custom_call" | custom-call | flops 6291456 | bytes 1048576 | tf_op jit(solution)/shard_map/correct/pallas_call | solution.py:30
  46.8 0.2 collective-permute-start.16
  47.0 0.4 collective-permute-start.15
  47.4 2.2 %collective-permute-done.15.b_ref.weight_b = f32[8,128]{1,0:T(8,128)S(1)} collective-permute-done((f32[8,128]{1,0:T(8,128)S(1)}, f32[8,128]{1,0:T(8,128)S(1)}, u32[]{:S(2)}, u32[]{:S(2)}) %collective-permute-start.15) | collective-permute-done | bytes 4128 | tf_op jit(solution)/shard_map/ppermute | solution.py:239
  49.5 1.8 %sent_half_0.3 = (bf16[2048,256]{1,0:T(8,128)(2,1)S(1)}, f32[512,256]{1,0:T(8,128)S(1)}) custom-call(f32[8,128]{1,0:T(8,128)S(1)} %get-tuple-element.54.a_ref.weight_a, f32[8,128]{1,0:T(8,128)S(1)} %collective-permute-done.15.b_ref.weight_b, bf16[1024,512]{1,0:T(8,128)(2,1)S(1)} %get-tuple-element.57.own_ref, ...), custom_call_target="tpu_custom_call" | custom-call | flops 1610612736 | bytes 1048576 | tf_op jit(solution)/shard_map/sent_half_0/pallas_call | solution.py:30
  51.4 1.1 %collective-permute-start.17 = (f16[512,256]{1,0:T(8,128)(2,1)S(1)}, f16[512,256]{1,0:T(8,128)(2,1)S(1)}, u32[]{:S(2)}, u32[]{:S(2)}) collective-permute-start(f16[512,256]{1,0:T(8,128)(2,1)S(1)} %convert_element_type.134), channel_id=1, source_target_pairs={{0,2},{1,5},{2,0},{3,7},{4,6},{5,1},{6,4},{7,3},{8,10},{9,13},{10,... | collective-permute-start | bytes 786440 | tf_op jit(solution)/shard_map/ppermute | solution.py:236
  52.5 1.8 %sent_half_1.3 = (bf16[2048,256]{1,0:T(8,128)(2,1)S(1)}, f32[512,256]{1,0:T(8,128)S(1)}) custom-call(f32[8,128]{1,0:T(8,128)S(1)} %get-tuple-element.54.a_ref.weight_a, f32[8,128]{1,0:T(8,128)S(1)} %collective-permute-done.15.b_ref.weight_b, bf16[1024,512]{1,0:T(8,128)(2,1)S(1)} %get-tuple-element.57.own_ref, ...), custom_call_target="tpu_custom_call" | custom-call | flops 1610612736 | bytes 1048576 | tf_op jit(solution)/shard_map/sent_half_1/pallas_call | solution.py:30
  54.3 1.1 %collective-permute-start.23 = (f16[512,256]{1,0:T(8,128)(2,1)S(1)}, f16[512,256]{1,0:T(8,128)(2,1)S(1)}, u32[]{:S(2)}, u32[]{:S(2)}) collective-permute-start(f16[512,256]{1,0:T(8,128)(2,1)S(1)} %convert_element_type.143), channel_id=1, source_target_pairs={{0,2},{1,5},{2,0},{3,7},{4,6},{5,1},{6,4},{7,3},{8,10},{9,13},{10,... | collective-permute-start | bytes 786440 | tf_op jit(solution)/shard_map/ppermute | solution.py:236
  55.4 0.7 kept_half.6
  56.1 1.7 %collective-permute-done.17 = f16[512,256]{1,0:T(8,128)(2,1)S(1)} collective-permute-done((f16[512,256]{1,0:T(8,128)(2,1)S(1)}, f16[512,256]{1,0:T(8,128)(2,1)S(1)}, u32[]{:S(2)}, u32[]{:S(2)}) %collective-permute-start.17) | collective-permute-done | bytes 262176 | tf_op jit(solution)/shard_map/ppermute | solution.py:236
  58.0 2.1 %collective-permute-start.18 = (f16[256,256]{1,0:T(8,128)(2,1)S(1)}, f16[256,256]{1,0:T(8,128)(2,1)S(1)}, u32[]{:S(2)}, u32[]{:S(2)}) collective-permute-start(f16[256,256]{1,0:T(8,128)(2,1)S(1)} %dynamic-slice_convert_fusion.1), channel_id=1, source_target_pairs={{0,4},{1,3},{2,6},{3,1},{4,0},{5,7},{6,2},{7,5},{8,12},{9,11},{10,... | collective-permute-start | bytes 393224 | tf_op jit(solution)/shard_map/ppermute | solution.py:236
  60.0 0.9 kept_half.7
  61.0 0.3 collective-permute-done.23
  61.4 2.1 %collective-permute-start.24 = (f16[256,256]{1,0:T(8,128)(2,1)S(1)}, f16[256,256]{1,0:T(8,128)(2,1)S(1)}, u32[]{:S(2)}, u32[]{:S(2)}) collective-permute-start(f16[256,256]{1,0:T(8,128)(2,1)S(1)} %dynamic-slice_convert_fusion), channel_id=1, source_target_pairs={{0,4},{1,3},{2,6},{3,1},{4,0},{5,7},{6,2},{7,5},{8,12},{9,11},{10,... | collective-permute-start | bytes 393224 | tf_op jit(solution)/shard_map/ppermute | solution.py:236
  63.6 3.2 %collective-permute-start.19 = (f16[256,256]{1,0:T(8,128)(2,1)S(1)}, f16[256,256]{1,0:T(8,128)(2,1)S(1)}, u32[]{:S(2)}, u32[]{:S(2)}) collective-permute-start(f16[256,256]{1,0:T(8,128)(2,1)S(1)} %add_convert_fusion.3), channel_id=1, source_target_pairs={{0,12},{1,13},{2,14},{3,15},{4,8},{5,9},{6,10},{7,11},{8,4},{9,5},... | collective-permute-start | bytes 393224 | tf_op jit(solution)/shard_map/ppermute | solution.py:236
  66.8 2.9 %collective-permute-start.25 = (f16[256,256]{1,0:T(8,128)(2,1)S(1)}, f16[256,256]{1,0:T(8,128)(2,1)S(1)}, u32[]{:S(2)}, u32[]{:S(2)}) collective-permute-start(f16[256,256]{1,0:T(8,128)(2,1)S(1)} %add_convert_fusion.1), channel_id=1, source_target_pairs={{0,12},{1,13},{2,14},{3,15},{4,8},{5,9},{6,10},{7,11},{8,4},{9,5},... | collective-permute-start | bytes 393224 | tf_op jit(solution)/shard_map/ppermute | solution.py:236
  69.7 2.8 %collective-permute-done.19 = f16[256,256]{1,0:T(8,128)(2,1)S(1)} collective-permute-done((f16[256,256]{1,0:T(8,128)(2,1)S(1)}, f16[256,256]{1,0:T(8,128)(2,1)S(1)}, u32[]{:S(2)}, u32[]{:S(2)}) %collective-permute-start.19) | collective-permute-done | bytes 131104 | tf_op jit(solution)/shard_map/ppermute | solution.py:236
  72.6 3.9 %collective-permute-start.22 = (f16[256,256]{1,0:T(8,128)(2,1)S(1)}, f16[256,256]{1,0:T(8,128)(2,1)S(1)}, u32[]{:S(2)}, u32[]{:S(2)}) collective-permute-start(f16[256,256]{1,0:T(8,128)(2,1)S(1)} %add_convert_fusion.2), channel_id=1, source_target_pairs={{0,6},{1,7},{2,4},{3,5},{4,2},{5,3},{6,0},{7,1},{8,14},{9,15},{10,... | collective-permute-start | bytes 393224 | tf_op jit(solution)/shard_map/ppermute | solution.py:265
  76.5 0.9 %collective-permute-start.21 = (f16[256,256]{1,0:T(8,128)(2,1)S(1)}, f16[256,256]{1,0:T(8,128)(2,1)S(1)}, u32[]{:S(2)}, u32[]{:S(2)}) collective-permute-start(f16[256,256]{1,0:T(8,128)(2,1)S(1)} %add_convert_fusion.2), channel_id=1, source_target_pairs={{0,2},{1,5},{2,0},{3,7},{4,6},{5,1},{6,4},{7,3},{8,10},{9,13},{10,... | collective-permute-start | bytes 393224 | tf_op jit(solution)/shard_map/ppermute | solution.py:236
  77.5 2.6 %collective-permute-start.28 = (f16[256,256]{1,0:T(8,128)(2,1)S(1)}, f16[256,256]{1,0:T(8,128)(2,1)S(1)}, u32[]{:S(2)}, u32[]{:S(2)}) collective-permute-start(f16[256,256]{1,0:T(8,128)(2,1)S(1)} %add_convert_fusion), channel_id=1, source_target_pairs={{0,6},{1,7},{2,4},{3,5},{4,2},{5,3},{6,0},{7,1},{8,14},{9,15},{10,... | collective-permute-start | bytes 393224 | tf_op jit(solution)/shard_map/ppermute | solution.py:265
  80.1 1.0 %collective-permute-start.27 = (f16[256,256]{1,0:T(8,128)(2,1)S(1)}, f16[256,256]{1,0:T(8,128)(2,1)S(1)}, u32[]{:S(2)}, u32[]{:S(2)}) collective-permute-start(f16[256,256]{1,0:T(8,128)(2,1)S(1)} %add_convert_fusion), channel_id=1, source_target_pairs={{0,2},{1,5},{2,0},{3,7},{4,6},{5,1},{6,4},{7,3},{8,10},{9,13},{10,... | collective-permute-start | bytes 393224 | tf_op jit(solution)/shard_map/ppermute | solution.py:236
  81.1 2.3 %collective-permute-start.26 = (f16[256,256]{1,0:T(8,128)(2,1)S(1)}, f16[256,256]{1,0:T(8,128)(2,1)S(1)}, u32[]{:S(2)}, u32[]{:S(2)}) collective-permute-start(f16[256,256]{1,0:T(8,128)(2,1)S(1)} %add_convert_fusion), channel_id=1, source_target_pairs={{0,4},{1,3},{2,6},{3,1},{4,0},{5,7},{6,2},{7,5},{8,12},{9,11},{10,... | collective-permute-start | bytes 393224 | tf_op jit(solution)/shard_map/ppermute | solution.py:236
  83.3 1.1 %collective-permute-done.21 = f16[256,256]{1,0:T(8,128)(2,1)S(1)} collective-permute-done((f16[256,256]{1,0:T(8,128)(2,1)S(1)}, f16[256,256]{1,0:T(8,128)(2,1)S(1)}, u32[]{:S(2)}, u32[]{:S(2)}) %collective-permute-start.21) | collective-permute-done | bytes 131104 | tf_op jit(solution)/shard_map/ppermute | solution.py:236
  84.4 0.2 broadcast_select_fusion.23
  84.6 0.1 maximum_convert_fusion.2.refs_0_
  84.7 1.9 %collective-permute-done.28 = f16[256,256]{1,0:T(8,128)(2,1)S(1)} collective-permute-done((f16[256,256]{1,0:T(8,128)(2,1)S(1)}, f16[256,256]{1,0:T(8,128)(2,1)S(1)}, u32[]{:S(2)}, u32[]{:S(2)}) %collective-permute-start.28) | collective-permute-done | bytes 131104 | tf_op jit(solution)/shard_map/ppermute | solution.py:265
  86.6 1.2 %collective-permute-done.27 = f16[256,256]{1,0:T(8,128)(2,1)S(1)} collective-permute-done((f16[256,256]{1,0:T(8,128)(2,1)S(1)}, f16[256,256]{1,0:T(8,128)(2,1)S(1)}, u32[]{:S(2)}, u32[]{:S(2)}) %collective-permute-start.27) | collective-permute-done | bytes 131104 | tf_op jit(solution)/shard_map/ppermute | solution.py:236
  87.8 0.2 broadcast_select_fusion.19
  88.0 0.1 maximum_convert_fusion.3.refs_1_
  88.1 0.5 correlate.3.corr_a
  88.6 1.2 %collective-permute-done.29.corr_b = f32[8,128]{1,0:T(8,128)S(1)} collective-permute-done((f32[8,128]{1,0:T(8,128)S(1)}, f32[8,128]{1,0:T(8,128)S(1)}, u32[]{:S(2)}, u32[]{:S(2)}) %collective-permute-start.29) | collective-permute-done | bytes 4128 | tf_op jit(solution)/shard_map/ppermute | solution.py:239
  89.8 1.1 %correct.3 = (f32[1024,512]{1,0:T(8,128)S(1)}, f32[8,128]{1,0:T(8,128)S(1)}) custom-call(f32[8,128]{1,0:T(8,128)S(1)} %correlate.3.corr_a, f32[8,128]{1,0:T(8,128)S(1)} %collective-permute-done.29.corr_b, f32[8,128]{1,0:T(8,128)S(1)} %get-tuple-element.54.a_ref.weight_a, f32[8,128]{1,0:T(8,128)S(1)} %collective-permute-done.15.b_ref.weight_b, ...), custom_call_target="tpu_custom_call" | custom-call | flops 6291456 | bytes 1048576 | tf_op jit(solution)/shard_map/correct/pallas_call | solution.py:30
  90.9 0.2 collective-permute-start.30
  91.1 1.0 %collective-permute-done.30.weight_b = f32[8,128]{1,0:T(8,128)S(1)} collective-permute-done((f32[8,128]{1,0:T(8,128)S(1)}, f32[8,128]{1,0:T(8,128)S(1)}, u32[]{:S(2)}, u32[]{:S(2)}) %collective-permute-start.30) | collective-permute-done | bytes 4128 | tf_op jit(solution)/shard_map/ppermute | solution.py:239
  92.1 1.4 %normalise.1 = f32[1024,512]{1,0:T(8,128)} custom-call(f32[8,128]{1,0:T(8,128)S(1)} %get-tuple-element.65.weight_a, f32[8,128]{1,0:T(8,128)S(1)} %collective-permute-done.30.weight_b, f32[1024,512]{1,0:T(8,128)S(1)} %get-tuple-element.66.vector_ref), custom_call_target="tpu_custom_call" | custom-call | flops 524288 | bytes 4194304 | tf_op jit(solution)/shard_map/normalise/pallas_call | solution.py:30
  (50 shorter events, 1.4 us)
Async XLA Ops:
  0.0 2.3 %copy-start.3 = (s32[2,8,8]{2,1,0:T(8,128)S(1)}, s32[2,8,8]{2,1,0:T(8,128)}, u32[]{:S(2)}) copy-start(s32[2,8,8]{2,1,0:T(8,128)} %param.9) | copy-start | bytes 1540
  1.7 3.0 %collective-permute-start.1 = (bf16[1024,512]{1,0:T(8,128)(2,1)S(1)}, bf16[1024,512]{1,0:T(8,128)(2,1)S(1)}, u32[]{:S(2)}, u32[]{:S(2)}) collective-permute-start(bf16[1024,512]{1,0:T(8,128)(2,1)S(1)} %get-tuple-element.42.own_ref), channel_id=1, source_target_pairs={{0,1},{1,0},{2,3},{3,2},{4,5},{5,4},{6,7},{7,6},{8,9},{9,8},{10,11... | collective-permute-start | bytes 3145736 | tf_op jit(solution)/shard_map/ppermute | solution.py:239
  2.3 2.5 %collective-permute-start = (f32[8,128]{1,0:T(8,128)S(1)}, f32[8,128]{1,0:T(8,128)S(1)}, u32[]{:S(2)}, u32[]{:S(2)}) collective-permute-start(f32[8,128]{1,0:T(8,128)S(1)} %get-tuple-element.39.a_ref.weight_a), channel_id=1, source_target_pairs={{0,1},{1,0},{2,3},{3,2},{4,5},{5,4},{6,7},{7,6},{8,9},{9,8},{10,11... | collective-permute-start | bytes 12296 | tf_op jit(solution)/shard_map/ppermute | solution.py:239
  2.4 2.3 %copy-start = (bf16[2,1024,512]{2,1,0:T(8,128)(2,1)S(1)}, bf16[2,1024,512]{2,1,0:T(8,128)(2,1)}, u32[]{:S(2)}) copy-start(bf16[2,1024,512]{2,1,0:T(8,128)(2,1)} %right_ref.7) | copy-start | bytes 6291460
  6.6 7.9 %collective-permute-start.2 = (f16[512,256]{1,0:T(8,128)(2,1)S(1)}, f16[512,256]{1,0:T(8,128)(2,1)S(1)}, u32[]{:S(2)}, u32[]{:S(2)}) collective-permute-start(f16[512,256]{1,0:T(8,128)(2,1)S(1)} %convert_element_type.116), channel_id=1, source_target_pairs={{0,2},{1,5},{2,0},{3,7},{4,6},{5,1},{6,4},{7,3},{8,10},{9,13},{10,... | collective-permute-start | bytes 786440 | tf_op jit(solution)/shard_map/ppermute | solution.py:236
  11.5 7.1 %collective-permute-start.8 = (f16[512,256]{1,0:T(8,128)(2,1)S(1)}, f16[512,256]{1,0:T(8,128)(2,1)S(1)}, u32[]{:S(2)}, u32[]{:S(2)}) collective-permute-start(f16[512,256]{1,0:T(8,128)(2,1)S(1)} %convert_element_type.125), channel_id=1, source_target_pairs={{0,2},{1,5},{2,0},{3,7},{4,6},{5,1},{6,4},{7,3},{8,10},{9,13},{10,... | collective-permute-start | bytes 786440 | tf_op jit(solution)/shard_map/ppermute | solution.py:236
  14.7 5.6 %collective-permute-start.3 = (f16[256,256]{1,0:T(8,128)(2,1)S(1)}, f16[256,256]{1,0:T(8,128)(2,1)S(1)}, u32[]{:S(2)}, u32[]{:S(2)}) collective-permute-start(f16[256,256]{1,0:T(8,128)(2,1)S(1)} %dynamic-slice_convert_fusion.3), channel_id=1, source_target_pairs={{0,4},{1,3},{2,6},{3,1},{4,0},{5,7},{6,2},{7,5},{8,12},{9,11},{10,... | collective-permute-start | bytes 393224 | tf_op jit(solution)/shard_map/ppermute | solution.py:236
  18.8 5.2 %collective-permute-start.9 = (f16[256,256]{1,0:T(8,128)(2,1)S(1)}, f16[256,256]{1,0:T(8,128)(2,1)S(1)}, u32[]{:S(2)}, u32[]{:S(2)}) collective-permute-start(f16[256,256]{1,0:T(8,128)(2,1)S(1)} %dynamic-slice_convert_fusion.2), channel_id=1, source_target_pairs={{0,4},{1,3},{2,6},{3,1},{4,0},{5,7},{6,2},{7,5},{8,12},{9,11},{10,... | collective-permute-start | bytes 393224 | tf_op jit(solution)/shard_map/ppermute | solution.py:236
  20.3 8.8 %collective-permute-start.4 = (f16[256,256]{1,0:T(8,128)(2,1)S(1)}, f16[256,256]{1,0:T(8,128)(2,1)S(1)}, u32[]{:S(2)}, u32[]{:S(2)}) collective-permute-start(f16[256,256]{1,0:T(8,128)(2,1)S(1)} %add_convert_fusion.7), channel_id=1, source_target_pairs={{0,12},{1,13},{2,14},{3,15},{4,8},{5,9},{6,10},{7,11},{8,4},{9,5},... | collective-permute-start | bytes 393224 | tf_op jit(solution)/shard_map/ppermute | solution.py:236
  24.0 11.0 %collective-permute-start.10 = (f16[256,256]{1,0:T(8,128)(2,1)S(1)}, f16[256,256]{1,0:T(8,128)(2,1)S(1)}, u32[]{:S(2)}, u32[]{:S(2)}) collective-permute-start(f16[256,256]{1,0:T(8,128)(2,1)S(1)} %add_convert_fusion.5), channel_id=1, source_target_pairs={{0,12},{1,13},{2,14},{3,15},{4,8},{5,9},{6,10},{7,11},{8,4},{9,5},... | collective-permute-start | bytes 393224 | tf_op jit(solution)/shard_map/ppermute | solution.py:236
  29.1 9.5 %collective-permute-start.7 = (f16[256,256]{1,0:T(8,128)(2,1)S(1)}, f16[256,256]{1,0:T(8,128)(2,1)S(1)}, u32[]{:S(2)}, u32[]{:S(2)}) collective-permute-start(f16[256,256]{1,0:T(8,128)(2,1)S(1)} %add_convert_fusion.6), channel_id=1, source_target_pairs={{0,6},{1,7},{2,4},{3,5},{4,2},{5,3},{6,0},{7,1},{8,14},{9,15},{10,... | collective-permute-start | bytes 393224 | tf_op jit(solution)/shard_map/ppermute | solution.py:265
  33.8 7.0 %collective-permute-start.6 = (f16[256,256]{1,0:T(8,128)(2,1)S(1)}, f16[256,256]{1,0:T(8,128)(2,1)S(1)}, u32[]{:S(2)}, u32[]{:S(2)}) collective-permute-start(f16[256,256]{1,0:T(8,128)(2,1)S(1)} %add_convert_fusion.6), channel_id=1, source_target_pairs={{0,2},{1,5},{2,0},{3,7},{4,6},{5,1},{6,4},{7,3},{8,10},{9,13},{10,... | collective-permute-start | bytes 393224 | tf_op jit(solution)/shard_map/ppermute | solution.py:236
  35.0 5.8 %collective-permute-start.5 = (f16[256,256]{1,0:T(8,128)(2,1)S(1)}, f16[256,256]{1,0:T(8,128)(2,1)S(1)}, u32[]{:S(2)}, u32[]{:S(2)}) collective-permute-start(f16[256,256]{1,0:T(8,128)(2,1)S(1)} %add_convert_fusion.6), channel_id=1, source_target_pairs={{0,4},{1,3},{2,6},{3,1},{4,0},{5,7},{6,2},{7,5},{8,12},{9,11},{10,... | collective-permute-start | bytes 393224 | tf_op jit(solution)/shard_map/ppermute | solution.py:236
  35.1 6.7 %collective-permute-start.13 = (f16[256,256]{1,0:T(8,128)(2,1)S(1)}, f16[256,256]{1,0:T(8,128)(2,1)S(1)}, u32[]{:S(2)}, u32[]{:S(2)}) collective-permute-start(f16[256,256]{1,0:T(8,128)(2,1)S(1)} %add_convert_fusion.4), channel_id=1, source_target_pairs={{0,6},{1,7},{2,4},{3,5},{4,2},{5,3},{6,0},{7,1},{8,14},{9,15},{10,... | collective-permute-start | bytes 393224 | tf_op jit(solution)/shard_map/ppermute | solution.py:265
  37.4 5.6 %collective-permute-start.12 = (f16[256,256]{1,0:T(8,128)(2,1)S(1)}, f16[256,256]{1,0:T(8,128)(2,1)S(1)}, u32[]{:S(2)}, u32[]{:S(2)}) collective-permute-start(f16[256,256]{1,0:T(8,128)(2,1)S(1)} %add_convert_fusion.4), channel_id=1, source_target_pairs={{0,2},{1,5},{2,0},{3,7},{4,6},{5,1},{6,4},{7,3},{8,10},{9,13},{10,... | collective-permute-start | bytes 393224 | tf_op jit(solution)/shard_map/ppermute | solution.py:236
  38.6 5.1 %collective-permute-start.11 = (f16[256,256]{1,0:T(8,128)(2,1)S(1)}, f16[256,256]{1,0:T(8,128)(2,1)S(1)}, u32[]{:S(2)}, u32[]{:S(2)}) collective-permute-start(f16[256,256]{1,0:T(8,128)(2,1)S(1)} %add_convert_fusion.4), channel_id=1, source_target_pairs={{0,4},{1,3},{2,6},{3,1},{4,0},{5,7},{6,2},{7,5},{8,12},{9,11},{10,... | collective-permute-start | bytes 393224 | tf_op jit(solution)/shard_map/ppermute | solution.py:236
  41.0 3.2 %copy-start.1 = (f32[1024,512]{1,0:T(8,128)S(1)}, f32[1024,512]{1,0:T(8,128)}, u32[]{:S(2)}) copy-start(f32[1024,512]{1,0:T(8,128)} %vector_ref.1) | copy-start | bytes 6291460
  44.1 1.6 %copy-start.2 = (f32[1024,512]{1,0:T(8,128)S(1)}, f32[1024,512]{1,0:T(8,128)}, u32[]{:S(2)}) copy-start(f32[1024,512]{1,0:T(8,128)} %diag_ref.3) | copy-start | bytes 6291460
  44.5 1.2 %collective-permute-start.14 = (f32[8,128]{1,0:T(8,128)S(1)}, f32[8,128]{1,0:T(8,128)S(1)}, u32[]{:S(2)}, u32[]{:S(2)}) collective-permute-start(f32[8,128]{1,0:T(8,128)S(1)} %correlate.2.corr_a), channel_id=1, source_target_pairs={{0,1},{1,0},{2,3},{3,2},{4,5},{5,4},{6,7},{7,6},{8,9},{9,8},{10,11... | collective-permute-start | bytes 12296 | tf_op jit(solution)/shard_map/ppermute | solution.py:239
  46.8 2.7 %collective-permute-start.16 = (bf16[1024,512]{1,0:T(8,128)(2,1)S(1)}, bf16[1024,512]{1,0:T(8,128)(2,1)S(1)}, u32[]{:S(2)}, u32[]{:S(2)}) collective-permute-start(bf16[1024,512]{1,0:T(8,128)(2,1)S(1)} %get-tuple-element.57.own_ref), channel_id=1, source_target_pairs={{0,1},{1,0},{2,3},{3,2},{4,5},{5,4},{6,7},{7,6},{8,9},{9,8},{10,11... | collective-permute-start | bytes 3145736 | tf_op jit(solution)/shard_map/ppermute | solution.py:239
  47.0 2.5 %collective-permute-start.15 = (f32[8,128]{1,0:T(8,128)S(1)}, f32[8,128]{1,0:T(8,128)S(1)}, u32[]{:S(2)}, u32[]{:S(2)}) collective-permute-start(f32[8,128]{1,0:T(8,128)S(1)} %get-tuple-element.54.a_ref.weight_a), channel_id=1, source_target_pairs={{0,1},{1,0},{2,3},{3,2},{4,5},{5,4},{6,7},{7,6},{8,9},{9,8},{10,11... | collective-permute-start | bytes 12296 | tf_op jit(solution)/shard_map/ppermute | solution.py:239
  51.4 6.4 %collective-permute-start.17 = (f16[512,256]{1,0:T(8,128)(2,1)S(1)}, f16[512,256]{1,0:T(8,128)(2,1)S(1)}, u32[]{:S(2)}, u32[]{:S(2)}) collective-permute-start(f16[512,256]{1,0:T(8,128)(2,1)S(1)} %convert_element_type.134), channel_id=1, source_target_pairs={{0,2},{1,5},{2,0},{3,7},{4,6},{5,1},{6,4},{7,3},{8,10},{9,13},{10,... | collective-permute-start | bytes 786440 | tf_op jit(solution)/shard_map/ppermute | solution.py:236
  54.3 6.9 %collective-permute-start.23 = (f16[512,256]{1,0:T(8,128)(2,1)S(1)}, f16[512,256]{1,0:T(8,128)(2,1)S(1)}, u32[]{:S(2)}, u32[]{:S(2)}) collective-permute-start(f16[512,256]{1,0:T(8,128)(2,1)S(1)} %convert_element_type.143), channel_id=1, source_target_pairs={{0,2},{1,5},{2,0},{3,7},{4,6},{5,1},{6,4},{7,3},{8,10},{9,13},{10,... | collective-permute-start | bytes 786440 | tf_op jit(solution)/shard_map/ppermute | solution.py:236
  58.0 5.6 %collective-permute-start.18 = (f16[256,256]{1,0:T(8,128)(2,1)S(1)}, f16[256,256]{1,0:T(8,128)(2,1)S(1)}, u32[]{:S(2)}, u32[]{:S(2)}) collective-permute-start(f16[256,256]{1,0:T(8,128)(2,1)S(1)} %dynamic-slice_convert_fusion.1), channel_id=1, source_target_pairs={{0,4},{1,3},{2,6},{3,1},{4,0},{5,7},{6,2},{7,5},{8,12},{9,11},{10,... | collective-permute-start | bytes 393224 | tf_op jit(solution)/shard_map/ppermute | solution.py:236
  61.4 5.4 %collective-permute-start.24 = (f16[256,256]{1,0:T(8,128)(2,1)S(1)}, f16[256,256]{1,0:T(8,128)(2,1)S(1)}, u32[]{:S(2)}, u32[]{:S(2)}) collective-permute-start(f16[256,256]{1,0:T(8,128)(2,1)S(1)} %dynamic-slice_convert_fusion), channel_id=1, source_target_pairs={{0,4},{1,3},{2,6},{3,1},{4,0},{5,7},{6,2},{7,5},{8,12},{9,11},{10,... | collective-permute-start | bytes 393224 | tf_op jit(solution)/shard_map/ppermute | solution.py:236
  63.6 9.0 %collective-permute-start.19 = (f16[256,256]{1,0:T(8,128)(2,1)S(1)}, f16[256,256]{1,0:T(8,128)(2,1)S(1)}, u32[]{:S(2)}, u32[]{:S(2)}) collective-permute-start(f16[256,256]{1,0:T(8,128)(2,1)S(1)} %add_convert_fusion.3), channel_id=1, source_target_pairs={{0,12},{1,13},{2,14},{3,15},{4,8},{5,9},{6,10},{7,11},{8,4},{9,5},... | collective-permute-start | bytes 393224 | tf_op jit(solution)/shard_map/ppermute | solution.py:236
  66.8 10.6 %collective-permute-start.25 = (f16[256,256]{1,0:T(8,128)(2,1)S(1)}, f16[256,256]{1,0:T(8,128)(2,1)S(1)}, u32[]{:S(2)}, u32[]{:S(2)}) collective-permute-start(f16[256,256]{1,0:T(8,128)(2,1)S(1)} %add_convert_fusion.1), channel_id=1, source_target_pairs={{0,12},{1,13},{2,14},{3,15},{4,8},{5,9},{6,10},{7,11},{8,4},{9,5},... | collective-permute-start | bytes 393224 | tf_op jit(solution)/shard_map/ppermute | solution.py:236
  72.6 8.5 %collective-permute-start.22 = (f16[256,256]{1,0:T(8,128)(2,1)S(1)}, f16[256,256]{1,0:T(8,128)(2,1)S(1)}, u32[]{:S(2)}, u32[]{:S(2)}) collective-permute-start(f16[256,256]{1,0:T(8,128)(2,1)S(1)} %add_convert_fusion.2), channel_id=1, source_target_pairs={{0,6},{1,7},{2,4},{3,5},{4,2},{5,3},{6,0},{7,1},{8,14},{9,15},{10,... | collective-permute-start | bytes 393224 | tf_op jit(solution)/shard_map/ppermute | solution.py:265
  76.5 7.9 %collective-permute-start.21 = (f16[256,256]{1,0:T(8,128)(2,1)S(1)}, f16[256,256]{1,0:T(8,128)(2,1)S(1)}, u32[]{:S(2)}, u32[]{:S(2)}) collective-permute-start(f16[256,256]{1,0:T(8,128)(2,1)S(1)} %add_convert_fusion.2), channel_id=1, source_target_pairs={{0,2},{1,5},{2,0},{3,7},{4,6},{5,1},{6,4},{7,3},{8,10},{9,13},{10,... | collective-permute-start | bytes 393224 | tf_op jit(solution)/shard_map/ppermute | solution.py:236
  77.5 7.0 %collective-permute-start.20 = (f16[256,256]{1,0:T(8,128)(2,1)S(1)}, f16[256,256]{1,0:T(8,128)(2,1)S(1)}, u32[]{:S(2)}, u32[]{:S(2)}) collective-permute-start(f16[256,256]{1,0:T(8,128)(2,1)S(1)} %add_convert_fusion.2), channel_id=1, source_target_pairs={{0,4},{1,3},{2,6},{3,1},{4,0},{5,7},{6,2},{7,5},{8,12},{9,11},{10,... | collective-permute-start | bytes 393224 | tf_op jit(solution)/shard_map/ppermute | solution.py:236
  77.5 9.1 %collective-permute-start.28 = (f16[256,256]{1,0:T(8,128)(2,1)S(1)}, f16[256,256]{1,0:T(8,128)(2,1)S(1)}, u32[]{:S(2)}, u32[]{:S(2)}) collective-permute-start(f16[256,256]{1,0:T(8,128)(2,1)S(1)} %add_convert_fusion), channel_id=1, source_target_pairs={{0,6},{1,7},{2,4},{3,5},{4,2},{5,3},{6,0},{7,1},{8,14},{9,15},{10,... | collective-permute-start | bytes 393224 | tf_op jit(solution)/shard_map/ppermute | solution.py:265
  80.1 7.7 %collective-permute-start.27 = (f16[256,256]{1,0:T(8,128)(2,1)S(1)}, f16[256,256]{1,0:T(8,128)(2,1)S(1)}, u32[]{:S(2)}, u32[]{:S(2)}) collective-permute-start(f16[256,256]{1,0:T(8,128)(2,1)S(1)} %add_convert_fusion), channel_id=1, source_target_pairs={{0,2},{1,5},{2,0},{3,7},{4,6},{5,1},{6,4},{7,3},{8,10},{9,13},{10,... | collective-permute-start | bytes 393224 | tf_op jit(solution)/shard_map/ppermute | solution.py:236
  81.1 6.7 %collective-permute-start.26 = (f16[256,256]{1,0:T(8,128)(2,1)S(1)}, f16[256,256]{1,0:T(8,128)(2,1)S(1)}, u32[]{:S(2)}, u32[]{:S(2)}) collective-permute-start(f16[256,256]{1,0:T(8,128)(2,1)S(1)} %add_convert_fusion), channel_id=1, source_target_pairs={{0,4},{1,3},{2,6},{3,1},{4,0},{5,7},{6,2},{7,5},{8,12},{9,11},{10,... | collective-permute-start | bytes 393224 | tf_op jit(solution)/shard_map/ppermute | solution.py:236
  88.5 1.2 %collective-permute-start.29 = (f32[8,128]{1,0:T(8,128)S(1)}, f32[8,128]{1,0:T(8,128)S(1)}, u32[]{:S(2)}, u32[]{:S(2)}) collective-permute-start(f32[8,128]{1,0:T(8,128)S(1)} %correlate.3.corr_a), channel_id=1, source_target_pairs={{0,1},{1,0},{2,3},{3,2},{4,5},{5,4},{6,7},{7,6},{8,9},{9,8},{10,11... | collective-permute-start | bytes 12296 | tf_op jit(solution)/shard_map/ppermute | solution.py:239
  90.9 1.2 %collective-permute-start.30 = (f32[8,128]{1,0:T(8,128)S(1)}, f32[8,128]{1,0:T(8,128)S(1)}, u32[]{:S(2)}, u32[]{:S(2)}) collective-permute-start(f32[8,128]{1,0:T(8,128)S(1)} %get-tuple-element.65.weight_a), channel_id=1, source_target_pairs={{0,1},{1,0},{2,3},{3,2},{4,5},{5,4},{6,7},{7,6},{8,9},{9,8},{10,11... | collective-permute-start | bytes 12296 | tf_op jit(solution)/shard_map/ppermute | solution.py:239

commit v9 on v8

--- a/solution.py
+++ b/solution.py
@@ -117,7 +117,23 @@
         out_ref[rows, :] = scale * jnp.dot(left_ref[rows, :], right_ref[...], preferred_element_type=F32)
 
 
-def sent_half(chunk, reach, weights, own, other, right, masked):
+def own_part(own, right):
+    pairs, width, cols = right.shape
+    step = width // 4
+
+    def kernel(own_ref, right_ref, part_ref):
+        here = pl.ds(pl.multiple_of(lax.axis_index("col") * cols, cols), cols)
+        for k in range(pairs):
+            near = right_ref[k, here, :]
+            for r in range(0, width, step):
+                part_ref[k * width + r:k * width + r + step, :] = jnp.dot(
+                    own_ref[r:r + step, :], near, preferred_element_type=F32)
+
+    return call(kernel, "own_part", SDS((pairs * width, cols), F32), VMEM, [VMEM] * 2, (own, right),
+                2 * pairs * width * cols * cols, 2 ** 20)
+
+
+def sent_half(chunk, reach, weights, own, other, right, masked, part):
     pairs, width, cols = right.shape
     size, half = cols // CHUNKS, width // 2
     at = slice(chunk * size, (chunk + 1) * size)
@@ -131,13 +147,16 @@
         for k in range(pairs):
             near, far = right_ref[k, here, at], right_ref[k, there, at]
             for r in range(0, width, step):
-                inner_ref[k * width + r:k * width + r + step, :] = (
-                    jnp.dot(own_ref[r:r + step, :], near, preferred_element_type=F32)
+                rows = slice(k * width + r, k * width + r + step)
+                inner_ref[rows, :] = (
+                    (jnp.dot(own_ref[r:r + step, :], near, preferred_element_type=F32) if part is None
+                     else own_ref[rows, at])
                     + jnp.dot(other_ref[r:r + step, :], far, preferred_element_type=F32)).astype(BF16)
         product(send_ref, scale, masked_ref, inner_ref, 2)
 
     return call(kernel, "sent_half_%d" % chunk, (SDS((pairs * width, size), BF16), SDS((half, size), F32)),
-                (VMEM, VMEM), [VMEM] * 6, (*weights, own, other, right, masked),
+                (VMEM, VMEM), [VMEM] * 6,
+                (*weights, own if part is None else part, other, right, masked),
                 3 * pairs * width * width * size, 2 ** 20)
 
 
@@ -277,9 +296,10 @@
     for step in range(STEPS):
         other = across(own)
         weights = (weight, across(weight))
+        part = own_part(own, right) if step else None
         inners, keeps, gots = [], [], []
         for c in range(CHUNKS):
-            inner, send = sent_half(c, reach, weights, own, other, right, sent)
+            inner, send = sent_half(c, reach, weights, own, other, right, sent, part)
             gots.append(begin(send))
             inners.append(inner)
             own, other = lax.optimization_barrier((own, other, inner))[:2]

time: 93.9 us -> 93.2 us (level)
    ppermute x7, waiting for transfers between devices: 5.47 us -> 4.21 us  [across(): return lax.ppermute(x, 'col', [(c, c ^ 1) for c in range(cols)])]
    ppermute x20, waiting for transfers between devices: 12 us -> 13.2 us  [swap(): return lax.ppermute(x, BOTH, pairing)]
    pallas_call x16 -> x17, Pallas kernels: 20.9 us -> 20.7 us  [call(): pl.pallas_call(kernel, out_shape=outs, in_specs=in_specs, out_specs=out_s...]
  transfers between devices with their start and end apart: 31 -> 31, of which waited for: 15 -> 15; matrix products, arithmetic and copies ran while one was open for 2% -> 2% of each run, Pallas kernels for 12% -> 13%
where the time goes in v9:
time: 93.2 us; the launch traced here: 93 us
  starting transfers between devices  49.9 us (54%)
  Pallas kernels  20.7 us (22%)
  waiting for transfers between devices  19.3 us (21%)
  other arithmetic  2.3 us (2%)
    ppermute x20, starting transfers between devices, swap(): return lax.ppermute(x, BOTH, pairing)  34.7 us
    pallas_call x17, Pallas kernels, call(): pl.pallas_call(kernel, out_shape=outs, in_specs=in_specs, out_specs=out_s...  20.7 us
    ppermute x4, starting transfers between devices, gathered(): lax.ppermute(piece, BOTH, [(o * cols + c, (o ^ 3) * cols + c) for o in ra...  13.7 us
    ppermute x20, waiting for transfers between devices, swap(): return lax.ppermute(x, BOTH, pairing)  13.2 us
    ppermute x7, waiting for transfers between devices, across(): return lax.ppermute(x, 'col', [(c, c ^ 1) for c in range(cols)])  4.21 us
    ppermute x4, waiting for transfers between devices, gathered(): lax.ppermute(piece, BOTH, [(o * cols + c, (o ^ 3) * cols + c) for o in ra...  1.9 us
  transfers between devices with their start and end apart: 31, of which 15 were waited for; matrix products, arithmetic and copies ran while one was open for 2% of the time, Pallas kernels for 13%

profile of v9, /device:TPU:0, one launch (start us, length us, event | category | flops | bytes accessed | tf_op | source)
XLA Modules:
  0.0 93.0 jit_solution(7725468693793849747)
XLA Ops:
  0.0 1.7 %open_vector.1 = (bf16[1024,512]{1,0:T(8,128)(2,1)S(1)}, f32[8,128]{1,0:T(8,128)S(1)}) custom-call(f32[1024,512]{1,0:T(8,128)} %vector_ref.1), custom_call_target="tpu_custom_call" | custom-call | flops 1572864 | bytes 4194304 | tf_op jit(solution)/shard_map/open_vector/pallas_call | solution.py:30
  1.7 0.5 collective-permute-start.1
  2.4 2.3 %sent_operators.1.masked_ref = bf16[512,2048]{1,0:T(8,128)(2,1)S(1)} custom-call(s32[128]{0:T(128)S(1)} %reshape.3.mask_ref, bf16[2,1024,1024]{2,1,0:T(8,128)(2,1)} %left_ref.3), custom_call_target="tpu_custom_call" | custom-call | flops 2097152 | bytes 4194304 | tf_op jit(solution)/shard_map/sent_operators/pallas_call | solution.py:30
  4.7 1.8 %sent_half_0.2 = (bf16[2048,256]{1,0:T(8,128)(2,1)S(1)}, f32[512,256]{1,0:T(8,128)S(1)}) custom-call(f32[8,128]{1,0:T(8,128)S(1)} %get-tuple-element.38.a_ref.weight_a, f32[8,128]{1,0:T(8,128)S(1)} %collective-permute-done.b_ref.weight_b, bf16[1024,512]{1,0:T(8,128)(2,1)S(1)} %get-tuple-element.41.own_ref, ...), custom_call_target="tpu_custom_call" | custom-call | flops 1610612736 | bytes 1048576 | tf_op jit(solution)/shard_map/sent_half_0/pallas_call | solution.py:30
  6.6 3.0 %collective-permute-start.2 = (f16[512,256]{1,0:T(8,128)(2,1)S(1)}, f16[512,256]{1,0:T(8,128)(2,1)S(1)}, u32[]{:S(2)}, u32[]{:S(2)}) collective-permute-start(f16[512,256]{1,0:T(8,128)(2,1)S(1)} %convert_element_type.116), channel_id=1, source_target_pairs={{0,2},{1,5},{2,0},{3,7},{4,6},{5,1},{6,4},{7,3},{8,10},{9,13},{10,... | collective-permute-start | bytes 786440 | tf_op jit(solution)/shard_map/ppermute | solution.py:255
  9.6 1.8 %sent_half_1.2 = (bf16[2048,256]{1,0:T(8,128)(2,1)S(1)}, f32[512,256]{1,0:T(8,128)S(1)}) custom-call(f32[8,128]{1,0:T(8,128)S(1)} %get-tuple-element.38.a_ref.weight_a, f32[8,128]{1,0:T(8,128)S(1)} %collective-permute-done.b_ref.weight_b, bf16[1024,512]{1,0:T(8,128)(2,1)S(1)} %get-tuple-element.41.own_ref, ...), custom_call_target="tpu_custom_call" | custom-call | flops 1610612736 | bytes 1048576 | tf_op jit(solution)/shard_map/sent_half_1/pallas_call | solution.py:30
  11.6 2.2 %kept_operators.1.masked_ref = bf16[512,2048]{1,0:T(8,128)(2,1)S(1)} custom-call(s32[128]{0:T(128)S(1)} %reshape.3.mask_ref, bf16[2,1024,1024]{2,1,0:T(8,128)(2,1)} %left_ref.3), custom_call_target="tpu_custom_call" | custom-call | flops 2097152 | bytes 4194304 | tf_op jit(solution)/shard_map/kept_operators/pallas_call | solution.py:30
  13.8 0.7 kept_half.4
  14.6 2.1 %collective-permute-start.3 = (f16[256,256]{1,0:T(8,128)(2,1)S(1)}, f16[256,256]{1,0:T(8,128)(2,1)S(1)}, u32[]{:S(2)}, u32[]{:S(2)}) collective-permute-start(f16[256,256]{1,0:T(8,128)(2,1)S(1)} %dynamic-slice_convert_fusion.3), channel_id=1, source_target_pairs={{0,4},{1,3},{2,6},{3,1},{4,0},{5,7},{6,2},{7,5},{8,12},{9,11},{10,... | collective-permute-start | bytes 393224 | tf_op jit(solution)/shard_map/ppermute | solution.py:255
  16.8 0.7 kept_half.5
  17.5 1.1 %collective-permute-done.8 = f16[512,256]{1,0:T(8,128)(2,1)S(1)} collective-permute-done((f16[512,256]{1,0:T(8,128)(2,1)S(1)}, f16[512,256]{1,0:T(8,128)(2,1)S(1)}, u32[]{:S(2)}, u32[]{:S(2)}) %collective-permute-start.8) | collective-permute-done | bytes 262176 | tf_op jit(solution)/shard_map/ppermute | solution.py:255
  18.7 1.5 %collective-permute-start.9 = (f16[256,256]{1,0:T(8,128)(2,1)S(1)}, f16[256,256]{1,0:T(8,128)(2,1)S(1)}, u32[]{:S(2)}, u32[]{:S(2)}) collective-permute-start(f16[256,256]{1,0:T(8,128)(2,1)S(1)} %dynamic-slice_convert_fusion.2), channel_id=1, source_target_pairs={{0,4},{1,3},{2,6},{3,1},{4,0},{5,7},{6,2},{7,5},{8,12},{9,11},{10,... | collective-permute-start | bytes 393224 | tf_op jit(solution)/shard_map/ppermute | solution.py:255
  20.3 3.6 %collective-permute-start.4 = (f16[256,256]{1,0:T(8,128)(2,1)S(1)}, f16[256,256]{1,0:T(8,128)(2,1)S(1)}, u32[]{:S(2)}, u32[]{:S(2)}) collective-permute-start(f16[256,256]{1,0:T(8,128)(2,1)S(1)} %add_convert_fusion.7), channel_id=1, source_target_pairs={{0,12},{1,13},{2,14},{3,15},{4,8},{5,9},{6,10},{7,11},{8,4},{9,5},... | collective-permute-start | bytes 393224 | tf_op jit(solution)/shard_map/ppermute | solution.py:255
  23.9 3.4 %collective-permute-start.10 = (f16[256,256]{1,0:T(8,128)(2,1)S(1)}, f16[256,256]{1,0:T(8,128)(2,1)S(1)}, u32[]{:S(2)}, u32[]{:S(2)}) collective-permute-start(f16[256,256]{1,0:T(8,128)(2,1)S(1)} %add_convert_fusion.5), channel_id=1, source_target_pairs={{0,12},{1,13},{2,14},{3,15},{4,8},{5,9},{6,10},{7,11},{8,4},{9,5},... | collective-permute-start | bytes 393224 | tf_op jit(solution)/shard_map/ppermute | solution.py:255
  27.3 1.7 %collective-permute-done.4 = f16[256,256]{1,0:T(8,128)(2,1)S(1)} collective-permute-done((f16[256,256]{1,0:T(8,128)(2,1)S(1)}, f16[256,256]{1,0:T(8,128)(2,1)S(1)}, u32[]{:S(2)}, u32[]{:S(2)}) %collective-permute-start.4) | collective-permute-done | bytes 131104 | tf_op jit(solution)/shard_map/ppermute | solution.py:255
  29.1 4.7 %collective-permute-start.7 = (f16[256,256]{1,0:T(8,128)(2,1)S(1)}, f16[256,256]{1,0:T(8,128)(2,1)S(1)}, u32[]{:S(2)}, u32[]{:S(2)}) collective-permute-start(f16[256,256]{1,0:T(8,128)(2,1)S(1)} %add_convert_fusion.6), channel_id=1, source_target_pairs={{0,6},{1,7},{2,4},{3,5},{4,2},{5,3},{6,0},{7,1},{8,14},{9,15},{10,... | collective-permute-start | bytes 393224 | tf_op jit(solution)/shard_map/ppermute | solution.py:284
  33.8 1.2 %collective-permute-start.6 = (f16[256,256]{1,0:T(8,128)(2,1)S(1)}, f16[256,256]{1,0:T(8,128)(2,1)S(1)}, u32[]{:S(2)}, u32[]{:S(2)}) collective-permute-start(f16[256,256]{1,0:T(8,128)(2,1)S(1)} %add_convert_fusion.6), channel_id=1, source_target_pairs={{0,2},{1,5},{2,0},{3,7},{4,6},{5,1},{6,4},{7,3},{8,10},{9,13},{10,... | collective-permute-start | bytes 393224 | tf_op jit(solution)/shard_map/ppermute | solution.py:255
  35.0 2.4 %collective-permute-start.13 = (f16[256,256]{1,0:T(8,128)(2,1)S(1)}, f16[256,256]{1,0:T(8,128)(2,1)S(1)}, u32[]{:S(2)}, u32[]{:S(2)}) collective-permute-start(f16[256,256]{1,0:T(8,128)(2,1)S(1)} %add_convert_fusion.4), channel_id=1, source_target_pairs={{0,6},{1,7},{2,4},{3,5},{4,2},{5,3},{6,0},{7,1},{8,14},{9,15},{10,... | collective-permute-start | bytes 393224 | tf_op jit(solution)/shard_map/ppermute | solution.py:284
  37.4 1.2 %collective-permute-start.12 = (f16[256,256]{1,0:T(8,128)(2,1)S(1)}, f16[256,256]{1,0:T(8,128)(2,1)S(1)}, u32[]{:S(2)}, u32[]{:S(2)}) collective-permute-start(f16[256,256]{1,0:T(8,128)(2,1)S(1)} %add_convert_fusion.4), channel_id=1, source_target_pairs={{0,2},{1,5},{2,0},{3,7},{4,6},{5,1},{6,4},{7,3},{8,10},{9,13},{10,... | collective-permute-start | bytes 393224 | tf_op jit(solution)/shard_map/ppermute | solution.py:255
  38.6 2.2 %collective-permute-start.11 = (f16[256,256]{1,0:T(8,128)(2,1)S(1)}, f16[256,256]{1,0:T(8,128)(2,1)S(1)}, u32[]{:S(2)}, u32[]{:S(2)}) collective-permute-start(f16[256,256]{1,0:T(8,128)(2,1)S(1)} %add_convert_fusion.4), channel_id=1, source_target_pairs={{0,4},{1,3},{2,6},{3,1},{4,0},{5,7},{6,2},{7,5},{8,12},{9,11},{10,... | collective-permute-start | bytes 393224 | tf_op jit(solution)/shard_map/ppermute | solution.py:255
  40.7 0.2 broadcast_select_fusion.31
  40.9 0.7 collective-permute-done.13
  41.7 1.3 %collective-permute-done.12 = f16[256,256]{1,0:T(8,128)(2,1)S(1)} collective-permute-done((f16[256,256]{1,0:T(8,128)(2,1)S(1)}, f16[256,256]{1,0:T(8,128)(2,1)S(1)}, u32[]{:S(2)}, u32[]{:S(2)}) %collective-permute-start.12) | collective-permute-done | bytes 131104 | tf_op jit(solution)/shard_map/ppermute | solution.py:255
  43.0 0.7 collective-permute-done.11
  43.7 0.2 broadcast_select_fusion.27
  43.9 0.2 maximum_convert_fusion
  44.1 0.3 correlate.2.corr_a
  44.5 1.2 %collective-permute-done.14.corr_b = f32[8,128]{1,0:T(8,128)S(1)} collective-permute-done((f32[8,128]{1,0:T(8,128)S(1)}, f32[8,128]{1,0:T(8,128)S(1)}, u32[]{:S(2)}, u32[]{:S(2)}) %collective-permute-start.14) | collective-permute-done | bytes 4128 | tf_op jit(solution)/shard_map/ppermute | solution.py:258
  45.7 1.0 %correct.2 = (f32[1024,512]{1,0:T(8,128)S(1)}, f32[8,128]{1,0:T(8,128)S(1)}, bf16[1024,512]{1,0:T(8,128)(2,1)S(1)}) custom-call(f32[8,128]{1,0:T(8,128)S(1)} %correlate.2.corr_a, f32[8,128]{1,0:T(8,128)S(1)} %collective-permute-done.14.corr_b, f32[8,128]{1,0:T(8,128)S(1)} %get-tuple-element.38.a_ref.weight_a, ...), custom_call_target="tpu_custom_call" | custom-call | flops 6291456 | bytes 1048576 | tf_op jit(solution)/shard_map/correct/pallas_call | solution.py:30
  46.7 0.2 collective-permute-start.16
  46.9 0.4 collective-permute-start.15
  47.3 1.2 %own_part.1.own_ref = f32[2048,512]{1,0:T(8,128)S(1)} custom-call(bf16[1024,512]{1,0:T(8,128)(2,1)S(1)} %get-tuple-element.54.own_ref, bf16[2,1024,512]{2,1,0:T(8,128)(2,1)S(1)} %copy-done), custom_call_target="tpu_custom_call" | custom-call | flops 1073741824 | bytes 1048576 | tf_op jit(solution)/shard_map/own_part/pallas_call | solution.py:30
  48.6 0.9 collective-permute-done.15.b_ref.weight_b
  49.5 1.3 %sent_half_0.3 = (bf16[2048,256]{1,0:T(8,128)(2,1)S(1)}, f32[512,256]{1,0:T(8,128)S(1)}) custom-call(f32[8,128]{1,0:T(8,128)S(1)} %get-tuple-element.53.a_ref.weight_a, f32[8,128]{1,0:T(8,128)S(1)} %collective-permute-done.15.b_ref.weight_b, f32[2048,512]{1,0:T(8,128)S(1)} %own_part.1.own_ref, bf16[1024,512]{1,0:T(8,128)(2,1)S(1)} %collective-permute-done.16.other_ref, ...), custom_call_target="tpu_custom_call" | custom-call | flops 1610612736 | bytes 1048576 | tf_op jit(solution)/shard_map/sent_half_0/pallas_call | solution.py:30
  50.8 1.1 %collective-permute-start.17 = (f16[512,256]{1,0:T(8,128)(2,1)S(1)}, f16[512,256]{1,0:T(8,128)(2,1)S(1)}, u32[]{:S(2)}, u32[]{:S(2)}) collective-permute-start(f16[512,256]{1,0:T(8,128)(2,1)S(1)} %convert_element_type.134), channel_id=1, source_target_pairs={{0,2},{1,5},{2,0},{3,7},{4,6},{5,1},{6,4},{7,3},{8,10},{9,13},{10,... | collective-permute-start | bytes 786440 | tf_op jit(solution)/shard_map/ppermute | solution.py:255
  51.9 1.3 %sent_half_1.3 = (bf16[2048,256]{1,0:T(8,128)(2,1)S(1)}, f32[512,256]{1,0:T(8,128)S(1)}) custom-call(f32[8,128]{1,0:T(8,128)S(1)} %get-tuple-element.53.a_ref.weight_a, f32[8,128]{1,0:T(8,128)S(1)} %collective-permute-done.15.b_ref.weight_b, f32[2048,512]{1,0:T(8,128)S(1)} %own_part.1.own_ref, bf16[1024,512]{1,0:T(8,128)(2,1)S(1)} %collective-permute-done.16.other_ref, ...), custom_call_target="tpu_custom_call" | custom-call | flops 1610612736 | bytes 1048576 | tf_op jit(solution)/shard_map/sent_half_1/pallas_call | solution.py:30
  53.3 1.1 %collective-permute-start.23 = (f16[512,256]{1,0:T(8,128)(2,1)S(1)}, f16[512,256]{1,0:T(8,128)(2,1)S(1)}, u32[]{:S(2)}, u32[]{:S(2)}) collective-permute-start(f16[512,256]{1,0:T(8,128)(2,1)S(1)} %convert_element_type.143), channel_id=1, source_target_pairs={{0,2},{1,5},{2,0},{3,7},{4,6},{5,1},{6,4},{7,3},{8,10},{9,13},{10,... | collective-permute-start | bytes 786440 | tf_op jit(solution)/shard_map/ppermute | solution.py:255
  54.3 0.7 kept_half.6
  55.1 2.2 %collective-permute-done.17 = f16[512,256]{1,0:T(8,128)(2,1)S(1)} collective-permute-done((f16[512,256]{1,0:T(8,128)(2,1)S(1)}, f16[512,256]{1,0:T(8,128)(2,1)S(1)}, u32[]{:S(2)}, u32[]{:S(2)}) %collective-permute-start.17) | collective-permute-done | bytes 262176 | tf_op jit(solution)/shard_map/ppermute | solution.py:255
  57.3 0.2 dynamic-slice_convert_fusion.1
  57.6 2.1 %collective-permute-start.18 = (f16[256,256]{1,0:T(8,128)(2,1)S(1)}, f16[256,256]{1,0:T(8,128)(2,1)S(1)}, u32[]{:S(2)}, u32[]{:S(2)}) collective-permute-start(f16[256,256]{1,0:T(8,128)(2,1)S(1)} %dynamic-slice_convert_fusion.1), channel_id=1, source_target_pairs={{0,4},{1,3},{2,6},{3,1},{4,0},{5,7},{6,2},{7,5},{8,12},{9,11},{10,... | collective-permute-start | bytes 393224 | tf_op jit(solution)/shard_map/ppermute | solution.py:255
  59.7 0.7 kept_half.7
  60.5 2.2 %collective-permute-start.24 = (f16[256,256]{1,0:T(8,128)(2,1)S(1)}, f16[256,256]{1,0:T(8,128)(2,1)S(1)}, u32[]{:S(2)}, u32[]{:S(2)}) collective-permute-start(f16[256,256]{1,0:T(8,128)(2,1)S(1)} %dynamic-slice_convert_fusion), channel_id=1, source_target_pairs={{0,4},{1,3},{2,6},{3,1},{4,0},{5,7},{6,2},{7,5},{8,12},{9,11},{10,... | collective-permute-start | bytes 393224 | tf_op jit(solution)/shard_map/ppermute | solution.py:255
  62.8 2.8 %collective-permute-start.19 = (f16[256,256]{1,0:T(8,128)(2,1)S(1)}, f16[256,256]{1,0:T(8,128)(2,1)S(1)}, u32[]{:S(2)}, u32[]{:S(2)}) collective-permute-start(f16[256,256]{1,0:T(8,128)(2,1)S(1)} %add_convert_fusion.3), channel_id=1, source_target_pairs={{0,12},{1,13},{2,14},{3,15},{4,8},{5,9},{6,10},{7,11},{8,4},{9,5},... | collective-permute-start | bytes 393224 | tf_op jit(solution)/shard_map/ppermute | solution.py:255
  65.6 0.5 collective-permute-done.24
  66.1 2.7 %collective-permute-start.25 = (f16[256,256]{1,0:T(8,128)(2,1)S(1)}, f16[256,256]{1,0:T(8,128)(2,1)S(1)}, u32[]{:S(2)}, u32[]{:S(2)}) collective-permute-start(f16[256,256]{1,0:T(8,128)(2,1)S(1)} %add_convert_fusion.1), channel_id=1, source_target_pairs={{0,12},{1,13},{2,14},{3,15},{4,8},{5,9},{6,10},{7,11},{8,4},{9,5},... | collective-permute-start | bytes 393224 | tf_op jit(solution)/shard_map/ppermute | solution.py:255
  68.8 3.0 %collective-permute-done.19 = f16[256,256]{1,0:T(8,128)(2,1)S(1)} collective-permute-done((f16[256,256]{1,0:T(8,128)(2,1)S(1)}, f16[256,256]{1,0:T(8,128)(2,1)S(1)}, u32[]{:S(2)}, u32[]{:S(2)}) %collective-permute-start.19) | collective-permute-done | bytes 131104 | tf_op jit(solution)/shard_map/ppermute | solution.py:255
  71.9 4.2 %collective-permute-start.22 = (f16[256,256]{1,0:T(8,128)(2,1)S(1)}, f16[256,256]{1,0:T(8,128)(2,1)S(1)}, u32[]{:S(2)}, u32[]{:S(2)}) collective-permute-start(f16[256,256]{1,0:T(8,128)(2,1)S(1)} %add_convert_fusion.2), channel_id=1, source_target_pairs={{0,6},{1,7},{2,4},{3,5},{4,2},{5,3},{6,0},{7,1},{8,14},{9,15},{10,... | collective-permute-start | bytes 393224 | tf_op jit(solution)/shard_map/ppermute | solution.py:284
  76.0 1.1 %collective-permute-start.21 = (f16[256,256]{1,0:T(8,128)(2,1)S(1)}, f16[256,256]{1,0:T(8,128)(2,1)S(1)}, u32[]{:S(2)}, u32[]{:S(2)}) collective-permute-start(f16[256,256]{1,0:T(8,128)(2,1)S(1)} %add_convert_fusion.2), channel_id=1, source_target_pairs={{0,2},{1,5},{2,0},{3,7},{4,6},{5,1},{6,4},{7,3},{8,10},{9,13},{10,... | collective-permute-start | bytes 393224 | tf_op jit(solution)/shard_map/ppermute | solution.py:255
  77.2 2.5 %collective-permute-start.28 = (f16[256,256]{1,0:T(8,128)(2,1)S(1)}, f16[256,256]{1,0:T(8,128)(2,1)S(1)}, u32[]{:S(2)}, u32[]{:S(2)}) collective-permute-start(f16[256,256]{1,0:T(8,128)(2,1)S(1)} %add_convert_fusion), channel_id=1, source_target_pairs={{0,6},{1,7},{2,4},{3,5},{4,2},{5,3},{6,0},{7,1},{8,14},{9,15},{10,... | collective-permute-start | bytes 393224 | tf_op jit(solution)/shard_map/ppermute | solution.py:284
  79.6 1.1 %collective-permute-start.27 = (f16[256,256]{1,0:T(8,128)(2,1)S(1)}, f16[256,256]{1,0:T(8,128)(2,1)S(1)}, u32[]{:S(2)}, u32[]{:S(2)}) collective-permute-start(f16[256,256]{1,0:T(8,128)(2,1)S(1)} %add_convert_fusion), channel_id=1, source_target_pairs={{0,2},{1,5},{2,0},{3,7},{4,6},{5,1},{6,4},{7,3},{8,10},{9,13},{10,... | collective-permute-start | bytes 393224 | tf_op jit(solution)/shard_map/ppermute | solution.py:255
  80.7 2.4 %collective-permute-start.26 = (f16[256,256]{1,0:T(8,128)(2,1)S(1)}, f16[256,256]{1,0:T(8,128)(2,1)S(1)}, u32[]{:S(2)}, u32[]{:S(2)}) collective-permute-start(f16[256,256]{1,0:T(8,128)(2,1)S(1)} %add_convert_fusion), channel_id=1, source_target_pairs={{0,4},{1,3},{2,6},{3,1},{4,0},{5,7},{6,2},{7,5},{8,12},{9,11},{10,... | collective-permute-start | bytes 393224 | tf_op jit(solution)/shard_map/ppermute | solution.py:255
  83.1 1.5 %collective-permute-done.21 = f16[256,256]{1,0:T(8,128)(2,1)S(1)} collective-permute-done((f16[256,256]{1,0:T(8,128)(2,1)S(1)}, f16[256,256]{1,0:T(8,128)(2,1)S(1)}, u32[]{:S(2)}, u32[]{:S(2)}) %collective-permute-start.21) | collective-permute-done | bytes 131104 | tf_op jit(solution)/shard_map/ppermute | solution.py:255
  84.6 0.2 broadcast_select_fusion.23
  84.7 0.1 maximum_convert_fusion.2.refs_0_
  84.9 1.2 %collective-permute-done.28 = f16[256,256]{1,0:T(8,128)(2,1)S(1)} collective-permute-done((f16[256,256]{1,0:T(8,128)(2,1)S(1)}, f16[256,256]{1,0:T(8,128)(2,1)S(1)}, u32[]{:S(2)}, u32[]{:S(2)}) %collective-permute-start.28) | collective-permute-done | bytes 131104 | tf_op jit(solution)/shard_map/ppermute | solution.py:284
  86.0 1.2 %collective-permute-done.27 = f16[256,256]{1,0:T(8,128)(2,1)S(1)} collective-permute-done((f16[256,256]{1,0:T(8,128)(2,1)S(1)}, f16[256,256]{1,0:T(8,128)(2,1)S(1)}, u32[]{:S(2)}, u32[]{:S(2)}) %collective-permute-start.27) | collective-permute-done | bytes 131104 | tf_op jit(solution)/shard_map/ppermute | solution.py:255
  87.2 0.2 broadcast_select_fusion.19
  87.5 0.4 correlate.3.corr_a
  87.9 1.2 %collective-permute-done.29.corr_b = f32[8,128]{1,0:T(8,128)S(1)} collective-permute-done((f32[8,128]{1,0:T(8,128)S(1)}, f32[8,128]{1,0:T(8,128)S(1)}, u32[]{:S(2)}, u32[]{:S(2)}) %collective-permute-start.29) | collective-permute-done | bytes 4128 | tf_op jit(solution)/shard_map/ppermute | solution.py:258
  89.1 1.1 %correct.3 = (f32[1024,512]{1,0:T(8,128)S(1)}, f32[8,128]{1,0:T(8,128)S(1)}) custom-call(f32[8,128]{1,0:T(8,128)S(1)} %correlate.3.corr_a, f32[8,128]{1,0:T(8,128)S(1)} %collective-permute-done.29.corr_b, f32[8,128]{1,0:T(8,128)S(1)} %get-tuple-element.53.a_ref.weight_a, f32[8,128]{1,0:T(8,128)S(1)} %collective-permute-done.15.b_ref.weight_b, ...), custom_call_target="tpu_custom_call" | custom-call | flops 6291456 | bytes 1048576 | tf_op jit(solution)/shard_map/correct/pallas_call | solution.py:30
  90.1 0.2 collective-permute-start.30
  90.4 1.0 %collective-permute-done.30.weight_b = f32[8,128]{1,0:T(8,128)S(1)} collective-permute-done((f32[8,128]{1,0:T(8,128)S(1)}, f32[8,128]{1,0:T(8,128)S(1)}, u32[]{:S(2)}, u32[]{:S(2)}) %collective-permute-start.30) | collective-permute-done | bytes 4128 | tf_op jit(solution)/shard_map/ppermute | solution.py:258
  91.4 1.4 %normalise.1 = f32[1024,512]{1,0:T(8,128)} custom-call(f32[8,128]{1,0:T(8,128)S(1)} %get-tuple-element.63.weight_a, f32[8,128]{1,0:T(8,128)S(1)} %collective-permute-done.30.weight_b, f32[1024,512]{1,0:T(8,128)S(1)} %get-tuple-element.64.vector_ref), custom_call_target="tpu_custom_call" | custom-call | flops 524288 | bytes 4194304 | tf_op jit(solution)/shard_map/normalise/pallas_call | solution.py:30
  (51 shorter events, 1.6 us)
Async XLA Ops:
  0.0 2.3 %copy-start.3 = (s32[2,8,8]{2,1,0:T(8,128)S(1)}, s32[2,8,8]{2,1,0:T(8,128)}, u32[]{:S(2)}) copy-start(s32[2,8,8]{2,1,0:T(8,128)} %param.9) | copy-start | bytes 1540
  1.7 3.0 %collective-permute-start.1 = (bf16[1024,512]{1,0:T(8,128)(2,1)S(1)}, bf16[1024,512]{1,0:T(8,128)(2,1)S(1)}, u32[]{:S(2)}, u32[]{:S(2)}) collective-permute-start(bf16[1024,512]{1,0:T(8,128)(2,1)S(1)} %get-tuple-element.41.own_ref), channel_id=1, source_target_pairs={{0,1},{1,0},{2,3},{3,2},{4,5},{5,4},{6,7},{7,6},{8,9},{9,8},{10,11... | collective-permute-start | bytes 3145736 | tf_op jit(solution)/shard_map/ppermute | solution.py:258
  2.3 2.5 %collective-permute-start = (f32[8,128]{1,0:T(8,128)S(1)}, f32[8,128]{1,0:T(8,128)S(1)}, u32[]{:S(2)}, u32[]{:S(2)}) collective-permute-start(f32[8,128]{1,0:T(8,128)S(1)} %get-tuple-element.38.a_ref.weight_a), channel_id=1, source_target_pairs={{0,1},{1,0},{2,3},{3,2},{4,5},{5,4},{6,7},{7,6},{8,9},{9,8},{10,11... | collective-permute-start | bytes 12296 | tf_op jit(solution)/shard_map/ppermute | solution.py:258
  2.4 2.3 %copy-start = (bf16[2,1024,512]{2,1,0:T(8,128)(2,1)S(1)}, bf16[2,1024,512]{2,1,0:T(8,128)(2,1)}, u32[]{:S(2)}) copy-start(bf16[2,1024,512]{2,1,0:T(8,128)(2,1)} %right_ref.9) | copy-start | bytes 6291460
  6.6 7.9 %collective-permute-start.2 = (f16[512,256]{1,0:T(8,128)(2,1)S(1)}, f16[512,256]{1,0:T(8,128)(2,1)S(1)}, u32[]{:S(2)}, u32[]{:S(2)}) collective-permute-start(f16[512,256]{1,0:T(8,128)(2,1)S(1)} %convert_element_type.116), channel_id=1, source_target_pairs={{0,2},{1,5},{2,0},{3,7},{4,6},{5,1},{6,4},{7,3},{8,10},{9,13},{10,... | collective-permute-start | bytes 786440 | tf_op jit(solution)/shard_map/ppermute | solution.py:255
  11.5 7.1 %collective-permute-start.8 = (f16[512,256]{1,0:T(8,128)(2,1)S(1)}, f16[512,256]{1,0:T(8,128)(2,1)S(1)}, u32[]{:S(2)}, u32[]{:S(2)}) collective-permute-start(f16[512,256]{1,0:T(8,128)(2,1)S(1)} %convert_element_type.125), channel_id=1, source_target_pairs={{0,2},{1,5},{2,0},{3,7},{4,6},{5,1},{6,4},{7,3},{8,10},{9,13},{10,... | collective-permute-start | bytes 786440 | tf_op jit(solution)/shard_map/ppermute | solution.py:255
  14.6 5.6 %collective-permute-start.3 = (f16[256,256]{1,0:T(8,128)(2,1)S(1)}, f16[256,256]{1,0:T(8,128)(2,1)S(1)}, u32[]{:S(2)}, u32[]{:S(2)}) collective-permute-start(f16[256,256]{1,0:T(8,128)(2,1)S(1)} %dynamic-slice_convert_fusion.3), channel_id=1, source_target_pairs={{0,4},{1,3},{2,6},{3,1},{4,0},{5,7},{6,2},{7,5},{8,12},{9,11},{10,... | collective-permute-start | bytes 393224 | tf_op jit(solution)/shard_map/ppermute | solution.py:255
  18.7 5.2 %collective-permute-start.9 = (f16[256,256]{1,0:T(8,128)(2,1)S(1)}, f16[256,256]{1,0:T(8,128)(2,1)S(1)}, u32[]{:S(2)}, u32[]{:S(2)}) collective-permute-start(f16[256,256]{1,0:T(8,128)(2,1)S(1)} %dynamic-slice_convert_fusion.2), channel_id=1, source_target_pairs={{0,4},{1,3},{2,6},{3,1},{4,0},{5,7},{6,2},{7,5},{8,12},{9,11},{10,... | collective-permute-start | bytes 393224 | tf_op jit(solution)/shard_map/ppermute | solution.py:255
  20.3 8.8 %collective-permute-start.4 = (f16[256,256]{1,0:T(8,128)(2,1)S(1)}, f16[256,256]{1,0:T(8,128)(2,1)S(1)}, u32[]{:S(2)}, u32[]{:S(2)}) collective-permute-start(f16[256,256]{1,0:T(8,128)(2,1)S(1)} %add_convert_fusion.7), channel_id=1, source_target_pairs={{0,12},{1,13},{2,14},{3,15},{4,8},{5,9},{6,10},{7,11},{8,4},{9,5},... | collective-permute-start | bytes 393224 | tf_op jit(solution)/shard_map/ppermute | solution.py:255
  23.9 11.0 %collective-permute-start.10 = (f16[256,256]{1,0:T(8,128)(2,1)S(1)}, f16[256,256]{1,0:T(8,128)(2,1)S(1)}, u32[]{:S(2)}, u32[]{:S(2)}) collective-permute-start(f16[256,256]{1,0:T(8,128)(2,1)S(1)} %add_convert_fusion.5), channel_id=1, source_target_pairs={{0,12},{1,13},{2,14},{3,15},{4,8},{5,9},{6,10},{7,11},{8,4},{9,5},... | collective-permute-start | bytes 393224 | tf_op jit(solution)/shard_map/ppermute | solution.py:255
  29.1 9.5 %collective-permute-start.7 = (f16[256,256]{1,0:T(8,128)(2,1)S(1)}, f16[256,256]{1,0:T(8,128)(2,1)S(1)}, u32[]{:S(2)}, u32[]{:S(2)}) collective-permute-start(f16[256,256]{1,0:T(8,128)(2,1)S(1)} %add_convert_fusion.6), channel_id=1, source_target_pairs={{0,6},{1,7},{2,4},{3,5},{4,2},{5,3},{6,0},{7,1},{8,14},{9,15},{10,... | collective-permute-start | bytes 393224 | tf_op jit(solution)/shard_map/ppermute | solution.py:284
  33.8 7.0 %collective-permute-start.6 = (f16[256,256]{1,0:T(8,128)(2,1)S(1)}, f16[256,256]{1,0:T(8,128)(2,1)S(1)}, u32[]{:S(2)}, u32[]{:S(2)}) collective-permute-start(f16[256,256]{1,0:T(8,128)(2,1)S(1)} %add_convert_fusion.6), channel_id=1, source_target_pairs={{0,2},{1,5},{2,0},{3,7},{4,6},{5,1},{6,4},{7,3},{8,10},{9,13},{10,... | collective-permute-start | bytes 393224 | tf_op jit(solution)/shard_map/ppermute | solution.py:255
  35.0 5.8 %collective-permute-start.5 = (f16[256,256]{1,0:T(8,128)(2,1)S(1)}, f16[256,256]{1,0:T(8,128)(2,1)S(1)}, u32[]{:S(2)}, u32[]{:S(2)}) collective-permute-start(f16[256,256]{1,0:T(8,128)(2,1)S(1)} %add_convert_fusion.6), channel_id=1, source_target_pairs={{0,4},{1,3},{2,6},{3,1},{4,0},{5,7},{6,2},{7,5},{8,12},{9,11},{10,... | collective-permute-start | bytes 393224 | tf_op jit(solution)/shard_map/ppermute | solution.py:255
  35.0 6.7 %collective-permute-start.13 = (f16[256,256]{1,0:T(8,128)(2,1)S(1)}, f16[256,256]{1,0:T(8,128)(2,1)S(1)}, u32[]{:S(2)}, u32[]{:S(2)}) collective-permute-start(f16[256,256]{1,0:T(8,128)(2,1)S(1)} %add_convert_fusion.4), channel_id=1, source_target_pairs={{0,6},{1,7},{2,4},{3,5},{4,2},{5,3},{6,0},{7,1},{8,14},{9,15},{10,... | collective-permute-start | bytes 393224 | tf_op jit(solution)/shard_map/ppermute | solution.py:284
  37.4 5.6 %collective-permute-start.12 = (f16[256,256]{1,0:T(8,128)(2,1)S(1)}, f16[256,256]{1,0:T(8,128)(2,1)S(1)}, u32[]{:S(2)}, u32[]{:S(2)}) collective-permute-start(f16[256,256]{1,0:T(8,128)(2,1)S(1)} %add_convert_fusion.4), channel_id=1, source_target_pairs={{0,2},{1,5},{2,0},{3,7},{4,6},{5,1},{6,4},{7,3},{8,10},{9,13},{10,... | collective-permute-start | bytes 393224 | tf_op jit(solution)/shard_map/ppermute | solution.py:255
  38.6 5.1 %collective-permute-start.11 = (f16[256,256]{1,0:T(8,128)(2,1)S(1)}, f16[256,256]{1,0:T(8,128)(2,1)S(1)}, u32[]{:S(2)}, u32[]{:S(2)}) collective-permute-start(f16[256,256]{1,0:T(8,128)(2,1)S(1)} %add_convert_fusion.4), channel_id=1, source_target_pairs={{0,4},{1,3},{2,6},{3,1},{4,0},{5,7},{6,2},{7,5},{8,12},{9,11},{10,... | collective-permute-start | bytes 393224 | tf_op jit(solution)/shard_map/ppermute | solution.py:255
  40.9 3.2 %copy-start.1 = (f32[1024,512]{1,0:T(8,128)S(1)}, f32[1024,512]{1,0:T(8,128)}, u32[]{:S(2)}) copy-start(f32[1024,512]{1,0:T(8,128)} %vector_ref.1) | copy-start | bytes 6291460
  44.1 1.6 %copy-start.2 = (f32[1024,512]{1,0:T(8,128)S(1)}, f32[1024,512]{1,0:T(8,128)}, u32[]{:S(2)}) copy-start(f32[1024,512]{1,0:T(8,128)} %diag_ref.3) | copy-start | bytes 6291460
  44.4 1.2 %collective-permute-start.14 = (f32[8,128]{1,0:T(8,128)S(1)}, f32[8,128]{1,0:T(8,128)S(1)}, u32[]{:S(2)}, u32[]{:S(2)}) collective-permute-start(f32[8,128]{1,0:T(8,128)S(1)} %correlate.2.corr_a), channel_id=1, source_target_pairs={{0,1},{1,0},{2,3},{3,2},{4,5},{5,4},{6,7},{7,6},{8,9},{9,8},{10,11... | collective-permute-start | bytes 12296 | tf_op jit(solution)/shard_map/ppermute | solution.py:258
  46.7 2.7 %collective-permute-start.16 = (bf16[1024,512]{1,0:T(8,128)(2,1)S(1)}, bf16[1024,512]{1,0:T(8,128)(2,1)S(1)}, u32[]{:S(2)}, u32[]{:S(2)}) collective-permute-start(bf16[1024,512]{1,0:T(8,128)(2,1)S(1)} %get-tuple-element.54.own_ref), channel_id=1, source_target_pairs={{0,1},{1,0},{2,3},{3,2},{4,5},{5,4},{6,7},{7,6},{8,9},{9,8},{10,11... | collective-permute-start | bytes 3145736 | tf_op jit(solution)/shard_map/ppermute | solution.py:258
  46.9 2.5 %collective-permute-start.15 = (f32[8,128]{1,0:T(8,128)S(1)}, f32[8,128]{1,0:T(8,128)S(1)}, u32[]{:S(2)}, u32[]{:S(2)}) collective-permute-start(f32[8,128]{1,0:T(8,128)S(1)} %get-tuple-element.53.a_ref.weight_a), channel_id=1, source_target_pairs={{0,1},{1,0},{2,3},{3,2},{4,5},{5,4},{6,7},{7,6},{8,9},{9,8},{10,11... | collective-permute-start | bytes 12296 | tf_op jit(solution)/shard_map/ppermute | solution.py:258
  50.8 6.4 %collective-permute-start.17 = (f16[512,256]{1,0:T(8,128)(2,1)S(1)}, f16[512,256]{1,0:T(8,128)(2,1)S(1)}, u32[]{:S(2)}, u32[]{:S(2)}) collective-permute-start(f16[512,256]{1,0:T(8,128)(2,1)S(1)} %convert_element_type.134), channel_id=1, source_target_pairs={{0,2},{1,5},{2,0},{3,7},{4,6},{5,1},{6,4},{7,3},{8,10},{9,13},{10,... | collective-permute-start | bytes 786440 | tf_op jit(solution)/shard_map/ppermute | solution.py:255
  53.3 7.1 %collective-permute-start.23 = (f16[512,256]{1,0:T(8,128)(2,1)S(1)}, f16[512,256]{1,0:T(8,128)(2,1)S(1)}, u32[]{:S(2)}, u32[]{:S(2)}) collective-permute-start(f16[512,256]{1,0:T(8,128)(2,1)S(1)} %convert_element_type.143), channel_id=1, source_target_pairs={{0,2},{1,5},{2,0},{3,7},{4,6},{5,1},{6,4},{7,3},{8,10},{9,13},{10,... | collective-permute-start | bytes 786440 | tf_op jit(solution)/shard_map/ppermute | solution.py:255
  57.6 5.2 %collective-permute-start.18 = (f16[256,256]{1,0:T(8,128)(2,1)S(1)}, f16[256,256]{1,0:T(8,128)(2,1)S(1)}, u32[]{:S(2)}, u32[]{:S(2)}) collective-permute-start(f16[256,256]{1,0:T(8,128)(2,1)S(1)} %dynamic-slice_convert_fusion.1), channel_id=1, source_target_pairs={{0,4},{1,3},{2,6},{3,1},{4,0},{5,7},{6,2},{7,5},{8,12},{9,11},{10,... | collective-permute-start | bytes 393224 | tf_op jit(solution)/shard_map/ppermute | solution.py:255
  60.5 5.5 %collective-permute-start.24 = (f16[256,256]{1,0:T(8,128)(2,1)S(1)}, f16[256,256]{1,0:T(8,128)(2,1)S(1)}, u32[]{:S(2)}, u32[]{:S(2)}) collective-permute-start(f16[256,256]{1,0:T(8,128)(2,1)S(1)} %dynamic-slice_convert_fusion), channel_id=1, source_target_pairs={{0,4},{1,3},{2,6},{3,1},{4,0},{5,7},{6,2},{7,5},{8,12},{9,11},{10,... | collective-permute-start | bytes 393224 | tf_op jit(solution)/shard_map/ppermute | solution.py:255
  62.8 9.0 %collective-permute-start.19 = (f16[256,256]{1,0:T(8,128)(2,1)S(1)}, f16[256,256]{1,0:T(8,128)(2,1)S(1)}, u32[]{:S(2)}, u32[]{:S(2)}) collective-permute-start(f16[256,256]{1,0:T(8,128)(2,1)S(1)} %add_convert_fusion.3), channel_id=1, source_target_pairs={{0,12},{1,13},{2,14},{3,15},{4,8},{5,9},{6,10},{7,11},{8,4},{9,5},... | collective-permute-start | bytes 393224 | tf_op jit(solution)/shard_map/ppermute | solution.py:255
  66.1 11.0 %collective-permute-start.25 = (f16[256,256]{1,0:T(8,128)(2,1)S(1)}, f16[256,256]{1,0:T(8,128)(2,1)S(1)}, u32[]{:S(2)}, u32[]{:S(2)}) collective-permute-start(f16[256,256]{1,0:T(8,128)(2,1)S(1)} %add_convert_fusion.1), channel_id=1, source_target_pairs={{0,12},{1,13},{2,14},{3,15},{4,8},{5,9},{6,10},{7,11},{8,4},{9,5},... | collective-permute-start | bytes 393224 | tf_op jit(solution)/shard_map/ppermute | solution.py:255
  71.9 8.9 %collective-permute-start.22 = (f16[256,256]{1,0:T(8,128)(2,1)S(1)}, f16[256,256]{1,0:T(8,128)(2,1)S(1)}, u32[]{:S(2)}, u32[]{:S(2)}) collective-permute-start(f16[256,256]{1,0:T(8,128)(2,1)S(1)} %add_convert_fusion.2), channel_id=1, source_target_pairs={{0,6},{1,7},{2,4},{3,5},{4,2},{5,3},{6,0},{7,1},{8,14},{9,15},{10,... | collective-permute-start | bytes 393224 | tf_op jit(solution)/shard_map/ppermute | solution.py:284
  76.0 8.5 %collective-permute-start.21 = (f16[256,256]{1,0:T(8,128)(2,1)S(1)}, f16[256,256]{1,0:T(8,128)(2,1)S(1)}, u32[]{:S(2)}, u32[]{:S(2)}) collective-permute-start(f16[256,256]{1,0:T(8,128)(2,1)S(1)} %add_convert_fusion.2), channel_id=1, source_target_pairs={{0,2},{1,5},{2,0},{3,7},{4,6},{5,1},{6,4},{7,3},{8,10},{9,13},{10,... | collective-permute-start | bytes 393224 | tf_op jit(solution)/shard_map/ppermute | solution.py:255
  77.1 7.5 %collective-permute-start.20 = (f16[256,256]{1,0:T(8,128)(2,1)S(1)}, f16[256,256]{1,0:T(8,128)(2,1)S(1)}, u32[]{:S(2)}, u32[]{:S(2)}) collective-permute-start(f16[256,256]{1,0:T(8,128)(2,1)S(1)} %add_convert_fusion.2), channel_id=1, source_target_pairs={{0,4},{1,3},{2,6},{3,1},{4,0},{5,7},{6,2},{7,5},{8,12},{9,11},{10,... | collective-permute-start | bytes 393224 | tf_op jit(solution)/shard_map/ppermute | solution.py:255
  77.2 8.9 %collective-permute-start.28 = (f16[256,256]{1,0:T(8,128)(2,1)S(1)}, f16[256,256]{1,0:T(8,128)(2,1)S(1)}, u32[]{:S(2)}, u32[]{:S(2)}) collective-permute-start(f16[256,256]{1,0:T(8,128)(2,1)S(1)} %add_convert_fusion), channel_id=1, source_target_pairs={{0,6},{1,7},{2,4},{3,5},{4,2},{5,3},{6,0},{7,1},{8,14},{9,15},{10,... | collective-permute-start | bytes 393224 | tf_op jit(solution)/shard_map/ppermute | solution.py:284
  79.6 7.5 %collective-permute-start.27 = (f16[256,256]{1,0:T(8,128)(2,1)S(1)}, f16[256,256]{1,0:T(8,128)(2,1)S(1)}, u32[]{:S(2)}, u32[]{:S(2)}) collective-permute-start(f16[256,256]{1,0:T(8,128)(2,1)S(1)} %add_convert_fusion), channel_id=1, source_target_pairs={{0,2},{1,5},{2,0},{3,7},{4,6},{5,1},{6,4},{7,3},{8,10},{9,13},{10,... | collective-permute-start | bytes 393224 | tf_op jit(solution)/shard_map/ppermute | solution.py:255
  80.7 6.5 %collective-permute-start.26 = (f16[256,256]{1,0:T(8,128)(2,1)S(1)}, f16[256,256]{1,0:T(8,128)(2,1)S(1)}, u32[]{:S(2)}, u32[]{:S(2)}) collective-permute-start(f16[256,256]{1,0:T(8,128)(2,1)S(1)} %add_convert_fusion), channel_id=1, source_target_pairs={{0,4},{1,3},{2,6},{3,1},{4,0},{5,7},{6,2},{7,5},{8,12},{9,11},{10,... | collective-permute-start | bytes 393224 | tf_op jit(solution)/shard_map/ppermute | solution.py:255
  87.8 1.2 %collective-permute-start.29 = (f32[8,128]{1,0:T(8,128)S(1)}, f32[8,128]{1,0:T(8,128)S(1)}, u32[]{:S(2)}, u32[]{:S(2)}) collective-permute-start(f32[8,128]{1,0:T(8,128)S(1)} %correlate.3.corr_a), channel_id=1, source_target_pairs={{0,1},{1,0},{2,3},{3,2},{4,5},{5,4},{6,7},{7,6},{8,9},{9,8},{10,11... | collective-permute-start | bytes 12296 | tf_op jit(solution)/shard_map/ppermute | solution.py:258
  90.1 1.2 %collective-permute-start.30 = (f32[8,128]{1,0:T(8,128)S(1)}, f32[8,128]{1,0:T(8,128)S(1)}, u32[]{:S(2)}, u32[]{:S(2)}) collective-permute-start(f32[8,128]{1,0:T(8,128)S(1)} %get-tuple-element.63.weight_a), channel_id=1, source_target_pairs={{0,1},{1,0},{2,3},{3,2},{4,5},{5,4},{6,7},{7,6},{8,9},{9,8},{10,11... | collective-permute-start | bytes 12296 | tf_op jit(solution)/shard_map/ppermute | solution.py:258

commit v10 on v9

--- a/solution.py
+++ b/solution.py
@@ -19,7 +19,7 @@
 VMEM = pl.BlockSpec(memory_space=pltpu.VMEM)
 SMEM = pl.BlockSpec(memory_space=pltpu.SMEM)
 ONE = SDS((8, 128), F32)
-ORDER = ((1, 2), (2, 1))
+ORDER = ((2, 1), (1, 2))
 
 
 def in_hbm(x):
@@ -259,7 +259,7 @@
 
     me, core = lax.axis_index("op").astype(jnp.uint32), lax.axis_index("col").astype(jnp.uint32)
     low, high = me & 1, ((me >> 1) ^ (me >> 2)) & 1
-    bit0, bit1 = jnp.where(core == 0, low, high), jnp.where(core == 0, high, low)
+    bit0, bit1 = jnp.where(core == 0, high, low), jnp.where(core == 0, low, high)
     low_near, low_half, zero = bit1 == 0, bit0 == 0, jnp.zeros((), jnp.uint32)
     keep_at, send_at = bit1 * quarter, (1 - bit1) * quarter
     wave_coef, keep_at, send_at, low_near, low_half = lax.optimization_barrier(

time: 93.2 us -> 93.2 us (level)
  waiting for transfers between devices: 19.3 us -> 24.1 us
  starting transfers between devices: 49.9 us -> 45.2 us
    ppermute x20, starting transfers between devices: 34.7 us -> 25.5 us  [swap(): return lax.ppermute(x, BOTH, pairing)]
    ppermute x4, starting transfers between devices: 13.7 us -> 18.1 us  [gathered(): lax.ppermute(piece, BOTH, [(o * cols + c, (o ^ 3) * cols + c) for o in ra...]
    ppermute x20, waiting for transfers between devices: 13.2 us -> 15.9 us  [swap(): return lax.ppermute(x, BOTH, pairing)]
    ppermute x4, waiting for transfers between devices: 1.9 us -> 4.04 us  [gathered(): lax.ppermute(piece, BOTH, [(o * cols + c, (o ^ 3) * cols + c) for o in ra...]
  transfers between devices with their start and end apart: 31 -> 31, of which waited for: 15 -> 22; matrix products, arithmetic and copies ran while one was open for 2% -> 2% of each run, Pallas kernels for 13% -> 13%
where the time goes in v10:
time: 93.2 us; the launch traced here: 93 us
  starting transfers between devices  45.2 us (48%)
  waiting for transfers between devices  24.1 us (26%)
  Pallas kernels  20.7 us (22%)
  other arithmetic  2.29 us (2%)
    ppermute x20, starting transfers between devices, swap(): return lax.ppermute(x, BOTH, pairing)  25.5 us
    pallas_call x17, Pallas kernels, call(): pl.pallas_call(kernel, out_shape=outs, in_specs=in_specs, out_specs=out_s...  20.7 us
    ppermute x4, starting transfers between devices, gathered(): lax.ppermute(piece, BOTH, [(o * cols + c, (o ^ 3) * cols + c) for o in ra...  18.1 us
    ppermute x20, waiting for transfers between devices, swap(): return lax.ppermute(x, BOTH, pairing)  15.9 us
    ppermute x7, waiting for transfers between devices, across(): return lax.ppermute(x, 'col', [(c, c ^ 1) for c in range(cols)])  4.21 us
    ppermute x4, waiting for transfers between devices, gathered(): lax.ppermute(piece, BOTH, [(o * cols + c, (o ^ 3) * cols + c) for o in ra...  4.04 us
  transfers between devices with their start and end apart: 31, of which 22 were waited for; matrix products, arithmetic and copies ran while one was open for 2% of the time, Pallas kernels for 13%

profile of v10, /device:TPU:0, one launch (start us, length us, event | category | flops | bytes accessed | tf_op | source)
XLA Modules:
  0.0 93.0 jit_solution(2498125750472435320)
XLA Ops:
  0.0 1.7 %open_vector.1 = (bf16[1024,512]{1,0:T(8,128)(2,1)S(1)}, f32[8,128]{1,0:T(8,128)S(1)}) custom-call(f32[1024,512]{1,0:T(8,128)} %vector_ref.1), custom_call_target="tpu_custom_call" | custom-call | flops 1572864 | bytes 4194304 | tf_op jit(solution)/shard_map/open_vector/pallas_call | solution.py:30
  1.7 0.5 collective-permute-start.1
  2.4 2.3 %sent_operators.1.masked_ref = bf16[512,2048]{1,0:T(8,128)(2,1)S(1)} custom-call(s32[128]{0:T(128)S(1)} %reshape.3.mask_ref, bf16[2,1024,1024]{2,1,0:T(8,128)(2,1)} %left_ref.3), custom_call_target="tpu_custom_call" | custom-call | flops 2097152 | bytes 4194304 | tf_op jit(solution)/shard_map/sent_operators/pallas_call | solution.py:30
  4.7 1.8 %sent_half_0.2 = (bf16[2048,256]{1,0:T(8,128)(2,1)S(1)}, f32[512,256]{1,0:T(8,128)S(1)}) custom-call(f32[8,128]{1,0:T(8,128)S(1)} %get-tuple-element.38.a_ref.weight_a, f32[8,128]{1,0:T(8,128)S(1)} %collective-permute-done.b_ref.weight_b, bf16[1024,512]{1,0:T(8,128)(2,1)S(1)} %get-tuple-element.41.own_ref, ...), custom_call_target="tpu_custom_call" | custom-call | flops 1610612736 | bytes 1048576 | tf_op jit(solution)/shard_map/sent_half_0/pallas_call | solution.py:30
  6.6 3.1 %collective-permute-start.2 = (f16[512,256]{1,0:T(8,128)(2,1)S(1)}, f16[512,256]{1,0:T(8,128)(2,1)S(1)}, u32[]{:S(2)}, u32[]{:S(2)}) collective-permute-start(f16[512,256]{1,0:T(8,128)(2,1)S(1)} %convert_element_type.116), channel_id=1, source_target_pairs={{0,4},{1,3},{2,6},{3,1},{4,0},{5,7},{6,2},{7,5},{8,12},{9,11},{10,... | collective-permute-start | bytes 786440 | tf_op jit(solution)/shard_map/ppermute | solution.py:255
  9.7 1.8 %sent_half_1.2 = (bf16[2048,256]{1,0:T(8,128)(2,1)S(1)}, f32[512,256]{1,0:T(8,128)S(1)}) custom-call(f32[8,128]{1,0:T(8,128)S(1)} %get-tuple-element.38.a_ref.weight_a, f32[8,128]{1,0:T(8,128)S(1)} %collective-permute-done.b_ref.weight_b, bf16[1024,512]{1,0:T(8,128)(2,1)S(1)} %get-tuple-element.41.own_ref, ...), custom_call_target="tpu_custom_call" | custom-call | flops 1610612736 | bytes 1048576 | tf_op jit(solution)/shard_map/sent_half_1/pallas_call | solution.py:30
  11.6 2.2 %kept_operators.1.masked_ref = bf16[512,2048]{1,0:T(8,128)(2,1)S(1)} custom-call(s32[128]{0:T(128)S(1)} %reshape.3.mask_ref, bf16[2,1024,1024]{2,1,0:T(8,128)(2,1)} %left_ref.3), custom_call_target="tpu_custom_call" | custom-call | flops 2097152 | bytes 4194304 | tf_op jit(solution)/shard_map/kept_operators/pallas_call | solution.py:30
  13.8 0.7 kept_half.4
  14.7 2.0 %collective-permute-start.3 = (f16[256,256]{1,0:T(8,128)(2,1)S(1)}, f16[256,256]{1,0:T(8,128)(2,1)S(1)}, u32[]{:S(2)}, u32[]{:S(2)}) collective-permute-start(f16[256,256]{1,0:T(8,128)(2,1)S(1)} %dynamic-slice_convert_fusion.3), channel_id=1, source_target_pairs={{0,2},{1,5},{2,0},{3,7},{4,6},{5,1},{6,4},{7,3},{8,10},{9,13},{10,... | collective-permute-start | bytes 393224 | tf_op jit(solution)/shard_map/ppermute | solution.py:255
  16.7 0.7 kept_half.5
  17.4 1.3 %collective-permute-done.8 = f16[512,256]{1,0:T(8,128)(2,1)S(1)} collective-permute-done((f16[512,256]{1,0:T(8,128)(2,1)S(1)}, f16[512,256]{1,0:T(8,128)(2,1)S(1)}, u32[]{:S(2)}, u32[]{:S(2)}) %collective-permute-start.8) | collective-permute-done | bytes 262176 | tf_op jit(solution)/shard_map/ppermute | solution.py:255
  18.9 1.4 %collective-permute-start.9 = (f16[256,256]{1,0:T(8,128)(2,1)S(1)}, f16[256,256]{1,0:T(8,128)(2,1)S(1)}, u32[]{:S(2)}, u32[]{:S(2)}) collective-permute-start(f16[256,256]{1,0:T(8,128)(2,1)S(1)} %dynamic-slice_convert_fusion.2), channel_id=1, source_target_pairs={{0,2},{1,5},{2,0},{3,7},{4,6},{5,1},{6,4},{7,3},{8,10},{9,13},{10,... | collective-permute-start | bytes 393224 | tf_op jit(solution)/shard_map/ppermute | solution.py:255
  20.3 3.5 %collective-permute-start.4 = (f16[256,256]{1,0:T(8,128)(2,1)S(1)}, f16[256,256]{1,0:T(8,128)(2,1)S(1)}, u32[]{:S(2)}, u32[]{:S(2)}) collective-permute-start(f16[256,256]{1,0:T(8,128)(2,1)S(1)} %add_convert_fusion.7), channel_id=1, source_target_pairs={{0,12},{1,13},{2,14},{3,15},{4,8},{5,9},{6,10},{7,11},{8,4},{9,5},... | collective-permute-start | bytes 393224 | tf_op jit(solution)/shard_map/ppermute | solution.py:255
  23.9 2.4 %collective-permute-start.10 = (f16[256,256]{1,0:T(8,128)(2,1)S(1)}, f16[256,256]{1,0:T(8,128)(2,1)S(1)}, u32[]{:S(2)}, u32[]{:S(2)}) collective-permute-start(f16[256,256]{1,0:T(8,128)(2,1)S(1)} %add_convert_fusion.5), channel_id=1, source_target_pairs={{0,12},{1,13},{2,14},{3,15},{4,8},{5,9},{6,10},{7,11},{8,4},{9,5},... | collective-permute-start | bytes 393224 | tf_op jit(solution)/shard_map/ppermute | solution.py:255
  26.3 1.6 %collective-permute-done.4 = f16[256,256]{1,0:T(8,128)(2,1)S(1)} collective-permute-done((f16[256,256]{1,0:T(8,128)(2,1)S(1)}, f16[256,256]{1,0:T(8,128)(2,1)S(1)}, u32[]{:S(2)}, u32[]{:S(2)}) %collective-permute-start.4) | collective-permute-done | bytes 131104 | tf_op jit(solution)/shard_map/ppermute | solution.py:255
  28.0 6.2 %collective-permute-start.7 = (f16[256,256]{1,0:T(8,128)(2,1)S(1)}, f16[256,256]{1,0:T(8,128)(2,1)S(1)}, u32[]{:S(2)}, u32[]{:S(2)}) collective-permute-start(f16[256,256]{1,0:T(8,128)(2,1)S(1)} %add_convert_fusion.6), channel_id=1, source_target_pairs={{0,6},{1,7},{2,4},{3,5},{4,2},{5,3},{6,0},{7,1},{8,14},{9,15},{10,... | collective-permute-start | bytes 393224 | tf_op jit(solution)/shard_map/ppermute | solution.py:284
  34.2 0.6 collective-permute-start.5
  34.9 2.9 %collective-permute-start.13 = (f16[256,256]{1,0:T(8,128)(2,1)S(1)}, f16[256,256]{1,0:T(8,128)(2,1)S(1)}, u32[]{:S(2)}, u32[]{:S(2)}) collective-permute-start(f16[256,256]{1,0:T(8,128)(2,1)S(1)} %add_convert_fusion.4), channel_id=1, source_target_pairs={{0,6},{1,7},{2,4},{3,5},{4,2},{5,3},{6,0},{7,1},{8,14},{9,15},{10,... | collective-permute-start | bytes 393224 | tf_op jit(solution)/shard_map/ppermute | solution.py:284
  37.8 0.8 collective-permute-done.7
  38.7 0.5 collective-permute-start.11
  39.2 1.5 %collective-permute-done.6 = f16[256,256]{1,0:T(8,128)(2,1)S(1)} collective-permute-done((f16[256,256]{1,0:T(8,128)(2,1)S(1)}, f16[256,256]{1,0:T(8,128)(2,1)S(1)}, u32[]{:S(2)}, u32[]{:S(2)}) %collective-permute-start.6) | collective-permute-done | bytes 131104 | tf_op jit(solution)/shard_map/ppermute | solution.py:255
  40.7 0.7 collective-permute-done.5
  41.6 1.3 %collective-permute-done.13 = f16[256,256]{1,0:T(8,128)(2,1)S(1)} collective-permute-done((f16[256,256]{1,0:T(8,128)(2,1)S(1)}, f16[256,256]{1,0:T(8,128)(2,1)S(1)}, u32[]{:S(2)}, u32[]{:S(2)}) %collective-permute-start.13) | collective-permute-done | bytes 131104 | tf_op jit(solution)/shard_map/ppermute | solution.py:284
  42.9 0.7 collective-permute-done.12
  43.5 0.7 collective-permute-done.11
  44.4 0.2 maximum_convert_fusion
  44.6 0.3 correlate.2.corr_a
  45.0 1.2 %collective-permute-done.14.corr_b = f32[8,128]{1,0:T(8,128)S(1)} collective-permute-done((f32[8,128]{1,0:T(8,128)S(1)}, f32[8,128]{1,0:T(8,128)S(1)}, u32[]{:S(2)}, u32[]{:S(2)}) %collective-permute-start.14) | collective-permute-done | bytes 4128 | tf_op jit(solution)/shard_map/ppermute | solution.py:258
  46.2 1.0 %correct.2 = (f32[1024,512]{1,0:T(8,128)S(1)}, f32[8,128]{1,0:T(8,128)S(1)}, bf16[1024,512]{1,0:T(8,128)(2,1)S(1)}) custom-call(f32[8,128]{1,0:T(8,128)S(1)} %correlate.2.corr_a, f32[8,128]{1,0:T(8,128)S(1)} %collective-permute-done.14.corr_b, f32[8,128]{1,0:T(8,128)S(1)} %get-tuple-element.38.a_ref.weight_a, ...), custom_call_target="tpu_custom_call" | custom-call | flops 6291456 | bytes 1048576 | tf_op jit(solution)/shard_map/correct/pallas_call | solution.py:30
  47.3 0.2 collective-permute-start.16
  47.5 0.4 collective-permute-start.15
  47.8 1.2 %own_part.1.own_ref = f32[2048,512]{1,0:T(8,128)S(1)} custom-call(bf16[1024,512]{1,0:T(8,128)(2,1)S(1)} %get-tuple-element.54.own_ref, bf16[2,1024,512]{2,1,0:T(8,128)(2,1)S(1)} %copy-done), custom_call_target="tpu_custom_call" | custom-call | flops 1073741824 | bytes 1048576 | tf_op jit(solution)/shard_map/own_part/pallas_call | solution.py:30
  49.1 0.9 collective-permute-done.15.b_ref.weight_b
  50.0 1.3 %sent_half_0.3 = (bf16[2048,256]{1,0:T(8,128)(2,1)S(1)}, f32[512,256]{1,0:T(8,128)S(1)}) custom-call(f32[8,128]{1,0:T(8,128)S(1)} %get-tuple-element.53.a_ref.weight_a, f32[8,128]{1,0:T(8,128)S(1)} %collective-permute-done.15.b_ref.weight_b, f32[2048,512]{1,0:T(8,128)S(1)} %own_part.1.own_ref, bf16[1024,512]{1,0:T(8,128)(2,1)S(1)} %collective-permute-done.16.other_ref, ...), custom_call_target="tpu_custom_call" | custom-call | flops 1610612736 | bytes 1048576 | tf_op jit(solution)/shard_map/sent_half_0/pallas_call | solution.py:30
  51.3 1.9 %collective-permute-start.17 = (f16[512,256]{1,0:T(8,128)(2,1)S(1)}, f16[512,256]{1,0:T(8,128)(2,1)S(1)}, u32[]{:S(2)}, u32[]{:S(2)}) collective-permute-start(f16[512,256]{1,0:T(8,128)(2,1)S(1)} %convert_element_type.134), channel_id=1, source_target_pairs={{0,4},{1,3},{2,6},{3,1},{4,0},{5,7},{6,2},{7,5},{8,12},{9,11},{10,... | collective-permute-start | bytes 786440 | tf_op jit(solution)/shard_map/ppermute | solution.py:255
  53.2 1.3 %sent_half_1.3 = (bf16[2048,256]{1,0:T(8,128)(2,1)S(1)}, f32[512,256]{1,0:T(8,128)S(1)}) custom-call(f32[8,128]{1,0:T(8,128)S(1)} %get-tuple-element.53.a_ref.weight_a, f32[8,128]{1,0:T(8,128)S(1)} %collective-permute-done.15.b_ref.weight_b, f32[2048,512]{1,0:T(8,128)S(1)} %own_part.1.own_ref, bf16[1024,512]{1,0:T(8,128)(2,1)S(1)} %collective-permute-done.16.other_ref, ...), custom_call_target="tpu_custom_call" | custom-call | flops 1610612736 | bytes 1048576 | tf_op jit(solution)/shard_map/sent_half_1/pallas_call | solution.py:30
  54.6 0.3 collective-permute-start.23
  54.9 0.7 kept_half.6
  55.6 2.2 %collective-permute-done.17 = f16[512,256]{1,0:T(8,128)(2,1)S(1)} collective-permute-done((f16[512,256]{1,0:T(8,128)(2,1)S(1)}, f16[512,256]{1,0:T(8,128)(2,1)S(1)}, u32[]{:S(2)}, u32[]{:S(2)}) %collective-permute-start.17) | collective-permute-done | bytes 262176 | tf_op jit(solution)/shard_map/ppermute | solution.py:255
  57.9 0.2 dynamic-slice_convert_fusion.1
  58.1 1.3 %collective-permute-start.18 = (f16[256,256]{1,0:T(8,128)(2,1)S(1)}, f16[256,256]{1,0:T(8,128)(2,1)S(1)}, u32[]{:S(2)}, u32[]{:S(2)}) collective-permute-start(f16[256,256]{1,0:T(8,128)(2,1)S(1)} %dynamic-slice_convert_fusion.1), channel_id=1, source_target_pairs={{0,2},{1,5},{2,0},{3,7},{4,6},{5,1},{6,4},{7,3},{8,10},{9,13},{10,... | collective-permute-start | bytes 393224 | tf_op jit(solution)/shard_map/ppermute | solution.py:255
  59.4 0.7 kept_half.7
  60.1 1.8 %collective-permute-done.23 = f16[512,256]{1,0:T(8,128)(2,1)S(1)} collective-permute-done((f16[512,256]{1,0:T(8,128)(2,1)S(1)}, f16[512,256]{1,0:T(8,128)(2,1)S(1)}, u32[]{:S(2)}, u32[]{:S(2)}) %collective-permute-start.23) | collective-permute-done | bytes 262176 | tf_op jit(solution)/shard_map/ppermute | solution.py:255
  62.0 1.5 %collective-permute-start.24 = (f16[256,256]{1,0:T(8,128)(2,1)S(1)}, f16[256,256]{1,0:T(8,128)(2,1)S(1)}, u32[]{:S(2)}, u32[]{:S(2)}) collective-permute-start(f16[256,256]{1,0:T(8,128)(2,1)S(1)} %dynamic-slice_convert_fusion), channel_id=1, source_target_pairs={{0,2},{1,5},{2,0},{3,7},{4,6},{5,1},{6,4},{7,3},{8,10},{9,13},{10,... | collective-permute-start | bytes 393224 | tf_op jit(solution)/shard_map/ppermute | solution.py:255
  63.6 3.0 %collective-permute-start.19 = (f16[256,256]{1,0:T(8,128)(2,1)S(1)}, f16[256,256]{1,0:T(8,128)(2,1)S(1)}, u32[]{:S(2)}, u32[]{:S(2)}) collective-permute-start(f16[256,256]{1,0:T(8,128)(2,1)S(1)} %add_convert_fusion.3), channel_id=1, source_target_pairs={{0,12},{1,13},{2,14},{3,15},{4,8},{5,9},{6,10},{7,11},{8,4},{9,5},... | collective-permute-start | bytes 393224 | tf_op jit(solution)/shard_map/ppermute | solution.py:255
  66.6 0.4 collective-permute-done.24
  67.1 2.6 %collective-permute-start.25 = (f16[256,256]{1,0:T(8,128)(2,1)S(1)}, f16[256,256]{1,0:T(8,128)(2,1)S(1)}, u32[]{:S(2)}, u32[]{:S(2)}) collective-permute-start(f16[256,256]{1,0:T(8,128)(2,1)S(1)} %add_convert_fusion.1), channel_id=1, source_target_pairs={{0,12},{1,13},{2,14},{3,15},{4,8},{5,9},{6,10},{7,11},{8,4},{9,5},... | collective-permute-start | bytes 393224 | tf_op jit(solution)/shard_map/ppermute | solution.py:255
  69.7 1.4 %collective-permute-done.19 = f16[256,256]{1,0:T(8,128)(2,1)S(1)} collective-permute-done((f16[256,256]{1,0:T(8,128)(2,1)S(1)}, f16[256,256]{1,0:T(8,128)(2,1)S(1)}, u32[]{:S(2)}, u32[]{:S(2)}) %collective-permute-start.19) | collective-permute-done | bytes 131104 | tf_op jit(solution)/shard_map/ppermute | solution.py:255
  71.2 6.0 %collective-permute-start.22 = (f16[256,256]{1,0:T(8,128)(2,1)S(1)}, f16[256,256]{1,0:T(8,128)(2,1)S(1)}, u32[]{:S(2)}, u32[]{:S(2)}) collective-permute-start(f16[256,256]{1,0:T(8,128)(2,1)S(1)} %add_convert_fusion.2), channel_id=1, source_target_pairs={{0,6},{1,7},{2,4},{3,5},{4,2},{5,3},{6,0},{7,1},{8,14},{9,15},{10,... | collective-permute-start | bytes 393224 | tf_op jit(solution)/shard_map/ppermute | solution.py:284
  77.2 0.7 collective-permute-start.20
  77.9 2.9 %collective-permute-start.28 = (f16[256,256]{1,0:T(8,128)(2,1)S(1)}, f16[256,256]{1,0:T(8,128)(2,1)S(1)}, u32[]{:S(2)}, u32[]{:S(2)}) collective-permute-start(f16[256,256]{1,0:T(8,128)(2,1)S(1)} %add_convert_fusion), channel_id=1, source_target_pairs={{0,6},{1,7},{2,4},{3,5},{4,2},{5,3},{6,0},{7,1},{8,14},{9,15},{10,... | collective-permute-start | bytes 393224 | tf_op jit(solution)/shard_map/ppermute | solution.py:284
  80.8 0.8 collective-permute-done.22
  81.6 0.6 collective-permute-start.26
  82.2 1.5 %collective-permute-done.21 = f16[256,256]{1,0:T(8,128)(2,1)S(1)} collective-permute-done((f16[256,256]{1,0:T(8,128)(2,1)S(1)}, f16[256,256]{1,0:T(8,128)(2,1)S(1)}, u32[]{:S(2)}, u32[]{:S(2)}) %collective-permute-start.21) | collective-permute-done | bytes 131104 | tf_op jit(solution)/shard_map/ppermute | solution.py:255
  83.7 0.7 collective-permute-done.20
  84.7 1.1 %collective-permute-done.28 = f16[256,256]{1,0:T(8,128)(2,1)S(1)} collective-permute-done((f16[256,256]{1,0:T(8,128)(2,1)S(1)}, f16[256,256]{1,0:T(8,128)(2,1)S(1)}, u32[]{:S(2)}, u32[]{:S(2)}) %collective-permute-start.28) | collective-permute-done | bytes 131104 | tf_op jit(solution)/shard_map/ppermute | solution.py:284
  85.8 0.7 collective-permute-done.27
  86.5 0.7 collective-permute-done.26
  87.5 0.4 correlate.3.corr_a
  87.9 1.2 %collective-permute-done.29.corr_b = f32[8,128]{1,0:T(8,128)S(1)} collective-permute-done((f32[8,128]{1,0:T(8,128)S(1)}, f32[8,128]{1,0:T(8,128)S(1)}, u32[]{:S(2)}, u32[]{:S(2)}) %collective-permute-start.29) | collective-permute-done | bytes 4128 | tf_op jit(solution)/shard_map/ppermute | solution.py:258
  89.1 1.1 %correct.3 = (f32[1024,512]{1,0:T(8,128)S(1)}, f32[8,128]{1,0:T(8,128)S(1)}) custom-call(f32[8,128]{1,0:T(8,128)S(1)} %correlate.3.corr_a, f32[8,128]{1,0:T(8,128)S(1)} %collective-permute-done.29.corr_b, f32[8,128]{1,0:T(8,128)S(1)} %get-tuple-element.53.a_ref.weight_a, f32[8,128]{1,0:T(8,128)S(1)} %collective-permute-done.15.b_ref.weight_b, ...), custom_call_target="tpu_custom_call" | custom-call | flops 6291456 | bytes 1048576 | tf_op jit(solution)/shard_map/correct/pallas_call | solution.py:30
  90.1 0.2 collective-permute-start.30
  90.4 1.0 %collective-permute-done.30.weight_b = f32[8,128]{1,0:T(8,128)S(1)} collective-permute-done((f32[8,128]{1,0:T(8,128)S(1)}, f32[8,128]{1,0:T(8,128)S(1)}, u32[]{:S(2)}, u32[]{:S(2)}) %collective-permute-start.30) | collective-permute-done | bytes 4128 | tf_op jit(solution)/shard_map/ppermute | solution.py:258
  91.4 1.4 %normalise.1 = f32[1024,512]{1,0:T(8,128)} custom-call(f32[8,128]{1,0:T(8,128)S(1)} %get-tuple-element.63.weight_a, f32[8,128]{1,0:T(8,128)S(1)} %collective-permute-done.30.weight_b, f32[1024,512]{1,0:T(8,128)S(1)} %get-tuple-element.64.vector_ref), custom_call_target="tpu_custom_call" | custom-call | flops 524288 | bytes 4194304 | tf_op jit(solution)/shard_map/normalise/pallas_call | solution.py:30
  (51 shorter events, 2.3 us)
Async XLA Ops:
  0.0 2.3 %copy-start.3 = (s32[2,8,8]{2,1,0:T(8,128)S(1)}, s32[2,8,8]{2,1,0:T(8,128)}, u32[]{:S(2)}) copy-start(s32[2,8,8]{2,1,0:T(8,128)} %param.9) | copy-start | bytes 1540
  1.7 3.0 %collective-permute-start.1 = (bf16[1024,512]{1,0:T(8,128)(2,1)S(1)}, bf16[1024,512]{1,0:T(8,128)(2,1)S(1)}, u32[]{:S(2)}, u32[]{:S(2)}) collective-permute-start(bf16[1024,512]{1,0:T(8,128)(2,1)S(1)} %get-tuple-element.41.own_ref), channel_id=1, source_target_pairs={{0,1},{1,0},{2,3},{3,2},{4,5},{5,4},{6,7},{7,6},{8,9},{9,8},{10,11... | collective-permute-start | bytes 3145736 | tf_op jit(solution)/shard_map/ppermute | solution.py:258
  2.3 2.5 %collective-permute-start = (f32[8,128]{1,0:T(8,128)S(1)}, f32[8,128]{1,0:T(8,128)S(1)}, u32[]{:S(2)}, u32[]{:S(2)}) collective-permute-start(f32[8,128]{1,0:T(8,128)S(1)} %get-tuple-element.38.a_ref.weight_a), channel_id=1, source_target_pairs={{0,1},{1,0},{2,3},{3,2},{4,5},{5,4},{6,7},{7,6},{8,9},{9,8},{10,11... | collective-permute-start | bytes 12296 | tf_op jit(solution)/shard_map/ppermute | solution.py:258
  2.4 2.3 %copy-start = (bf16[2,1024,512]{2,1,0:T(8,128)(2,1)S(1)}, bf16[2,1024,512]{2,1,0:T(8,128)(2,1)}, u32[]{:S(2)}) copy-start(bf16[2,1024,512]{2,1,0:T(8,128)(2,1)} %right_ref.9) | copy-start | bytes 6291460
  6.6 8.0 %collective-permute-start.2 = (f16[512,256]{1,0:T(8,128)(2,1)S(1)}, f16[512,256]{1,0:T(8,128)(2,1)S(1)}, u32[]{:S(2)}, u32[]{:S(2)}) collective-permute-start(f16[512,256]{1,0:T(8,128)(2,1)S(1)} %convert_element_type.116), channel_id=1, source_target_pairs={{0,4},{1,3},{2,6},{3,1},{4,0},{5,7},{6,2},{7,5},{8,12},{9,11},{10,... | collective-permute-start | bytes 786440 | tf_op jit(solution)/shard_map/ppermute | solution.py:255
  11.5 7.2 %collective-permute-start.8 = (f16[512,256]{1,0:T(8,128)(2,1)S(1)}, f16[512,256]{1,0:T(8,128)(2,1)S(1)}, u32[]{:S(2)}, u32[]{:S(2)}) collective-permute-start(f16[512,256]{1,0:T(8,128)(2,1)S(1)} %convert_element_type.125), channel_id=1, source_target_pairs={{0,4},{1,3},{2,6},{3,1},{4,0},{5,7},{6,2},{7,5},{8,12},{9,11},{10,... | collective-permute-start | bytes 786440 | tf_op jit(solution)/shard_map/ppermute | solution.py:255
  14.7 5.6 %collective-permute-start.3 = (f16[256,256]{1,0:T(8,128)(2,1)S(1)}, f16[256,256]{1,0:T(8,128)(2,1)S(1)}, u32[]{:S(2)}, u32[]{:S(2)}) collective-permute-start(f16[256,256]{1,0:T(8,128)(2,1)S(1)} %dynamic-slice_convert_fusion.3), channel_id=1, source_target_pairs={{0,2},{1,5},{2,0},{3,7},{4,6},{5,1},{6,4},{7,3},{8,10},{9,13},{10,... | collective-permute-start | bytes 393224 | tf_op jit(solution)/shard_map/ppermute | solution.py:255
  18.9 5.0 %collective-permute-start.9 = (f16[256,256]{1,0:T(8,128)(2,1)S(1)}, f16[256,256]{1,0:T(8,128)(2,1)S(1)}, u32[]{:S(2)}, u32[]{:S(2)}) collective-permute-start(f16[256,256]{1,0:T(8,128)(2,1)S(1)} %dynamic-slice_convert_fusion.2), channel_id=1, source_target_pairs={{0,2},{1,5},{2,0},{3,7},{4,6},{5,1},{6,4},{7,3},{8,10},{9,13},{10,... | collective-permute-start | bytes 393224 | tf_op jit(solution)/shard_map/ppermute | solution.py:255
  20.3 7.6 %collective-permute-start.4 = (f16[256,256]{1,0:T(8,128)(2,1)S(1)}, f16[256,256]{1,0:T(8,128)(2,1)S(1)}, u32[]{:S(2)}, u32[]{:S(2)}) collective-permute-start(f16[256,256]{1,0:T(8,128)(2,1)S(1)} %add_convert_fusion.7), channel_id=1, source_target_pairs={{0,12},{1,13},{2,14},{3,15},{4,8},{5,9},{6,10},{7,11},{8,4},{9,5},... | collective-permute-start | bytes 393224 | tf_op jit(solution)/shard_map/ppermute | solution.py:255
  23.9 10.9 %collective-permute-start.10 = (f16[256,256]{1,0:T(8,128)(2,1)S(1)}, f16[256,256]{1,0:T(8,128)(2,1)S(1)}, u32[]{:S(2)}, u32[]{:S(2)}) collective-permute-start(f16[256,256]{1,0:T(8,128)(2,1)S(1)} %add_convert_fusion.5), channel_id=1, source_target_pairs={{0,12},{1,13},{2,14},{3,15},{4,8},{5,9},{6,10},{7,11},{8,4},{9,5},... | collective-permute-start | bytes 393224 | tf_op jit(solution)/shard_map/ppermute | solution.py:255
  28.0 10.7 %collective-permute-start.7 = (f16[256,256]{1,0:T(8,128)(2,1)S(1)}, f16[256,256]{1,0:T(8,128)(2,1)S(1)}, u32[]{:S(2)}, u32[]{:S(2)}) collective-permute-start(f16[256,256]{1,0:T(8,128)(2,1)S(1)} %add_convert_fusion.6), channel_id=1, source_target_pairs={{0,6},{1,7},{2,4},{3,5},{4,2},{5,3},{6,0},{7,1},{8,14},{9,15},{10,... | collective-permute-start | bytes 393224 | tf_op jit(solution)/shard_map/ppermute | solution.py:284
  34.2 6.5 %collective-permute-start.6 = (f16[256,256]{1,0:T(8,128)(2,1)S(1)}, f16[256,256]{1,0:T(8,128)(2,1)S(1)}, u32[]{:S(2)}, u32[]{:S(2)}) collective-permute-start(f16[256,256]{1,0:T(8,128)(2,1)S(1)} %add_convert_fusion.6), channel_id=1, source_target_pairs={{0,4},{1,3},{2,6},{3,1},{4,0},{5,7},{6,2},{7,5},{8,12},{9,11},{10,... | collective-permute-start | bytes 393224 | tf_op jit(solution)/shard_map/ppermute | solution.py:255
  34.2 7.2 %collective-permute-start.5 = (f16[256,256]{1,0:T(8,128)(2,1)S(1)}, f16[256,256]{1,0:T(8,128)(2,1)S(1)}, u32[]{:S(2)}, u32[]{:S(2)}) collective-permute-start(f16[256,256]{1,0:T(8,128)(2,1)S(1)} %add_convert_fusion.6), channel_id=1, source_target_pairs={{0,2},{1,5},{2,0},{3,7},{4,6},{5,1},{6,4},{7,3},{8,10},{9,13},{10,... | collective-permute-start | bytes 393224 | tf_op jit(solution)/shard_map/ppermute | solution.py:255
  34.9 7.9 %collective-permute-start.13 = (f16[256,256]{1,0:T(8,128)(2,1)S(1)}, f16[256,256]{1,0:T(8,128)(2,1)S(1)}, u32[]{:S(2)}, u32[]{:S(2)}) collective-permute-start(f16[256,256]{1,0:T(8,128)(2,1)S(1)} %add_convert_fusion.4), channel_id=1, source_target_pairs={{0,6},{1,7},{2,4},{3,5},{4,2},{5,3},{6,0},{7,1},{8,14},{9,15},{10,... | collective-permute-start | bytes 393224 | tf_op jit(solution)/shard_map/ppermute | solution.py:284
  37.8 5.7 %collective-permute-start.12 = (f16[256,256]{1,0:T(8,128)(2,1)S(1)}, f16[256,256]{1,0:T(8,128)(2,1)S(1)}, u32[]{:S(2)}, u32[]{:S(2)}) collective-permute-start(f16[256,256]{1,0:T(8,128)(2,1)S(1)} %add_convert_fusion.4), channel_id=1, source_target_pairs={{0,4},{1,3},{2,6},{3,1},{4,0},{5,7},{6,2},{7,5},{8,12},{9,11},{10,... | collective-permute-start | bytes 393224 | tf_op jit(solution)/shard_map/ppermute | solution.py:255
  38.7 5.5 %collective-permute-start.11 = (f16[256,256]{1,0:T(8,128)(2,1)S(1)}, f16[256,256]{1,0:T(8,128)(2,1)S(1)}, u32[]{:S(2)}, u32[]{:S(2)}) collective-permute-start(f16[256,256]{1,0:T(8,128)(2,1)S(1)} %add_convert_fusion.4), channel_id=1, source_target_pairs={{0,2},{1,5},{2,0},{3,7},{4,6},{5,1},{6,4},{7,3},{8,10},{9,13},{10,... | collective-permute-start | bytes 393224 | tf_op jit(solution)/shard_map/ppermute | solution.py:255
  41.6 3.0 %copy-start.1 = (f32[1024,512]{1,0:T(8,128)S(1)}, f32[1024,512]{1,0:T(8,128)}, u32[]{:S(2)}) copy-start(f32[1024,512]{1,0:T(8,128)} %vector_ref.1) | copy-start | bytes 6291460
  44.6 1.6 %copy-start.2 = (f32[1024,512]{1,0:T(8,128)S(1)}, f32[1024,512]{1,0:T(8,128)}, u32[]{:S(2)}) copy-start(f32[1024,512]{1,0:T(8,128)} %diag_ref.3) | copy-start | bytes 6291460
  44.9 1.2 %collective-permute-start.14 = (f32[8,128]{1,0:T(8,128)S(1)}, f32[8,128]{1,0:T(8,128)S(1)}, u32[]{:S(2)}, u32[]{:S(2)}) collective-permute-start(f32[8,128]{1,0:T(8,128)S(1)} %correlate.2.corr_a), channel_id=1, source_target_pairs={{0,1},{1,0},{2,3},{3,2},{4,5},{5,4},{6,7},{7,6},{8,9},{9,8},{10,11... | collective-permute-start | bytes 12296 | tf_op jit(solution)/shard_map/ppermute | solution.py:258
  47.3 2.7 %collective-permute-start.16 = (bf16[1024,512]{1,0:T(8,128)(2,1)S(1)}, bf16[1024,512]{1,0:T(8,128)(2,1)S(1)}, u32[]{:S(2)}, u32[]{:S(2)}) collective-permute-start(bf16[1024,512]{1,0:T(8,128)(2,1)S(1)} %get-tuple-element.54.own_ref), channel_id=1, source_target_pairs={{0,1},{1,0},{2,3},{3,2},{4,5},{5,4},{6,7},{7,6},{8,9},{9,8},{10,11... | collective-permute-start | bytes 3145736 | tf_op jit(solution)/shard_map/ppermute | solution.py:258
  47.5 2.5 %collective-permute-start.15 = (f32[8,128]{1,0:T(8,128)S(1)}, f32[8,128]{1,0:T(8,128)S(1)}, u32[]{:S(2)}, u32[]{:S(2)}) collective-permute-start(f32[8,128]{1,0:T(8,128)S(1)} %get-tuple-element.53.a_ref.weight_a), channel_id=1, source_target_pairs={{0,1},{1,0},{2,3},{3,2},{4,5},{5,4},{6,7},{7,6},{8,9},{9,8},{10,11... | collective-permute-start | bytes 12296 | tf_op jit(solution)/shard_map/ppermute | solution.py:258
  51.3 6.4 %collective-permute-start.17 = (f16[512,256]{1,0:T(8,128)(2,1)S(1)}, f16[512,256]{1,0:T(8,128)(2,1)S(1)}, u32[]{:S(2)}, u32[]{:S(2)}) collective-permute-start(f16[512,256]{1,0:T(8,128)(2,1)S(1)} %convert_element_type.134), channel_id=1, source_target_pairs={{0,4},{1,3},{2,6},{3,1},{4,0},{5,7},{6,2},{7,5},{8,12},{9,11},{10,... | collective-permute-start | bytes 786440 | tf_op jit(solution)/shard_map/ppermute | solution.py:255
  54.6 7.3 %collective-permute-start.23 = (f16[512,256]{1,0:T(8,128)(2,1)S(1)}, f16[512,256]{1,0:T(8,128)(2,1)S(1)}, u32[]{:S(2)}, u32[]{:S(2)}) collective-permute-start(f16[512,256]{1,0:T(8,128)(2,1)S(1)} %convert_element_type.143), channel_id=1, source_target_pairs={{0,4},{1,3},{2,6},{3,1},{4,0},{5,7},{6,2},{7,5},{8,12},{9,11},{10,... | collective-permute-start | bytes 786440 | tf_op jit(solution)/shard_map/ppermute | solution.py:255
  58.1 5.4 %collective-permute-start.18 = (f16[256,256]{1,0:T(8,128)(2,1)S(1)}, f16[256,256]{1,0:T(8,128)(2,1)S(1)}, u32[]{:S(2)}, u32[]{:S(2)}) collective-permute-start(f16[256,256]{1,0:T(8,128)(2,1)S(1)} %dynamic-slice_convert_fusion.1), channel_id=1, source_target_pairs={{0,2},{1,5},{2,0},{3,7},{4,6},{5,1},{6,4},{7,3},{8,10},{9,13},{10,... | collective-permute-start | bytes 393224 | tf_op jit(solution)/shard_map/ppermute | solution.py:255
  62.0 5.0 %collective-permute-start.24 = (f16[256,256]{1,0:T(8,128)(2,1)S(1)}, f16[256,256]{1,0:T(8,128)(2,1)S(1)}, u32[]{:S(2)}, u32[]{:S(2)}) collective-permute-start(f16[256,256]{1,0:T(8,128)(2,1)S(1)} %dynamic-slice_convert_fusion), channel_id=1, source_target_pairs={{0,2},{1,5},{2,0},{3,7},{4,6},{5,1},{6,4},{7,3},{8,10},{9,13},{10,... | collective-permute-start | bytes 393224 | tf_op jit(solution)/shard_map/ppermute | solution.py:255
  63.6 7.5 %collective-permute-start.19 = (f16[256,256]{1,0:T(8,128)(2,1)S(1)}, f16[256,256]{1,0:T(8,128)(2,1)S(1)}, u32[]{:S(2)}, u32[]{:S(2)}) collective-permute-start(f16[256,256]{1,0:T(8,128)(2,1)S(1)} %add_convert_fusion.3), channel_id=1, source_target_pairs={{0,12},{1,13},{2,14},{3,15},{4,8},{5,9},{6,10},{7,11},{8,4},{9,5},... | collective-permute-start | bytes 393224 | tf_op jit(solution)/shard_map/ppermute | solution.py:255
  67.1 10.8 %collective-permute-start.25 = (f16[256,256]{1,0:T(8,128)(2,1)S(1)}, f16[256,256]{1,0:T(8,128)(2,1)S(1)}, u32[]{:S(2)}, u32[]{:S(2)}) collective-permute-start(f16[256,256]{1,0:T(8,128)(2,1)S(1)} %add_convert_fusion.1), channel_id=1, source_target_pairs={{0,12},{1,13},{2,14},{3,15},{4,8},{5,9},{6,10},{7,11},{8,4},{9,5},... | collective-permute-start | bytes 393224 | tf_op jit(solution)/shard_map/ppermute | solution.py:255
  71.2 10.5 %collective-permute-start.22 = (f16[256,256]{1,0:T(8,128)(2,1)S(1)}, f16[256,256]{1,0:T(8,128)(2,1)S(1)}, u32[]{:S(2)}, u32[]{:S(2)}) collective-permute-start(f16[256,256]{1,0:T(8,128)(2,1)S(1)} %add_convert_fusion.2), channel_id=1, source_target_pairs={{0,6},{1,7},{2,4},{3,5},{4,2},{5,3},{6,0},{7,1},{8,14},{9,15},{10,... | collective-permute-start | bytes 393224 | tf_op jit(solution)/shard_map/ppermute | solution.py:284
  77.2 6.5 %collective-permute-start.21 = (f16[256,256]{1,0:T(8,128)(2,1)S(1)}, f16[256,256]{1,0:T(8,128)(2,1)S(1)}, u32[]{:S(2)}, u32[]{:S(2)}) collective-permute-start(f16[256,256]{1,0:T(8,128)(2,1)S(1)} %add_convert_fusion.2), channel_id=1, source_target_pairs={{0,4},{1,3},{2,6},{3,1},{4,0},{5,7},{6,2},{7,5},{8,12},{9,11},{10,... | collective-permute-start | bytes 393224 | tf_op jit(solution)/shard_map/ppermute | solution.py:255
  77.2 7.2 %collective-permute-start.20 = (f16[256,256]{1,0:T(8,128)(2,1)S(1)}, f16[256,256]{1,0:T(8,128)(2,1)S(1)}, u32[]{:S(2)}, u32[]{:S(2)}) collective-permute-start(f16[256,256]{1,0:T(8,128)(2,1)S(1)} %add_convert_fusion.2), channel_id=1, source_target_pairs={{0,2},{1,5},{2,0},{3,7},{4,6},{5,1},{6,4},{7,3},{8,10},{9,13},{10,... | collective-permute-start | bytes 393224 | tf_op jit(solution)/shard_map/ppermute | solution.py:255
  77.9 7.9 %collective-permute-start.28 = (f16[256,256]{1,0:T(8,128)(2,1)S(1)}, f16[256,256]{1,0:T(8,128)(2,1)S(1)}, u32[]{:S(2)}, u32[]{:S(2)}) collective-permute-start(f16[256,256]{1,0:T(8,128)(2,1)S(1)} %add_convert_fusion), channel_id=1, source_target_pairs={{0,6},{1,7},{2,4},{3,5},{4,2},{5,3},{6,0},{7,1},{8,14},{9,15},{10,... | collective-permute-start | bytes 393224 | tf_op jit(solution)/shard_map/ppermute | solution.py:284
  80.8 5.7 %collective-permute-start.27 = (f16[256,256]{1,0:T(8,128)(2,1)S(1)}, f16[256,256]{1,0:T(8,128)(2,1)S(1)}, u32[]{:S(2)}, u32[]{:S(2)}) collective-permute-start(f16[256,256]{1,0:T(8,128)(2,1)S(1)} %add_convert_fusion), channel_id=1, source_target_pairs={{0,4},{1,3},{2,6},{3,1},{4,0},{5,7},{6,2},{7,5},{8,12},{9,11},{10,... | collective-permute-start | bytes 393224 | tf_op jit(solution)/shard_map/ppermute | solution.py:255
  81.6 5.6 %collective-permute-start.26 = (f16[256,256]{1,0:T(8,128)(2,1)S(1)}, f16[256,256]{1,0:T(8,128)(2,1)S(1)}, u32[]{:S(2)}, u32[]{:S(2)}) collective-permute-start(f16[256,256]{1,0:T(8,128)(2,1)S(1)} %add_convert_fusion), channel_id=1, source_target_pairs={{0,2},{1,5},{2,0},{3,7},{4,6},{5,1},{6,4},{7,3},{8,10},{9,13},{10,... | collective-permute-start | bytes 393224 | tf_op jit(solution)/shard_map/ppermute | solution.py:255
  87.8 1.2 %collective-permute-start.29 = (f32[8,128]{1,0:T(8,128)S(1)}, f32[8,128]{1,0:T(8,128)S(1)}, u32[]{:S(2)}, u32[]{:S(2)}) collective-permute-start(f32[8,128]{1,0:T(8,128)S(1)} %correlate.3.corr_a), channel_id=1, source_target_pairs={{0,1},{1,0},{2,3},{3,2},{4,5},{5,4},{6,7},{7,6},{8,9},{9,8},{10,11... | collective-permute-start | bytes 12296 | tf_op jit(solution)/shard_map/ppermute | solution.py:258
  90.1 1.2 %collective-permute-start.30 = (f32[8,128]{1,0:T(8,128)S(1)}, f32[8,128]{1,0:T(8,128)S(1)}, u32[]{:S(2)}, u32[]{:S(2)}) collective-permute-start(f32[8,128]{1,0:T(8,128)S(1)} %get-tuple-element.63.weight_a), channel_id=1, source_target_pairs={{0,1},{1,0},{2,3},{3,2},{4,5},{5,4},{6,7},{7,6},{8,9},{9,8},{10,11... | collective-permute-start | bytes 12296 | tf_op jit(solution)/shard_map/ppermute | solution.py:258
